TPU v7x, 512 devices: a whole 4x4x16 slice. The times are simulated.
512 devices in a mesh: band: 2 (over x_lo), dx: 16 (over z), dy: 16 (over y, x_hi, core).
Axes of the slice: x: 4 (x_hi: 2, x_lo: 2; x = x_hi * 2 + x_lo), y: 4, z: 16, core: 2. Of those that a mesh axis runs over, the one named last changes fastest.
Arguments:
- orbital_block: float32 [16, 192, 128, 128], P('band', 'dx', 'dy'), may hold values from -6 to 6
- potential: float32 [192, 128, 128], P('dx', 'dy'), may hold values from -2 to 0
- resident: bfloat16 [256, 192, 128, 128], P('band', 'dx', 'dy'), may hold values from -0.01953125 to 0.01953125
Outputs:
- projected_block: float32 [16, 192, 128, 128], P('band', 'dx', 'dy')
- block_gram: float32 [16, 16], P('band')
All inputs are finite; a program needn't handle non-finite values.
Results may differ from a plain program's by a relative error of at most 0.0035.
Values may be sent and summed in bfloat16 or wider, within the bound.
No kernel may reach another device: no remote copies, remote signals or barrier semaphores. Data moves between devices by JAX's collectives and lax.ppermute only.
A program may use at most 64 MiB of HBM per device.

v0:
```python
import jax
import jax.numpy as jnp
from jax import lax
from jax.sharding import PartitionSpec as P

DEGREE = 4


STENCIL_WEIGHTS = (
    -5369.0 / 1800.0,
    12.0 / 7.0,
    -15.0 / 56.0,
    10.0 / 189.0,
    -1.0 / 112.0,
    2.0 / 1925.0,
    -1.0 / 16632.0,
)
FILTER_CENTER = 23.0
FILTER_HALF = 21.0


def with_halo(cells, sides, width):
    for axis, dim in sides:
        count = lax.axis_size(axis)
        head = lax.slice_in_dim(cells, 0, width, axis=dim)
        tail = lax.slice_in_dim(cells, cells.shape[dim] - width, cells.shape[dim], axis=dim)
        cells = jnp.concatenate(
            [
                lax.ppermute(tail, axis, [(i, (i + 1) % count) for i in range(count)]),
                cells,
                lax.ppermute(head, axis, [((i + 1) % count, i) for i in range(count)]),
            ],
            axis=dim,
        )
    return cells


def apply_hamiltonian(orbital_field, potential):
    rows_x, rows_y, depth_cells = (
        orbital_field.shape[1],
        orbital_field.shape[2],
        orbital_field.shape[3],
    )
    padded = with_halo(orbital_field, (("dx", 1), ("dy", 2)), 6)
    zpadded = jnp.pad(orbital_field, ((0, 0), (0, 0), (0, 0), (6, 6)))
    stencil_sum = 3.0 * STENCIL_WEIGHTS[0] * orbital_field
    for offset in range(1, 7):
        beside_all = (
            padded[:, 6 + offset : 6 + offset + rows_x, 6 : 6 + rows_y]
            + padded[:, 6 - offset : 6 - offset + rows_x, 6 : 6 + rows_y]
        )
        beside_all = (
            beside_all
            + padded[:, 6 : 6 + rows_x, 6 + offset : 6 + offset + rows_y]
            + padded[:, 6 : 6 + rows_x, 6 - offset : 6 - offset + rows_y]
        )
        beside_all = (
            beside_all
            + zpadded[:, :, :, 6 + offset : 6 + offset + depth_cells]
            + zpadded[:, :, :, 6 - offset : 6 - offset + depth_cells]
        )
        stencil_sum = stencil_sum + STENCIL_WEIGHTS[offset] * beside_all
    return -2.0 * stencil_sum + potential[None] * orbital_field


def shifted(orbital_field, potential):
    return (
        apply_hamiltonian(orbital_field, potential) - FILTER_CENTER * orbital_field
    ) / FILTER_HALF


def shards(orbital_block, potential, resident):
    previous = orbital_block
    current = shifted(orbital_block, potential)
    for degree_step in range(DEGREE - 1):
        following = 2.0 * shifted(current, potential) - previous
        previous, current = (current, following)
    own_count = current.shape[0]
    cell_count = current.shape[1] * current.shape[2] * current.shape[3]
    flattened = current.reshape(own_count, cell_count)
    everyone = lax.all_gather(resident, "band", axis=0, tiled=True).reshape(-1, cell_count)
    local_correlations = jnp.dot(
        everyone, flattened.astype(jnp.bfloat16).T, preferred_element_type=jnp.float32
    )
    correlations = lax.psum(local_correlations, ("dx", "dy"))
    projected = flattened - jnp.dot(
        correlations.astype(jnp.bfloat16).T, everyone, preferred_element_type=jnp.float32
    )
    gathered = lax.all_gather(projected.astype(jnp.bfloat16), "band", axis=0, tiled=True).astype(
        projected.dtype
    )
    partial_gram = jnp.dot(
        projected, gathered.T, precision=lax.Precision.HIGHEST, preferred_element_type=jnp.float32
    )
    total_cells = cell_count * lax.axis_size("dx") * lax.axis_size("dy")
    gram_matrix = lax.psum(partial_gram, ("dx", "dy")) / total_cells
    return (projected.reshape(current.shape), gram_matrix)


def solution(mesh):
    placed = (P("band", "dx", "dy", None), P("dx", "dy", None), P("band", "dx", "dy", None))
    return jax.shard_map(
        shards,
        mesh=mesh,
        in_specs=placed,
        out_specs=(P("band", "dx", "dy", None), P("band", None)),
        check_vma=False,
    )
```

profile of v0, /device:TPU:1, one launch (start us, length us, event | category | flops | bytes accessed | tf_op | source)
XLA Modules:
  0.0 1511.8 jit_solution(15781704155301182445)
XLA Ops:
  8.3 12.0 collective-permute-start
  22.2 3.0 collective-permute-done
  25.3 5.0 collective-permute-done.1
  30.5 3.8 collective-permute-start.2
  34.3 4.5 collective-permute-start.3
  38.9 8.1 collective-permute-done.2
  47.0 4.3 collective-permute-done.3
  51.6 2.5 broadcast_multiply_fusion
  56.2 3.4 collective-permute-start.5
  61.3 3.1 collective-permute-done.5
  64.7 5.7 collective-permute-start.6
  70.4 3.3 collective-permute-start.7
  73.7 15.2 %collective-permute-done.6 = f32[8,24,6,128]{3,1,2,0:T(8,128)S(1)} collective-permute-done((f32[8,24,6,128]{3,1,2,0:T(8,128)S(1)}, f32[8,24,6,128]{3,1,2,0:T(8,128)S(1)}, u32[]{:S(2)}, u32[]{:S(2)}) %collective-permute-start.6) | collective-permute-done | bytes 589856 | tf_op jit(solution)/shard_map/ppermute | solution.py:31
  89.0 6.3 collective-permute-done.7
  95.5 2.6 fusion.122
  100.1 3.4 collective-permute-start.9
  103.5 2.2 collective-permute-done.8
  105.7 2.7 collective-permute-done.9
  108.7 10.3 collective-permute-start.10
  121.0 21.0 %collective-permute-done.10 = f32[8,24,6,128]{3,1,2,0:T(8,128)S(1)} collective-permute-done((f32[8,24,6,128]{3,1,2,0:T(8,128)S(1)}, f32[8,24,6,128]{3,1,2,0:T(8,128)S(1)}, u32[]{:S(2)}, u32[]{:S(2)}) %collective-permute-start.10) | collective-permute-done | bytes 589856 | tf_op jit(solution)/shard_map/ppermute | solution.py:31
  141.9 4.5 collective-permute-done.11
  146.7 2.6 fusion.71
  151.3 3.4 collective-permute-start.13
  156.9 2.7 collective-permute-done.13
  159.9 7.1 collective-permute-start.14
  168.9 10.4 collective-permute-done.14
  180.6 2.6 fusion.227
  183.5 4.7 fusion.4
  188.3 655.4 %psum.14 = bf16[256,8]{0,1:T(8,128)(2,1)S(1)} all-reduce(f32[256,8]{0,1:T(8,128)S(1)} %fusion.4), channel_id=1, replica_groups=mesh['band'=2,'dx'=16,'dy'=16] {'dx','dy'}, use_global_device_ids=true, to_apply=%region_0.1 | all-reduce | flops 2048 | bytes 12288 | tf_op jit(solution)/shard_map/psum | solution.py:85
  843.6 4.6 fusion.238
  848.2 5.2 all_gather.7
  854.0 649.5 %psum.15 = f32[8,16]{1,0:T(8,128)S(1)} all-reduce(f32[8,16]{1,0:T(8,128)S(1)} %fusion.239), channel_id=1, replica_groups=mesh['band'=2,'dx'=16,'dy'=16] {'dx','dy'}, use_global_device_ids=true, to_apply=%region_1.2 | all-reduce | flops 128 | bytes 1024 | tf_op jit(solution)/shard_map/psum | solution.py:96
  (40 shorter events, 22.1 us)
Async XLA Ops:
  7.2 176.4 %all-gather.2.cloned.1.call-start = ((), (), s32[]{:S(2)}) async-start(), calls=%async_computation | async-start | bytes 9437184 | tf_op jit(solution)/shard_map/all_gather | solution.py:81
  8.3 16.9 %collective-permute-start = (f32[8,6,8,128]{3,1,2,0:T(8,128)S(1)}, f32[8,6,8,128]{3,1,2,0:T(8,128)S(1)}, u32[]{:S(2)}, u32[]{:S(2)}) collective-permute-start(f32[8,6,8,128]{3,1,2,0:T(8,128)S(1)} %get-tuple-element.33), channel_id=1, source_target_pairs={{16,0},{32,16},{48,32},{64,48},{80,64},{96,80},{112,96},{128,112},... | collective-permute-start | bytes 589832 | tf_op jit(solution)/shard_map/ppermute | solution.py:31
  20.3 10.0 collective-permute-start.1
  30.4 8.4 copy-start.1
  30.5 16.5 %collective-permute-start.2 = (f32[8,24,6,128]{3,1,2,0:T(8,128)S(1)}, f32[8,24,6,128]{3,1,2,0:T(8,128)S(1)}, u32[]{:S(2)}, u32[]{:S(2)}) collective-permute-start(f32[8,24,6,128]{3,1,2,0:T(8,128)S(1)} %get-tuple-element.24), channel_id=1, source_target_pairs={{1,0},{2,1},{3,2},{4,3},{5,4},{6,5},{7,6},{8,7},{9,8},{10,9},{11,1... | collective-permute-start | bytes 1769480 | tf_op jit(solution)/shard_map/ppermute | solution.py:31
  34.3 17.0 %collective-permute-start.3 = (f32[8,24,6,128]{3,1,2,0:T(8,128)S(1)}, f32[8,24,6,128]{3,1,2,0:T(8,128)S(1)}, u32[]{:S(2)}, u32[]{:S(2)}) collective-permute-start(f32[8,24,6,128]{3,1,2,0:T(8,128)S(1)} %get-tuple-element.25), channel_id=1, source_target_pairs={{0,1},{1,2},{2,3},{3,4},{4,5},{5,6},{6,7},{7,8},{8,9},{9,10},{10,1... | collective-permute-start | bytes 1769480 | tf_op jit(solution)/shard_map/ppermute | solution.py:29
  54.2 7.1 collective-permute-start.4
  56.2 8.3 collective-permute-start.5
  64.7 24.3 %collective-permute-start.6 = (f32[8,24,6,128]{3,1,2,0:T(8,128)S(1)}, f32[8,24,6,128]{3,1,2,0:T(8,128)S(1)}, u32[]{:S(2)}, u32[]{:S(2)}) collective-permute-start(f32[8,24,6,128]{3,1,2,0:T(8,128)S(1)} %get-tuple-element.22), channel_id=1, source_target_pairs={{1,0},{2,1},{3,2},{4,3},{5,4},{6,5},{7,6},{8,7},{9,8},{10,9},{11,1... | collective-permute-start | bytes 1769480 | tf_op jit(solution)/shard_map/ppermute | solution.py:31
  70.4 24.8 %collective-permute-start.7 = (f32[8,24,6,128]{3,1,2,0:T(8,128)S(1)}, f32[8,24,6,128]{3,1,2,0:T(8,128)S(1)}, u32[]{:S(2)}, u32[]{:S(2)}) collective-permute-start(f32[8,24,6,128]{3,1,2,0:T(8,128)S(1)} %get-tuple-element.23), channel_id=1, source_target_pairs={{0,1},{1,2},{2,3},{3,4},{4,5},{5,6},{6,7},{7,8},{8,9},{9,10},{10,1... | collective-permute-start | bytes 1769480 | tf_op jit(solution)/shard_map/ppermute | solution.py:29
  73.7 21.8 %copy-start = (f32[8,12,8,128]{3,2,1,0:T(8,128)S(1)}, f32[8,12,8,128]{3,2,1,0:T(8,128)}, u32[]{:S(2)}) copy-start(f32[8,12,8,128]{3,2,1,0:T(8,128)} %param.3) | copy-start | bytes 1179652
  98.2 7.5 collective-permute-start.8
  100.1 8.3 collective-permute-start.9
  108.7 33.2 %collective-permute-start.10 = (f32[8,24,6,128]{3,1,2,0:T(8,128)S(1)}, f32[8,24,6,128]{3,1,2,0:T(8,128)S(1)}, u32[]{:S(2)}, u32[]{:S(2)}) collective-permute-start(f32[8,24,6,128]{3,1,2,0:T(8,128)S(1)} %get-tuple-element.20), channel_id=1, source_target_pairs={{1,0},{2,1},{3,2},{4,3},{5,4},{6,5},{7,6},{8,7},{9,8},{10,9},{11,1... | collective-permute-start | bytes 1769480 | tf_op jit(solution)/shard_map/ppermute | solution.py:31
  119.0 27.4 %collective-permute-start.11 = (f32[8,24,6,128]{3,1,2,0:T(8,128)S(1)}, f32[8,24,6,128]{3,1,2,0:T(8,128)S(1)}, u32[]{:S(2)}, u32[]{:S(2)}) collective-permute-start(f32[8,24,6,128]{3,1,2,0:T(8,128)S(1)} %get-tuple-element.21), channel_id=1, source_target_pairs={{0,1},{1,2},{2,3},{3,4},{4,5},{5,6},{6,7},{7,8},{8,9},{9,10},{10,1... | collective-permute-start | bytes 1769480 | tf_op jit(solution)/shard_map/ppermute | solution.py:29
  149.4 7.5 collective-permute-start.12
  151.3 8.3 collective-permute-start.13
  159.9 19.4 %collective-permute-start.14 = (f32[8,24,6,128]{3,1,2,0:T(8,128)S(1)}, f32[8,24,6,128]{3,1,2,0:T(8,128)S(1)}, u32[]{:S(2)}, u32[]{:S(2)}) collective-permute-start(f32[8,24,6,128]{3,1,2,0:T(8,128)S(1)} %get-tuple-element.18), channel_id=1, source_target_pairs={{1,0},{2,1},{3,2},{4,3},{5,4},{6,5},{7,6},{8,7},{9,8},{10,9},{11,1... | collective-permute-start | bytes 1769480 | tf_op jit(solution)/shard_map/ppermute | solution.py:31
  167.0 13.4 collective-permute-start.15
Sparse Core Ops, SparseCore 0:
  59.7 108.4 all-gather.1
where the time goes:
time: 1510 us
  blocking collectives  1310 us (87%)
  waiting for transfers between devices  93.8 us (6%)
  starting transfers between devices  68.3 us (5%)
    psum x1, blocking collectives, shards(): correlations = lax.psum(local_correlations, ('dx', 'dy'))  655 us
    psum x1, blocking collectives, shards(): gram_matrix = lax.psum(partial_gram, ('dx', 'dy')) / total_cells  650 us
    ppermute x8, waiting for transfers between devices, with_halo(): lax.ppermute(head, axis, [((i + 1) % count, i) for i in range(count)])  63.9 us
    ppermute x8, starting transfers between devices, with_halo(): lax.ppermute(head, axis, [((i + 1) % count, i) for i in range(count)])  44.6 us
  transfers between devices with their start and end apart: 17, of which 16 were waited for; matrix products, arithmetic and copies ran while one was open for 1% of the time, Pallas kernels for 0%

commit v1 on v0

v1 whole, which is shorter than its diff:
```python
import jax
import jax.numpy as jnp
from jax import lax
from jax.sharding import PartitionSpec as P

DEGREE = 4


STENCIL_WEIGHTS = (
    -5369.0 / 1800.0,
    12.0 / 7.0,
    -15.0 / 56.0,
    10.0 / 189.0,
    -1.0 / 112.0,
    2.0 / 1925.0,
    -1.0 / 16632.0,
)
FILTER_CENTER = 23.0
FILTER_HALF = 21.0
WIDTH = 6


def neighbour_layers(cells, axis, dim):
    count = lax.axis_size(axis)
    size = cells.shape[dim]
    high = cells.astype(jnp.bfloat16)

    def packed(start, near):
        layers = lax.slice_in_dim(high, start, start + WIDTH, axis=dim)
        edge = lax.slice_in_dim(cells, near, near + 1, axis=dim)
        rest = edge - lax.slice_in_dim(high, near, near + 1, axis=dim).astype(jnp.float32)
        return jnp.concatenate([layers, rest.astype(jnp.bfloat16)], axis=dim)

    tail = lax.ppermute(
        packed(size - WIDTH, size - 1), axis, [(i, (i + 1) % count) for i in range(count)]
    )
    head = lax.ppermute(packed(0, 0), axis, [((i + 1) % count, i) for i in range(count)])

    def unpacked(got, near):
        layers = lax.slice_in_dim(got, 0, WIDTH, axis=dim).astype(jnp.float32)
        rest = lax.slice_in_dim(got, WIDTH, WIDTH + 1, axis=dim).astype(jnp.float32)
        pads = [(0, 0)] * got.ndim
        pads[dim] = (near, WIDTH - 1 - near)
        return layers + jnp.pad(rest, pads)

    return unpacked(tail, WIDTH - 1), unpacked(head, 0)


def apply_hamiltonian(orbital_field, potential):
    rows_x, rows_y, depth_cells = orbital_field.shape[1:]
    left, right = neighbour_layers(orbital_field, "dx", 1)
    below, above = neighbour_layers(orbital_field, "dy", 2)
    along_x = jnp.concatenate([left, orbital_field, right], axis=1)
    along_y = jnp.concatenate([below, orbital_field, above], axis=2)
    along_z = jnp.pad(orbital_field, ((0, 0), (0, 0), (0, 0), (WIDTH, WIDTH)))
    stencil_sum = 3.0 * STENCIL_WEIGHTS[0] * orbital_field
    for offset in range(1, WIDTH + 1):
        lo, hi = WIDTH - offset, WIDTH + offset
        beside_all = (
            along_x[:, lo : lo + rows_x]
            + along_x[:, hi : hi + rows_x]
            + along_y[:, :, lo : lo + rows_y]
            + along_y[:, :, hi : hi + rows_y]
            + along_z[:, :, :, lo : lo + depth_cells]
            + along_z[:, :, :, hi : hi + depth_cells]
        )
        stencil_sum = stencil_sum + STENCIL_WEIGHTS[offset] * beside_all
    return -2.0 * stencil_sum + potential[None] * orbital_field


def shifted(orbital_field, potential):
    return (
        apply_hamiltonian(orbital_field, potential) - FILTER_CENTER * orbital_field
    ) / FILTER_HALF


def sum_over_grid(values):
    for axis in ("dx", "dy"):
        count = lax.axis_size(axis)
        sent = jnp.broadcast_to(values[None], (count,) + values.shape)
        values = jnp.sum(lax.all_to_all(sent, axis, 0, 0), axis=0)
    return values


def other_band(values):
    return lax.ppermute(values, "band", [(0, 1), (1, 0)])


def shards(orbital_block, potential, resident):
    previous = orbital_block
    current = shifted(orbital_block, potential)
    for degree_step in range(DEGREE - 1):
        following = 2.0 * shifted(current, potential) - previous
        previous, current = (current, following)
    own_count = current.shape[0]
    cell_count = current.shape[1] * current.shape[2] * current.shape[3]
    filtered = current.reshape(own_count, cell_count)
    rounded = filtered.astype(jnp.bfloat16)
    rounded_other = other_band(rounded)
    own_resident = resident.reshape(-1, cell_count)
    both = jnp.concatenate([rounded, rounded_other], axis=0)
    local = lax.dot_general(
        both, own_resident, (((1,), (1,)), ((), ())), preferred_element_type=jnp.float32
    )
    correlations = sum_over_grid(local).astype(jnp.bfloat16)
    correction = jnp.dot(correlations, own_resident, preferred_element_type=jnp.float32)
    mine, theirs = correction[:own_count], correction[own_count:]
    sent = jnp.concatenate([theirs, mine], axis=0).astype(jnp.bfloat16)
    got = other_band(sent).astype(jnp.float32)
    projected = filtered - mine - got[:own_count]
    projected_other = rounded_other.astype(jnp.float32) - theirs - got[own_count:]
    partial_own = lax.dot_general(
        projected,
        projected,
        (((1,), (1,)), ((), ())),
        precision=lax.Precision.HIGHEST,
        preferred_element_type=jnp.float32,
    )
    partial_other = lax.dot_general(
        projected,
        projected_other,
        (((1,), (1,)), ((), ())),
        precision=lax.Precision.HIGHEST,
        preferred_element_type=jnp.float32,
    )
    first = jnp.concatenate([partial_own, partial_other], axis=1)
    second = jnp.concatenate([partial_other, partial_own], axis=1)
    partial_gram = jnp.where(lax.axis_index("band") == 0, first, second)
    total_cells = cell_count * lax.axis_size("dx") * lax.axis_size("dy")
    gram_matrix = sum_over_grid(partial_gram) / total_cells
    return (projected.reshape(current.shape), gram_matrix)


def solution(mesh):
    placed = (P("band", "dx", "dy", None), P("dx", "dy", None), P("band", "dx", "dy", None))
    return jax.shard_map(
        shards,
        mesh=mesh,
        in_specs=placed,
        out_specs=(P("band", "dx", "dy", None), P("band", None)),
        check_vma=False,
    )
```

time: 1510 us -> 189 us (0.13)
  blocking collectives: 1310 us -> 54.8 us
  waiting for transfers between devices: 93.8 us -> 38.1 us
    psum x2 -> x0, blocking collectives: 1300 us -> none  [the longest x1 655 us: shards(): correlations = lax.psum(local_correlations, ('dx', 'dy'))]
    ppermute x16 -> x18, waiting for transfers between devices: 93.7 us -> 31.9 us  [the longest x8 16 us: neighbour_layers(): lax.ppermute(packed(0, 0), axis, [((i + 1) % count, i) for i in range(cou...]
    all_to_all x0 -> x3, blocking collectives: none -> 54.8 us  [sum_over_grid(): values = jnp.sum(lax.all_to_all(sent, axis, 0, 0), axis=0)]
    ppermute x16 -> x18, starting transfers between devices: 68.3 us -> 63.7 us  [the longest x8 37.4 us: neighbour_layers(): lax.ppermute(packed(0, 0), axis, [((i + 1) % count, i) for i in range(cou...]
  transfers between devices with their start and end apart: 17 -> 19, of which waited for: 16 -> 10; matrix products, arithmetic and copies ran while one was open for 1% -> 2% of each run, Pallas kernels for 0% -> 0%
where the time goes in v1:
time: 189 us; the launch traced here: 188 us
  starting transfers between devices  69.9 us (37%)
  blocking collectives  54.8 us (29%)
  waiting for transfers between devices  38.1 us (20%)
  other arithmetic  15 us (8%)
  matrix products  5.76 us (3%)
  local copies, waits for them, and re-layouts  3.43 us (2%)
    all_to_all x3, blocking collectives, sum_over_grid(): values = jnp.sum(lax.all_to_all(sent, axis, 0, 0), axis=0)  54.8 us
    ppermute x8, starting transfers between devices, neighbour_layers(): lax.ppermute(packed(0, 0), axis, [((i + 1) % count, i) for i in range(cou...  37.4 us
    ppermute x8, starting transfers between devices, neighbour_layers(): lax.ppermute(packed(size - WIDTH, size - 1), axis, [(i, (i + 1) % count)...  20.5 us
    ppermute x8, waiting for transfers between devices, neighbour_layers(): lax.ppermute(packed(0, 0), axis, [((i + 1) % count, i) for i in range(cou...  16 us
    ppermute x2, waiting for transfers between devices, other_band(): return lax.ppermute(values, 'band', [(0, 1), (1, 0)])  12.6 us
    convert_element_type x4, other arithmetic, neighbour_layers(): high = cells.astype(jnp.bfloat16)  6.54 us
    all_to_all x1, starting transfers between devices, sum_over_grid(): values = jnp.sum(lax.all_to_all(sent, axis, 0, 0), axis=0)  6.24 us
    all_to_all x1, waiting for transfers between devices, sum_over_grid(): values = jnp.sum(lax.all_to_all(sent, axis, 0, 0), axis=0)  6.22 us
  transfers between devices with their start and end apart: 19, of which 10 were waited for; matrix products, arithmetic and copies ran while one was open for 2% of the time, Pallas kernels for 0%

profile of v1, /device:TPU:1, one launch (start us, length us, event | category | flops | bytes accessed | tf_op | source)
XLA Modules:
  0.0 188.4 jit_solution(15707822546133098327)
XLA Ops:
  3.2 6.0 %collective-permute-start.2 = (bf16[8,12,7,128]{3,2,1,0:T(8,128)(2,1)S(1)}, bf16[8,12,7,128]{3,2,1,0:T(8,128)(2,1)S(1)}, u32[]{:S(2)}, u32[]{:S(2)}) collective-permute-start(bf16[8,12,7,128]{3,2,1,0:T(8,128)(2,1)S(1)} %pad_maximum_fusion.17), channel_id=1, source_target_pairs={{0,1},{1,2},{2,3},{3,4},{4,5},{5,6},{6,7},{7,8},{8,9},{9,10},{10,1... | collective-permute-start | bytes 516104 | tf_op jit(solution)/shard_map/ppermute | solution.py:34
  10.1 11.1 %collective-permute-start.1 = (bf16[8,7,8,128]{3,2,1,0:T(8,128)(2,1)S(1)}, bf16[8,7,8,128]{3,2,1,0:T(8,128)(2,1)S(1)}, u32[]{:S(2)}, u32[]{:S(2)}) collective-permute-start(bf16[8,7,8,128]{3,2,1,0:T(8,128)(2,1)S(1)} %pad_maximum_fusion.26), channel_id=1, source_target_pairs={{16,0},{32,16},{48,32},{64,48},{80,64},{96,80},{112,96},{128,112},... | collective-permute-start | bytes 344072 | tf_op jit(solution)/shard_map/ppermute | solution.py:37
  21.2 1.9 %collective-permute-start = (bf16[8,7,8,128]{3,2,1,0:T(8,128)(2,1)S(1)}, bf16[8,7,8,128]{3,2,1,0:T(8,128)(2,1)S(1)}, u32[]{:S(2)}, u32[]{:S(2)}) collective-permute-start(bf16[8,7,8,128]{3,2,1,0:T(8,128)(2,1)S(1)} %pad_maximum_fusion.25), channel_id=1, source_target_pairs={{0,16},{16,32},{32,48},{48,64},{64,80},{80,96},{96,112},{112,128},... | collective-permute-start | bytes 344072 | tf_op jit(solution)/shard_map/ppermute | solution.py:34
  23.3 1.9 %collective-permute-start.3 = (bf16[8,12,7,128]{3,2,1,0:T(8,128)(2,1)S(1)}, bf16[8,12,7,128]{3,2,1,0:T(8,128)(2,1)S(1)}, u32[]{:S(2)}, u32[]{:S(2)}) collective-permute-start(bf16[8,12,7,128]{3,2,1,0:T(8,128)(2,1)S(1)} %pad_maximum_fusion.18), channel_id=1, source_target_pairs={{1,0},{2,1},{3,2},{4,3},{5,4},{6,5},{7,6},{8,7},{9,8},{10,9},{11,1... | collective-permute-start | bytes 516104 | tf_op jit(solution)/shard_map/ppermute | solution.py:37
  25.3 2.7 %collective-permute-done = bf16[8,7,8,128]{3,2,1,0:T(8,128)(2,1)S(1)} collective-permute-done((bf16[8,7,8,128]{3,2,1,0:T(8,128)(2,1)S(1)}, bf16[8,7,8,128]{3,2,1,0:T(8,128)(2,1)S(1)}, u32[]{:S(2)}, u32[]{:S(2)}) %collective-permute-start) | collective-permute-done | bytes 114720 | tf_op jit(solution)/shard_map/ppermute | solution.py:34
  28.2 3.6 %collective-permute-done.3 = bf16[8,12,7,128]{3,2,1,0:T(8,128)(2,1)S(1)} collective-permute-done((bf16[8,12,7,128]{3,2,1,0:T(8,128)(2,1)S(1)}, bf16[8,12,7,128]{3,2,1,0:T(8,128)(2,1)S(1)}, u32[]{:S(2)}, u32[]{:S(2)}) %collective-permute-start.3) | collective-permute-done | bytes 172064 | tf_op jit(solution)/shard_map/ppermute | solution.py:37
  34.0 1.9 %collective-permute-start.4 = (bf16[8,7,8,128]{3,2,1,0:T(8,128)(2,1)S(1)}, bf16[8,7,8,128]{3,2,1,0:T(8,128)(2,1)S(1)}, u32[]{:S(2)}, u32[]{:S(2)}) collective-permute-start(bf16[8,7,8,128]{3,2,1,0:T(8,128)(2,1)S(1)} %pad_maximum_fusion.27), channel_id=1, source_target_pairs={{0,16},{16,32},{32,48},{48,64},{64,80},{80,96},{96,112},{112,128},... | collective-permute-start | bytes 344072 | tf_op jit(solution)/shard_map/ppermute | solution.py:34
  36.0 4.6 %collective-permute-start.5 = (bf16[8,7,8,128]{3,2,1,0:T(8,128)(2,1)S(1)}, bf16[8,7,8,128]{3,2,1,0:T(8,128)(2,1)S(1)}, u32[]{:S(2)}, u32[]{:S(2)}) collective-permute-start(bf16[8,7,8,128]{3,2,1,0:T(8,128)(2,1)S(1)} %pad_maximum_fusion.28), channel_id=1, source_target_pairs={{16,0},{32,16},{48,32},{64,48},{80,64},{96,80},{112,96},{128,112},... | collective-permute-start | bytes 344072 | tf_op jit(solution)/shard_map/ppermute | solution.py:37
  40.7 2.3 %collective-permute-start.6 = (bf16[8,12,7,128]{3,2,1,0:T(8,128)(2,1)S(1)}, bf16[8,12,7,128]{3,2,1,0:T(8,128)(2,1)S(1)}, u32[]{:S(2)}, u32[]{:S(2)}) collective-permute-start(bf16[8,12,7,128]{3,2,1,0:T(8,128)(2,1)S(1)} %pad_maximum_fusion.19), channel_id=1, source_target_pairs={{0,1},{1,2},{2,3},{3,4},{4,5},{5,6},{6,7},{7,8},{8,9},{9,10},{10,1... | collective-permute-start | bytes 516104 | tf_op jit(solution)/shard_map/ppermute | solution.py:34
  43.1 2.0 %collective-permute-start.7 = (bf16[8,12,7,128]{3,2,1,0:T(8,128)(2,1)S(1)}, bf16[8,12,7,128]{3,2,1,0:T(8,128)(2,1)S(1)}, u32[]{:S(2)}, u32[]{:S(2)}) collective-permute-start(bf16[8,12,7,128]{3,2,1,0:T(8,128)(2,1)S(1)} %pad_maximum_fusion.20), channel_id=1, source_target_pairs={{1,0},{2,1},{3,2},{4,3},{5,4},{6,5},{7,6},{8,7},{9,8},{10,9},{11,1... | collective-permute-start | bytes 516104 | tf_op jit(solution)/shard_map/ppermute | solution.py:37
  45.7 5.9 %collective-permute-done.7 = bf16[8,12,7,128]{3,2,1,0:T(8,128)(2,1)S(1)} collective-permute-done((bf16[8,12,7,128]{3,2,1,0:T(8,128)(2,1)S(1)}, bf16[8,12,7,128]{3,2,1,0:T(8,128)(2,1)S(1)}, u32[]{:S(2)}, u32[]{:S(2)}) %collective-permute-start.7) | collective-permute-done | bytes 172064 | tf_op jit(solution)/shard_map/ppermute | solution.py:37
  51.7 1.8 fusion.308
  53.8 1.9 %collective-permute-start.8 = (bf16[8,7,8,128]{3,2,1,0:T(8,128)(2,1)S(1)}, bf16[8,7,8,128]{3,2,1,0:T(8,128)(2,1)S(1)}, u32[]{:S(2)}, u32[]{:S(2)}) collective-permute-start(bf16[8,7,8,128]{3,2,1,0:T(8,128)(2,1)S(1)} %pad_maximum_fusion.29), channel_id=1, source_target_pairs={{0,16},{16,32},{32,48},{48,64},{64,80},{80,96},{96,112},{112,128},... | collective-permute-start | bytes 344072 | tf_op jit(solution)/shard_map/ppermute | solution.py:34
  55.8 4.6 %collective-permute-start.9 = (bf16[8,7,8,128]{3,2,1,0:T(8,128)(2,1)S(1)}, bf16[8,7,8,128]{3,2,1,0:T(8,128)(2,1)S(1)}, u32[]{:S(2)}, u32[]{:S(2)}) collective-permute-start(bf16[8,7,8,128]{3,2,1,0:T(8,128)(2,1)S(1)} %pad_maximum_fusion.30), channel_id=1, source_target_pairs={{16,0},{32,16},{48,32},{64,48},{80,64},{96,80},{112,96},{128,112},... | collective-permute-start | bytes 344072 | tf_op jit(solution)/shard_map/ppermute | solution.py:37
  60.5 2.3 %collective-permute-start.10 = (bf16[8,12,7,128]{3,2,1,0:T(8,128)(2,1)S(1)}, bf16[8,12,7,128]{3,2,1,0:T(8,128)(2,1)S(1)}, u32[]{:S(2)}, u32[]{:S(2)}) collective-permute-start(bf16[8,12,7,128]{3,2,1,0:T(8,128)(2,1)S(1)} %pad_maximum_fusion.21), channel_id=1, source_target_pairs={{0,1},{1,2},{2,3},{3,4},{4,5},{5,6},{6,7},{7,8},{8,9},{9,10},{10,1... | collective-permute-start | bytes 516104 | tf_op jit(solution)/shard_map/ppermute | solution.py:34
  62.9 3.5 %collective-permute-start.11 = (bf16[8,12,7,128]{3,2,1,0:T(8,128)(2,1)S(1)}, bf16[8,12,7,128]{3,2,1,0:T(8,128)(2,1)S(1)}, u32[]{:S(2)}, u32[]{:S(2)}) collective-permute-start(bf16[8,12,7,128]{3,2,1,0:T(8,128)(2,1)S(1)} %pad_maximum_fusion.22), channel_id=1, source_target_pairs={{1,0},{2,1},{3,2},{4,3},{5,4},{6,5},{7,6},{8,7},{9,8},{10,9},{11,1... | collective-permute-start | bytes 516104 | tf_op jit(solution)/shard_map/ppermute | solution.py:37
  66.7 5.0 %collective-permute-done.11 = bf16[8,12,7,128]{3,2,1,0:T(8,128)(2,1)S(1)} collective-permute-done((bf16[8,12,7,128]{3,2,1,0:T(8,128)(2,1)S(1)}, bf16[8,12,7,128]{3,2,1,0:T(8,128)(2,1)S(1)}, u32[]{:S(2)}, u32[]{:S(2)}) %collective-permute-start.11) | collective-permute-done | bytes 172064 | tf_op jit(solution)/shard_map/ppermute | solution.py:37
  71.8 1.8 fusion.306
  74.0 2.2 %collective-permute-start.14 = (bf16[8,12,7,128]{3,2,1,0:T(8,128)(2,1)S(1)}, bf16[8,12,7,128]{3,2,1,0:T(8,128)(2,1)S(1)}, u32[]{:S(2)}, u32[]{:S(2)}) collective-permute-start(bf16[8,12,7,128]{3,2,1,0:T(8,128)(2,1)S(1)} %pad_maximum_fusion.23), channel_id=1, source_target_pairs={{0,1},{1,2},{2,3},{3,4},{4,5},{5,6},{6,7},{7,8},{8,9},{9,10},{10,1... | collective-permute-start | bytes 516104 | tf_op jit(solution)/shard_map/ppermute | solution.py:34
  76.3 5.2 %collective-permute-start.15 = (bf16[8,12,7,128]{3,2,1,0:T(8,128)(2,1)S(1)}, bf16[8,12,7,128]{3,2,1,0:T(8,128)(2,1)S(1)}, u32[]{:S(2)}, u32[]{:S(2)}) collective-permute-start(bf16[8,12,7,128]{3,2,1,0:T(8,128)(2,1)S(1)} %pad_maximum_fusion.24), channel_id=1, source_target_pairs={{1,0},{2,1},{3,2},{4,3},{5,4},{6,5},{7,6},{8,7},{9,8},{10,9},{11,1... | collective-permute-start | bytes 516104 | tf_op jit(solution)/shard_map/ppermute | solution.py:37
  81.5 1.9 %collective-permute-start.12 = (bf16[8,7,8,128]{3,2,1,0:T(8,128)(2,1)S(1)}, bf16[8,7,8,128]{3,2,1,0:T(8,128)(2,1)S(1)}, u32[]{:S(2)}, u32[]{:S(2)}) collective-permute-start(bf16[8,7,8,128]{3,2,1,0:T(8,128)(2,1)S(1)} %pad_maximum_fusion.31), channel_id=1, source_target_pairs={{0,16},{16,32},{32,48},{48,64},{64,80},{80,96},{96,112},{112,128},... | collective-permute-start | bytes 344072 | tf_op jit(solution)/shard_map/ppermute | solution.py:34
  83.5 4.6 %collective-permute-start.13 = (bf16[8,7,8,128]{3,2,1,0:T(8,128)(2,1)S(1)}, bf16[8,7,8,128]{3,2,1,0:T(8,128)(2,1)S(1)}, u32[]{:S(2)}, u32[]{:S(2)}) collective-permute-start(bf16[8,7,8,128]{3,2,1,0:T(8,128)(2,1)S(1)} %pad_maximum_fusion.32), channel_id=1, source_target_pairs={{16,0},{32,16},{48,32},{64,48},{80,64},{96,80},{112,96},{128,112},... | collective-permute-start | bytes 344072 | tf_op jit(solution)/shard_map/ppermute | solution.py:37
  92.2 3.1 %collective-permute-start.16 = (bf16[8,12288]{1,0:T(8,128)(2,1)S(1)}, bf16[8,12288]{1,0:T(8,128)(2,1)S(1)}, u32[]{:S(2)}, u32[]{:S(2)}) collective-permute-start(bf16[8,12288]{1,0:T(8,128)(2,1)S(1)} %bitcast.24), channel_id=1, source_target_pairs={{0,256},{256,0},{1,257},{257,1},{2,258},{258,2},{3,259},{259,3},{4... | collective-permute-start | bytes 589832 | tf_op jit(solution)/shard_map/ppermute | solution.py:86
  95.3 3.3 %collective-permute-done.16 = bf16[8,12288]{1,0:T(8,128)(2,1)S(1)} collective-permute-done((bf16[8,12288]{1,0:T(8,128)(2,1)S(1)}, bf16[8,12288]{1,0:T(8,128)(2,1)S(1)}, u32[]{:S(2)}, u32[]{:S(2)}) %collective-permute-start.16) | collective-permute-done | bytes 196640 | tf_op jit(solution)/shard_map/ppermute | solution.py:86
  99.6 19.6 %all_to_all.20 = f32[16,16,128]{2,1,0:T(8,128)S(1)} all-to-all(f32[16,16,128]{2,1,0:T(8,128)S(1)} %broadcast_in_dim.8), channel_id=1, replica_groups=mesh['band'=2,'dx'=16,'dy'=16] {'dx'}, dimensions={0} | all-to-all | bytes 262144 | tf_op jit(solution)/shard_map/all_to_all | solution.py:81
  119.2 20.9 %all_to_all.21 = f32[16,16,128]{2,1,0:T(8,128)S(1)} all-to-all(f32[16,16,128]{2,1,0:T(8,128)S(1)} %broadcast_in_dim.9), channel_id=1, replica_groups=mesh['band'=2,'dx'=16,'dy'=16] {'dy'}, dimensions={0} | all-to-all | bytes 262144 | tf_op jit(solution)/shard_map/all_to_all | solution.py:81
  140.1 2.9 %fusion = f32[16,12288]{1,0:T(8,128)S(1)} fusion(bf16[16,8,96,128]{3,2,1,0:T(8,128)(2,1)} %bitcast.22, bf16[16,128]{1,0:T(8,128)(2,1)S(1)} %reduce_sum.37), kind=kOutput, calls=%fused_computation | convolution fusion | flops 50331648 | bytes 3936256 | tf_op jit(solution)/shard_map/dot_general | solution.py:106
  143.1 2.6 %collective-permute-start.17 = (bf16[16,12288]{1,0:T(8,128)(2,1)S(1)}, bf16[16,12288]{1,0:T(8,128)(2,1)S(1)}, u32[]{:S(2)}, u32[]{:S(2)}) collective-permute-start(bf16[16,12288]{1,0:T(8,128)(2,1)S(1)} %pad_maximum_fusion.16), channel_id=1, source_target_pairs={{0,256},{256,0},{1,257},{257,1},{2,258},{258,2},{3,259},{259,3},{4... | collective-permute-start | bytes 1179656 | tf_op jit(solution)/shard_map/ppermute | solution.py:86
  145.7 9.3 %collective-permute-done.17 = bf16[16,12288]{1,0:T(8,128)(2,1)S(1)} collective-permute-done((bf16[16,12288]{1,0:T(8,128)(2,1)S(1)}, bf16[16,12288]{1,0:T(8,128)(2,1)S(1)}, u32[]{:S(2)}, u32[]{:S(2)}) %collective-permute-start.17) | collective-permute-done | bytes 393248 | tf_op jit(solution)/shard_map/ppermute | solution.py:86
  157.4 14.3 %all_to_all.22 = f32[16,1,128]{2,1,0:T(1,128)S(1)} all-to-all(f32[16,1,128]{2,1,0:T(1,128)S(1)} %reshape.49), channel_id=1, replica_groups=mesh['band'=2,'dx'=16,'dy'=16] {'dx'}, dimensions={0} | all-to-all | bytes 16384 | tf_op jit(solution)/shard_map/all_to_all | solution.py:81
  173.8 6.2 %all-to-all-start.3 = ((f32[16,1,128]{2,1,0:T(1,128)}), f32[16,1,128]{2,1,0:T(1,128)S(1)}, u32[]{:S(2)}, u32[]{:S(2)}) async-start(f32[16,1,128]{2,1,0:T(1,128)} %reshape.51), calls=%async_computation.3 | async-start | bytes 16384 | tf_op jit(solution)/shard_map/all_to_all | solution.py:81
  180.8 6.2 %all-to-all-done.3 = f32[16,1,128]{2,1,0:T(1,128)S(1)} async-done(((f32[16,1,128]{2,1,0:T(1,128)}), f32[16,1,128]{2,1,0:T(1,128)S(1)}, u32[]{:S(2)}, u32[]{:S(2)}) %all-to-all-start.3) | async-done | bytes 8224 | tf_op jit(solution)/shard_map/all_to_all | solution.py:81
  (113 shorter events, 19.8 us)
Async XLA Ops:
  0.6 31.3 %copy-start = (f32[8,12,8,128]{3,2,1,0:T(8,128)S(1)}, f32[8,12,8,128]{3,2,1,0:T(8,128)}, u32[]{:S(2)}) copy-start(f32[8,12,8,128]{3,2,1,0:T(8,128)} %param.3) | copy-start | bytes 1179652
  0.6 24.6 %copy-start.2 = (f32[12,8,128]{2,1,0:T(8,128)S(1)}, f32[12,8,128]{2,1,0:T(8,128)}, u32[]{:S(2)}) copy-start(f32[12,8,128]{2,1,0:T(8,128)} %param.4) | copy-start | bytes 147460
  3.2 24.8 %collective-permute-start.2 = (bf16[8,12,7,128]{3,2,1,0:T(8,128)(2,1)S(1)}, bf16[8,12,7,128]{3,2,1,0:T(8,128)(2,1)S(1)}, u32[]{:S(2)}, u32[]{:S(2)}) collective-permute-start(bf16[8,12,7,128]{3,2,1,0:T(8,128)(2,1)S(1)} %pad_maximum_fusion.17), channel_id=1, source_target_pairs={{0,1},{1,2},{2,3},{3,4},{4,5},{5,6},{6,7},{7,8},{8,9},{9,10},{10,1... | collective-permute-start | bytes 516104 | tf_op jit(solution)/shard_map/ppermute | solution.py:34
  10.1 15.2 %collective-permute-start.1 = (bf16[8,7,8,128]{3,2,1,0:T(8,128)(2,1)S(1)}, bf16[8,7,8,128]{3,2,1,0:T(8,128)(2,1)S(1)}, u32[]{:S(2)}, u32[]{:S(2)}) collective-permute-start(bf16[8,7,8,128]{3,2,1,0:T(8,128)(2,1)S(1)} %pad_maximum_fusion.26), channel_id=1, source_target_pairs={{16,0},{32,16},{48,32},{64,48},{80,64},{96,80},{112,96},{128,112},... | collective-permute-start | bytes 344072 | tf_op jit(solution)/shard_map/ppermute | solution.py:37
  21.2 6.7 %collective-permute-start = (bf16[8,7,8,128]{3,2,1,0:T(8,128)(2,1)S(1)}, bf16[8,7,8,128]{3,2,1,0:T(8,128)(2,1)S(1)}, u32[]{:S(2)}, u32[]{:S(2)}) collective-permute-start(bf16[8,7,8,128]{3,2,1,0:T(8,128)(2,1)S(1)} %pad_maximum_fusion.25), channel_id=1, source_target_pairs={{0,16},{16,32},{32,48},{48,64},{64,80},{80,96},{96,112},{112,128},... | collective-permute-start | bytes 344072 | tf_op jit(solution)/shard_map/ppermute | solution.py:34
  23.3 8.5 %collective-permute-start.3 = (bf16[8,12,7,128]{3,2,1,0:T(8,128)(2,1)S(1)}, bf16[8,12,7,128]{3,2,1,0:T(8,128)(2,1)S(1)}, u32[]{:S(2)}, u32[]{:S(2)}) collective-permute-start(bf16[8,12,7,128]{3,2,1,0:T(8,128)(2,1)S(1)} %pad_maximum_fusion.18), channel_id=1, source_target_pairs={{1,0},{2,1},{3,2},{4,3},{5,4},{6,5},{7,6},{8,7},{9,8},{10,9},{11,1... | collective-permute-start | bytes 516104 | tf_op jit(solution)/shard_map/ppermute | solution.py:37
  34.0 11.1 %collective-permute-start.4 = (bf16[8,7,8,128]{3,2,1,0:T(8,128)(2,1)S(1)}, bf16[8,7,8,128]{3,2,1,0:T(8,128)(2,1)S(1)}, u32[]{:S(2)}, u32[]{:S(2)}) collective-permute-start(bf16[8,7,8,128]{3,2,1,0:T(8,128)(2,1)S(1)} %pad_maximum_fusion.27), channel_id=1, source_target_pairs={{0,16},{16,32},{32,48},{48,64},{64,80},{80,96},{96,112},{112,128},... | collective-permute-start | bytes 344072 | tf_op jit(solution)/shard_map/ppermute | solution.py:34
  36.0 9.2 %collective-permute-start.5 = (bf16[8,7,8,128]{3,2,1,0:T(8,128)(2,1)S(1)}, bf16[8,7,8,128]{3,2,1,0:T(8,128)(2,1)S(1)}, u32[]{:S(2)}, u32[]{:S(2)}) collective-permute-start(bf16[8,7,8,128]{3,2,1,0:T(8,128)(2,1)S(1)} %pad_maximum_fusion.28), channel_id=1, source_target_pairs={{16,0},{32,16},{48,32},{64,48},{80,64},{96,80},{112,96},{128,112},... | collective-permute-start | bytes 344072 | tf_op jit(solution)/shard_map/ppermute | solution.py:37
  40.7 4.9 %collective-permute-start.6 = (bf16[8,12,7,128]{3,2,1,0:T(8,128)(2,1)S(1)}, bf16[8,12,7,128]{3,2,1,0:T(8,128)(2,1)S(1)}, u32[]{:S(2)}, u32[]{:S(2)}) collective-permute-start(bf16[8,12,7,128]{3,2,1,0:T(8,128)(2,1)S(1)} %pad_maximum_fusion.19), channel_id=1, source_target_pairs={{0,1},{1,2},{2,3},{3,4},{4,5},{5,6},{6,7},{7,8},{8,9},{9,10},{10,1... | collective-permute-start | bytes 516104 | tf_op jit(solution)/shard_map/ppermute | solution.py:34
  43.1 8.5 %collective-permute-start.7 = (bf16[8,12,7,128]{3,2,1,0:T(8,128)(2,1)S(1)}, bf16[8,12,7,128]{3,2,1,0:T(8,128)(2,1)S(1)}, u32[]{:S(2)}, u32[]{:S(2)}) collective-permute-start(bf16[8,12,7,128]{3,2,1,0:T(8,128)(2,1)S(1)} %pad_maximum_fusion.20), channel_id=1, source_target_pairs={{1,0},{2,1},{3,2},{4,3},{5,4},{6,5},{7,6},{8,7},{9,8},{10,9},{11,1... | collective-permute-start | bytes 516104 | tf_op jit(solution)/shard_map/ppermute | solution.py:37
  53.8 12.6 %collective-permute-start.8 = (bf16[8,7,8,128]{3,2,1,0:T(8,128)(2,1)S(1)}, bf16[8,7,8,128]{3,2,1,0:T(8,128)(2,1)S(1)}, u32[]{:S(2)}, u32[]{:S(2)}) collective-permute-start(bf16[8,7,8,128]{3,2,1,0:T(8,128)(2,1)S(1)} %pad_maximum_fusion.29), channel_id=1, source_target_pairs={{0,16},{16,32},{32,48},{48,64},{64,80},{80,96},{96,112},{112,128},... | collective-permute-start | bytes 344072 | tf_op jit(solution)/shard_map/ppermute | solution.py:34
  55.8 10.7 %collective-permute-start.9 = (bf16[8,7,8,128]{3,2,1,0:T(8,128)(2,1)S(1)}, bf16[8,7,8,128]{3,2,1,0:T(8,128)(2,1)S(1)}, u32[]{:S(2)}, u32[]{:S(2)}) collective-permute-start(bf16[8,7,8,128]{3,2,1,0:T(8,128)(2,1)S(1)} %pad_maximum_fusion.30), channel_id=1, source_target_pairs={{16,0},{32,16},{48,32},{64,48},{80,64},{96,80},{112,96},{128,112},... | collective-permute-start | bytes 344072 | tf_op jit(solution)/shard_map/ppermute | solution.py:37
  60.5 6.0 %collective-permute-start.10 = (bf16[8,12,7,128]{3,2,1,0:T(8,128)(2,1)S(1)}, bf16[8,12,7,128]{3,2,1,0:T(8,128)(2,1)S(1)}, u32[]{:S(2)}, u32[]{:S(2)}) collective-permute-start(bf16[8,12,7,128]{3,2,1,0:T(8,128)(2,1)S(1)} %pad_maximum_fusion.21), channel_id=1, source_target_pairs={{0,1},{1,2},{2,3},{3,4},{4,5},{5,6},{6,7},{7,8},{8,9},{9,10},{10,1... | collective-permute-start | bytes 516104 | tf_op jit(solution)/shard_map/ppermute | solution.py:34
  62.9 8.8 %collective-permute-start.11 = (bf16[8,12,7,128]{3,2,1,0:T(8,128)(2,1)S(1)}, bf16[8,12,7,128]{3,2,1,0:T(8,128)(2,1)S(1)}, u32[]{:S(2)}, u32[]{:S(2)}) collective-permute-start(bf16[8,12,7,128]{3,2,1,0:T(8,128)(2,1)S(1)} %pad_maximum_fusion.22), channel_id=1, source_target_pairs={{1,0},{2,1},{3,2},{4,3},{5,4},{6,5},{7,6},{8,7},{9,8},{10,9},{11,1... | collective-permute-start | bytes 516104 | tf_op jit(solution)/shard_map/ppermute | solution.py:37
  74.0 24.6 %copy-start.1 = (bf16[128,12,8,128]{3,2,1,0:T(8,128)(2,1)S(1)}, bf16[128,12,8,128]{3,2,1,0:T(8,128)(2,1)}, u32[]{:S(2)}) copy-start(bf16[128,12,8,128]{3,2,1,0:T(8,128)(2,1)} %param.5) | copy-start | bytes 9437188
  74.0 15.8 %collective-permute-start.14 = (bf16[8,12,7,128]{3,2,1,0:T(8,128)(2,1)S(1)}, bf16[8,12,7,128]{3,2,1,0:T(8,128)(2,1)S(1)}, u32[]{:S(2)}, u32[]{:S(2)}) collective-permute-start(bf16[8,12,7,128]{3,2,1,0:T(8,128)(2,1)S(1)} %pad_maximum_fusion.23), channel_id=1, source_target_pairs={{0,1},{1,2},{2,3},{3,4},{4,5},{5,6},{6,7},{7,8},{8,9},{9,10},{10,1... | collective-permute-start | bytes 516104 | tf_op jit(solution)/shard_map/ppermute | solution.py:34
  76.3 13.7 %collective-permute-start.15 = (bf16[8,12,7,128]{3,2,1,0:T(8,128)(2,1)S(1)}, bf16[8,12,7,128]{3,2,1,0:T(8,128)(2,1)S(1)}, u32[]{:S(2)}, u32[]{:S(2)}) collective-permute-start(bf16[8,12,7,128]{3,2,1,0:T(8,128)(2,1)S(1)} %pad_maximum_fusion.24), channel_id=1, source_target_pairs={{1,0},{2,1},{3,2},{4,3},{5,4},{6,5},{7,6},{8,7},{9,8},{10,9},{11,1... | collective-permute-start | bytes 516104 | tf_op jit(solution)/shard_map/ppermute | solution.py:37
  81.5 6.7 %collective-permute-start.12 = (bf16[8,7,8,128]{3,2,1,0:T(8,128)(2,1)S(1)}, bf16[8,7,8,128]{3,2,1,0:T(8,128)(2,1)S(1)}, u32[]{:S(2)}, u32[]{:S(2)}) collective-permute-start(bf16[8,7,8,128]{3,2,1,0:T(8,128)(2,1)S(1)} %pad_maximum_fusion.31), channel_id=1, source_target_pairs={{0,16},{16,32},{32,48},{48,64},{64,80},{80,96},{96,112},{112,128},... | collective-permute-start | bytes 344072 | tf_op jit(solution)/shard_map/ppermute | solution.py:34
  83.5 6.4 %collective-permute-start.13 = (bf16[8,7,8,128]{3,2,1,0:T(8,128)(2,1)S(1)}, bf16[8,7,8,128]{3,2,1,0:T(8,128)(2,1)S(1)}, u32[]{:S(2)}, u32[]{:S(2)}) collective-permute-start(bf16[8,7,8,128]{3,2,1,0:T(8,128)(2,1)S(1)} %pad_maximum_fusion.32), channel_id=1, source_target_pairs={{16,0},{32,16},{48,32},{64,48},{80,64},{96,80},{112,96},{128,112},... | collective-permute-start | bytes 344072 | tf_op jit(solution)/shard_map/ppermute | solution.py:37
  92.2 6.4 %collective-permute-start.16 = (bf16[8,12288]{1,0:T(8,128)(2,1)S(1)}, bf16[8,12288]{1,0:T(8,128)(2,1)S(1)}, u32[]{:S(2)}, u32[]{:S(2)}) collective-permute-start(bf16[8,12288]{1,0:T(8,128)(2,1)S(1)} %bitcast.24), channel_id=1, source_target_pairs={{0,256},{256,0},{1,257},{257,1},{2,258},{258,2},{3,259},{259,3},{4... | collective-permute-start | bytes 589832 | tf_op jit(solution)/shard_map/ppermute | solution.py:86
  143.1 11.9 %collective-permute-start.17 = (bf16[16,12288]{1,0:T(8,128)(2,1)S(1)}, bf16[16,12288]{1,0:T(8,128)(2,1)S(1)}, u32[]{:S(2)}, u32[]{:S(2)}) collective-permute-start(bf16[16,12288]{1,0:T(8,128)(2,1)S(1)} %pad_maximum_fusion.16), channel_id=1, source_target_pairs={{0,256},{256,0},{1,257},{257,1},{2,258},{258,2},{3,259},{259,3},{4... | collective-permute-start | bytes 1179656 | tf_op jit(solution)/shard_map/ppermute | solution.py:86
  173.8 13.3 %all-to-all-start.3 = ((f32[16,1,128]{2,1,0:T(1,128)}), f32[16,1,128]{2,1,0:T(1,128)S(1)}, u32[]{:S(2)}, u32[]{:S(2)}) async-start(f32[16,1,128]{2,1,0:T(1,128)} %reshape.51), calls=%async_computation.3 | async-start | bytes 16384 | tf_op jit(solution)/shard_map/all_to_all | solution.py:81

commit v2 on v0

v2 whole, which is shorter than its diff:
```python
import functools

import jax
import jax.numpy as jnp
from jax import lax
from jax.experimental import pallas as pl
from jax.experimental.pallas import tpu as pltpu
from jax.sharding import PartitionSpec as P

DEGREE = 4


STENCIL_WEIGHTS = (
    -5369.0 / 1800.0,
    12.0 / 7.0,
    -15.0 / 56.0,
    10.0 / 189.0,
    -1.0 / 112.0,
    2.0 / 1925.0,
    -1.0 / 16632.0,
)
FILTER_CENTER = 23.0
FILTER_HALF = 21.0
WIDTH = 6
SENT = WIDTH + 1
VMEM_BYTES = 24 * 1024 * 1024


def pack_layer(out_ref, at, layer):
    rows = layer.shape[0] * layer.shape[1]
    out_ref[at * rows : (at + 1) * rows, :] = layer.reshape(rows, layer.shape[2]).astype(
        jnp.bfloat16
    )


def pack_halos(field_ref, to_left, to_right, to_below, to_above):
    size_x, size_y = field_ref.shape[:2]
    for at in range(WIDTH):
        pack_layer(to_left, at, field_ref[at])
        pack_layer(to_right, at, field_ref[size_x - WIDTH + at])
        pack_layer(to_below, at, field_ref[:, at])
        pack_layer(to_above, at, field_ref[:, size_y - WIDTH + at])
    for out_ref, layer in (
        (to_left, field_ref[0]),
        (to_right, field_ref[size_x - 1]),
        (to_below, field_ref[:, 0]),
        (to_above, field_ref[:, size_y - 1]),
    ):
        pack_layer(out_ref, WIDTH, layer - layer.astype(jnp.bfloat16).astype(jnp.float32))


def start_kernel(cells_ref, field_ref, *halo_refs):
    size_x, size_y, own = field_ref.shape[:3]
    for x in range(size_x):
        for y in range(size_y):
            rows = pl.ds(x * size_y + y, own, stride=size_x * size_y)
            field_ref[x, y] = cells_ref[rows, :]
    pack_halos(field_ref, *halo_refs)


def layer_of(halo_ref, at, near, shape):
    rows = shape[0] * shape[1]
    layer = halo_ref[at * rows : (at + 1) * rows, :].astype(jnp.float32)
    if at == near:
        layer = layer + halo_ref[WIDTH * rows : SENT * rows, :].astype(jnp.float32)
    return layer.reshape(shape)


def step_kernel(scale, has_previous, last, extras, *refs):
    field_ref, potential_ref, left, right, below, above = refs[:6]
    at = 6
    previous_ref = None
    if has_previous:
        previous_ref = refs[at]
        at += 1
    at += extras
    outs = refs[at:-2]
    along_x, along_y = refs[-2:]
    size_x, size_y, own, depth = field_ref.shape
    layer_x, layer_y = (size_y, own, depth), (size_x, own, depth)
    for k in range(WIDTH):
        along_x[k] = layer_of(left, k, WIDTH - 1, layer_x)
        along_x[WIDTH + size_x + k] = layer_of(right, k, 0, layer_x)
        along_y[:, k] = layer_of(below, k, WIDTH - 1, layer_y)
        along_y[:, WIDTH + size_y + k] = layer_of(above, k, 0, layer_y)
    along_x[WIDTH : WIDTH + size_x] = field_ref[...]
    along_y[:, WIDTH : WIDTH + size_y] = field_ref[...]

    weights = [-2.0 * scale * w for w in STENCIL_WEIGHTS]
    middle = 3.0 * weights[0] - scale * FILTER_CENTER
    lane = lax.broadcasted_iota(jnp.int32, (1, depth), 1)
    up = [None] + [jnp.where(lane >= k, weights[k], 0.0) for k in range(1, WIDTH + 1)]
    down = [None] + [jnp.where(lane < depth - k, weights[k], 0.0) for k in range(1, WIDTH + 1)]

    @pl.loop(0, size_x)
    def _(x):
        for y in range(size_y):
            centre = along_y[x, WIDTH + y]
            factor = middle + scale * potential_ref[pl.ds(x * size_y + y, 1), :]
            total = factor * centre
            if has_previous:
                total = total - previous_ref[x, y]
            for k in range(1, WIDTH + 1):
                beside = (along_x[x + WIDTH + k, y] + along_x[x + WIDTH - k, y]) + (
                    along_y[x, WIDTH + y + k] + along_y[x, WIDTH + y - k]
                )
                total = total + weights[k] * beside
                total = total + up[k] * pltpu.roll(centre, k, 1)
                total = total + down[k] * pltpu.roll(centre, depth - k, 1)
            if last:
                outs[0][pl.ds(x * size_y + y, own, stride=size_x * size_y), :] = total
            else:
                outs[0][x, y] = total

    if not last:
        pack_halos(*outs)


def halo_shapes(size_x, size_y, own, depth):
    to_x = jax.ShapeDtypeStruct((SENT * size_y * own, depth), jnp.bfloat16)
    to_y = jax.ShapeDtypeStruct((SENT * size_x * own, depth), jnp.bfloat16)
    return [to_x, to_x, to_y, to_y]


def params():
    return pltpu.CompilerParams(vmem_limit_bytes=VMEM_BYTES)


def start(orbital_block):
    own, size_x, size_y, depth = orbital_block.shape
    field = jax.ShapeDtypeStruct((size_x, size_y, own, depth), jnp.float32)
    return pl.pallas_call(
        start_kernel,
        out_shape=[field] + halo_shapes(size_x, size_y, own, depth),
        compiler_params=params(),
    )(orbital_block.reshape(own * size_x * size_y, depth))


def filter_step(field, potential, halos, previous, last, extras=()):
    size_x, size_y, own, depth = field.shape
    scale = (1.0 if previous is None else 2.0) / FILTER_HALF
    if last:
        out_shape = [jax.ShapeDtypeStruct((own * size_x * size_y, depth), jnp.float32)]
    else:
        out_shape = [jax.ShapeDtypeStruct(field.shape, jnp.float32)]
        out_shape += halo_shapes(size_x, size_y, own, depth)
    before = [] if previous is None else [previous]
    vmem = pl.BlockSpec(memory_space=pltpu.VMEM)
    return pl.pallas_call(
        functools.partial(step_kernel, scale, previous is not None, last, len(extras)),
        out_shape=out_shape,
        in_specs=[vmem] * (6 + len(before)) + [pl.BlockSpec(memory_space=pl.ANY)] * len(extras),
        out_specs=[vmem] * len(out_shape),
        scratch_shapes=[
            pltpu.VMEM((size_x + 2 * WIDTH, size_y, own, depth), jnp.float32),
            pltpu.VMEM((size_x, size_y + 2 * WIDTH, own, depth), jnp.float32),
        ],
        compiler_params=params(),
    )(field, potential, *halos, *before, *extras)


def exchange(to_left, to_right, to_below, to_above):
    def moved(values, axis, by):
        count = lax.axis_size(axis)
        return lax.ppermute(values, axis, [(i, (i + by) % count) for i in range(count)])

    left = moved(to_right, "dx", 1)
    right = moved(to_left, "dx", -1)
    below = moved(to_above, "dy", 1)
    above = moved(to_below, "dy", -1)
    return left, right, below, above


def sum_over_grid(values):
    for axis in ("dx", "dy"):
        count = lax.axis_size(axis)
        sent = jnp.broadcast_to(values[None], (count,) + values.shape)
        values = jnp.sum(lax.all_to_all(sent, axis, 0, 0), axis=0)
    return values


def other_band(values):
    return lax.ppermute(values, "band", [(0, 1), (1, 0)])


def rows_dot(first, second, **kwargs):
    return lax.dot_general(
        first, second, (((1,), (1,)), ((), ())), preferred_element_type=jnp.float32, **kwargs
    )


def shards(orbital_block, potential, resident):
    own_count, size_x, size_y, depth = orbital_block.shape
    cell_count = size_x * size_y * depth
    flat_potential = potential.reshape(size_x * size_y, depth)
    band = lax.axis_index("band")
    half = size_x // 2

    kept = jnp.where(band == 0, resident[:, :half], resident[:, half:])
    given = jnp.where(band == 0, resident[:, half:], resident[:, :half])
    got_resident = other_band(given)

    field, *sent = start(orbital_block)
    fields = [field]
    field, *sent = filter_step(field, flat_potential, exchange(*sent), None, False)
    fields.append(field)
    halos = exchange(*sent)
    field, *sent = filter_step(
        field, flat_potential, halos, fields[0], False, (got_resident,)
    )
    fields.append(field)
    own_resident = resident.reshape(-1, cell_count)
    count = own_resident.shape[0]
    within = rows_dot(own_resident, own_resident)
    across = rows_dot(kept.reshape(count, -1), got_resident.reshape(count, -1))
    overlaps = jnp.stack([within, across])
    halos = exchange(*sent)
    field, *sent = filter_step(field, flat_potential, halos, fields[1], False, (overlaps,))
    overlaps = lax.psum(lax.psum(overlaps, "dx"), "dy")
    overlaps_other = other_band(overlaps)
    (filtered,) = filter_step(field, flat_potential, exchange(*sent), fields[2], True)

    filtered = filtered.reshape(own_count, cell_count)
    rounded = filtered.astype(jnp.bfloat16)
    rest = (filtered - rounded.astype(jnp.float32)).astype(jnp.bfloat16)
    rounded_other = other_band(rounded)
    both = jnp.concatenate([rounded, rounded_other], axis=0)
    parts = jnp.concatenate([both, rest], axis=0)
    local = rows_dot(both, own_resident)
    products = rows_dot(parts, parts)
    n = own_count
    squares_own = products[:n, :n] + products[:n, 2 * n :] + products[2 * n :, :n]
    squares_other = products[:n, n : 2 * n] + products[2 * n :, n : 2 * n]
    squares = jnp.concatenate([squares_own, squares_other], axis=1)
    squares = jnp.pad(squares, ((0, 0), (0, count - 2 * n)))
    summed = sum_over_grid(jnp.concatenate([local, squares], axis=0))
    correlations, squares = summed[: 2 * n], summed[2 * n :, : 2 * n]

    correlations_other = other_band(correlations)
    correlations_rounded = correlations.astype(jnp.bfloat16)
    correction = jnp.dot(correlations_rounded, own_resident, preferred_element_type=jnp.float32)
    got = other_band(correction[n:].astype(jnp.bfloat16))
    projected = filtered - correction[:n] - got.astype(jnp.float32)

    exact = functools.partial(rows_dot, precision=lax.Precision.HIGHEST)
    correlations_other = jnp.concatenate([correlations_other[n:], correlations_other[:n]], axis=0)
    whole = jnp.concatenate([correlations, correlations_other], axis=1)
    whole_rounded = whole.astype(jnp.bfloat16).astype(jnp.float32)
    between = overlaps[1] + overlaps_other[1].T
    overlap = jnp.concatenate(
        [
            jnp.concatenate([overlaps[0], between], axis=1),
            jnp.concatenate([between.T, overlaps_other[0]], axis=1),
        ],
        axis=0,
    )
    weighted = exact(whole_rounded[:n], overlap)
    gram = squares - exact(whole[:n], whole_rounded)
    gram = gram + exact(weighted, whole_rounded)
    gram = gram - exact(whole_rounded[:n], whole)
    turned = jnp.concatenate([gram[:, n:], gram[:, :n]], axis=1)
    gram = jnp.where(band == 0, gram, turned)
    total_cells = cell_count * lax.axis_size("dx") * lax.axis_size("dy")
    return (projected.reshape(orbital_block.shape), gram / total_cells)


def solution(mesh):
    placed = (P("band", "dx", "dy", None), P("dx", "dy", None), P("band", "dx", "dy", None))
    return jax.shard_map(
        shards,
        mesh=mesh,
        in_specs=placed,
        out_specs=(P("band", "dx", "dy", None), P("band", None)),
        check_vma=False,
    )
```

time: 1510 us -> 484 us (0.32)
  blocking collectives: 1310 us -> 0 us
  waiting for transfers between devices: 93.8 us -> 334 us
  starting transfers between devices: 68.3 us -> 103 us
    psum x2 -> x0, blocking collectives: 1300 us -> none  [the longest x1 655 us: shards(): correlations = lax.psum(local_correlations, ('dx', 'dy'))]
    psum x0 -> x2, waiting for transfers between devices: none -> 292 us  [shards(): overlaps = lax.psum(lax.psum(overlaps, 'dx'), 'dy')]
    ppermute x16 -> x21, waiting for transfers between devices: 93.7 us -> 35.9 us  [the longest x16 26.6 us: moved(): lax.ppermute(values, axis, [(i, (i + by) % count) for i in range(count)])]
    ppermute x16 -> x21, starting transfers between devices: 68.3 us -> 86.5 us  [the longest x16 73 us: moved(): lax.ppermute(values, axis, [(i, (i + by) % count) for i in range(count)])]
    all_to_all x0 -> x2, starting transfers between devices: none -> 16.5 us  [sum_over_grid(): values = jnp.sum(lax.all_to_all(sent, axis, 0, 0), axis=0)]
  transfers between devices with their start and end apart: 17 -> 25, of which waited for: 16 -> 13; matrix products, arithmetic and copies ran while one was open for 1% -> 2% of each run, Pallas kernels for 0% -> 1%
where the time goes in v2:
time: 484 us; the launch traced here: 483 us
  waiting for transfers between devices  334 us (69%)
  starting transfers between devices  103 us (21%)
  between operations  14.5 us (3%)
  Pallas kernels  9.22 us (2%)
  local copies, waits for them, and re-layouts  7.7 us (2%)
  matrix products  7.28 us (2%)
  other arithmetic  6.66 us (1%)
    psum x2, waiting for transfers between devices, shards(): overlaps = lax.psum(lax.psum(overlaps, 'dx'), 'dy')  292 us
    ppermute x16, starting transfers between devices, moved(): lax.ppermute(values, axis, [(i, (i + by) % count) for i in range(count)])  73 us
    ppermute x16, waiting for transfers between devices, moved(): lax.ppermute(values, axis, [(i, (i + by) % count) for i in range(count)])  26.6 us
    all_to_all x2, starting transfers between devices, sum_over_grid(): values = jnp.sum(lax.all_to_all(sent, axis, 0, 0), axis=0)  16.5 us
    ppermute x5, starting transfers between devices, other_band(): return lax.ppermute(values, 'band', [(0, 1), (1, 0)])  13.5 us
  transfers between devices with their start and end apart: 25, of which 13 were waited for; matrix products, arithmetic and copies ran while one was open for 2% of the time, Pallas kernels for 1%

profile of v2, /device:TPU:1, one launch (start us, length us, event | category | flops | bytes accessed | tf_op | source)
XLA Modules:
  0.0 482.6 jit_solution(6820825905821865265)
XLA Ops:
  7.2 2.3 broadcast_select_fusion
  9.5 3.9 collective-permute-start.8
  13.7 5.2 %collective-permute-start.2 = (bf16[672,128]{1,0:T(8,128)(2,1)S(1)}, bf16[672,128]{1,0:T(8,128)(2,1)S(1)}, u32[]{:S(2)}, u32[]{:S(2)}) collective-permute-start(bf16[672,128]{1,0:T(8,128)(2,1)S(1)} %get-tuple-element.25), channel_id=1, source_target_pairs={{0,1},{1,2},{2,3},{3,4},{4,5},{5,6},{6,7},{7,8},{8,9},{9,10},{10,1... | collective-permute-start | bytes 516104 | tf_op jit(solution)/shard_map/ppermute | solution.py:165
  18.9 3.5 collective-permute-start.3
  24.4 9.5 %collective-permute-start.1 = (bf16[448,128]{1,0:T(8,128)(2,1)S(1)}, bf16[448,128]{1,0:T(8,128)(2,1)S(1)}, u32[]{:S(2)}, u32[]{:S(2)}) collective-permute-start(bf16[448,128]{1,0:T(8,128)(2,1)S(1)} %get-tuple-element.24), channel_id=1, source_target_pairs={{0,240},{16,0},{32,16},{48,32},{64,48},{80,64},{96,80},{112,96},{1... | collective-permute-start | bytes 344072 | tf_op jit(solution)/shard_map/ppermute | solution.py:165
  35.7 10.5 %collective-permute-done.2.refs_4_ = bf16[672,128]{1,0:T(8,128)(2,1)S(1)} collective-permute-done((bf16[672,128]{1,0:T(8,128)(2,1)S(1)}, bf16[672,128]{1,0:T(8,128)(2,1)S(1)}, u32[]{:S(2)}, u32[]{:S(2)}) %collective-permute-start.2) | collective-permute-done | bytes 172064 | tf_op jit(solution)/shard_map/ppermute | solution.py:165
  46.2 8.3 %collective-permute-done.3.refs_5_ = bf16[672,128]{1,0:T(8,128)(2,1)S(1)} collective-permute-done((bf16[672,128]{1,0:T(8,128)(2,1)S(1)}, bf16[672,128]{1,0:T(8,128)(2,1)S(1)}, u32[]{:S(2)}, u32[]{:S(2)}) %collective-permute-start.3) | collective-permute-done | bytes 172064 | tf_op jit(solution)/shard_map/ppermute | solution.py:165
  54.5 2.2 shard_map.51
  58.7 3.6 collective-permute-start.7
  62.3 3.5 collective-permute-start.4
  65.8 9.5 %collective-permute-start.5 = (bf16[448,128]{1,0:T(8,128)(2,1)S(1)}, bf16[448,128]{1,0:T(8,128)(2,1)S(1)}, u32[]{:S(2)}, u32[]{:S(2)}) collective-permute-start(bf16[448,128]{1,0:T(8,128)(2,1)S(1)} %get-tuple-element.29), channel_id=1, source_target_pairs={{0,240},{16,0},{32,16},{48,32},{64,48},{80,64},{96,80},{112,96},{1... | collective-permute-start | bytes 344072 | tf_op jit(solution)/shard_map/ppermute | solution.py:165
  77.1 2.2 shard_map.52
  79.4 4.6 collective-permute-start.11
  84.0 5.4 %collective-permute-start.12 = (bf16[672,128]{1,0:T(8,128)(2,1)S(1)}, bf16[672,128]{1,0:T(8,128)(2,1)S(1)}, u32[]{:S(2)}, u32[]{:S(2)}) collective-permute-start(bf16[672,128]{1,0:T(8,128)(2,1)S(1)} %get-tuple-element.36), channel_id=1, source_target_pairs={{0,15},{1,0},{2,1},{3,2},{4,3},{5,4},{6,5},{7,6},{8,7},{9,8},{10,9... | collective-permute-start | bytes 516104 | tf_op jit(solution)/shard_map/ppermute | solution.py:165
  89.4 5.3 %collective-permute-start.10 = (bf16[448,128]{1,0:T(8,128)(2,1)S(1)}, bf16[448,128]{1,0:T(8,128)(2,1)S(1)}, u32[]{:S(2)}, u32[]{:S(2)}) collective-permute-start(bf16[448,128]{1,0:T(8,128)(2,1)S(1)} %get-tuple-element.34), channel_id=1, source_target_pairs={{0,240},{16,0},{32,16},{48,32},{64,48},{80,64},{96,80},{112,96},{1... | collective-permute-start | bytes 344072 | tf_op jit(solution)/shard_map/ppermute | solution.py:165
  97.2 4.2 collective-permute-done.9.refs_2_
  101.4 2.2 shard_map.53
  103.7 3.8 collective-permute-start.15
  107.5 6.8 %collective-permute-start.16 = (bf16[672,128]{1,0:T(8,128)(2,1)S(1)}, bf16[672,128]{1,0:T(8,128)(2,1)S(1)}, u32[]{:S(2)}, u32[]{:S(2)}) collective-permute-start(bf16[672,128]{1,0:T(8,128)(2,1)S(1)} %get-tuple-element.41), channel_id=1, source_target_pairs={{0,15},{1,0},{2,1},{3,2},{4,3},{5,4},{6,5},{7,6},{8,7},{9,8},{10,9... | collective-permute-start | bytes 516104 | tf_op jit(solution)/shard_map/ppermute | solution.py:165
  116.2 4.6 collective-permute-start.14
  122.6 2.3 shard_map.54
  126.9 4.5 collective-permute-done.17
  131.9 3.1 fusion.2
  135.6 9.4 %all-to-all-start = ((f32[16,24,128]{2,1,0:T(8,128)}), f32[16,24,128]{2,1,0:T(8,128)}, u32[]{:S(2)}, u32[]{:S(2)}) async-start(f32[16,24,128]{2,1,0:T(8,128)} %broadcast_in_dim.4), calls=%async_computation | async-start | bytes 393216 | tf_op jit(solution)/shard_map/all_to_all | solution.py:178
  145.8 131.3 %all-reduce.4.cloned.1.call-done = f32[2,128,128]{2,1,0:T(8,128)} async-done(((f32[2,128,128]{2,1,0:T(8,128)}), f32[2,128,128]{2,1,0:T(8,128)}) %all-reduce.4.cloned.1.call-update) | async-done | bytes 131088 | tf_op jit(solution)/shard_map/psum | solution.py:219
  277.1 161.0 %all-reduce.6.cloned.1.call-done = f32[2,128,128]{2,1,0:T(8,128)} async-done(((f32[2,128,128]{2,1,0:T(8,128)}), f32[2,128,128]{2,1,0:T(8,128)}) %all-reduce.6.cloned.1.call-update) | async-done | bytes 131088 | tf_op jit(solution)/shard_map/psum | solution.py:219
  441.7 2.2 collective-permute-done.20
  447.9 7.1 %all-to-all-start.1 = ((f32[16,24,128]{2,1,0:T(8,128)}), f32[16,24,128]{2,1,0:T(8,128)}, u32[]{:S(2)}, u32[]{:S(2)}) async-start(f32[16,24,128]{2,1,0:T(8,128)} %broadcast_in_dim.5), calls=%async_computation.1 | async-start | bytes 393216 | tf_op jit(solution)/shard_map/all_to_all | solution.py:178
  458.1 5.2 %all-to-all-done.1 = f32[16,24,128]{2,1,0:T(8,128)} async-done(((f32[16,24,128]{2,1,0:T(8,128)}), f32[16,24,128]{2,1,0:T(8,128)}, u32[]{:S(2)}, u32[]{:S(2)}) %all-to-all-start.1) | async-done | bytes 196640 | tf_op jit(solution)/shard_map/all_to_all | solution.py:178
  464.3 2.3 collective-permute-start.19
  467.6 3.1 collective-permute-start.18
  472.2 2.6 collective-permute-done.18
  (77 shorter events, 32.8 us)
Async XLA Ops:
  7.2 47.3 %copy-start.1 = (f32[12,8,128]{2,1,0:T(8,128)S(1)}, f32[12,8,128]{2,1,0:T(8,128)}, u32[]{:S(2)}) copy-start(f32[12,8,128]{2,1,0:T(8,128)} %param.4) | copy-start | bytes 147460
  7.2 68.1 %copy-start.3 = (bf16[128,12,8,128]{3,2,1,0:T(8,128)(2,1)S(1)}, bf16[128,12,8,128]{3,2,1,0:T(8,128)(2,1)}, u32[]{:S(2)}) copy-start(bf16[128,12,8,128]{3,2,1,0:T(8,128)(2,1)} %param.5) | copy-start | bytes 9437188
  9.5 67.7 %collective-permute-start.8 = (bf16[128,6,8,128]{3,2,1,0:T(8,128)(2,1)S(1)}, bf16[128,6,8,128]{3,2,1,0:T(8,128)(2,1)S(1)}, u32[]{:S(2)}, u32[]{:S(2)}) collective-permute-start(bf16[128,6,8,128]{3,2,1,0:T(8,128)(2,1)S(1)} %get-tuple-element.49), channel_id=1, source_target_pairs={{0,256},{256,0},{1,257},{257,1},{2,258},{258,2},{3,259},{259,3},{4... | collective-permute-start | bytes 4718600 | tf_op jit(solution)/shard_map/ppermute | solution.py:183
  13.7 32.5 %collective-permute-start.2 = (bf16[672,128]{1,0:T(8,128)(2,1)S(1)}, bf16[672,128]{1,0:T(8,128)(2,1)S(1)}, u32[]{:S(2)}, u32[]{:S(2)}) collective-permute-start(bf16[672,128]{1,0:T(8,128)(2,1)S(1)} %get-tuple-element.25), channel_id=1, source_target_pairs={{0,1},{1,2},{2,3},{3,4},{4,5},{5,6},{6,7},{7,8},{8,9},{9,10},{10,1... | collective-permute-start | bytes 516104 | tf_op jit(solution)/shard_map/ppermute | solution.py:165
  18.9 35.6 %collective-permute-start.3 = (bf16[672,128]{1,0:T(8,128)(2,1)S(1)}, bf16[672,128]{1,0:T(8,128)(2,1)S(1)}, u32[]{:S(2)}, u32[]{:S(2)}) collective-permute-start(bf16[672,128]{1,0:T(8,128)(2,1)S(1)} %get-tuple-element.26), channel_id=1, source_target_pairs={{0,15},{1,0},{2,1},{3,2},{4,3},{5,4},{6,5},{7,6},{8,7},{9,8},{10,9... | collective-permute-start | bytes 516104 | tf_op jit(solution)/shard_map/ppermute | solution.py:165
  22.4 11.7 %collective-permute-start = (bf16[448,128]{1,0:T(8,128)(2,1)S(1)}, bf16[448,128]{1,0:T(8,128)(2,1)S(1)}, u32[]{:S(2)}, u32[]{:S(2)}) collective-permute-start(bf16[448,128]{1,0:T(8,128)(2,1)S(1)} %get-tuple-element.23), channel_id=1, source_target_pairs={{0,16},{16,32},{32,48},{48,64},{64,80},{80,96},{96,112},{112,128},... | collective-permute-start | bytes 344072 | tf_op jit(solution)/shard_map/ppermute | solution.py:165
  24.4 11.3 %collective-permute-start.1 = (bf16[448,128]{1,0:T(8,128)(2,1)S(1)}, bf16[448,128]{1,0:T(8,128)(2,1)S(1)}, u32[]{:S(2)}, u32[]{:S(2)}) collective-permute-start(bf16[448,128]{1,0:T(8,128)(2,1)S(1)} %get-tuple-element.24), channel_id=1, source_target_pairs={{0,240},{16,0},{32,16},{48,32},{64,48},{80,64},{96,80},{112,96},{1... | collective-permute-start | bytes 344072 | tf_op jit(solution)/shard_map/ppermute | solution.py:165
  56.7 20.4 %collective-permute-start.6 = (bf16[672,128]{1,0:T(8,128)(2,1)S(1)}, bf16[672,128]{1,0:T(8,128)(2,1)S(1)}, u32[]{:S(2)}, u32[]{:S(2)}) collective-permute-start(bf16[672,128]{1,0:T(8,128)(2,1)S(1)} %get-tuple-element.30), channel_id=1, source_target_pairs={{0,1},{1,2},{2,3},{3,4},{4,5},{5,6},{6,7},{7,8},{8,9},{9,10},{10,1... | collective-permute-start | bytes 516104 | tf_op jit(solution)/shard_map/ppermute | solution.py:165
  58.7 18.5 %collective-permute-start.7 = (bf16[672,128]{1,0:T(8,128)(2,1)S(1)}, bf16[672,128]{1,0:T(8,128)(2,1)S(1)}, u32[]{:S(2)}, u32[]{:S(2)}) collective-permute-start(bf16[672,128]{1,0:T(8,128)(2,1)S(1)} %get-tuple-element.31), channel_id=1, source_target_pairs={{0,15},{1,0},{2,1},{3,2},{4,3},{5,4},{6,5},{7,6},{8,7},{9,8},{10,9... | collective-permute-start | bytes 516104 | tf_op jit(solution)/shard_map/ppermute | solution.py:165
  62.3 14.8 %collective-permute-start.4 = (bf16[448,128]{1,0:T(8,128)(2,1)S(1)}, bf16[448,128]{1,0:T(8,128)(2,1)S(1)}, u32[]{:S(2)}, u32[]{:S(2)}) collective-permute-start(bf16[448,128]{1,0:T(8,128)(2,1)S(1)} %get-tuple-element.28), channel_id=1, source_target_pairs={{0,16},{16,32},{32,48},{48,64},{64,80},{80,96},{96,112},{112,128},... | collective-permute-start | bytes 344072 | tf_op jit(solution)/shard_map/ppermute | solution.py:165
  65.8 11.3 %collective-permute-start.5 = (bf16[448,128]{1,0:T(8,128)(2,1)S(1)}, bf16[448,128]{1,0:T(8,128)(2,1)S(1)}, u32[]{:S(2)}, u32[]{:S(2)}) collective-permute-start(bf16[448,128]{1,0:T(8,128)(2,1)S(1)} %get-tuple-element.29), channel_id=1, source_target_pairs={{0,240},{16,0},{32,16},{48,32},{64,48},{80,64},{96,80},{112,96},{1... | collective-permute-start | bytes 344072 | tf_op jit(solution)/shard_map/ppermute | solution.py:165
  79.4 22.0 %collective-permute-start.11 = (bf16[672,128]{1,0:T(8,128)(2,1)S(1)}, bf16[672,128]{1,0:T(8,128)(2,1)S(1)}, u32[]{:S(2)}, u32[]{:S(2)}) collective-permute-start(bf16[672,128]{1,0:T(8,128)(2,1)S(1)} %get-tuple-element.35), channel_id=1, source_target_pairs={{0,1},{1,2},{2,3},{3,4},{4,5},{5,6},{6,7},{7,8},{8,9},{9,10},{10,1... | collective-permute-start | bytes 516104 | tf_op jit(solution)/shard_map/ppermute | solution.py:165
  84.0 17.4 %collective-permute-start.12 = (bf16[672,128]{1,0:T(8,128)(2,1)S(1)}, bf16[672,128]{1,0:T(8,128)(2,1)S(1)}, u32[]{:S(2)}, u32[]{:S(2)}) collective-permute-start(bf16[672,128]{1,0:T(8,128)(2,1)S(1)} %get-tuple-element.36), channel_id=1, source_target_pairs={{0,15},{1,0},{2,1},{3,2},{4,3},{5,4},{6,5},{7,6},{8,7},{9,8},{10,9... | collective-permute-start | bytes 516104 | tf_op jit(solution)/shard_map/ppermute | solution.py:165
  89.4 7.8 %collective-permute-start.10 = (bf16[448,128]{1,0:T(8,128)(2,1)S(1)}, bf16[448,128]{1,0:T(8,128)(2,1)S(1)}, u32[]{:S(2)}, u32[]{:S(2)}) collective-permute-start(bf16[448,128]{1,0:T(8,128)(2,1)S(1)} %get-tuple-element.34), channel_id=1, source_target_pairs={{0,240},{16,0},{32,16},{48,32},{64,48},{80,64},{96,80},{112,96},{1... | collective-permute-start | bytes 344072 | tf_op jit(solution)/shard_map/ppermute | solution.py:165
  94.7 6.7 %collective-permute-start.9 = (bf16[448,128]{1,0:T(8,128)(2,1)S(1)}, bf16[448,128]{1,0:T(8,128)(2,1)S(1)}, u32[]{:S(2)}, u32[]{:S(2)}) collective-permute-start(bf16[448,128]{1,0:T(8,128)(2,1)S(1)} %get-tuple-element.33), channel_id=1, source_target_pairs={{0,16},{16,32},{32,48},{48,64},{64,80},{80,96},{96,112},{112,128},... | collective-permute-start | bytes 344072 | tf_op jit(solution)/shard_map/ppermute | solution.py:165
  97.2 27.6 %copy-start = (f32[2,128,128]{2,1,0:T(8,128)}, f32[2,128,128]{2,1,0:T(8,128)S(1)}, u32[]{:S(2)}) copy-start(f32[2,128,128]{2,1,0:T(8,128)S(1)} %pad_maximum_fusion.refs_7_) | copy-start | bytes 393220
  103.7 18.9 %collective-permute-start.15 = (bf16[672,128]{1,0:T(8,128)(2,1)S(1)}, bf16[672,128]{1,0:T(8,128)(2,1)S(1)}, u32[]{:S(2)}, u32[]{:S(2)}) collective-permute-start(bf16[672,128]{1,0:T(8,128)(2,1)S(1)} %get-tuple-element.40), channel_id=1, source_target_pairs={{0,1},{1,2},{2,3},{3,4},{4,5},{5,6},{6,7},{7,8},{8,9},{9,10},{10,1... | collective-permute-start | bytes 516104 | tf_op jit(solution)/shard_map/ppermute | solution.py:165
  107.5 15.1 %collective-permute-start.16 = (bf16[672,128]{1,0:T(8,128)(2,1)S(1)}, bf16[672,128]{1,0:T(8,128)(2,1)S(1)}, u32[]{:S(2)}, u32[]{:S(2)}) collective-permute-start(bf16[672,128]{1,0:T(8,128)(2,1)S(1)} %get-tuple-element.41), channel_id=1, source_target_pairs={{0,15},{1,0},{2,1},{3,2},{4,3},{5,4},{6,5},{7,6},{8,7},{9,8},{10,9... | collective-permute-start | bytes 516104 | tf_op jit(solution)/shard_map/ppermute | solution.py:165
  114.3 6.7 %collective-permute-start.13 = (bf16[448,128]{1,0:T(8,128)(2,1)S(1)}, bf16[448,128]{1,0:T(8,128)(2,1)S(1)}, u32[]{:S(2)}, u32[]{:S(2)}) collective-permute-start(bf16[448,128]{1,0:T(8,128)(2,1)S(1)} %get-tuple-element.38), channel_id=1, source_target_pairs={{0,16},{16,32},{32,48},{48,64},{64,80},{80,96},{96,112},{112,128},... | collective-permute-start | bytes 344072 | tf_op jit(solution)/shard_map/ppermute | solution.py:165
  116.2 6.4 %collective-permute-start.14 = (bf16[448,128]{1,0:T(8,128)(2,1)S(1)}, bf16[448,128]{1,0:T(8,128)(2,1)S(1)}, u32[]{:S(2)}, u32[]{:S(2)}) collective-permute-start(bf16[448,128]{1,0:T(8,128)(2,1)S(1)} %get-tuple-element.39), channel_id=1, source_target_pairs={{0,240},{16,0},{32,16},{48,32},{64,48},{80,64},{96,80},{112,96},{1... | collective-permute-start | bytes 344072 | tf_op jit(solution)/shard_map/ppermute | solution.py:165
  125.0 6.4 %collective-permute-start.17 = (bf16[8,12288]{1,0:T(8,128)(2,1)S(1)}, bf16[8,12288]{1,0:T(8,128)(2,1)S(1)}, u32[]{:S(2)}, u32[]{:S(2)}) collective-permute-start(bf16[8,12288]{1,0:T(8,128)(2,1)S(1)} %get-tuple-element.47), channel_id=1, source_target_pairs={{0,256},{256,0},{1,257},{257,1},{2,258},{258,2},{3,259},{259,3},{4... | collective-permute-start | bytes 589832 | tf_op jit(solution)/shard_map/ppermute | solution.py:183
  131.9 334.8 %copy-start.4 = (bf16[128,12,8,128]{3,2,1,0:T(8,128)(2,1)S(1)}, bf16[128,12,8,128]{3,2,1,0:T(8,128)(2,1)}, u32[]{:S(2)}) copy-start(bf16[128,12,8,128]{3,2,1,0:T(8,128)(2,1)} %param.5) | copy-start | bytes 9437188
  135.6 310.6 %all-to-all-start = ((f32[16,24,128]{2,1,0:T(8,128)}), f32[16,24,128]{2,1,0:T(8,128)}, u32[]{:S(2)}, u32[]{:S(2)}) async-start(f32[16,24,128]{2,1,0:T(8,128)} %broadcast_in_dim.4), calls=%async_computation | async-start | bytes 393216 | tf_op jit(solution)/shard_map/all_to_all | solution.py:178
  145.0 132.1 %all-reduce.4.cloned.1.call-start = ((), (), s32[]{:S(2)}) async-start(), calls=%async_computation.2 | async-start | bytes 262144 | tf_op jit(solution)/shard_map/psum | solution.py:219
  145.7 292.4 %all-reduce.6.cloned.1.call-start = ((), (), s32[]{:S(2)}) async-start(), calls=%async_computation.3 | async-start | bytes 262144 | tf_op jit(solution)/shard_map/psum | solution.py:219
  438.1 5.9 %collective-permute-start.20 = (f32[2,128,128]{2,1,0:T(8,128)}, f32[2,128,128]{2,1,0:T(8,128)S(1)}, u32[]{:S(2)}, u32[]{:S(2)}) collective-permute-start(f32[2,128,128]{2,1,0:T(8,128)} %all-reduce.6.cloned.1.call-done), channel_id=1, source_target_pairs={{0,256},{256,0},{1,257},{257,1},{2,258},{258,2},{3,259},{259,3},{4... | collective-permute-start | bytes 393224 | tf_op jit(solution)/shard_map/ppermute | solution.py:183
  447.9 15.4 %all-to-all-start.1 = ((f32[16,24,128]{2,1,0:T(8,128)}), f32[16,24,128]{2,1,0:T(8,128)}, u32[]{:S(2)}, u32[]{:S(2)}) async-start(f32[16,24,128]{2,1,0:T(8,128)} %broadcast_in_dim.5), calls=%async_computation.1 | async-start | bytes 393216 | tf_op jit(solution)/shard_map/all_to_all | solution.py:178
  464.3 6.6 %copy-start.5 = (f32[128,128]{1,0:T(8,128)S(1)}, f32[128,128]{1,0:T(8,128)}, u32[]{:S(2)}) copy-start(f32[128,128]{1,0:T(8,128)} %fusion.37) | copy-start | bytes 196612
  464.3 6.6 %copy-start.6 = (f32[128,128]{1,0:T(8,128)S(1)}, f32[128,128]{1,0:T(8,128)}, u32[]{:S(2)}) copy-start(f32[128,128]{1,0:T(8,128)} %slice_bitcast_fusion.2) | copy-start | bytes 196612
  464.3 6.6 %copy-start.7 = (f32[128,128]{1,0:T(8,128)S(1)}, f32[128,128]{1,0:T(8,128)}, u32[]{:S(2)}) copy-start(f32[128,128]{1,0:T(8,128)} %copy.17) | copy-start | bytes 196612
  464.3 6.4 %collective-permute-start.19 = (f32[16,128]{1,0:T(8,128)S(1)}, f32[16,128]{1,0:T(8,128)S(1)}, u32[]{:S(2)}, u32[]{:S(2)}) collective-permute-start(f32[16,128]{1,0:T(8,128)S(1)} %slice.93), channel_id=1, source_target_pairs={{0,256},{256,0},{1,257},{257,1},{2,258},{258,2},{3,259},{259,3},{4... | collective-permute-start | bytes 24584 | tf_op jit(solution)/shard_map/ppermute | solution.py:183
  467.6 7.2 %collective-permute-start.18 = (bf16[8,12288]{1,0:T(8,128)(2,1)S(1)}, bf16[8,12288]{1,0:T(8,128)(2,1)S(1)}, u32[]{:S(2)}, u32[]{:S(2)}) collective-permute-start(bf16[8,12288]{1,0:T(8,128)(2,1)S(1)} %slice.136), channel_id=1, source_target_pairs={{0,256},{256,0},{1,257},{257,1},{2,258},{258,2},{3,259},{259,3},{4... | collective-permute-start | bytes 589832 | tf_op jit(solution)/shard_map/ppermute | solution.py:183
  (2 other events, 12.9 us)
Sparse Core Ops, SparseCore 0:
  148.1 128.9 all-reduce.3
  280.2 157.7 all-reduce.5

commit v3 on v1

v3 whole, which is shorter than its diff:
```python
import functools

import jax
import jax.numpy as jnp
import ml_dtypes
import numpy as np
from jax import lax
from jax.experimental import pallas as pl
from jax.experimental.pallas import tpu as pltpu
from jax.sharding import PartitionSpec as P

DEGREE = 4


STENCIL_WEIGHTS = (
    -5369.0 / 1800.0,
    12.0 / 7.0,
    -15.0 / 56.0,
    10.0 / 189.0,
    -1.0 / 112.0,
    2.0 / 1925.0,
    -1.0 / 16632.0,
)
FILTER_CENTER = 23.0
FILTER_HALF = 21.0
WIDTH = 6
SENT = WIDTH + 1
VMEM_BYTES = 24 * 1024 * 1024


def pack_layer(out_ref, at, layer):
    rows = layer.shape[0] * layer.shape[1]
    out_ref[at * rows : (at + 1) * rows, :] = layer.reshape(rows, layer.shape[2]).astype(
        jnp.bfloat16
    )


def pack_messages(parity_ref, field_ref, x_even, x_odd, y_even, y_odd):
    def layer(dim, at):
        return field_ref[at] if dim == 0 else field_ref[:, at]

    for dim, even, odd in ((0, x_even, x_odd), (1, y_even, y_odd)):
        size = field_ref.shape[dim]
        for out_ref, tail in ((even, 1 - parity_ref[dim]), (odd, parity_ref[dim])):
            for at in range(WIDTH):
                pack_layer(out_ref, at, layer(dim, tail * (size - WIDTH) + at))
            nearest = layer(dim, tail * (size - 1))
            pack_layer(out_ref, WIDTH, nearest - nearest.astype(jnp.bfloat16).astype(jnp.float32))


def unpack_messages(parity_ref, halo_x, halo_y, x_even, x_odd, y_even, y_odd):
    for dim, halo, even, odd in ((0, halo_x, x_even, x_odd), (1, halo_y, y_even, y_odd)):
        shape = halo.shape[1:] if dim == 0 else halo.shape[:1] + halo.shape[2:]
        rows = shape[0] * shape[1]
        parity = parity_ref[dim]
        for got, after, near in ((even, 1 - parity, WIDTH - parity), (odd, parity, WIDTH - 1 + parity)):
            def read(at):
                return got[at * rows : (at + 1) * rows, :].astype(jnp.float32).reshape(shape)

            for at in range(WIDTH):
                place = after * WIDTH + at
                if dim == 0:
                    halo[place] = read(at)
                else:
                    halo[:, place] = read(at)
            if dim == 0:
                halo[near] += read(WIDTH)
            else:
                halo[:, near] += read(WIDTH)


def start_kernel(parity_ref, cells_ref, field_ref, *messages):
    size_x, size_y, own = field_ref.shape[:3]
    for x in range(size_x):
        for y in range(size_y):
            rows = pl.ds(x * size_y + y, own, stride=size_x * size_y)
            field_ref[x, y] = cells_ref[rows, :]
    pack_messages(parity_ref, field_ref, *messages)


def step_kernel(scale, has_previous, last, parity_ref, field_ref, potential_ref, band_ref, rest_ref, *refs):
    messages, refs = refs[:4], refs[4:]
    previous_ref = None
    if has_previous:
        previous_ref, refs = refs[0], refs[1:]
    outs, (halo_x, halo_y, total_ref) = refs[:-3], refs[-3:]
    size_x, size_y, own, depth = field_ref.shape
    unpack_messages(parity_ref, halo_x, halo_y, *messages)

    cells = field_ref[...].reshape(size_x * size_y * own, depth)
    high = cells.astype(jnp.bfloat16)
    low = (cells - high.astype(jnp.float32)).astype(jnp.bfloat16)
    along_z = jnp.dot(
        jnp.concatenate([high, low], axis=1), band_ref[...], preferred_element_type=jnp.float32
    ) + jnp.dot(high, rest_ref[...], preferred_element_type=jnp.float32)
    total_ref[...] = along_z.reshape(field_ref.shape)
    weights = [-2.0 * scale * w for w in STENCIL_WEIGHTS]

    @pl.loop(0, size_y)
    def _(y):
        line = [halo_x[k, y] for k in range(WIDTH)]
        line += [field_ref[x, y] for x in range(size_x)]
        line += [halo_x[WIDTH + k, y] for k in range(WIDTH)]
        for x in range(size_x):
            at = WIDTH + x
            total = total_ref[x, y]
            total = total + (scale * potential_ref[pl.ds(x * size_y + y, 1), :]) * line[at]
            if has_previous:
                total = total - previous_ref[x, y]
            for k in range(1, WIDTH + 1):
                total = total + weights[k] * (line[at + k] + line[at - k])
            total_ref[x, y] = total

    @pl.loop(0, size_x)
    def _(x):
        line = [halo_y[x, k] for k in range(WIDTH)]
        line += [field_ref[x, y] for y in range(size_y)]
        line += [halo_y[x, WIDTH + k] for k in range(WIDTH)]
        for y in range(size_y):
            at = WIDTH + y
            total = total_ref[x, y]
            for k in range(1, WIDTH + 1):
                total = total + weights[k] * (line[at + k] + line[at - k])
            if last:
                outs[0][pl.ds(x * size_y + y, own, stride=size_x * size_y), :] = total
            else:
                outs[0][x, y] = total

    if not last:
        pack_messages(parity_ref, *outs)


def message_shapes(size_x, size_y, own, depth):
    to_x = jax.ShapeDtypeStruct((SENT * size_y * own, depth), jnp.bfloat16)
    to_y = jax.ShapeDtypeStruct((SENT * size_x * own, depth), jnp.bfloat16)
    return [to_x, to_x, to_y, to_y]


def params():
    return pltpu.CompilerParams(vmem_limit_bytes=VMEM_BYTES)


def in_vmem(count):
    return [pl.BlockSpec(memory_space=pltpu.VMEM)] * count


def start(parity, orbital_block):
    own, size_x, size_y, depth = orbital_block.shape
    field = jax.ShapeDtypeStruct((size_x, size_y, own, depth), jnp.float32)
    return pl.pallas_call(
        start_kernel,
        out_shape=[field] + message_shapes(size_x, size_y, own, depth),
        in_specs=[pl.BlockSpec(memory_space=pltpu.SMEM)] + in_vmem(1),
        out_specs=in_vmem(5),
        compiler_params=params(),
    )(parity, orbital_block.reshape(own * size_x * size_y, depth))


def depth_matrices(scale, depth):
    weights = [-2.0 * scale * w for w in STENCIL_WEIGHTS]
    away = np.abs(np.arange(depth)[:, None] - np.arange(depth)[None, :])
    matrix = np.zeros((depth, depth), np.float32)
    for k in range(1, WIDTH + 1):
        matrix[away == k] = weights[k]
    matrix[away == 0] = 3.0 * weights[0] - scale * FILTER_CENTER
    high = matrix.astype(ml_dtypes.bfloat16)
    rest = (matrix - high.astype(np.float32)).astype(ml_dtypes.bfloat16)
    return jnp.asarray(np.concatenate([high, high], axis=0)), jnp.asarray(rest)


def filter_step(parity, field, potential, messages, previous, last):
    size_x, size_y, own, depth = field.shape
    scale = (1.0 if previous is None else 2.0) / FILTER_HALF
    if last:
        out_shape = [jax.ShapeDtypeStruct((own * size_x * size_y, depth), jnp.float32)]
    else:
        out_shape = [jax.ShapeDtypeStruct(field.shape, jnp.float32)]
        out_shape += message_shapes(size_x, size_y, own, depth)
    before = [] if previous is None else [previous]
    return pl.pallas_call(
        functools.partial(step_kernel, scale, previous is not None, last),
        out_shape=out_shape,
        in_specs=[pl.BlockSpec(memory_space=pltpu.SMEM)] + in_vmem(8 + len(before)),
        out_specs=in_vmem(len(out_shape)),
        scratch_shapes=[
            pltpu.VMEM((2 * WIDTH, size_y, own, depth), jnp.float32),
            pltpu.VMEM((size_x, 2 * WIDTH, own, depth), jnp.float32),
            pltpu.VMEM(field.shape, jnp.float32),
        ],
        compiler_params=params(),
    )(parity, field, potential, *depth_matrices(scale, depth), *messages, *before)


def swap(x_even, x_odd, y_even, y_odd):
    def swapped(values, axis, first):
        count = lax.axis_size(axis)
        step = lambda i: 1 if (i - first) % 2 == 0 else -1
        return lax.ppermute(values, axis, [(i, (i + step(i)) % count) for i in range(count)])

    return (
        swapped(x_even, "dx", 0),
        swapped(x_odd, "dx", 1),
        swapped(y_even, "dy", 0),
        swapped(y_odd, "dy", 1),
    )


def sum_over_grid(values):
    for axis in ("dx", "dy"):
        count = lax.axis_size(axis)
        sent = jnp.broadcast_to(values[None], (count,) + values.shape)
        values = jnp.sum(lax.all_to_all(sent, axis, 0, 0), axis=0)
    return values


def other_band(values):
    return lax.ppermute(values, "band", [(0, 1), (1, 0)])


def rows_dot(first, second, **kwargs):
    return lax.dot_general(
        first, second, (((1,), (1,)), ((), ())), preferred_element_type=jnp.float32, **kwargs
    )


def shards(orbital_block, potential, resident):
    own_count, size_x, size_y, depth = orbital_block.shape
    cell_count = size_x * size_y * depth
    flat_potential = potential.reshape(size_x * size_y, depth)
    parity = jnp.stack([lax.axis_index("dx") % 2, lax.axis_index("dy") % 2]).astype(jnp.int32)

    field, *messages = start(parity, orbital_block)
    previous = None
    for degree_step in range(DEGREE):
        last = degree_step == DEGREE - 1
        following, *messages = filter_step(
            parity, field, flat_potential, swap(*messages), previous, last
        )
        previous, field = field, following
    filtered = field.reshape(own_count, cell_count)

    rounded = filtered.astype(jnp.bfloat16)
    rounded_other = other_band(rounded)
    own_resident = resident.reshape(-1, cell_count)
    both = jnp.concatenate([rounded, rounded_other], axis=0)
    correlations = sum_over_grid(rows_dot(both, own_resident)).astype(jnp.bfloat16)
    correction = jnp.dot(correlations, own_resident, preferred_element_type=jnp.float32)
    mine, theirs = correction[:own_count], correction[own_count:]
    sent = jnp.concatenate([theirs, mine], axis=0).astype(jnp.bfloat16)
    got = other_band(sent).astype(jnp.float32)
    projected = filtered - mine - got[:own_count]
    projected_other = rounded_other.astype(jnp.float32) - theirs - got[own_count:]
    exact = functools.partial(rows_dot, precision=lax.Precision.HIGHEST)
    partial_own = exact(projected, projected)
    partial_other = exact(projected, projected_other)
    first = jnp.concatenate([partial_own, partial_other], axis=1)
    second = jnp.concatenate([partial_other, partial_own], axis=1)
    partial_gram = jnp.where(lax.axis_index("band") == 0, first, second)
    lanes = 128
    partial_gram = jnp.pad(partial_gram, ((0, 0), (0, lanes - 2 * own_count)))
    total_cells = cell_count * lax.axis_size("dx") * lax.axis_size("dy")
    gram_matrix = sum_over_grid(partial_gram)[:, : 2 * own_count] / total_cells
    return (projected.reshape(orbital_block.shape), gram_matrix)


def solution(mesh):
    placed = (P("band", "dx", "dy", None), P("dx", "dy", None), P("band", "dx", "dy", None))
    return jax.shard_map(
        shards,
        mesh=mesh,
        in_specs=placed,
        out_specs=(P("band", "dx", "dy", None), P("band", None)),
        check_vma=False,
    )
```

time: 189 us -> 187 us (0.989)
  other arithmetic: 15 us -> 1.02 us
  waiting for transfers between devices: 38.1 us -> 29.8 us
  Pallas kernels: 0 us -> 7.57 us
  local copies, waits for them, and re-layouts: 3.43 us -> 8.95 us
  starting transfers between devices: 69.9 us -> 75 us
  matrix products: 5.76 us -> 7.65 us
    ppermute x16, waiting for transfers between devices: 19.3 us -> 9.44 us  [swapped(): lax.ppermute(values, axis, [(i, (i + step(i)) % count) for i in range(cou...]
    convert_element_type x12 -> x1, other arithmetic: 8.97 us -> 0.02 us  [shards(): rounded = filtered.astype(jnp.bfloat16)]
    pallas_call x0 -> x5, Pallas kernels: none -> 7.57 us  [the longest x4 6.73 us: filter_step(): pl.pallas_call(functools.partial(step_kernel, scale, previous is not None...]
    unnamed x12 -> x23, local copies, waits for them, and re-layouts: 2.02 us -> 8.17 us
    ppermute x16, starting transfers between devices: 58 us -> 64.1 us  [swapped(): lax.ppermute(values, axis, [(i, (i + step(i)) % count) for i in range(cou...]
  transfers between devices with their start and end apart: 19 -> 19, of which waited for: 10 -> 7; matrix products, arithmetic and copies ran while one was open for 2% -> 0% of each run, Pallas kernels for 0% -> 0%
where the time goes in v3:
time: 187 us; the launch traced here: 186 us
  starting transfers between devices  75 us (40%)
  blocking collectives  55 us (29%)
  waiting for transfers between devices  29.8 us (16%)
  local copies, waits for them, and re-layouts  8.95 us (5%)
  matrix products  7.65 us (4%)
  Pallas kernels  7.57 us (4%)
    ppermute x16, starting transfers between devices, swapped(): lax.ppermute(values, axis, [(i, (i + step(i)) % count) for i in range(cou...  64.1 us
    all_to_all x3, blocking collectives, sum_over_grid(): values = jnp.sum(lax.all_to_all(sent, axis, 0, 0), axis=0)  55 us
    ppermute x2, waiting for transfers between devices, other_band(): return lax.ppermute(values, 'band', [(0, 1), (1, 0)])  13.8 us
    ppermute x16, waiting for transfers between devices, swapped(): lax.ppermute(values, axis, [(i, (i + step(i)) % count) for i in range(cou...  9.44 us
    unnamed x23, local copies, waits for them, and re-layouts  8.17 us
    pallas_call x4, Pallas kernels, filter_step(): pl.pallas_call(functools.partial(step_kernel, scale, previous is not None...  6.73 us
    all_to_all x1, waiting for transfers between devices, sum_over_grid(): values = jnp.sum(lax.all_to_all(sent, axis, 0, 0), axis=0)  6.57 us
    all_to_all x1, starting transfers between devices, sum_over_grid(): values = jnp.sum(lax.all_to_all(sent, axis, 0, 0), axis=0)  6.39 us
  transfers between devices with their start and end apart: 19, of which 7 were waited for; matrix products, arithmetic and copies ran while one was open for 0% of the time, Pallas kernels for 0%

profile of v3, /device:TPU:1, one launch (start us, length us, event | category | flops | bytes accessed | tf_op | source)
XLA Modules:
  0.0 185.9 jit_solution(11999483203590540072)
XLA Ops:
  2.6 8.8 %collective-permute-start.2 = (bf16[672,128]{1,0:T(8,128)(2,1)S(1)}, bf16[672,128]{1,0:T(8,128)(2,1)S(1)}, u32[]{:S(2)}, u32[]{:S(2)}) collective-permute-start(bf16[672,128]{1,0:T(8,128)(2,1)S(1)} %get-tuple-element.25), channel_id=1, source_target_pairs={{0,1},{1,0},{2,3},{3,2},{4,5},{5,4},{6,7},{7,6},{8,9},{9,8},{10,11... | collective-permute-start | bytes 516104 | tf_op jit(solution)/shard_map/ppermute | solution.py:198
  11.4 1.9 %collective-permute-start.3 = (bf16[672,128]{1,0:T(8,128)(2,1)S(1)}, bf16[672,128]{1,0:T(8,128)(2,1)S(1)}, u32[]{:S(2)}, u32[]{:S(2)}) collective-permute-start(bf16[672,128]{1,0:T(8,128)(2,1)S(1)} %get-tuple-element.26), channel_id=1, source_target_pairs={{0,15},{1,2},{2,1},{3,4},{4,3},{5,6},{6,5},{7,8},{8,7},{9,10},{10,... | collective-permute-start | bytes 516104 | tf_op jit(solution)/shard_map/ppermute | solution.py:198
  13.3 1.9 %collective-permute-start = (bf16[448,128]{1,0:T(8,128)(2,1)S(1)}, bf16[448,128]{1,0:T(8,128)(2,1)S(1)}, u32[]{:S(2)}, u32[]{:S(2)}) collective-permute-start(bf16[448,128]{1,0:T(8,128)(2,1)S(1)} %get-tuple-element.23), channel_id=1, source_target_pairs={{0,16},{16,0},{32,48},{48,32},{64,80},{80,64},{96,112},{112,96},{1... | collective-permute-start | bytes 344072 | tf_op jit(solution)/shard_map/ppermute | solution.py:198
  15.2 9.1 %collective-permute-start.1 = (bf16[448,128]{1,0:T(8,128)(2,1)S(1)}, bf16[448,128]{1,0:T(8,128)(2,1)S(1)}, u32[]{:S(2)}, u32[]{:S(2)}) collective-permute-start(bf16[448,128]{1,0:T(8,128)(2,1)S(1)} %get-tuple-element.24), channel_id=1, source_target_pairs={{0,240},{16,32},{32,16},{48,64},{64,48},{80,96},{96,80},{112,128},... | collective-permute-start | bytes 344072 | tf_op jit(solution)/shard_map/ppermute | solution.py:198
  24.4 2.2 %collective-permute-done.1.refs_1_ = bf16[448,128]{1,0:T(8,128)(2,1)S(1)} collective-permute-done((bf16[448,128]{1,0:T(8,128)(2,1)S(1)}, bf16[448,128]{1,0:T(8,128)(2,1)S(1)}, u32[]{:S(2)}, u32[]{:S(2)}) %collective-permute-start.1) | collective-permute-done | bytes 114720 | tf_op jit(solution)/shard_map/ppermute | solution.py:198
  30.6 6.0 %collective-permute-start.6 = (bf16[672,128]{1,0:T(8,128)(2,1)S(1)}, bf16[672,128]{1,0:T(8,128)(2,1)S(1)}, u32[]{:S(2)}, u32[]{:S(2)}) collective-permute-start(bf16[672,128]{1,0:T(8,128)(2,1)S(1)} %get-tuple-element.30), channel_id=1, source_target_pairs={{0,1},{1,0},{2,3},{3,2},{4,5},{5,4},{6,7},{7,6},{8,9},{9,8},{10,11... | collective-permute-start | bytes 516104 | tf_op jit(solution)/shard_map/ppermute | solution.py:198
  36.6 1.9 %collective-permute-start.7 = (bf16[672,128]{1,0:T(8,128)(2,1)S(1)}, bf16[672,128]{1,0:T(8,128)(2,1)S(1)}, u32[]{:S(2)}, u32[]{:S(2)}) collective-permute-start(bf16[672,128]{1,0:T(8,128)(2,1)S(1)} %get-tuple-element.31), channel_id=1, source_target_pairs={{0,15},{1,2},{2,1},{3,4},{4,3},{5,6},{6,5},{7,8},{8,7},{9,10},{10,... | collective-permute-start | bytes 516104 | tf_op jit(solution)/shard_map/ppermute | solution.py:198
  38.5 1.9 %collective-permute-start.4 = (bf16[448,128]{1,0:T(8,128)(2,1)S(1)}, bf16[448,128]{1,0:T(8,128)(2,1)S(1)}, u32[]{:S(2)}, u32[]{:S(2)}) collective-permute-start(bf16[448,128]{1,0:T(8,128)(2,1)S(1)} %get-tuple-element.28), channel_id=1, source_target_pairs={{0,16},{16,0},{32,48},{48,32},{64,80},{80,64},{96,112},{112,96},{1... | collective-permute-start | bytes 344072 | tf_op jit(solution)/shard_map/ppermute | solution.py:198
  40.5 4.9 %collective-permute-start.5 = (bf16[448,128]{1,0:T(8,128)(2,1)S(1)}, bf16[448,128]{1,0:T(8,128)(2,1)S(1)}, u32[]{:S(2)}, u32[]{:S(2)}) collective-permute-start(bf16[448,128]{1,0:T(8,128)(2,1)S(1)} %get-tuple-element.29), channel_id=1, source_target_pairs={{0,240},{16,32},{32,16},{48,64},{64,48},{80,96},{96,80},{112,128},... | collective-permute-start | bytes 344072 | tf_op jit(solution)/shard_map/ppermute | solution.py:198
  45.3 2.7 %collective-permute-done.5.refs_1_ = bf16[448,128]{1,0:T(8,128)(2,1)S(1)} collective-permute-done((bf16[448,128]{1,0:T(8,128)(2,1)S(1)}, bf16[448,128]{1,0:T(8,128)(2,1)S(1)}, u32[]{:S(2)}, u32[]{:S(2)}) %collective-permute-start.5) | collective-permute-done | bytes 114720 | tf_op jit(solution)/shard_map/ppermute | solution.py:198
  52.2 3.3 %collective-permute-start.10 = (bf16[672,128]{1,0:T(8,128)(2,1)S(1)}, bf16[672,128]{1,0:T(8,128)(2,1)S(1)}, u32[]{:S(2)}, u32[]{:S(2)}) collective-permute-start(bf16[672,128]{1,0:T(8,128)(2,1)S(1)} %get-tuple-element.35), channel_id=1, source_target_pairs={{0,1},{1,0},{2,3},{3,2},{4,5},{5,4},{6,7},{7,6},{8,9},{9,8},{10,11... | collective-permute-start | bytes 516104 | tf_op jit(solution)/shard_map/ppermute | solution.py:198
  55.4 4.1 %collective-permute-start.11 = (bf16[672,128]{1,0:T(8,128)(2,1)S(1)}, bf16[672,128]{1,0:T(8,128)(2,1)S(1)}, u32[]{:S(2)}, u32[]{:S(2)}) collective-permute-start(bf16[672,128]{1,0:T(8,128)(2,1)S(1)} %get-tuple-element.36), channel_id=1, source_target_pairs={{0,15},{1,2},{2,1},{3,4},{4,3},{5,6},{6,5},{7,8},{8,7},{9,10},{10,... | collective-permute-start | bytes 516104 | tf_op jit(solution)/shard_map/ppermute | solution.py:198
  59.5 2.4 %collective-permute-start.8 = (bf16[448,128]{1,0:T(8,128)(2,1)S(1)}, bf16[448,128]{1,0:T(8,128)(2,1)S(1)}, u32[]{:S(2)}, u32[]{:S(2)}) collective-permute-start(bf16[448,128]{1,0:T(8,128)(2,1)S(1)} %get-tuple-element.33), channel_id=1, source_target_pairs={{0,16},{16,0},{32,48},{48,32},{64,80},{80,64},{96,112},{112,96},{1... | collective-permute-start | bytes 344072 | tf_op jit(solution)/shard_map/ppermute | solution.py:198
  62.0 4.9 %collective-permute-start.9 = (bf16[448,128]{1,0:T(8,128)(2,1)S(1)}, bf16[448,128]{1,0:T(8,128)(2,1)S(1)}, u32[]{:S(2)}, u32[]{:S(2)}) collective-permute-start(bf16[448,128]{1,0:T(8,128)(2,1)S(1)} %get-tuple-element.34), channel_id=1, source_target_pairs={{0,240},{16,32},{32,16},{48,64},{64,48},{80,96},{96,80},{112,128},... | collective-permute-start | bytes 344072 | tf_op jit(solution)/shard_map/ppermute | solution.py:198
  66.8 2.2 %collective-permute-done.9.refs_1_ = bf16[448,128]{1,0:T(8,128)(2,1)S(1)} collective-permute-done((bf16[448,128]{1,0:T(8,128)(2,1)S(1)}, bf16[448,128]{1,0:T(8,128)(2,1)S(1)}, u32[]{:S(2)}, u32[]{:S(2)}) %collective-permute-start.9) | collective-permute-done | bytes 114720 | tf_op jit(solution)/shard_map/ppermute | solution.py:198
  72.3 4.5 %collective-permute-start.14 = (bf16[672,128]{1,0:T(8,128)(2,1)S(1)}, bf16[672,128]{1,0:T(8,128)(2,1)S(1)}, u32[]{:S(2)}, u32[]{:S(2)}) collective-permute-start(bf16[672,128]{1,0:T(8,128)(2,1)S(1)} %get-tuple-element.40), channel_id=1, source_target_pairs={{0,1},{1,0},{2,3},{3,2},{4,5},{5,4},{6,7},{7,6},{8,9},{9,8},{10,11... | collective-permute-start | bytes 516104 | tf_op jit(solution)/shard_map/ppermute | solution.py:198
  76.8 1.9 %collective-permute-start.15 = (bf16[672,128]{1,0:T(8,128)(2,1)S(1)}, bf16[672,128]{1,0:T(8,128)(2,1)S(1)}, u32[]{:S(2)}, u32[]{:S(2)}) collective-permute-start(bf16[672,128]{1,0:T(8,128)(2,1)S(1)} %get-tuple-element.41), channel_id=1, source_target_pairs={{0,15},{1,2},{2,1},{3,4},{4,3},{5,6},{6,5},{7,8},{8,7},{9,10},{10,... | collective-permute-start | bytes 516104 | tf_op jit(solution)/shard_map/ppermute | solution.py:198
  78.7 1.9 %collective-permute-start.12 = (bf16[448,128]{1,0:T(8,128)(2,1)S(1)}, bf16[448,128]{1,0:T(8,128)(2,1)S(1)}, u32[]{:S(2)}, u32[]{:S(2)}) collective-permute-start(bf16[448,128]{1,0:T(8,128)(2,1)S(1)} %get-tuple-element.38), channel_id=1, source_target_pairs={{0,16},{16,0},{32,48},{48,32},{64,80},{80,64},{96,112},{112,96},{1... | collective-permute-start | bytes 344072 | tf_op jit(solution)/shard_map/ppermute | solution.py:198
  80.6 4.7 %collective-permute-start.13 = (bf16[448,128]{1,0:T(8,128)(2,1)S(1)}, bf16[448,128]{1,0:T(8,128)(2,1)S(1)}, u32[]{:S(2)}, u32[]{:S(2)}) collective-permute-start(bf16[448,128]{1,0:T(8,128)(2,1)S(1)} %get-tuple-element.39), channel_id=1, source_target_pairs={{0,240},{16,32},{32,16},{48,64},{64,48},{80,96},{96,80},{112,128},... | collective-permute-start | bytes 344072 | tf_op jit(solution)/shard_map/ppermute | solution.py:198
  85.3 2.4 %collective-permute-done.13.refs_1_ = bf16[448,128]{1,0:T(8,128)(2,1)S(1)} collective-permute-done((bf16[448,128]{1,0:T(8,128)(2,1)S(1)}, bf16[448,128]{1,0:T(8,128)(2,1)S(1)}, u32[]{:S(2)}, u32[]{:S(2)}) %collective-permute-start.13) | collective-permute-done | bytes 114720 | tf_op jit(solution)/shard_map/ppermute | solution.py:198
  87.7 1.7 shard_map.126
  89.5 2.3 %collective-permute-start.16 = (bf16[8,12288]{1,0:T(8,128)(2,1)S(1)}, bf16[8,12288]{1,0:T(8,128)(2,1)S(1)}, u32[]{:S(2)}, u32[]{:S(2)}) collective-permute-start(bf16[8,12288]{1,0:T(8,128)(2,1)S(1)} %convert_element_type.15), channel_id=1, source_target_pairs={{0,256},{256,0},{1,257},{257,1},{2,258},{258,2},{3,259},{259,3},{4... | collective-permute-start | bytes 589832 | tf_op jit(solution)/shard_map/ppermute | solution.py:217
  91.8 4.1 %collective-permute-done.16 = bf16[8,12288]{1,0:T(8,128)(2,1)S(1)} collective-permute-done((bf16[8,12288]{1,0:T(8,128)(2,1)S(1)}, bf16[8,12288]{1,0:T(8,128)(2,1)S(1)}, u32[]{:S(2)}, u32[]{:S(2)}) %collective-permute-start.16) | collective-permute-done | bytes 196640 | tf_op jit(solution)/shard_map/ppermute | solution.py:217
  95.9 2.9 %fusion.2 = f32[16,128]{1,0:T(8,128)S(1)} fusion(bf16[16,8,96,128]{3,2,1,0:T(8,128)(2,1)} %bitcast.22, bf16[8,12288]{1,0:T(8,128)(2,1)S(1)} %collective-permute-done.16, bf16[8,12288]{1,0:T(8,128)(2,1)S(1)} %convert_element_type.15), kind=kOutput, calls=%fused_computation.2 | convolution fusion | flops 51118080 | bytes 3547136 | tf_op jit(solution)/shard_map/dot_general | solution.py:221
  98.8 20.2 %all_to_all.20 = f32[16,16,128]{2,1,0:T(8,128)S(1)} all-to-all(f32[16,16,128]{2,1,0:T(8,128)S(1)} %broadcast_in_dim.8), channel_id=1, replica_groups=mesh['band'=2,'dx'=16,'dy'=16] {'dx'}, dimensions={0} | all-to-all | bytes 262144 | tf_op jit(solution)/shard_map/all_to_all | solution.py:212
  119.0 19.8 %all_to_all.21 = f32[16,16,128]{2,1,0:T(8,128)S(1)} all-to-all(f32[16,16,128]{2,1,0:T(8,128)S(1)} %broadcast_in_dim.9), channel_id=1, replica_groups=mesh['band'=2,'dx'=16,'dy'=16] {'dy'}, dimensions={0} | all-to-all | bytes 262144 | tf_op jit(solution)/shard_map/all_to_all | solution.py:212
  138.8 2.9 %fusion = f32[16,12288]{1,0:T(8,128)S(1)} fusion(bf16[16,8,96,128]{3,2,1,0:T(8,128)(2,1)} %bitcast.23, bf16[16,128]{1,0:T(8,128)(2,1)S(1)} %reduce_sum.37), kind=kOutput, calls=%fused_computation | convolution fusion | flops 50331648 | bytes 3936256 | tf_op jit(solution)/shard_map/dot_general | solution.py:247
  141.7 2.2 %collective-permute-start.17 = (bf16[16,12288]{1,0:T(8,128)(2,1)S(1)}, bf16[16,12288]{1,0:T(8,128)(2,1)S(1)}, u32[]{:S(2)}, u32[]{:S(2)}) collective-permute-start(bf16[16,12288]{1,0:T(8,128)(2,1)S(1)} %pad_maximum_fusion), channel_id=1, source_target_pairs={{0,256},{256,0},{1,257},{257,1},{2,258},{258,2},{3,259},{259,3},{4... | collective-permute-start | bytes 1179656 | tf_op jit(solution)/shard_map/ppermute | solution.py:217
  144.0 9.7 %collective-permute-done.17 = bf16[16,12288]{1,0:T(8,128)(2,1)S(1)} collective-permute-done((bf16[16,12288]{1,0:T(8,128)(2,1)S(1)}, bf16[16,12288]{1,0:T(8,128)(2,1)S(1)}, u32[]{:S(2)}, u32[]{:S(2)}) %collective-permute-start.17) | collective-permute-done | bytes 393248 | tf_op jit(solution)/shard_map/ppermute | solution.py:217
  155.8 15.1 %all_to_all.22 = f32[16,8,128]{2,1,0:T(8,128)S(1)} all-to-all(f32[16,8,128]{2,1,0:T(8,128)S(1)} %broadcast_in_dim.10), channel_id=1, replica_groups=mesh['band'=2,'dx'=16,'dy'=16] {'dx'}, dimensions={0} | all-to-all | bytes 131072 | tf_op jit(solution)/shard_map/all_to_all | solution.py:212
  171.5 6.4 %all-to-all-start.3 = ((f32[16,8,128]{2,1,0:T(8,128)}), f32[16,8,128]{2,1,0:T(8,128)S(1)}, u32[]{:S(2)}, u32[]{:S(2)}) async-start(f32[16,8,128]{2,1,0:T(8,128)} %broadcast_in_dim.11), calls=%async_computation.3 | async-start | bytes 131072 | tf_op jit(solution)/shard_map/all_to_all | solution.py:212
  178.7 6.6 %all-to-all-done.3 = f32[16,8,128]{2,1,0:T(8,128)S(1)} async-done(((f32[16,8,128]{2,1,0:T(8,128)}), f32[16,8,128]{2,1,0:T(8,128)S(1)}, u32[]{:S(2)}, u32[]{:S(2)}) %all-to-all-start.3) | async-done | bytes 65568 | tf_op jit(solution)/shard_map/all_to_all | solution.py:212
  (59 shorter events, 17.8 us)
Async XLA Ops:
  0.6 68.4 %copy-start.5 = (bf16[256,128]{1,0:T(8,128)(2,1)S(1)}, bf16[256,128]{1,0:T(8,128)(2,1)}, u32[]{:S(2)}) copy-start(bf16[256,128]{1,0:T(8,128)(2,1)} %constant.47.clone.band_ref) | copy-start | bytes 196612
  0.6 87.0 %copy-start.3 = (f32[12,8,128]{2,1,0:T(8,128)S(1)}, f32[12,8,128]{2,1,0:T(8,128)}, u32[]{:S(2)}) copy-start(f32[12,8,128]{2,1,0:T(8,128)} %param.12) | copy-start | bytes 147460
  0.7 1.0 copy-start.6
  2.6 23.9 %collective-permute-start.2 = (bf16[672,128]{1,0:T(8,128)(2,1)S(1)}, bf16[672,128]{1,0:T(8,128)(2,1)S(1)}, u32[]{:S(2)}, u32[]{:S(2)}) collective-permute-start(bf16[672,128]{1,0:T(8,128)(2,1)S(1)} %get-tuple-element.25), channel_id=1, source_target_pairs={{0,1},{1,0},{2,3},{3,2},{4,5},{5,4},{6,7},{7,6},{8,9},{9,8},{10,11... | collective-permute-start | bytes 516104 | tf_op jit(solution)/shard_map/ppermute | solution.py:198
  11.4 15.1 %collective-permute-start.3 = (bf16[672,128]{1,0:T(8,128)(2,1)S(1)}, bf16[672,128]{1,0:T(8,128)(2,1)S(1)}, u32[]{:S(2)}, u32[]{:S(2)}) collective-permute-start(bf16[672,128]{1,0:T(8,128)(2,1)S(1)} %get-tuple-element.26), channel_id=1, source_target_pairs={{0,15},{1,2},{2,1},{3,4},{4,3},{5,6},{6,5},{7,8},{8,7},{9,10},{10,... | collective-permute-start | bytes 516104 | tf_op jit(solution)/shard_map/ppermute | solution.py:198
  13.3 11.0 %collective-permute-start = (bf16[448,128]{1,0:T(8,128)(2,1)S(1)}, bf16[448,128]{1,0:T(8,128)(2,1)S(1)}, u32[]{:S(2)}, u32[]{:S(2)}) collective-permute-start(bf16[448,128]{1,0:T(8,128)(2,1)S(1)} %get-tuple-element.23), channel_id=1, source_target_pairs={{0,16},{16,0},{32,48},{48,32},{64,80},{80,64},{96,112},{112,96},{1... | collective-permute-start | bytes 344072 | tf_op jit(solution)/shard_map/ppermute | solution.py:198
  15.2 11.3 %collective-permute-start.1 = (bf16[448,128]{1,0:T(8,128)(2,1)S(1)}, bf16[448,128]{1,0:T(8,128)(2,1)S(1)}, u32[]{:S(2)}, u32[]{:S(2)}) collective-permute-start(bf16[448,128]{1,0:T(8,128)(2,1)S(1)} %get-tuple-element.24), channel_id=1, source_target_pairs={{0,240},{16,32},{32,16},{48,64},{64,48},{80,96},{96,80},{112,128},... | collective-permute-start | bytes 344072 | tf_op jit(solution)/shard_map/ppermute | solution.py:198
  26.5 0.8 copy-start
  27.3 0.8 copy-start.9
  28.2 0.8 copy-start.10
  30.6 17.5 %collective-permute-start.6 = (bf16[672,128]{1,0:T(8,128)(2,1)S(1)}, bf16[672,128]{1,0:T(8,128)(2,1)S(1)}, u32[]{:S(2)}, u32[]{:S(2)}) collective-permute-start(bf16[672,128]{1,0:T(8,128)(2,1)S(1)} %get-tuple-element.30), channel_id=1, source_target_pairs={{0,1},{1,0},{2,3},{3,2},{4,5},{5,4},{6,7},{7,6},{8,9},{9,8},{10,11... | collective-permute-start | bytes 516104 | tf_op jit(solution)/shard_map/ppermute | solution.py:198
  36.6 11.5 %collective-permute-start.7 = (bf16[672,128]{1,0:T(8,128)(2,1)S(1)}, bf16[672,128]{1,0:T(8,128)(2,1)S(1)}, u32[]{:S(2)}, u32[]{:S(2)}) collective-permute-start(bf16[672,128]{1,0:T(8,128)(2,1)S(1)} %get-tuple-element.31), channel_id=1, source_target_pairs={{0,15},{1,2},{2,1},{3,4},{4,3},{5,6},{6,5},{7,8},{8,7},{9,10},{10,... | collective-permute-start | bytes 516104 | tf_op jit(solution)/shard_map/ppermute | solution.py:198
  38.5 6.8 %collective-permute-start.4 = (bf16[448,128]{1,0:T(8,128)(2,1)S(1)}, bf16[448,128]{1,0:T(8,128)(2,1)S(1)}, u32[]{:S(2)}, u32[]{:S(2)}) collective-permute-start(bf16[448,128]{1,0:T(8,128)(2,1)S(1)} %get-tuple-element.28), channel_id=1, source_target_pairs={{0,16},{16,0},{32,48},{48,32},{64,80},{80,64},{96,112},{112,96},{1... | collective-permute-start | bytes 344072 | tf_op jit(solution)/shard_map/ppermute | solution.py:198
  40.5 7.6 %collective-permute-start.5 = (bf16[448,128]{1,0:T(8,128)(2,1)S(1)}, bf16[448,128]{1,0:T(8,128)(2,1)S(1)}, u32[]{:S(2)}, u32[]{:S(2)}) collective-permute-start(bf16[448,128]{1,0:T(8,128)(2,1)S(1)} %get-tuple-element.29), channel_id=1, source_target_pairs={{0,240},{16,32},{32,16},{48,64},{64,48},{80,96},{96,80},{112,128},... | collective-permute-start | bytes 344072 | tf_op jit(solution)/shard_map/ppermute | solution.py:198
  48.1 0.8 copy-start.1
  48.9 0.8 copy-start.4
  49.7 0.8 copy-start.7
  52.2 16.8 %collective-permute-start.10 = (bf16[672,128]{1,0:T(8,128)(2,1)S(1)}, bf16[672,128]{1,0:T(8,128)(2,1)S(1)}, u32[]{:S(2)}, u32[]{:S(2)}) collective-permute-start(bf16[672,128]{1,0:T(8,128)(2,1)S(1)} %get-tuple-element.35), channel_id=1, source_target_pairs={{0,1},{1,0},{2,3},{3,2},{4,5},{5,4},{6,7},{7,6},{8,9},{9,8},{10,11... | collective-permute-start | bytes 516104 | tf_op jit(solution)/shard_map/ppermute | solution.py:198
  55.4 13.6 %collective-permute-start.11 = (bf16[672,128]{1,0:T(8,128)(2,1)S(1)}, bf16[672,128]{1,0:T(8,128)(2,1)S(1)}, u32[]{:S(2)}, u32[]{:S(2)}) collective-permute-start(bf16[672,128]{1,0:T(8,128)(2,1)S(1)} %get-tuple-element.36), channel_id=1, source_target_pairs={{0,15},{1,2},{2,1},{3,4},{4,3},{5,6},{6,5},{7,8},{8,7},{9,10},{10,... | collective-permute-start | bytes 516104 | tf_op jit(solution)/shard_map/ppermute | solution.py:198
  59.5 7.3 %collective-permute-start.8 = (bf16[448,128]{1,0:T(8,128)(2,1)S(1)}, bf16[448,128]{1,0:T(8,128)(2,1)S(1)}, u32[]{:S(2)}, u32[]{:S(2)}) collective-permute-start(bf16[448,128]{1,0:T(8,128)(2,1)S(1)} %get-tuple-element.33), channel_id=1, source_target_pairs={{0,16},{16,0},{32,48},{48,32},{64,80},{80,64},{96,112},{112,96},{1... | collective-permute-start | bytes 344072 | tf_op jit(solution)/shard_map/ppermute | solution.py:198
  62.0 7.0 %collective-permute-start.9 = (bf16[448,128]{1,0:T(8,128)(2,1)S(1)}, bf16[448,128]{1,0:T(8,128)(2,1)S(1)}, u32[]{:S(2)}, u32[]{:S(2)}) collective-permute-start(bf16[448,128]{1,0:T(8,128)(2,1)S(1)} %get-tuple-element.34), channel_id=1, source_target_pairs={{0,240},{16,32},{32,16},{48,64},{64,48},{80,96},{96,80},{112,128},... | collective-permute-start | bytes 344072 | tf_op jit(solution)/shard_map/ppermute | solution.py:198
  69.0 0.8 copy-start.2
  69.8 0.8 copy-start.8
  72.3 15.4 %collective-permute-start.14 = (bf16[672,128]{1,0:T(8,128)(2,1)S(1)}, bf16[672,128]{1,0:T(8,128)(2,1)S(1)}, u32[]{:S(2)}, u32[]{:S(2)}) collective-permute-start(bf16[672,128]{1,0:T(8,128)(2,1)S(1)} %get-tuple-element.40), channel_id=1, source_target_pairs={{0,1},{1,0},{2,3},{3,2},{4,5},{5,4},{6,7},{7,6},{8,9},{9,8},{10,11... | collective-permute-start | bytes 516104 | tf_op jit(solution)/shard_map/ppermute | solution.py:198
  76.8 10.9 %collective-permute-start.15 = (bf16[672,128]{1,0:T(8,128)(2,1)S(1)}, bf16[672,128]{1,0:T(8,128)(2,1)S(1)}, u32[]{:S(2)}, u32[]{:S(2)}) collective-permute-start(bf16[672,128]{1,0:T(8,128)(2,1)S(1)} %get-tuple-element.41), channel_id=1, source_target_pairs={{0,15},{1,2},{2,1},{3,4},{4,3},{5,6},{6,5},{7,8},{8,7},{9,10},{10,... | collective-permute-start | bytes 516104 | tf_op jit(solution)/shard_map/ppermute | solution.py:198
  78.7 6.6 %collective-permute-start.12 = (bf16[448,128]{1,0:T(8,128)(2,1)S(1)}, bf16[448,128]{1,0:T(8,128)(2,1)S(1)}, u32[]{:S(2)}, u32[]{:S(2)}) collective-permute-start(bf16[448,128]{1,0:T(8,128)(2,1)S(1)} %get-tuple-element.38), channel_id=1, source_target_pairs={{0,16},{16,0},{32,48},{48,32},{64,80},{80,64},{96,112},{112,96},{1... | collective-permute-start | bytes 344072 | tf_op jit(solution)/shard_map/ppermute | solution.py:198
  80.6 7.0 %collective-permute-start.13 = (bf16[448,128]{1,0:T(8,128)(2,1)S(1)}, bf16[448,128]{1,0:T(8,128)(2,1)S(1)}, u32[]{:S(2)}, u32[]{:S(2)}) collective-permute-start(bf16[448,128]{1,0:T(8,128)(2,1)S(1)} %get-tuple-element.39), channel_id=1, source_target_pairs={{0,240},{16,32},{32,16},{48,64},{64,48},{80,96},{96,80},{112,128},... | collective-permute-start | bytes 344072 | tf_op jit(solution)/shard_map/ppermute | solution.py:198
  89.5 6.4 %collective-permute-start.16 = (bf16[8,12288]{1,0:T(8,128)(2,1)S(1)}, bf16[8,12288]{1,0:T(8,128)(2,1)S(1)}, u32[]{:S(2)}, u32[]{:S(2)}) collective-permute-start(bf16[8,12288]{1,0:T(8,128)(2,1)S(1)} %convert_element_type.15), channel_id=1, source_target_pairs={{0,256},{256,0},{1,257},{257,1},{2,258},{258,2},{3,259},{259,3},{4... | collective-permute-start | bytes 589832 | tf_op jit(solution)/shard_map/ppermute | solution.py:217
  141.7 11.9 %collective-permute-start.17 = (bf16[16,12288]{1,0:T(8,128)(2,1)S(1)}, bf16[16,12288]{1,0:T(8,128)(2,1)S(1)}, u32[]{:S(2)}, u32[]{:S(2)}) collective-permute-start(bf16[16,12288]{1,0:T(8,128)(2,1)S(1)} %pad_maximum_fusion), channel_id=1, source_target_pairs={{0,256},{256,0},{1,257},{257,1},{2,258},{258,2},{3,259},{259,3},{4... | collective-permute-start | bytes 1179656 | tf_op jit(solution)/shard_map/ppermute | solution.py:217
  171.5 13.8 %all-to-all-start.3 = ((f32[16,8,128]{2,1,0:T(8,128)}), f32[16,8,128]{2,1,0:T(8,128)S(1)}, u32[]{:S(2)}, u32[]{:S(2)}) async-start(f32[16,8,128]{2,1,0:T(8,128)} %broadcast_in_dim.11), calls=%async_computation.3 | async-start | bytes 131072 | tf_op jit(solution)/shard_map/all_to_all | solution.py:212

commit v4 on v3

--- a/solution.py
+++ b/solution.py
@@ -2,8 +2,6 @@
 
 import jax
 import jax.numpy as jnp
-import ml_dtypes
-import numpy as np
 from jax import lax
 from jax.experimental import pallas as pl
 from jax.experimental.pallas import tpu as pltpu
@@ -25,7 +23,8 @@
 FILTER_HALF = 21.0
 WIDTH = 6
 SENT = WIDTH + 1
-VMEM_BYTES = 24 * 1024 * 1024
+SENT_SCALE = 1.0 / 64.0
+VMEM_BYTES = 8 * 1024 * 1024
 
 
 def pack_layer(out_ref, at, layer):
@@ -69,8 +68,19 @@
                 halo[:, near] += read(WIDTH)
 
 
-def start_kernel(parity_ref, cells_ref, field_ref, *messages):
-    size_x, size_y, own = field_ref.shape[:3]
+def start_kernel(parity_ref, cells_ref, potential_ref, field_ref, kept_ref, band_ref, rest_ref, *messages):
+    size_x, size_y, own, depth = field_ref.shape
+    kept_ref[...] = potential_ref[...]
+    row = lax.broadcasted_iota(jnp.int32, (depth, depth), 0)
+    away = jnp.abs(row - lax.broadcasted_iota(jnp.int32, (depth, depth), 1))
+    weights = [-2.0 * w / FILTER_HALF for w in STENCIL_WEIGHTS]
+    matrix = jnp.where(away == 0, 3.0 * weights[0] - FILTER_CENTER / FILTER_HALF, 0.0)
+    for k in range(1, WIDTH + 1):
+        matrix = jnp.where(away == k, weights[k], matrix)
+    high = matrix.astype(jnp.bfloat16)
+    band_ref[:depth, :] = high
+    band_ref[depth:, :] = high
+    rest_ref[...] = (matrix - high.astype(jnp.float32)).astype(jnp.bfloat16)
     for x in range(size_x):
         for y in range(size_y):
             rows = pl.ds(x * size_y + y, own, stride=size_x * size_y)
@@ -78,7 +88,9 @@
     pack_messages(parity_ref, field_ref, *messages)
 
 
-def step_kernel(scale, has_previous, last, parity_ref, field_ref, potential_ref, band_ref, rest_ref, *refs):
+def step_kernel(has_previous, last, parity_ref, field_ref, potential_ref, band_ref, rest_ref, *refs):
+    factor = 2.0 if has_previous else 1.0
+    scale = factor / FILTER_HALF
     messages, refs = refs[:4], refs[4:]
     previous_ref = None
     if has_previous:
@@ -93,7 +105,7 @@
     along_z = jnp.dot(
         jnp.concatenate([high, low], axis=1), band_ref[...], preferred_element_type=jnp.float32
     ) + jnp.dot(high, rest_ref[...], preferred_element_type=jnp.float32)
-    total_ref[...] = along_z.reshape(field_ref.shape)
+    total_ref[...] = (factor * along_z).reshape(field_ref.shape)
     weights = [-2.0 * scale * w for w in STENCIL_WEIGHTS]
 
     @pl.loop(0, size_y)
@@ -144,33 +156,26 @@
     return [pl.BlockSpec(memory_space=pltpu.VMEM)] * count
 
 
-def start(parity, orbital_block):
+def start(parity, orbital_block, potential):
     own, size_x, size_y, depth = orbital_block.shape
     field = jax.ShapeDtypeStruct((size_x, size_y, own, depth), jnp.float32)
     return pl.pallas_call(
         start_kernel,
-        out_shape=[field] + message_shapes(size_x, size_y, own, depth),
-        in_specs=[pl.BlockSpec(memory_space=pltpu.SMEM)] + in_vmem(1),
-        out_specs=in_vmem(5),
+        out_shape=[
+            field,
+            jax.ShapeDtypeStruct(potential.shape, jnp.float32),
+            jax.ShapeDtypeStruct((2 * depth, depth), jnp.bfloat16),
+            jax.ShapeDtypeStruct((depth, depth), jnp.bfloat16),
+        ]
+        + message_shapes(size_x, size_y, own, depth),
+        in_specs=[pl.BlockSpec(memory_space=pltpu.SMEM)] + in_vmem(2),
+        out_specs=in_vmem(8),
         compiler_params=params(),
-    )(parity, orbital_block.reshape(own * size_x * size_y, depth))
-
-
-def depth_matrices(scale, depth):
-    weights = [-2.0 * scale * w for w in STENCIL_WEIGHTS]
-    away = np.abs(np.arange(depth)[:, None] - np.arange(depth)[None, :])
-    matrix = np.zeros((depth, depth), np.float32)
-    for k in range(1, WIDTH + 1):
-        matrix[away == k] = weights[k]
-    matrix[away == 0] = 3.0 * weights[0] - scale * FILTER_CENTER
-    high = matrix.astype(ml_dtypes.bfloat16)
-    rest = (matrix - high.astype(np.float32)).astype(ml_dtypes.bfloat16)
-    return jnp.asarray(np.concatenate([high, high], axis=0)), jnp.asarray(rest)
-
-
-def filter_step(parity, field, potential, messages, previous, last):
+    )(parity, orbital_block.reshape(own * size_x * size_y, depth), potential)
+
+
+def filter_step(parity, field, fixed, messages, previous, last):
     size_x, size_y, own, depth = field.shape
-    scale = (1.0 if previous is None else 2.0) / FILTER_HALF
     if last:
         out_shape = [jax.ShapeDtypeStruct((own * size_x * size_y, depth), jnp.float32)]
     else:
@@ -178,7 +183,7 @@
         out_shape += message_shapes(size_x, size_y, own, depth)
     before = [] if previous is None else [previous]
     return pl.pallas_call(
-        functools.partial(step_kernel, scale, previous is not None, last),
+        functools.partial(step_kernel, previous is not None, last),
         out_shape=out_shape,
         in_specs=[pl.BlockSpec(memory_space=pltpu.SMEM)] + in_vmem(8 + len(before)),
         out_specs=in_vmem(len(out_shape)),
@@ -188,7 +193,7 @@
             pltpu.VMEM(field.shape, jnp.float32),
         ],
         compiler_params=params(),
-    )(parity, field, potential, *depth_matrices(scale, depth), *messages, *before)
+    )(parity, field, *fixed, *messages, *before)
 
 
 def swap(x_even, x_odd, y_even, y_odd):
@@ -205,11 +210,11 @@
     )
 
 
-def sum_over_grid(values):
+def sum_over_grid(values, sent_type):
     for axis in ("dx", "dy"):
         count = lax.axis_size(axis)
-        sent = jnp.broadcast_to(values[None], (count,) + values.shape)
-        values = jnp.sum(lax.all_to_all(sent, axis, 0, 0), axis=0)
+        sent = jnp.broadcast_to(values.astype(sent_type)[None], (count,) + values.shape)
+        values = jnp.sum(lax.all_to_all(sent, axis, 0, 0).astype(jnp.float32), axis=0)
     return values
 
 
@@ -229,12 +234,13 @@
     flat_potential = potential.reshape(size_x * size_y, depth)
     parity = jnp.stack([lax.axis_index("dx") % 2, lax.axis_index("dy") % 2]).astype(jnp.int32)
 
-    field, *messages = start(parity, orbital_block)
+    field, *rest = start(parity, orbital_block, flat_potential)
+    fixed, messages = rest[:3], rest[3:]
     previous = None
     for degree_step in range(DEGREE):
         last = degree_step == DEGREE - 1
         following, *messages = filter_step(
-            parity, field, flat_potential, swap(*messages), previous, last
+            parity, field, fixed, swap(*messages), previous, last
         )
         previous, field = field, following
     filtered = field.reshape(own_count, cell_count)
@@ -243,7 +249,8 @@
     rounded_other = other_band(rounded)
     own_resident = resident.reshape(-1, cell_count)
     both = jnp.concatenate([rounded, rounded_other], axis=0)
-    correlations = sum_over_grid(rows_dot(both, own_resident)).astype(jnp.bfloat16)
+    local = rows_dot(both, own_resident) * SENT_SCALE
+    correlations = (sum_over_grid(local, jnp.float16) / SENT_SCALE).astype(jnp.bfloat16)
     correction = jnp.dot(correlations, own_resident, preferred_element_type=jnp.float32)
     mine, theirs = correction[:own_count], correction[own_count:]
     sent = jnp.concatenate([theirs, mine], axis=0).astype(jnp.bfloat16)
@@ -251,15 +258,13 @@
     projected = filtered - mine - got[:own_count]
     projected_other = rounded_other.astype(jnp.float32) - theirs - got[own_count:]
     exact = functools.partial(rows_dot, precision=lax.Precision.HIGHEST)
-    partial_own = exact(projected, projected)
-    partial_other = exact(projected, projected_other)
-    first = jnp.concatenate([partial_own, partial_other], axis=1)
-    second = jnp.concatenate([partial_other, partial_own], axis=1)
-    partial_gram = jnp.where(lax.axis_index("band") == 0, first, second)
+    partial_gram = exact(projected, jnp.concatenate([projected, projected_other], axis=0))
+    turned = jnp.roll(partial_gram, own_count, axis=1)
+    partial_gram = jnp.where(lax.axis_index("band") == 0, partial_gram, turned)
     lanes = 128
     partial_gram = jnp.pad(partial_gram, ((0, 0), (0, lanes - 2 * own_count)))
     total_cells = cell_count * lax.axis_size("dx") * lax.axis_size("dy")
-    gram_matrix = sum_over_grid(partial_gram)[:, : 2 * own_count] / total_cells
+    gram_matrix = sum_over_grid(partial_gram, jnp.float32)[:, : 2 * own_count] / total_cells
     return (projected.reshape(orbital_block.shape), gram_matrix)
 
 

time: 187 us -> 176 us (0.941)
  local copies, waits for them, and re-layouts: 8.95 us -> 3.51 us
  matrix products: 7.65 us -> 4.79 us
  blocking collectives: 55 us -> 52.3 us
    unnamed x23 -> x7, local copies, waits for them, and re-layouts: 8.17 us -> 2.62 us
    all_to_all x3, blocking collectives: 55 us -> 52.3 us  [sum_over_grid(): lax.all_to_all(sent, axis, 0, 0).astype(jnp.float32)]
    dot_general x1, matrix products: 2.85 us -> 0.96 us  [shards(): jnp.dot(correlations, own_resident, preferred_element_type=jnp.float32)]
    dot_general x3 -> x2, matrix products: 4.8 us -> 3.83 us  [rows_dot(): lax.dot_general(first, second, (((1,), (1,)), ((), ())), preferred_elemen...]
where the time goes in v4:
time: 176 us; the launch traced here: 175 us
  starting transfers between devices  74.8 us (42%)
  blocking collectives  52.3 us (30%)
  waiting for transfers between devices  30.1 us (17%)
  Pallas kernels  7.65 us (4%)
  matrix products  4.79 us (3%)
  local copies, waits for them, and re-layouts  3.51 us (2%)
    ppermute x16, starting transfers between devices, swapped(): lax.ppermute(values, axis, [(i, (i + step(i)) % count) for i in range(cou...  64 us
    all_to_all x3, blocking collectives, sum_over_grid(): lax.all_to_all(sent, axis, 0, 0).astype(jnp.float32)  52.3 us
    ppermute x2, waiting for transfers between devices, other_band(): return lax.ppermute(values, 'band', [(0, 1), (1, 0)])  14.1 us
    ppermute x16, waiting for transfers between devices, swapped(): lax.ppermute(values, axis, [(i, (i + step(i)) % count) for i in range(cou...  9.46 us
    pallas_call x4, Pallas kernels, filter_step(): pl.pallas_call(functools.partial(step_kernel, previous is not None, last)...  6.76 us
    all_to_all x1, waiting for transfers between devices, sum_over_grid(): lax.all_to_all(sent, axis, 0, 0).astype(jnp.float32)  6.57 us
    all_to_all x1, starting transfers between devices, sum_over_grid(): lax.all_to_all(sent, axis, 0, 0).astype(jnp.float32)  5.96 us
    ppermute x2, starting transfers between devices, other_band(): return lax.ppermute(values, 'band', [(0, 1), (1, 0)])  4.75 us
  transfers between devices with their start and end apart: 19, of which 7 were waited for; matrix products, arithmetic and copies ran while one was open for 0% of the time, Pallas kernels for 0%

profile of v4, /device:TPU:1, one launch (start us, length us, event | category | flops | bytes accessed | tf_op | source)
XLA Modules:
  0.0 175.0 jit_solution(7913139636077177176)
XLA Ops:
  3.4 8.8 %collective-permute-start.2 = (bf16[672,128]{1,0:T(8,128)(2,1)S(1)}, bf16[672,128]{1,0:T(8,128)(2,1)S(1)}, u32[]{:S(2)}, u32[]{:S(2)}) collective-permute-start(bf16[672,128]{1,0:T(8,128)(2,1)S(1)} %get-tuple-element.31), channel_id=1, source_target_pairs={{0,1},{1,0},{2,3},{3,2},{4,5},{5,4},{6,7},{7,6},{8,9},{9,8},{10,11... | collective-permute-start | bytes 516104 | tf_op jit(solution)/shard_map/ppermute | solution.py:203
  12.2 1.9 %collective-permute-start.3 = (bf16[672,128]{1,0:T(8,128)(2,1)S(1)}, bf16[672,128]{1,0:T(8,128)(2,1)S(1)}, u32[]{:S(2)}, u32[]{:S(2)}) collective-permute-start(bf16[672,128]{1,0:T(8,128)(2,1)S(1)} %get-tuple-element.32), channel_id=1, source_target_pairs={{0,15},{1,2},{2,1},{3,4},{4,3},{5,6},{6,5},{7,8},{8,7},{9,10},{10,... | collective-permute-start | bytes 516104 | tf_op jit(solution)/shard_map/ppermute | solution.py:203
  14.1 1.9 %collective-permute-start = (bf16[448,128]{1,0:T(8,128)(2,1)S(1)}, bf16[448,128]{1,0:T(8,128)(2,1)S(1)}, u32[]{:S(2)}, u32[]{:S(2)}) collective-permute-start(bf16[448,128]{1,0:T(8,128)(2,1)S(1)} %get-tuple-element.29), channel_id=1, source_target_pairs={{0,16},{16,0},{32,48},{48,32},{64,80},{80,64},{96,112},{112,96},{1... | collective-permute-start | bytes 344072 | tf_op jit(solution)/shard_map/ppermute | solution.py:203
  16.1 9.1 %collective-permute-start.1 = (bf16[448,128]{1,0:T(8,128)(2,1)S(1)}, bf16[448,128]{1,0:T(8,128)(2,1)S(1)}, u32[]{:S(2)}, u32[]{:S(2)}) collective-permute-start(bf16[448,128]{1,0:T(8,128)(2,1)S(1)} %get-tuple-element.30), channel_id=1, source_target_pairs={{0,240},{16,32},{32,16},{48,64},{64,48},{80,96},{96,80},{112,128},... | collective-permute-start | bytes 344072 | tf_op jit(solution)/shard_map/ppermute | solution.py:203
  25.2 2.2 %collective-permute-done.1.refs_1_ = bf16[448,128]{1,0:T(8,128)(2,1)S(1)} collective-permute-done((bf16[448,128]{1,0:T(8,128)(2,1)S(1)}, bf16[448,128]{1,0:T(8,128)(2,1)S(1)}, u32[]{:S(2)}, u32[]{:S(2)}) %collective-permute-start.1) | collective-permute-done | bytes 114720 | tf_op jit(solution)/shard_map/ppermute | solution.py:203
  29.0 6.0 %collective-permute-start.6 = (bf16[672,128]{1,0:T(8,128)(2,1)S(1)}, bf16[672,128]{1,0:T(8,128)(2,1)S(1)}, u32[]{:S(2)}, u32[]{:S(2)}) collective-permute-start(bf16[672,128]{1,0:T(8,128)(2,1)S(1)} %get-tuple-element.36), channel_id=1, source_target_pairs={{0,1},{1,0},{2,3},{3,2},{4,5},{5,4},{6,7},{7,6},{8,9},{9,8},{10,11... | collective-permute-start | bytes 516104 | tf_op jit(solution)/shard_map/ppermute | solution.py:203
  35.0 1.9 %collective-permute-start.7 = (bf16[672,128]{1,0:T(8,128)(2,1)S(1)}, bf16[672,128]{1,0:T(8,128)(2,1)S(1)}, u32[]{:S(2)}, u32[]{:S(2)}) collective-permute-start(bf16[672,128]{1,0:T(8,128)(2,1)S(1)} %get-tuple-element.37), channel_id=1, source_target_pairs={{0,15},{1,2},{2,1},{3,4},{4,3},{5,6},{6,5},{7,8},{8,7},{9,10},{10,... | collective-permute-start | bytes 516104 | tf_op jit(solution)/shard_map/ppermute | solution.py:203
  37.0 1.9 %collective-permute-start.4 = (bf16[448,128]{1,0:T(8,128)(2,1)S(1)}, bf16[448,128]{1,0:T(8,128)(2,1)S(1)}, u32[]{:S(2)}, u32[]{:S(2)}) collective-permute-start(bf16[448,128]{1,0:T(8,128)(2,1)S(1)} %get-tuple-element.34), channel_id=1, source_target_pairs={{0,16},{16,0},{32,48},{48,32},{64,80},{80,64},{96,112},{112,96},{1... | collective-permute-start | bytes 344072 | tf_op jit(solution)/shard_map/ppermute | solution.py:203
  38.9 4.8 %collective-permute-start.5 = (bf16[448,128]{1,0:T(8,128)(2,1)S(1)}, bf16[448,128]{1,0:T(8,128)(2,1)S(1)}, u32[]{:S(2)}, u32[]{:S(2)}) collective-permute-start(bf16[448,128]{1,0:T(8,128)(2,1)S(1)} %get-tuple-element.35), channel_id=1, source_target_pairs={{0,240},{16,32},{32,16},{48,64},{64,48},{80,96},{96,80},{112,128},... | collective-permute-start | bytes 344072 | tf_op jit(solution)/shard_map/ppermute | solution.py:203
  43.7 2.7 %collective-permute-done.5.refs_1_ = bf16[448,128]{1,0:T(8,128)(2,1)S(1)} collective-permute-done((bf16[448,128]{1,0:T(8,128)(2,1)S(1)}, bf16[448,128]{1,0:T(8,128)(2,1)S(1)}, u32[]{:S(2)}, u32[]{:S(2)}) %collective-permute-start.5) | collective-permute-done | bytes 114720 | tf_op jit(solution)/shard_map/ppermute | solution.py:203
  46.5 1.7 shard_map.52
  48.2 3.2 %collective-permute-start.10 = (bf16[672,128]{1,0:T(8,128)(2,1)S(1)}, bf16[672,128]{1,0:T(8,128)(2,1)S(1)}, u32[]{:S(2)}, u32[]{:S(2)}) collective-permute-start(bf16[672,128]{1,0:T(8,128)(2,1)S(1)} %get-tuple-element.41), channel_id=1, source_target_pairs={{0,1},{1,0},{2,3},{3,2},{4,5},{5,4},{6,7},{7,6},{8,9},{9,8},{10,11... | collective-permute-start | bytes 516104 | tf_op jit(solution)/shard_map/ppermute | solution.py:203
  51.4 4.1 %collective-permute-start.11 = (bf16[672,128]{1,0:T(8,128)(2,1)S(1)}, bf16[672,128]{1,0:T(8,128)(2,1)S(1)}, u32[]{:S(2)}, u32[]{:S(2)}) collective-permute-start(bf16[672,128]{1,0:T(8,128)(2,1)S(1)} %get-tuple-element.42), channel_id=1, source_target_pairs={{0,15},{1,2},{2,1},{3,4},{4,3},{5,6},{6,5},{7,8},{8,7},{9,10},{10,... | collective-permute-start | bytes 516104 | tf_op jit(solution)/shard_map/ppermute | solution.py:203
  55.6 2.4 %collective-permute-start.8 = (bf16[448,128]{1,0:T(8,128)(2,1)S(1)}, bf16[448,128]{1,0:T(8,128)(2,1)S(1)}, u32[]{:S(2)}, u32[]{:S(2)}) collective-permute-start(bf16[448,128]{1,0:T(8,128)(2,1)S(1)} %get-tuple-element.39), channel_id=1, source_target_pairs={{0,16},{16,0},{32,48},{48,32},{64,80},{80,64},{96,112},{112,96},{1... | collective-permute-start | bytes 344072 | tf_op jit(solution)/shard_map/ppermute | solution.py:203
  58.0 4.8 %collective-permute-start.9 = (bf16[448,128]{1,0:T(8,128)(2,1)S(1)}, bf16[448,128]{1,0:T(8,128)(2,1)S(1)}, u32[]{:S(2)}, u32[]{:S(2)}) collective-permute-start(bf16[448,128]{1,0:T(8,128)(2,1)S(1)} %get-tuple-element.40), channel_id=1, source_target_pairs={{0,240},{16,32},{32,16},{48,64},{64,48},{80,96},{96,80},{112,128},... | collective-permute-start | bytes 344072 | tf_op jit(solution)/shard_map/ppermute | solution.py:203
  62.9 2.2 %collective-permute-done.9.refs_1_ = bf16[448,128]{1,0:T(8,128)(2,1)S(1)} collective-permute-done((bf16[448,128]{1,0:T(8,128)(2,1)S(1)}, bf16[448,128]{1,0:T(8,128)(2,1)S(1)}, u32[]{:S(2)}, u32[]{:S(2)}) %collective-permute-start.9) | collective-permute-done | bytes 114720 | tf_op jit(solution)/shard_map/ppermute | solution.py:203
  66.7 4.5 %collective-permute-start.14 = (bf16[672,128]{1,0:T(8,128)(2,1)S(1)}, bf16[672,128]{1,0:T(8,128)(2,1)S(1)}, u32[]{:S(2)}, u32[]{:S(2)}) collective-permute-start(bf16[672,128]{1,0:T(8,128)(2,1)S(1)} %get-tuple-element.46), channel_id=1, source_target_pairs={{0,1},{1,0},{2,3},{3,2},{4,5},{5,4},{6,7},{7,6},{8,9},{9,8},{10,11... | collective-permute-start | bytes 516104 | tf_op jit(solution)/shard_map/ppermute | solution.py:203
  71.2 1.9 %collective-permute-start.15 = (bf16[672,128]{1,0:T(8,128)(2,1)S(1)}, bf16[672,128]{1,0:T(8,128)(2,1)S(1)}, u32[]{:S(2)}, u32[]{:S(2)}) collective-permute-start(bf16[672,128]{1,0:T(8,128)(2,1)S(1)} %get-tuple-element.47), channel_id=1, source_target_pairs={{0,15},{1,2},{2,1},{3,4},{4,3},{5,6},{6,5},{7,8},{8,7},{9,10},{10,... | collective-permute-start | bytes 516104 | tf_op jit(solution)/shard_map/ppermute | solution.py:203
  73.2 1.9 %collective-permute-start.12 = (bf16[448,128]{1,0:T(8,128)(2,1)S(1)}, bf16[448,128]{1,0:T(8,128)(2,1)S(1)}, u32[]{:S(2)}, u32[]{:S(2)}) collective-permute-start(bf16[448,128]{1,0:T(8,128)(2,1)S(1)} %get-tuple-element.44), channel_id=1, source_target_pairs={{0,16},{16,0},{32,48},{48,32},{64,80},{80,64},{96,112},{112,96},{1... | collective-permute-start | bytes 344072 | tf_op jit(solution)/shard_map/ppermute | solution.py:203
  75.1 4.7 %collective-permute-start.13 = (bf16[448,128]{1,0:T(8,128)(2,1)S(1)}, bf16[448,128]{1,0:T(8,128)(2,1)S(1)}, u32[]{:S(2)}, u32[]{:S(2)}) collective-permute-start(bf16[448,128]{1,0:T(8,128)(2,1)S(1)} %get-tuple-element.45), channel_id=1, source_target_pairs={{0,240},{16,32},{32,16},{48,64},{64,48},{80,96},{96,80},{112,128},... | collective-permute-start | bytes 344072 | tf_op jit(solution)/shard_map/ppermute | solution.py:203
  79.8 2.4 %collective-permute-done.13.refs_1_ = bf16[448,128]{1,0:T(8,128)(2,1)S(1)} collective-permute-done((bf16[448,128]{1,0:T(8,128)(2,1)S(1)}, bf16[448,128]{1,0:T(8,128)(2,1)S(1)}, u32[]{:S(2)}, u32[]{:S(2)}) %collective-permute-start.13) | collective-permute-done | bytes 114720 | tf_op jit(solution)/shard_map/ppermute | solution.py:203
  82.1 1.7 shard_map.54
  84.0 2.5 %collective-permute-start.16 = (bf16[8,12288]{1,0:T(8,128)(2,1)S(1)}, bf16[8,12288]{1,0:T(8,128)(2,1)S(1)}, u32[]{:S(2)}, u32[]{:S(2)}) collective-permute-start(bf16[8,12288]{1,0:T(8,128)(2,1)S(1)} %convert_element_type.31), channel_id=1, source_target_pairs={{0,256},{256,0},{1,257},{257,1},{2,258},{258,2},{3,259},{259,3},{4... | collective-permute-start | bytes 589832 | tf_op jit(solution)/shard_map/ppermute | solution.py:222
  86.5 4.2 %collective-permute-done.16 = bf16[8,12288]{1,0:T(8,128)(2,1)S(1)} collective-permute-done((bf16[8,12288]{1,0:T(8,128)(2,1)S(1)}, bf16[8,12288]{1,0:T(8,128)(2,1)S(1)}, u32[]{:S(2)}, u32[]{:S(2)}) %collective-permute-start.16) | collective-permute-done | bytes 196640 | tf_op jit(solution)/shard_map/ppermute | solution.py:222
  90.7 2.9 %fusion.9 = f16[16,128]{1,0:T(8,128)(2,1)S(1)} fusion(bf16[16,8,96,128]{3,2,1,0:T(8,128)(2,1)} %bitcast.20, bf16[8,12288]{1,0:T(8,128)(2,1)S(1)} %collective-permute-done.16, bf16[8,12288]{1,0:T(8,128)(2,1)S(1)} %convert_element_type.31), kind=kOutput, calls=%fused_computation.7 | convolution fusion | flops 51122176 | bytes 3543040 | tf_op jit(solution)/shard_map/dot_general | solution.py:226
  93.6 19.7 %all_to_all.20 = f16[16,16,128]{2,1,0:T(8,128)(2,1)S(1)} all-to-all(f16[16,16,128]{2,1,0:T(8,128)(2,1)S(1)} %broadcast_in_dim.8), channel_id=1, replica_groups=mesh['band'=2,'dx'=16,'dy'=16] {'dx'}, dimensions={0} | all-to-all | bytes 131072 | tf_op jit(solution)/shard_map/all_to_all | solution.py:217
  113.3 18.3 %all_to_all.21 = f16[16,16,128]{2,1,0:T(8,128)(2,1)S(1)} all-to-all(f16[16,16,128]{2,1,0:T(8,128)(2,1)S(1)} %broadcast_in_dim.9), channel_id=1, replica_groups=mesh['band'=2,'dx'=16,'dy'=16] {'dy'}, dimensions={0} | all-to-all | bytes 131072 | tf_op jit(solution)/shard_map/all_to_all | solution.py:217
  132.7 2.2 %collective-permute-start.17 = (bf16[16,12288]{1,0:T(8,128)(2,1)S(1)}, bf16[16,12288]{1,0:T(8,128)(2,1)S(1)}, u32[]{:S(2)}, u32[]{:S(2)}) collective-permute-start(bf16[16,12288]{1,0:T(8,128)(2,1)S(1)} %pad_maximum_fusion), channel_id=1, source_target_pairs={{0,256},{256,0},{1,257},{257,1},{2,258},{258,2},{3,259},{259,3},{4... | collective-permute-start | bytes 1179656 | tf_op jit(solution)/shard_map/ppermute | solution.py:222
  135.0 9.9 %collective-permute-done.17 = bf16[16,12288]{1,0:T(8,128)(2,1)S(1)} collective-permute-done((bf16[16,12288]{1,0:T(8,128)(2,1)S(1)}, bf16[16,12288]{1,0:T(8,128)(2,1)S(1)}, u32[]{:S(2)}, u32[]{:S(2)}) %collective-permute-start.17) | collective-permute-done | bytes 393248 | tf_op jit(solution)/shard_map/ppermute | solution.py:222
  146.2 14.2 %all_to_all.22 = f32[16,8,128]{2,1,0:T(8,128)S(1)} all-to-all(f32[16,8,128]{2,1,0:T(8,128)S(1)} %broadcast_in_dim.10), channel_id=1, replica_groups=mesh['band'=2,'dx'=16,'dy'=16] {'dx'}, dimensions={0} | all-to-all | bytes 131072 | tf_op jit(solution)/shard_map/all_to_all | solution.py:217
  161.1 6.0 %all-to-all-start.3 = ((f32[16,8,128]{2,1,0:T(8,128)}), f32[16,8,128]{2,1,0:T(8,128)S(1)}, u32[]{:S(2)}, u32[]{:S(2)}) async-start(f32[16,8,128]{2,1,0:T(8,128)} %broadcast_in_dim.11), calls=%async_computation.3 | async-start | bytes 131072 | tf_op jit(solution)/shard_map/all_to_all | solution.py:217
  167.9 6.6 %all-to-all-done.3 = f32[16,8,128]{2,1,0:T(8,128)S(1)} async-done(((f32[16,8,128]{2,1,0:T(8,128)}), f32[16,8,128]{2,1,0:T(8,128)S(1)}, u32[]{:S(2)}, u32[]{:S(2)}) %all-to-all-start.3) | async-done | bytes 65568 | tf_op jit(solution)/shard_map/all_to_all | solution.py:217
  (44 shorter events, 10.8 us)
Async XLA Ops:
  0.7 1.0 copy-start
  1.7 0.8 copy-start.1
  3.4 23.9 %collective-permute-start.2 = (bf16[672,128]{1,0:T(8,128)(2,1)S(1)}, bf16[672,128]{1,0:T(8,128)(2,1)S(1)}, u32[]{:S(2)}, u32[]{:S(2)}) collective-permute-start(bf16[672,128]{1,0:T(8,128)(2,1)S(1)} %get-tuple-element.31), channel_id=1, source_target_pairs={{0,1},{1,0},{2,3},{3,2},{4,5},{5,4},{6,7},{7,6},{8,9},{9,8},{10,11... | collective-permute-start | bytes 516104 | tf_op jit(solution)/shard_map/ppermute | solution.py:203
  12.2 15.1 %collective-permute-start.3 = (bf16[672,128]{1,0:T(8,128)(2,1)S(1)}, bf16[672,128]{1,0:T(8,128)(2,1)S(1)}, u32[]{:S(2)}, u32[]{:S(2)}) collective-permute-start(bf16[672,128]{1,0:T(8,128)(2,1)S(1)} %get-tuple-element.32), channel_id=1, source_target_pairs={{0,15},{1,2},{2,1},{3,4},{4,3},{5,6},{6,5},{7,8},{8,7},{9,10},{10,... | collective-permute-start | bytes 516104 | tf_op jit(solution)/shard_map/ppermute | solution.py:203
  14.1 11.0 %collective-permute-start = (bf16[448,128]{1,0:T(8,128)(2,1)S(1)}, bf16[448,128]{1,0:T(8,128)(2,1)S(1)}, u32[]{:S(2)}, u32[]{:S(2)}) collective-permute-start(bf16[448,128]{1,0:T(8,128)(2,1)S(1)} %get-tuple-element.29), channel_id=1, source_target_pairs={{0,16},{16,0},{32,48},{48,32},{64,80},{80,64},{96,112},{112,96},{1... | collective-permute-start | bytes 344072 | tf_op jit(solution)/shard_map/ppermute | solution.py:203
  16.1 11.3 %collective-permute-start.1 = (bf16[448,128]{1,0:T(8,128)(2,1)S(1)}, bf16[448,128]{1,0:T(8,128)(2,1)S(1)}, u32[]{:S(2)}, u32[]{:S(2)}) collective-permute-start(bf16[448,128]{1,0:T(8,128)(2,1)S(1)} %get-tuple-element.30), channel_id=1, source_target_pairs={{0,240},{16,32},{32,16},{48,64},{64,48},{80,96},{96,80},{112,128},... | collective-permute-start | bytes 344072 | tf_op jit(solution)/shard_map/ppermute | solution.py:203
  29.0 17.5 %collective-permute-start.6 = (bf16[672,128]{1,0:T(8,128)(2,1)S(1)}, bf16[672,128]{1,0:T(8,128)(2,1)S(1)}, u32[]{:S(2)}, u32[]{:S(2)}) collective-permute-start(bf16[672,128]{1,0:T(8,128)(2,1)S(1)} %get-tuple-element.36), channel_id=1, source_target_pairs={{0,1},{1,0},{2,3},{3,2},{4,5},{5,4},{6,7},{7,6},{8,9},{9,8},{10,11... | collective-permute-start | bytes 516104 | tf_op jit(solution)/shard_map/ppermute | solution.py:203
  35.0 11.5 %collective-permute-start.7 = (bf16[672,128]{1,0:T(8,128)(2,1)S(1)}, bf16[672,128]{1,0:T(8,128)(2,1)S(1)}, u32[]{:S(2)}, u32[]{:S(2)}) collective-permute-start(bf16[672,128]{1,0:T(8,128)(2,1)S(1)} %get-tuple-element.37), channel_id=1, source_target_pairs={{0,15},{1,2},{2,1},{3,4},{4,3},{5,6},{6,5},{7,8},{8,7},{9,10},{10,... | collective-permute-start | bytes 516104 | tf_op jit(solution)/shard_map/ppermute | solution.py:203
  37.0 6.8 %collective-permute-start.4 = (bf16[448,128]{1,0:T(8,128)(2,1)S(1)}, bf16[448,128]{1,0:T(8,128)(2,1)S(1)}, u32[]{:S(2)}, u32[]{:S(2)}) collective-permute-start(bf16[448,128]{1,0:T(8,128)(2,1)S(1)} %get-tuple-element.34), channel_id=1, source_target_pairs={{0,16},{16,0},{32,48},{48,32},{64,80},{80,64},{96,112},{112,96},{1... | collective-permute-start | bytes 344072 | tf_op jit(solution)/shard_map/ppermute | solution.py:203
  38.9 7.6 %collective-permute-start.5 = (bf16[448,128]{1,0:T(8,128)(2,1)S(1)}, bf16[448,128]{1,0:T(8,128)(2,1)S(1)}, u32[]{:S(2)}, u32[]{:S(2)}) collective-permute-start(bf16[448,128]{1,0:T(8,128)(2,1)S(1)} %get-tuple-element.35), channel_id=1, source_target_pairs={{0,240},{16,32},{32,16},{48,64},{64,48},{80,96},{96,80},{112,128},... | collective-permute-start | bytes 344072 | tf_op jit(solution)/shard_map/ppermute | solution.py:203
  48.2 16.8 %collective-permute-start.10 = (bf16[672,128]{1,0:T(8,128)(2,1)S(1)}, bf16[672,128]{1,0:T(8,128)(2,1)S(1)}, u32[]{:S(2)}, u32[]{:S(2)}) collective-permute-start(bf16[672,128]{1,0:T(8,128)(2,1)S(1)} %get-tuple-element.41), channel_id=1, source_target_pairs={{0,1},{1,0},{2,3},{3,2},{4,5},{5,4},{6,7},{7,6},{8,9},{9,8},{10,11... | collective-permute-start | bytes 516104 | tf_op jit(solution)/shard_map/ppermute | solution.py:203
  51.4 13.6 %collective-permute-start.11 = (bf16[672,128]{1,0:T(8,128)(2,1)S(1)}, bf16[672,128]{1,0:T(8,128)(2,1)S(1)}, u32[]{:S(2)}, u32[]{:S(2)}) collective-permute-start(bf16[672,128]{1,0:T(8,128)(2,1)S(1)} %get-tuple-element.42), channel_id=1, source_target_pairs={{0,15},{1,2},{2,1},{3,4},{4,3},{5,6},{6,5},{7,8},{8,7},{9,10},{10,... | collective-permute-start | bytes 516104 | tf_op jit(solution)/shard_map/ppermute | solution.py:203
  55.6 7.3 %collective-permute-start.8 = (bf16[448,128]{1,0:T(8,128)(2,1)S(1)}, bf16[448,128]{1,0:T(8,128)(2,1)S(1)}, u32[]{:S(2)}, u32[]{:S(2)}) collective-permute-start(bf16[448,128]{1,0:T(8,128)(2,1)S(1)} %get-tuple-element.39), channel_id=1, source_target_pairs={{0,16},{16,0},{32,48},{48,32},{64,80},{80,64},{96,112},{112,96},{1... | collective-permute-start | bytes 344072 | tf_op jit(solution)/shard_map/ppermute | solution.py:203
  58.0 7.0 %collective-permute-start.9 = (bf16[448,128]{1,0:T(8,128)(2,1)S(1)}, bf16[448,128]{1,0:T(8,128)(2,1)S(1)}, u32[]{:S(2)}, u32[]{:S(2)}) collective-permute-start(bf16[448,128]{1,0:T(8,128)(2,1)S(1)} %get-tuple-element.40), channel_id=1, source_target_pairs={{0,240},{16,32},{32,16},{48,64},{64,48},{80,96},{96,80},{112,128},... | collective-permute-start | bytes 344072 | tf_op jit(solution)/shard_map/ppermute | solution.py:203
  66.7 15.4 %collective-permute-start.14 = (bf16[672,128]{1,0:T(8,128)(2,1)S(1)}, bf16[672,128]{1,0:T(8,128)(2,1)S(1)}, u32[]{:S(2)}, u32[]{:S(2)}) collective-permute-start(bf16[672,128]{1,0:T(8,128)(2,1)S(1)} %get-tuple-element.46), channel_id=1, source_target_pairs={{0,1},{1,0},{2,3},{3,2},{4,5},{5,4},{6,7},{7,6},{8,9},{9,8},{10,11... | collective-permute-start | bytes 516104 | tf_op jit(solution)/shard_map/ppermute | solution.py:203
  71.2 10.9 %collective-permute-start.15 = (bf16[672,128]{1,0:T(8,128)(2,1)S(1)}, bf16[672,128]{1,0:T(8,128)(2,1)S(1)}, u32[]{:S(2)}, u32[]{:S(2)}) collective-permute-start(bf16[672,128]{1,0:T(8,128)(2,1)S(1)} %get-tuple-element.47), channel_id=1, source_target_pairs={{0,15},{1,2},{2,1},{3,4},{4,3},{5,6},{6,5},{7,8},{8,7},{9,10},{10,... | collective-permute-start | bytes 516104 | tf_op jit(solution)/shard_map/ppermute | solution.py:203
  73.2 6.6 %collective-permute-start.12 = (bf16[448,128]{1,0:T(8,128)(2,1)S(1)}, bf16[448,128]{1,0:T(8,128)(2,1)S(1)}, u32[]{:S(2)}, u32[]{:S(2)}) collective-permute-start(bf16[448,128]{1,0:T(8,128)(2,1)S(1)} %get-tuple-element.44), channel_id=1, source_target_pairs={{0,16},{16,0},{32,48},{48,32},{64,80},{80,64},{96,112},{112,96},{1... | collective-permute-start | bytes 344072 | tf_op jit(solution)/shard_map/ppermute | solution.py:203
  75.1 7.1 %collective-permute-start.13 = (bf16[448,128]{1,0:T(8,128)(2,1)S(1)}, bf16[448,128]{1,0:T(8,128)(2,1)S(1)}, u32[]{:S(2)}, u32[]{:S(2)}) collective-permute-start(bf16[448,128]{1,0:T(8,128)(2,1)S(1)} %get-tuple-element.45), channel_id=1, source_target_pairs={{0,240},{16,32},{32,16},{48,64},{64,48},{80,96},{96,80},{112,128},... | collective-permute-start | bytes 344072 | tf_op jit(solution)/shard_map/ppermute | solution.py:203
  83.9 47.8 %copy-start.2 = (bf16[128,12,8,128]{3,2,1,0:T(8,128)(2,1)S(1)}, bf16[128,12,8,128]{3,2,1,0:T(8,128)(2,1)}, u32[]{:S(2)}) copy-start(bf16[128,12,8,128]{3,2,1,0:T(8,128)(2,1)} %param.5) | copy-start | bytes 9437188
  84.0 6.7 %collective-permute-start.16 = (bf16[8,12288]{1,0:T(8,128)(2,1)S(1)}, bf16[8,12288]{1,0:T(8,128)(2,1)S(1)}, u32[]{:S(2)}, u32[]{:S(2)}) collective-permute-start(bf16[8,12288]{1,0:T(8,128)(2,1)S(1)} %convert_element_type.31), channel_id=1, source_target_pairs={{0,256},{256,0},{1,257},{257,1},{2,258},{258,2},{3,259},{259,3},{4... | collective-permute-start | bytes 589832 | tf_op jit(solution)/shard_map/ppermute | solution.py:222
  132.7 12.1 %collective-permute-start.17 = (bf16[16,12288]{1,0:T(8,128)(2,1)S(1)}, bf16[16,12288]{1,0:T(8,128)(2,1)S(1)}, u32[]{:S(2)}, u32[]{:S(2)}) collective-permute-start(bf16[16,12288]{1,0:T(8,128)(2,1)S(1)} %pad_maximum_fusion), channel_id=1, source_target_pairs={{0,256},{256,0},{1,257},{257,1},{2,258},{258,2},{3,259},{259,3},{4... | collective-permute-start | bytes 1179656 | tf_op jit(solution)/shard_map/ppermute | solution.py:222
  161.1 13.3 %all-to-all-start.3 = ((f32[16,8,128]{2,1,0:T(8,128)}), f32[16,8,128]{2,1,0:T(8,128)S(1)}, u32[]{:S(2)}, u32[]{:S(2)}) async-start(f32[16,8,128]{2,1,0:T(8,128)} %broadcast_in_dim.11), calls=%async_computation.3 | async-start | bytes 131072 | tf_op jit(solution)/shard_map/all_to_all | solution.py:217

commit v5 on v4

--- a/solution.py
+++ b/solution.py
@@ -34,7 +34,7 @@
     )
 
 
-def pack_messages(parity_ref, field_ref, x_even, x_odd, y_even, y_odd):
+def pack_messages(parity_ref, field_ref, y_odd, x_even, x_odd, y_even):
     def layer(dim, at):
         return field_ref[at] if dim == 0 else field_ref[:, at]
 
@@ -45,9 +45,13 @@
                 pack_layer(out_ref, at, layer(dim, tail * (size - WIDTH) + at))
             nearest = layer(dim, tail * (size - 1))
             pack_layer(out_ref, WIDTH, nearest - nearest.astype(jnp.bfloat16).astype(jnp.float32))
-
-
-def unpack_messages(parity_ref, halo_x, halo_y, x_even, x_odd, y_even, y_odd):
+            used = SENT * nearest.shape[0] * nearest.shape[1]
+            if used < out_ref.shape[0]:
+                rows = out_ref.shape[0] - used
+                out_ref[used:, :] = jnp.zeros((rows, out_ref.shape[1]), jnp.bfloat16)
+
+
+def unpack_messages(parity_ref, halo_x, halo_y, y_odd, x_even, x_odd, y_even):
     for dim, halo, even, odd in ((0, halo_x, x_even, x_odd), (1, halo_y, y_even, y_odd)):
         shape = halo.shape[1:] if dim == 0 else halo.shape[:1] + halo.shape[2:]
         rows = shape[0] * shape[1]
@@ -143,9 +147,8 @@
 
 
 def message_shapes(size_x, size_y, own, depth):
-    to_x = jax.ShapeDtypeStruct((SENT * size_y * own, depth), jnp.bfloat16)
-    to_y = jax.ShapeDtypeStruct((SENT * size_x * own, depth), jnp.bfloat16)
-    return [to_x, to_x, to_y, to_y]
+    rows = SENT * max(size_x, size_y) * own
+    return [jax.ShapeDtypeStruct((rows, depth), jnp.bfloat16)] * 4
 
 
 def params():
@@ -196,17 +199,17 @@
     )(parity, field, *fixed, *messages, *before)
 
 
-def swap(x_even, x_odd, y_even, y_odd):
+def swap(y_odd, x_even, x_odd, y_even):
     def swapped(values, axis, first):
         count = lax.axis_size(axis)
         step = lambda i: 1 if (i - first) % 2 == 0 else -1
         return lax.ppermute(values, axis, [(i, (i + step(i)) % count) for i in range(count)])
 
     return (
+        swapped(y_odd, "dy", 1),
         swapped(x_even, "dx", 0),
         swapped(x_odd, "dx", 1),
         swapped(y_even, "dy", 0),
-        swapped(y_odd, "dy", 1),
     )
 
 
@@ -248,8 +251,9 @@
     rounded = filtered.astype(jnp.bfloat16)
     rounded_other = other_band(rounded)
     own_resident = resident.reshape(-1, cell_count)
-    both = jnp.concatenate([rounded, rounded_other], axis=0)
-    local = rows_dot(both, own_resident) * SENT_SCALE
+    local_own = rows_dot(rounded, own_resident)
+    local_other = rows_dot(rounded_other, own_resident)
+    local = jnp.concatenate([local_own, local_other], axis=0) * SENT_SCALE
     correlations = (sum_over_grid(local, jnp.float16) / SENT_SCALE).astype(jnp.bfloat16)
     correction = jnp.dot(correlations, own_resident, preferred_element_type=jnp.float32)
     mine, theirs = correction[:own_count], correction[own_count:]

time: 176 us -> 175 us (level)
  waiting for transfers between devices: 30.1 us -> 24.5 us
  other arithmetic: 1.04 us -> 3.94 us
  local copies, waits for them, and re-layouts: 3.51 us -> 6.14 us
    ppermute x16, waiting for transfers between devices: 9.46 us -> 3.98 us  [swapped(): lax.ppermute(values, axis, [(i, (i + step(i)) % count) for i in range(cou...]
    ppermute x16, starting transfers between devices: 64 us -> 65.9 us  [swapped(): lax.ppermute(values, axis, [(i, (i + step(i)) % count) for i in range(cou...]
    dot_general x2 -> x3, matrix products: 3.83 us -> 2.84 us  [rows_dot(): lax.dot_general(first, second, (((1,), (1,)), ((), ())), preferred_elemen...]
  transfers between devices with their start and end apart: 19 -> 19, of which waited for: 7 -> 8; matrix products, arithmetic and copies ran while one was open for 0% -> 1% of each run, Pallas kernels for 0% -> 0%
where the time goes in v5:
time: 175 us; the launch traced here: 174 us
  starting transfers between devices  76.3 us (44%)
  blocking collectives  50.8 us (29%)
  waiting for transfers between devices  24.5 us (14%)
  Pallas kernels  7.68 us (4%)
  local copies, waits for them, and re-layouts  6.14 us (4%)
  other arithmetic  3.94 us (2%)
  matrix products  3.8 us (2%)
    ppermute x16, starting transfers between devices, swapped(): lax.ppermute(values, axis, [(i, (i + step(i)) % count) for i in range(cou...  65.9 us
    all_to_all x3, blocking collectives, sum_over_grid(): lax.all_to_all(sent, axis, 0, 0).astype(jnp.float32)  50.8 us
    ppermute x2, waiting for transfers between devices, other_band(): return lax.ppermute(values, 'band', [(0, 1), (1, 0)])  14 us
    pallas_call x4, Pallas kernels, filter_step(): pl.pallas_call(functools.partial(step_kernel, previous is not None, last)...  6.79 us
    all_to_all x1, waiting for transfers between devices, sum_over_grid(): lax.all_to_all(sent, axis, 0, 0).astype(jnp.float32)  6.57 us
    all_to_all x1, starting transfers between devices, sum_over_grid(): lax.all_to_all(sent, axis, 0, 0).astype(jnp.float32)  5.93 us
    ppermute x2, starting transfers between devices, other_band(): return lax.ppermute(values, 'band', [(0, 1), (1, 0)])  4.52 us
    ppermute x16, waiting for transfers between devices, swapped(): lax.ppermute(values, axis, [(i, (i + step(i)) % count) for i in range(cou...  3.98 us
  transfers between devices with their start and end apart: 19, of which 8 were waited for; matrix products, arithmetic and copies ran while one was open for 1% of the time, Pallas kernels for 0%

profile of v5, /device:TPU:1, one launch (start us, length us, event | category | flops | bytes accessed | tf_op | source)
XLA Modules:
  0.0 174.2 jit_solution(2468280921013282765)
XLA Ops:
  3.4 6.0 %collective-permute-start = (bf16[672,128]{1,0:T(8,128)(2,1)S(1)}, bf16[672,128]{1,0:T(8,128)(2,1)S(1)}, u32[]{:S(2)}, u32[]{:S(2)}) collective-permute-start(bf16[672,128]{1,0:T(8,128)(2,1)S(1)} %get-tuple-element.29), channel_id=1, source_target_pairs={{0,15},{1,2},{2,1},{3,4},{4,3},{5,6},{6,5},{7,8},{8,7},{9,10},{10,... | collective-permute-start | bytes 516104 | tf_op jit(solution)/shard_map/ppermute | solution.py:206
  9.5 3.5 %collective-permute-start.1 = (bf16[672,128]{1,0:T(8,128)(2,1)S(1)}, bf16[672,128]{1,0:T(8,128)(2,1)S(1)}, u32[]{:S(2)}, u32[]{:S(2)}) collective-permute-start(bf16[672,128]{1,0:T(8,128)(2,1)S(1)} %get-tuple-element.30), channel_id=1, source_target_pairs={{0,16},{16,0},{32,48},{48,32},{64,80},{80,64},{96,112},{112,96},{1... | collective-permute-start | bytes 516104 | tf_op jit(solution)/shard_map/ppermute | solution.py:206
  13.0 10.2 %collective-permute-start.2 = (bf16[672,128]{1,0:T(8,128)(2,1)S(1)}, bf16[672,128]{1,0:T(8,128)(2,1)S(1)}, u32[]{:S(2)}, u32[]{:S(2)}) collective-permute-start(bf16[672,128]{1,0:T(8,128)(2,1)S(1)} %get-tuple-element.31), channel_id=1, source_target_pairs={{0,240},{16,32},{32,16},{48,64},{64,48},{80,96},{96,80},{112,128},... | collective-permute-start | bytes 516104 | tf_op jit(solution)/shard_map/ppermute | solution.py:206
  23.2 4.8 %collective-permute-start.3 = (bf16[672,128]{1,0:T(8,128)(2,1)S(1)}, bf16[672,128]{1,0:T(8,128)(2,1)S(1)}, u32[]{:S(2)}, u32[]{:S(2)}) collective-permute-start(bf16[672,128]{1,0:T(8,128)(2,1)S(1)} %get-tuple-element.32), channel_id=1, source_target_pairs={{0,1},{1,0},{2,3},{3,2},{4,5},{5,4},{6,7},{7,6},{8,9},{9,8},{10,11... | collective-permute-start | bytes 516104 | tf_op jit(solution)/shard_map/ppermute | solution.py:206
  29.0 1.7 shard_map.51
  30.7 1.9 %collective-permute-start.4 = (bf16[672,128]{1,0:T(8,128)(2,1)S(1)}, bf16[672,128]{1,0:T(8,128)(2,1)S(1)}, u32[]{:S(2)}, u32[]{:S(2)}) collective-permute-start(bf16[672,128]{1,0:T(8,128)(2,1)S(1)} %get-tuple-element.34), channel_id=1, source_target_pairs={{0,15},{1,2},{2,1},{3,4},{4,3},{5,6},{6,5},{7,8},{8,7},{9,10},{10,... | collective-permute-start | bytes 516104 | tf_op jit(solution)/shard_map/ppermute | solution.py:206
  32.6 1.9 %collective-permute-start.5 = (bf16[672,128]{1,0:T(8,128)(2,1)S(1)}, bf16[672,128]{1,0:T(8,128)(2,1)S(1)}, u32[]{:S(2)}, u32[]{:S(2)}) collective-permute-start(bf16[672,128]{1,0:T(8,128)(2,1)S(1)} %get-tuple-element.35), channel_id=1, source_target_pairs={{0,16},{16,0},{32,48},{48,32},{64,80},{80,64},{96,112},{112,96},{1... | collective-permute-start | bytes 516104 | tf_op jit(solution)/shard_map/ppermute | solution.py:206
  34.6 4.6 %collective-permute-start.6 = (bf16[672,128]{1,0:T(8,128)(2,1)S(1)}, bf16[672,128]{1,0:T(8,128)(2,1)S(1)}, u32[]{:S(2)}, u32[]{:S(2)}) collective-permute-start(bf16[672,128]{1,0:T(8,128)(2,1)S(1)} %get-tuple-element.36), channel_id=1, source_target_pairs={{0,240},{16,32},{32,16},{48,64},{64,48},{80,96},{96,80},{112,128},... | collective-permute-start | bytes 516104 | tf_op jit(solution)/shard_map/ppermute | solution.py:206
  39.1 3.1 %collective-permute-start.7 = (bf16[672,128]{1,0:T(8,128)(2,1)S(1)}, bf16[672,128]{1,0:T(8,128)(2,1)S(1)}, u32[]{:S(2)}, u32[]{:S(2)}) collective-permute-start(bf16[672,128]{1,0:T(8,128)(2,1)S(1)} %get-tuple-element.37), channel_id=1, source_target_pairs={{0,1},{1,0},{2,3},{3,2},{4,5},{5,4},{6,7},{7,6},{8,9},{9,8},{10,11... | collective-permute-start | bytes 516104 | tf_op jit(solution)/shard_map/ppermute | solution.py:206
  43.3 1.7 shard_map.52
  45.0 6.7 %collective-permute-start.8 = (bf16[672,128]{1,0:T(8,128)(2,1)S(1)}, bf16[672,128]{1,0:T(8,128)(2,1)S(1)}, u32[]{:S(2)}, u32[]{:S(2)}) collective-permute-start(bf16[672,128]{1,0:T(8,128)(2,1)S(1)} %get-tuple-element.39), channel_id=1, source_target_pairs={{0,15},{1,2},{2,1},{3,4},{4,3},{5,6},{6,5},{7,8},{8,7},{9,10},{10,... | collective-permute-start | bytes 516104 | tf_op jit(solution)/shard_map/ppermute | solution.py:206
  51.6 2.2 %collective-permute-start.9 = (bf16[672,128]{1,0:T(8,128)(2,1)S(1)}, bf16[672,128]{1,0:T(8,128)(2,1)S(1)}, u32[]{:S(2)}, u32[]{:S(2)}) collective-permute-start(bf16[672,128]{1,0:T(8,128)(2,1)S(1)} %get-tuple-element.40), channel_id=1, source_target_pairs={{0,16},{16,0},{32,48},{48,32},{64,80},{80,64},{96,112},{112,96},{1... | collective-permute-start | bytes 516104 | tf_op jit(solution)/shard_map/ppermute | solution.py:206
  53.8 3.4 %collective-permute-start.10 = (bf16[672,128]{1,0:T(8,128)(2,1)S(1)}, bf16[672,128]{1,0:T(8,128)(2,1)S(1)}, u32[]{:S(2)}, u32[]{:S(2)}) collective-permute-start(bf16[672,128]{1,0:T(8,128)(2,1)S(1)} %get-tuple-element.41), channel_id=1, source_target_pairs={{0,240},{16,32},{32,16},{48,64},{64,48},{80,96},{96,80},{112,128},... | collective-permute-start | bytes 516104 | tf_op jit(solution)/shard_map/ppermute | solution.py:206
  57.2 5.1 %collective-permute-start.11 = (bf16[672,128]{1,0:T(8,128)(2,1)S(1)}, bf16[672,128]{1,0:T(8,128)(2,1)S(1)}, u32[]{:S(2)}, u32[]{:S(2)}) collective-permute-start(bf16[672,128]{1,0:T(8,128)(2,1)S(1)} %get-tuple-element.42), channel_id=1, source_target_pairs={{0,1},{1,0},{2,3},{3,2},{4,5},{5,4},{6,7},{7,6},{8,9},{9,8},{10,11... | collective-permute-start | bytes 516104 | tf_op jit(solution)/shard_map/ppermute | solution.py:206
  63.3 1.7 shard_map.53
  65.0 2.8 %collective-permute-start.12 = (bf16[672,128]{1,0:T(8,128)(2,1)S(1)}, bf16[672,128]{1,0:T(8,128)(2,1)S(1)}, u32[]{:S(2)}, u32[]{:S(2)}) collective-permute-start(bf16[672,128]{1,0:T(8,128)(2,1)S(1)} %get-tuple-element.44), channel_id=1, source_target_pairs={{0,15},{1,2},{2,1},{3,4},{4,3},{5,6},{6,5},{7,8},{8,7},{9,10},{10,... | collective-permute-start | bytes 516104 | tf_op jit(solution)/shard_map/ppermute | solution.py:206
  67.8 1.9 %collective-permute-start.13 = (bf16[672,128]{1,0:T(8,128)(2,1)S(1)}, bf16[672,128]{1,0:T(8,128)(2,1)S(1)}, u32[]{:S(2)}, u32[]{:S(2)}) collective-permute-start(bf16[672,128]{1,0:T(8,128)(2,1)S(1)} %get-tuple-element.45), channel_id=1, source_target_pairs={{0,16},{16,0},{32,48},{48,32},{64,80},{80,64},{96,112},{112,96},{1... | collective-permute-start | bytes 516104 | tf_op jit(solution)/shard_map/ppermute | solution.py:206
  69.7 3.2 %collective-permute-start.14 = (bf16[672,128]{1,0:T(8,128)(2,1)S(1)}, bf16[672,128]{1,0:T(8,128)(2,1)S(1)}, u32[]{:S(2)}, u32[]{:S(2)}) collective-permute-start(bf16[672,128]{1,0:T(8,128)(2,1)S(1)} %get-tuple-element.46), channel_id=1, source_target_pairs={{0,240},{16,32},{32,16},{48,64},{64,48},{80,96},{96,80},{112,128},... | collective-permute-start | bytes 516104 | tf_op jit(solution)/shard_map/ppermute | solution.py:206
  73.0 4.6 %collective-permute-start.15 = (bf16[672,128]{1,0:T(8,128)(2,1)S(1)}, bf16[672,128]{1,0:T(8,128)(2,1)S(1)}, u32[]{:S(2)}, u32[]{:S(2)}) collective-permute-start(bf16[672,128]{1,0:T(8,128)(2,1)S(1)} %get-tuple-element.47), channel_id=1, source_target_pairs={{0,1},{1,0},{2,3},{3,2},{4,5},{5,4},{6,7},{7,6},{8,9},{9,8},{10,11... | collective-permute-start | bytes 516104 | tf_op jit(solution)/shard_map/ppermute | solution.py:206
  78.6 1.7 shard_map.54
  81.8 1.0 convert_element_type.41
  82.8 1.0 convert_element_type.42
  83.9 2.3 %collective-permute-start.16 = (bf16[8,12288]{1,0:T(8,128)(2,1)S(1)}, bf16[8,12288]{1,0:T(8,128)(2,1)S(1)}, u32[]{:S(2)}, u32[]{:S(2)}) collective-permute-start(bf16[8,12288]{1,0:T(8,128)(2,1)S(1)} %convert_element_type.42), channel_id=1, source_target_pairs={{0,256},{256,0},{1,257},{257,1},{2,258},{258,2},{3,259},{259,3},{4... | collective-permute-start | bytes 589832 | tf_op jit(solution)/shard_map/ppermute | solution.py:225
  87.2 4.0 %collective-permute-done.16 = bf16[8,12288]{1,0:T(8,128)(2,1)S(1)} collective-permute-done((bf16[8,12288]{1,0:T(8,128)(2,1)S(1)}, bf16[8,12288]{1,0:T(8,128)(2,1)S(1)}, u32[]{:S(2)}, u32[]{:S(2)}) %collective-permute-start.16) | collective-permute-done | bytes 196640 | tf_op jit(solution)/shard_map/ppermute | solution.py:225
  92.1 18.0 %all_to_all.20 = f16[16,16,128]{2,1,0:T(8,128)(2,1)S(1)} all-to-all(f16[16,16,128]{2,1,0:T(8,128)(2,1)S(1)} %broadcast_in_dim.8), channel_id=1, replica_groups=mesh['band'=2,'dx'=16,'dy'=16] {'dx'}, dimensions={0} | all-to-all | bytes 131072 | tf_op jit(solution)/shard_map/all_to_all | solution.py:220
  110.2 18.6 %all_to_all.21 = f16[16,16,128]{2,1,0:T(8,128)(2,1)S(1)} all-to-all(f16[16,16,128]{2,1,0:T(8,128)(2,1)S(1)} %broadcast_in_dim.9), channel_id=1, replica_groups=mesh['band'=2,'dx'=16,'dy'=16] {'dy'}, dimensions={0} | all-to-all | bytes 131072 | tf_op jit(solution)/shard_map/all_to_all | solution.py:220
  130.7 2.2 %collective-permute-start.17 = (bf16[16,12288]{1,0:T(8,128)(2,1)S(1)}, bf16[16,12288]{1,0:T(8,128)(2,1)S(1)}, u32[]{:S(2)}, u32[]{:S(2)}) collective-permute-start(bf16[16,12288]{1,0:T(8,128)(2,1)S(1)} %pad_maximum_fusion), channel_id=1, source_target_pairs={{0,256},{256,0},{1,257},{257,1},{2,258},{258,2},{3,259},{259,3},{4... | collective-permute-start | bytes 1179656 | tf_op jit(solution)/shard_map/ppermute | solution.py:225
  132.9 10.0 %collective-permute-done.17 = bf16[16,12288]{1,0:T(8,128)(2,1)S(1)} collective-permute-done((bf16[16,12288]{1,0:T(8,128)(2,1)S(1)}, bf16[16,12288]{1,0:T(8,128)(2,1)S(1)}, u32[]{:S(2)}, u32[]{:S(2)}) %collective-permute-start.17) | collective-permute-done | bytes 393248 | tf_op jit(solution)/shard_map/ppermute | solution.py:225
  142.9 1.3 slice_subtract_fusion
  145.4 14.2 %all_to_all.22 = f32[16,8,128]{2,1,0:T(8,128)S(1)} all-to-all(f32[16,8,128]{2,1,0:T(8,128)S(1)} %broadcast_in_dim.10), channel_id=1, replica_groups=mesh['band'=2,'dx'=16,'dy'=16] {'dx'}, dimensions={0} | all-to-all | bytes 131072 | tf_op jit(solution)/shard_map/all_to_all | solution.py:220
  160.3 5.9 %all-to-all-start.3 = ((f32[16,8,128]{2,1,0:T(8,128)}), f32[16,8,128]{2,1,0:T(8,128)S(1)}, u32[]{:S(2)}, u32[]{:S(2)}) async-start(f32[16,8,128]{2,1,0:T(8,128)} %broadcast_in_dim.11), calls=%async_computation.3 | async-start | bytes 131072 | tf_op jit(solution)/shard_map/all_to_all | solution.py:220
  167.0 6.6 %all-to-all-done.3 = f32[16,8,128]{2,1,0:T(8,128)S(1)} async-done(((f32[16,8,128]{2,1,0:T(8,128)}), f32[16,8,128]{2,1,0:T(8,128)S(1)}, u32[]{:S(2)}, u32[]{:S(2)}) %all-to-all-start.3) | async-done | bytes 65568 | tf_op jit(solution)/shard_map/all_to_all | solution.py:220
  (54 shorter events, 15.4 us)
Async XLA Ops:
  0.7 1.0 copy-start
  1.7 0.8 copy-start.1
  3.4 24.6 %collective-permute-start = (bf16[672,128]{1,0:T(8,128)(2,1)S(1)}, bf16[672,128]{1,0:T(8,128)(2,1)S(1)}, u32[]{:S(2)}, u32[]{:S(2)}) collective-permute-start(bf16[672,128]{1,0:T(8,128)(2,1)S(1)} %get-tuple-element.29), channel_id=1, source_target_pairs={{0,15},{1,2},{2,1},{3,4},{4,3},{5,6},{6,5},{7,8},{8,7},{9,10},{10,... | collective-permute-start | bytes 516104 | tf_op jit(solution)/shard_map/ppermute | solution.py:206
  9.5 18.5 %collective-permute-start.1 = (bf16[672,128]{1,0:T(8,128)(2,1)S(1)}, bf16[672,128]{1,0:T(8,128)(2,1)S(1)}, u32[]{:S(2)}, u32[]{:S(2)}) collective-permute-start(bf16[672,128]{1,0:T(8,128)(2,1)S(1)} %get-tuple-element.30), channel_id=1, source_target_pairs={{0,16},{16,0},{32,48},{48,32},{64,80},{80,64},{96,112},{112,96},{1... | collective-permute-start | bytes 516104 | tf_op jit(solution)/shard_map/ppermute | solution.py:206
  13.0 15.0 %collective-permute-start.2 = (bf16[672,128]{1,0:T(8,128)(2,1)S(1)}, bf16[672,128]{1,0:T(8,128)(2,1)S(1)}, u32[]{:S(2)}, u32[]{:S(2)}) collective-permute-start(bf16[672,128]{1,0:T(8,128)(2,1)S(1)} %get-tuple-element.31), channel_id=1, source_target_pairs={{0,240},{16,32},{32,16},{48,64},{64,48},{80,96},{96,80},{112,128},... | collective-permute-start | bytes 516104 | tf_op jit(solution)/shard_map/ppermute | solution.py:206
  23.2 5.8 %collective-permute-start.3 = (bf16[672,128]{1,0:T(8,128)(2,1)S(1)}, bf16[672,128]{1,0:T(8,128)(2,1)S(1)}, u32[]{:S(2)}, u32[]{:S(2)}) collective-permute-start(bf16[672,128]{1,0:T(8,128)(2,1)S(1)} %get-tuple-element.32), channel_id=1, source_target_pairs={{0,1},{1,0},{2,3},{3,2},{4,5},{5,4},{6,7},{7,6},{8,9},{9,8},{10,11... | collective-permute-start | bytes 516104 | tf_op jit(solution)/shard_map/ppermute | solution.py:206
  30.7 11.5 %collective-permute-start.4 = (bf16[672,128]{1,0:T(8,128)(2,1)S(1)}, bf16[672,128]{1,0:T(8,128)(2,1)S(1)}, u32[]{:S(2)}, u32[]{:S(2)}) collective-permute-start(bf16[672,128]{1,0:T(8,128)(2,1)S(1)} %get-tuple-element.34), channel_id=1, source_target_pairs={{0,15},{1,2},{2,1},{3,4},{4,3},{5,6},{6,5},{7,8},{8,7},{9,10},{10,... | collective-permute-start | bytes 516104 | tf_op jit(solution)/shard_map/ppermute | solution.py:206
  32.6 9.6 %collective-permute-start.5 = (bf16[672,128]{1,0:T(8,128)(2,1)S(1)}, bf16[672,128]{1,0:T(8,128)(2,1)S(1)}, u32[]{:S(2)}, u32[]{:S(2)}) collective-permute-start(bf16[672,128]{1,0:T(8,128)(2,1)S(1)} %get-tuple-element.35), channel_id=1, source_target_pairs={{0,16},{16,0},{32,48},{48,32},{64,80},{80,64},{96,112},{112,96},{1... | collective-permute-start | bytes 516104 | tf_op jit(solution)/shard_map/ppermute | solution.py:206
  34.6 7.8 %collective-permute-start.6 = (bf16[672,128]{1,0:T(8,128)(2,1)S(1)}, bf16[672,128]{1,0:T(8,128)(2,1)S(1)}, u32[]{:S(2)}, u32[]{:S(2)}) collective-permute-start(bf16[672,128]{1,0:T(8,128)(2,1)S(1)} %get-tuple-element.36), channel_id=1, source_target_pairs={{0,240},{16,32},{32,16},{48,64},{64,48},{80,96},{96,80},{112,128},... | collective-permute-start | bytes 516104 | tf_op jit(solution)/shard_map/ppermute | solution.py:206
  39.1 4.1 %collective-permute-start.7 = (bf16[672,128]{1,0:T(8,128)(2,1)S(1)}, bf16[672,128]{1,0:T(8,128)(2,1)S(1)}, u32[]{:S(2)}, u32[]{:S(2)}) collective-permute-start(bf16[672,128]{1,0:T(8,128)(2,1)S(1)} %get-tuple-element.37), channel_id=1, source_target_pairs={{0,1},{1,0},{2,3},{3,2},{4,5},{5,4},{6,7},{7,6},{8,9},{9,8},{10,11... | collective-permute-start | bytes 516104 | tf_op jit(solution)/shard_map/ppermute | solution.py:206
  45.0 41.3 %copy-start.2 = (bf16[128,12,8,128]{3,2,1,0:T(8,128)(2,1)S(1)}, bf16[128,12,8,128]{3,2,1,0:T(8,128)(2,1)}, u32[]{:S(2)}) copy-start(bf16[128,12,8,128]{3,2,1,0:T(8,128)(2,1)} %param.5) | copy-start | bytes 9437188
  45.0 17.3 %collective-permute-start.8 = (bf16[672,128]{1,0:T(8,128)(2,1)S(1)}, bf16[672,128]{1,0:T(8,128)(2,1)S(1)}, u32[]{:S(2)}, u32[]{:S(2)}) collective-permute-start(bf16[672,128]{1,0:T(8,128)(2,1)S(1)} %get-tuple-element.39), channel_id=1, source_target_pairs={{0,15},{1,2},{2,1},{3,4},{4,3},{5,6},{6,5},{7,8},{8,7},{9,10},{10,... | collective-permute-start | bytes 516104 | tf_op jit(solution)/shard_map/ppermute | solution.py:206
  51.6 10.6 %collective-permute-start.9 = (bf16[672,128]{1,0:T(8,128)(2,1)S(1)}, bf16[672,128]{1,0:T(8,128)(2,1)S(1)}, u32[]{:S(2)}, u32[]{:S(2)}) collective-permute-start(bf16[672,128]{1,0:T(8,128)(2,1)S(1)} %get-tuple-element.40), channel_id=1, source_target_pairs={{0,16},{16,0},{32,48},{48,32},{64,80},{80,64},{96,112},{112,96},{1... | collective-permute-start | bytes 516104 | tf_op jit(solution)/shard_map/ppermute | solution.py:206
  53.8 8.5 %collective-permute-start.10 = (bf16[672,128]{1,0:T(8,128)(2,1)S(1)}, bf16[672,128]{1,0:T(8,128)(2,1)S(1)}, u32[]{:S(2)}, u32[]{:S(2)}) collective-permute-start(bf16[672,128]{1,0:T(8,128)(2,1)S(1)} %get-tuple-element.41), channel_id=1, source_target_pairs={{0,240},{16,32},{32,16},{48,64},{64,48},{80,96},{96,80},{112,128},... | collective-permute-start | bytes 516104 | tf_op jit(solution)/shard_map/ppermute | solution.py:206
  57.2 6.1 %collective-permute-start.11 = (bf16[672,128]{1,0:T(8,128)(2,1)S(1)}, bf16[672,128]{1,0:T(8,128)(2,1)S(1)}, u32[]{:S(2)}, u32[]{:S(2)}) collective-permute-start(bf16[672,128]{1,0:T(8,128)(2,1)S(1)} %get-tuple-element.42), channel_id=1, source_target_pairs={{0,1},{1,0},{2,3},{3,2},{4,5},{5,4},{6,7},{7,6},{8,9},{9,8},{10,11... | collective-permute-start | bytes 516104 | tf_op jit(solution)/shard_map/ppermute | solution.py:206
  65.0 12.6 %collective-permute-start.12 = (bf16[672,128]{1,0:T(8,128)(2,1)S(1)}, bf16[672,128]{1,0:T(8,128)(2,1)S(1)}, u32[]{:S(2)}, u32[]{:S(2)}) collective-permute-start(bf16[672,128]{1,0:T(8,128)(2,1)S(1)} %get-tuple-element.44), channel_id=1, source_target_pairs={{0,15},{1,2},{2,1},{3,4},{4,3},{5,6},{6,5},{7,8},{8,7},{9,10},{10,... | collective-permute-start | bytes 516104 | tf_op jit(solution)/shard_map/ppermute | solution.py:206
  67.8 9.8 %collective-permute-start.13 = (bf16[672,128]{1,0:T(8,128)(2,1)S(1)}, bf16[672,128]{1,0:T(8,128)(2,1)S(1)}, u32[]{:S(2)}, u32[]{:S(2)}) collective-permute-start(bf16[672,128]{1,0:T(8,128)(2,1)S(1)} %get-tuple-element.45), channel_id=1, source_target_pairs={{0,16},{16,0},{32,48},{48,32},{64,80},{80,64},{96,112},{112,96},{1... | collective-permute-start | bytes 516104 | tf_op jit(solution)/shard_map/ppermute | solution.py:206
  69.7 7.9 %collective-permute-start.14 = (bf16[672,128]{1,0:T(8,128)(2,1)S(1)}, bf16[672,128]{1,0:T(8,128)(2,1)S(1)}, u32[]{:S(2)}, u32[]{:S(2)}) collective-permute-start(bf16[672,128]{1,0:T(8,128)(2,1)S(1)} %get-tuple-element.46), channel_id=1, source_target_pairs={{0,240},{16,32},{32,16},{48,64},{64,48},{80,96},{96,80},{112,128},... | collective-permute-start | bytes 516104 | tf_op jit(solution)/shard_map/ppermute | solution.py:206
  73.0 5.7 %collective-permute-start.15 = (bf16[672,128]{1,0:T(8,128)(2,1)S(1)}, bf16[672,128]{1,0:T(8,128)(2,1)S(1)}, u32[]{:S(2)}, u32[]{:S(2)}) collective-permute-start(bf16[672,128]{1,0:T(8,128)(2,1)S(1)} %get-tuple-element.47), channel_id=1, source_target_pairs={{0,1},{1,0},{2,3},{3,2},{4,5},{5,4},{6,7},{7,6},{8,9},{9,8},{10,11... | collective-permute-start | bytes 516104 | tf_op jit(solution)/shard_map/ppermute | solution.py:206
  83.9 7.3 %collective-permute-start.16 = (bf16[8,12288]{1,0:T(8,128)(2,1)S(1)}, bf16[8,12288]{1,0:T(8,128)(2,1)S(1)}, u32[]{:S(2)}, u32[]{:S(2)}) collective-permute-start(bf16[8,12288]{1,0:T(8,128)(2,1)S(1)} %convert_element_type.42), channel_id=1, source_target_pairs={{0,256},{256,0},{1,257},{257,1},{2,258},{258,2},{3,259},{259,3},{4... | collective-permute-start | bytes 589832 | tf_op jit(solution)/shard_map/ppermute | solution.py:225
  91.2 38.6 %copy-start.5 = (bf16[8,12288]{1,0:T(8,128)(2,1)}, bf16[8,12288]{1,0:T(8,128)(2,1)S(1)}, u32[]{:S(2)}) copy-start(bf16[8,12288]{1,0:T(8,128)(2,1)S(1)} %collective-permute-done.16) | copy-start | bytes 589828
  128.8 14.1 %copy-start.4 = (f32[8,12288]{1,0:T(8,128)S(1)}, f32[8,12288]{1,0:T(8,128)}, u32[]{:S(2)}) copy-start(f32[8,12288]{1,0:T(8,128)} %reshape.43) | copy-start | bytes 1179652
  129.8 0.9 copy-start.3
  130.7 12.1 %collective-permute-start.17 = (bf16[16,12288]{1,0:T(8,128)(2,1)S(1)}, bf16[16,12288]{1,0:T(8,128)(2,1)S(1)}, u32[]{:S(2)}, u32[]{:S(2)}) collective-permute-start(bf16[16,12288]{1,0:T(8,128)(2,1)S(1)} %pad_maximum_fusion), channel_id=1, source_target_pairs={{0,256},{256,0},{1,257},{257,1},{2,258},{258,2},{3,259},{259,3},{4... | collective-permute-start | bytes 1179656 | tf_op jit(solution)/shard_map/ppermute | solution.py:225
  160.3 13.3 %all-to-all-start.3 = ((f32[16,8,128]{2,1,0:T(8,128)}), f32[16,8,128]{2,1,0:T(8,128)S(1)}, u32[]{:S(2)}, u32[]{:S(2)}) async-start(f32[16,8,128]{2,1,0:T(8,128)} %broadcast_in_dim.11), calls=%async_computation.3 | async-start | bytes 131072 | tf_op jit(solution)/shard_map/all_to_all | solution.py:220

commit v6 on v5

--- a/solution.py
+++ b/solution.py
@@ -92,16 +92,12 @@
     pack_messages(parity_ref, field_ref, *messages)
 
 
-def step_kernel(has_previous, last, parity_ref, field_ref, potential_ref, band_ref, rest_ref, *refs):
+def inner_kernel(has_previous, field_ref, potential_ref, band_ref, rest_ref, *refs):
+    previous_ref = refs[0] if has_previous else None
+    total_ref = refs[-1]
     factor = 2.0 if has_previous else 1.0
     scale = factor / FILTER_HALF
-    messages, refs = refs[:4], refs[4:]
-    previous_ref = None
-    if has_previous:
-        previous_ref, refs = refs[0], refs[1:]
-    outs, (halo_x, halo_y, total_ref) = refs[:-3], refs[-3:]
     size_x, size_y, own, depth = field_ref.shape
-    unpack_messages(parity_ref, halo_x, halo_y, *messages)
 
     cells = field_ref[...].reshape(size_x * size_y * own, depth)
     high = cells.astype(jnp.bfloat16)
@@ -112,33 +108,58 @@
     total_ref[...] = (factor * along_z).reshape(field_ref.shape)
     weights = [-2.0 * scale * w for w in STENCIL_WEIGHTS]
 
+    def inside(total, line, at):
+        for k in range(1, WIDTH + 1):
+            near = [line[i] for i in (at - k, at + k) if 0 <= i < len(line)]
+            if near:
+                total = total + weights[k] * sum(near[1:], near[0])
+        return total
+
     @pl.loop(0, size_y)
     def _(y):
-        line = [halo_x[k, y] for k in range(WIDTH)]
-        line += [field_ref[x, y] for x in range(size_x)]
-        line += [halo_x[WIDTH + k, y] for k in range(WIDTH)]
+        line = [field_ref[x, y] for x in range(size_x)]
         for x in range(size_x):
-            at = WIDTH + x
             total = total_ref[x, y]
-            total = total + (scale * potential_ref[pl.ds(x * size_y + y, 1), :]) * line[at]
+            total = total + (scale * potential_ref[pl.ds(x * size_y + y, 1), :]) * line[x]
             if has_previous:
                 total = total - previous_ref[x, y]
-            for k in range(1, WIDTH + 1):
-                total = total + weights[k] * (line[at + k] + line[at - k])
-            total_ref[x, y] = total
+            total_ref[x, y] = inside(total, line, x)
 
     @pl.loop(0, size_x)
     def _(x):
-        line = [halo_y[x, k] for k in range(WIDTH)]
-        line += [field_ref[x, y] for y in range(size_y)]
-        line += [halo_y[x, WIDTH + k] for k in range(WIDTH)]
+        line = [field_ref[x, y] for y in range(size_y)]
         for y in range(size_y):
-            at = WIDTH + y
-            total = total_ref[x, y]
-            for k in range(1, WIDTH + 1):
-                total = total + weights[k] * (line[at + k] + line[at - k])
+            total_ref[x, y] = inside(total_ref[x, y], line, y)
+
+
+def outer_kernel(factor, last, parity_ref, inner_ref, *refs):
+    messages, outs, (halo_x, halo_y, total_ref) = refs[:4], refs[4:-3], refs[-3:]
+    size_x, size_y, own, depth = inner_ref.shape
+    unpack_messages(parity_ref, halo_x, halo_y, *messages)
+    weights = [-2.0 * factor / FILTER_HALF * w for w in STENCIL_WEIGHTS]
+
+    def outside(total, line, at, size):
+        for k in range(1, WIDTH + 1):
+            if at - k < 0:
+                total = total + weights[k] * line[WIDTH + at - k]
+            if at + k >= size:
+                total = total + weights[k] * line[WIDTH + at + k - size]
+        return total
+
+    @pl.loop(0, size_y)
+    def _(y):
+        line = [halo_x[k, y] for k in range(2 * WIDTH)]
+        for x in range(size_x):
+            total_ref[x, y] = outside(inner_ref[x, y], line, x, size_x)
+
+    @pl.loop(0, size_x)
+    def _(x):
+        line = [halo_y[x, k] for k in range(2 * WIDTH)]
+        for y in range(size_y):
+            total = outside(total_ref[x, y], line, y, size_y)
             if last:
-                outs[0][pl.ds(x * size_y + y, own, stride=size_x * size_y), :] = total
+                place = pl.multiple_of((x * size_y + y) * depth, depth)
+                outs[0][:, pl.ds(place, depth)] = total
             else:
                 outs[0][x, y] = total
 
@@ -179,16 +200,26 @@
 
 def filter_step(parity, field, fixed, messages, previous, last):
     size_x, size_y, own, depth = field.shape
+    field_shape = jax.ShapeDtypeStruct(field.shape, jnp.float32)
+    before = [] if previous is None else [previous]
+    inner = pl.pallas_call(
+        functools.partial(inner_kernel, previous is not None),
+        out_shape=field_shape,
+        in_specs=in_vmem(4 + len(before)),
+        out_specs=in_vmem(1)[0],
+        compiler_params=params(),
+        cost_estimate=pl.CostEstimate(
+            flops=6 * field.size * depth, bytes_accessed=12 * field.size, transcendentals=0
+        ),
+    )(field, *fixed, *before)
     if last:
-        out_shape = [jax.ShapeDtypeStruct((own * size_x * size_y, depth), jnp.float32)]
+        out_shape = [jax.ShapeDtypeStruct((own, size_x * size_y * depth), jnp.float32)]
     else:
-        out_shape = [jax.ShapeDtypeStruct(field.shape, jnp.float32)]
-        out_shape += message_shapes(size_x, size_y, own, depth)
-    before = [] if previous is None else [previous]
+        out_shape = [field_shape] + message_shapes(size_x, size_y, own, depth)
     return pl.pallas_call(
-        functools.partial(step_kernel, previous is not None, last),
+        functools.partial(outer_kernel, 1.0 if previous is None else 2.0, last),
         out_shape=out_shape,
-        in_specs=[pl.BlockSpec(memory_space=pltpu.SMEM)] + in_vmem(8 + len(before)),
+        in_specs=[pl.BlockSpec(memory_space=pltpu.SMEM)] + in_vmem(5),
         out_specs=in_vmem(len(out_shape)),
         scratch_shapes=[
             pltpu.VMEM((2 * WIDTH, size_y, own, depth), jnp.float32),
@@ -196,7 +227,7 @@
             pltpu.VMEM(field.shape, jnp.float32),
         ],
         compiler_params=params(),
-    )(parity, field, *fixed, *messages, *before)
+    )(parity, inner, *messages)
 
 
 def swap(y_odd, x_even, x_odd, y_even):
@@ -246,7 +277,7 @@
             parity, field, fixed, swap(*messages), previous, last
         )
         previous, field = field, following
-    filtered = field.reshape(own_count, cell_count)
+    filtered = field
 
     rounded = filtered.astype(jnp.bfloat16)
     rounded_other = other_band(rounded)

time: 175 us -> 167 us (0.954)
  waiting for transfers between devices: 24.5 us -> 21.1 us
  other arithmetic: 3.94 us -> 1.05 us
  local copies, waits for them, and re-layouts: 6.14 us -> 3.43 us
    ppermute x16, waiting for transfers between devices: 3.98 us -> 0.63 us  [swapped(): lax.ppermute(values, axis, [(i, (i + step(i)) % count) for i in range(cou...]
    pallas_call x4 -> x8, Pallas kernels: 6.79 us -> 7.71 us  [the longest x4 4.4 us: filter_step(): pl.pallas_call(functools.partial(outer_kernel, 1.0 if previous is None el...]
    unnamed x13 -> x7, local copies, waits for them, and re-layouts: 3.5 us -> 2.62 us
  transfers between devices with their start and end apart: 19 -> 19, of which waited for: 8 -> 7; matrix products, arithmetic and copies ran while one was open for 1% -> 1% of each run, Pallas kernels for 0% -> 2%
where the time goes in v6:
time: 167 us; the launch traced here: 166 us
  starting transfers between devices  76.3 us (46%)
  blocking collectives  50.8 us (30%)
  waiting for transfers between devices  21.1 us (13%)
  Pallas kernels  8.61 us (5%)
  matrix products  3.8 us (2%)
  local copies, waits for them, and re-layouts  3.43 us (2%)
    ppermute x16, starting transfers between devices, swapped(): lax.ppermute(values, axis, [(i, (i + step(i)) % count) for i in range(cou...  65.9 us
    all_to_all x3, blocking collectives, sum_over_grid(): lax.all_to_all(sent, axis, 0, 0).astype(jnp.float32)  50.8 us
    ppermute x2, waiting for transfers between devices, other_band(): return lax.ppermute(values, 'band', [(0, 1), (1, 0)])  13.9 us
    all_to_all x1, waiting for transfers between devices, sum_over_grid(): lax.all_to_all(sent, axis, 0, 0).astype(jnp.float32)  6.57 us
    all_to_all x1, starting transfers between devices, sum_over_grid(): lax.all_to_all(sent, axis, 0, 0).astype(jnp.float32)  5.86 us
    ppermute x2, starting transfers between devices, other_band(): return lax.ppermute(values, 'band', [(0, 1), (1, 0)])  4.54 us
    pallas_call x4, Pallas kernels, filter_step(): pl.pallas_call(functools.partial(outer_kernel, 1.0 if previous is None el...  4.4 us
  transfers between devices with their start and end apart: 19, of which 7 were waited for; matrix products, arithmetic and copies ran while one was open for 1% of the time, Pallas kernels for 2%

profile of v6, /device:TPU:1, one launch (start us, length us, event | category | flops | bytes accessed | tf_op | source)
XLA Modules:
  0.0 166.2 jit_solution(12804024260688337821)
XLA Ops:
  0.7 1.0 copy-done
  3.4 6.0 %collective-permute-start = (bf16[672,128]{1,0:T(8,128)(2,1)S(1)}, bf16[672,128]{1,0:T(8,128)(2,1)S(1)}, u32[]{:S(2)}, u32[]{:S(2)}) collective-permute-start(bf16[672,128]{1,0:T(8,128)(2,1)S(1)} %get-tuple-element.29), channel_id=1, source_target_pairs={{0,15},{1,2},{2,1},{3,4},{4,3},{5,6},{6,5},{7,8},{8,7},{9,10},{10,... | collective-permute-start | bytes 516104 | tf_op jit(solution)/shard_map/ppermute | solution.py:237
  9.5 3.5 %collective-permute-start.1 = (bf16[672,128]{1,0:T(8,128)(2,1)S(1)}, bf16[672,128]{1,0:T(8,128)(2,1)S(1)}, u32[]{:S(2)}, u32[]{:S(2)}) collective-permute-start(bf16[672,128]{1,0:T(8,128)(2,1)S(1)} %get-tuple-element.30), channel_id=1, source_target_pairs={{0,16},{16,0},{32,48},{48,32},{64,80},{80,64},{96,112},{112,96},{1... | collective-permute-start | bytes 516104 | tf_op jit(solution)/shard_map/ppermute | solution.py:237
  13.0 10.2 %collective-permute-start.2 = (bf16[672,128]{1,0:T(8,128)(2,1)S(1)}, bf16[672,128]{1,0:T(8,128)(2,1)S(1)}, u32[]{:S(2)}, u32[]{:S(2)}) collective-permute-start(bf16[672,128]{1,0:T(8,128)(2,1)S(1)} %get-tuple-element.31), channel_id=1, source_target_pairs={{0,240},{16,32},{32,16},{48,64},{64,48},{80,96},{96,80},{112,128},... | collective-permute-start | bytes 516104 | tf_op jit(solution)/shard_map/ppermute | solution.py:237
  23.2 4.8 %collective-permute-start.3 = (bf16[672,128]{1,0:T(8,128)(2,1)S(1)}, bf16[672,128]{1,0:T(8,128)(2,1)S(1)}, u32[]{:S(2)}, u32[]{:S(2)}) collective-permute-start(bf16[672,128]{1,0:T(8,128)(2,1)S(1)} %get-tuple-element.32), channel_id=1, source_target_pairs={{0,1},{1,0},{2,3},{3,2},{4,5},{5,4},{6,7},{7,6},{8,9},{9,8},{10,11... | collective-permute-start | bytes 516104 | tf_op jit(solution)/shard_map/ppermute | solution.py:237
  29.0 1.1 shard_map.52
  30.2 1.9 %collective-permute-start.4 = (bf16[672,128]{1,0:T(8,128)(2,1)S(1)}, bf16[672,128]{1,0:T(8,128)(2,1)S(1)}, u32[]{:S(2)}, u32[]{:S(2)}) collective-permute-start(bf16[672,128]{1,0:T(8,128)(2,1)S(1)} %get-tuple-element.34), channel_id=1, source_target_pairs={{0,15},{1,2},{2,1},{3,4},{4,3},{5,6},{6,5},{7,8},{8,7},{9,10},{10,... | collective-permute-start | bytes 516104 | tf_op jit(solution)/shard_map/ppermute | solution.py:237
  32.1 1.9 %collective-permute-start.5 = (bf16[672,128]{1,0:T(8,128)(2,1)S(1)}, bf16[672,128]{1,0:T(8,128)(2,1)S(1)}, u32[]{:S(2)}, u32[]{:S(2)}) collective-permute-start(bf16[672,128]{1,0:T(8,128)(2,1)S(1)} %get-tuple-element.35), channel_id=1, source_target_pairs={{0,16},{16,0},{32,48},{48,32},{64,80},{80,64},{96,112},{112,96},{1... | collective-permute-start | bytes 516104 | tf_op jit(solution)/shard_map/ppermute | solution.py:237
  34.0 4.6 %collective-permute-start.6 = (bf16[672,128]{1,0:T(8,128)(2,1)S(1)}, bf16[672,128]{1,0:T(8,128)(2,1)S(1)}, u32[]{:S(2)}, u32[]{:S(2)}) collective-permute-start(bf16[672,128]{1,0:T(8,128)(2,1)S(1)} %get-tuple-element.36), channel_id=1, source_target_pairs={{0,240},{16,32},{32,16},{48,64},{64,48},{80,96},{96,80},{112,128},... | collective-permute-start | bytes 516104 | tf_op jit(solution)/shard_map/ppermute | solution.py:237
  38.6 3.1 %collective-permute-start.7 = (bf16[672,128]{1,0:T(8,128)(2,1)S(1)}, bf16[672,128]{1,0:T(8,128)(2,1)S(1)}, u32[]{:S(2)}, u32[]{:S(2)}) collective-permute-start(bf16[672,128]{1,0:T(8,128)(2,1)S(1)} %get-tuple-element.37), channel_id=1, source_target_pairs={{0,1},{1,0},{2,3},{3,2},{4,5},{5,4},{6,7},{7,6},{8,9},{9,8},{10,11... | collective-permute-start | bytes 516104 | tf_op jit(solution)/shard_map/ppermute | solution.py:237
  42.7 1.1 shard_map.54
  43.8 6.7 %collective-permute-start.8 = (bf16[672,128]{1,0:T(8,128)(2,1)S(1)}, bf16[672,128]{1,0:T(8,128)(2,1)S(1)}, u32[]{:S(2)}, u32[]{:S(2)}) collective-permute-start(bf16[672,128]{1,0:T(8,128)(2,1)S(1)} %get-tuple-element.39), channel_id=1, source_target_pairs={{0,15},{1,2},{2,1},{3,4},{4,3},{5,6},{6,5},{7,8},{8,7},{9,10},{10,... | collective-permute-start | bytes 516104 | tf_op jit(solution)/shard_map/ppermute | solution.py:237
  50.5 2.2 %collective-permute-start.9 = (bf16[672,128]{1,0:T(8,128)(2,1)S(1)}, bf16[672,128]{1,0:T(8,128)(2,1)S(1)}, u32[]{:S(2)}, u32[]{:S(2)}) collective-permute-start(bf16[672,128]{1,0:T(8,128)(2,1)S(1)} %get-tuple-element.40), channel_id=1, source_target_pairs={{0,16},{16,0},{32,48},{48,32},{64,80},{80,64},{96,112},{112,96},{1... | collective-permute-start | bytes 516104 | tf_op jit(solution)/shard_map/ppermute | solution.py:237
  52.7 3.3 %collective-permute-start.10 = (bf16[672,128]{1,0:T(8,128)(2,1)S(1)}, bf16[672,128]{1,0:T(8,128)(2,1)S(1)}, u32[]{:S(2)}, u32[]{:S(2)}) collective-permute-start(bf16[672,128]{1,0:T(8,128)(2,1)S(1)} %get-tuple-element.41), channel_id=1, source_target_pairs={{0,240},{16,32},{32,16},{48,64},{64,48},{80,96},{96,80},{112,128},... | collective-permute-start | bytes 516104 | tf_op jit(solution)/shard_map/ppermute | solution.py:237
  56.0 5.1 %collective-permute-start.11 = (bf16[672,128]{1,0:T(8,128)(2,1)S(1)}, bf16[672,128]{1,0:T(8,128)(2,1)S(1)}, u32[]{:S(2)}, u32[]{:S(2)}) collective-permute-start(bf16[672,128]{1,0:T(8,128)(2,1)S(1)} %get-tuple-element.42), channel_id=1, source_target_pairs={{0,1},{1,0},{2,3},{3,2},{4,5},{5,4},{6,7},{7,6},{8,9},{9,8},{10,11... | collective-permute-start | bytes 516104 | tf_op jit(solution)/shard_map/ppermute | solution.py:237
  62.1 1.1 shard_map.56
  63.3 2.8 %collective-permute-start.12 = (bf16[672,128]{1,0:T(8,128)(2,1)S(1)}, bf16[672,128]{1,0:T(8,128)(2,1)S(1)}, u32[]{:S(2)}, u32[]{:S(2)}) collective-permute-start(bf16[672,128]{1,0:T(8,128)(2,1)S(1)} %get-tuple-element.44), channel_id=1, source_target_pairs={{0,15},{1,2},{2,1},{3,4},{4,3},{5,6},{6,5},{7,8},{8,7},{9,10},{10,... | collective-permute-start | bytes 516104 | tf_op jit(solution)/shard_map/ppermute | solution.py:237
  66.1 1.9 %collective-permute-start.13 = (bf16[672,128]{1,0:T(8,128)(2,1)S(1)}, bf16[672,128]{1,0:T(8,128)(2,1)S(1)}, u32[]{:S(2)}, u32[]{:S(2)}) collective-permute-start(bf16[672,128]{1,0:T(8,128)(2,1)S(1)} %get-tuple-element.45), channel_id=1, source_target_pairs={{0,16},{16,0},{32,48},{48,32},{64,80},{80,64},{96,112},{112,96},{1... | collective-permute-start | bytes 516104 | tf_op jit(solution)/shard_map/ppermute | solution.py:237
  68.0 3.2 %collective-permute-start.14 = (bf16[672,128]{1,0:T(8,128)(2,1)S(1)}, bf16[672,128]{1,0:T(8,128)(2,1)S(1)}, u32[]{:S(2)}, u32[]{:S(2)}) collective-permute-start(bf16[672,128]{1,0:T(8,128)(2,1)S(1)} %get-tuple-element.46), channel_id=1, source_target_pairs={{0,240},{16,32},{32,16},{48,64},{64,48},{80,96},{96,80},{112,128},... | collective-permute-start | bytes 516104 | tf_op jit(solution)/shard_map/ppermute | solution.py:237
  71.2 4.7 %collective-permute-start.15 = (bf16[672,128]{1,0:T(8,128)(2,1)S(1)}, bf16[672,128]{1,0:T(8,128)(2,1)S(1)}, u32[]{:S(2)}, u32[]{:S(2)}) collective-permute-start(bf16[672,128]{1,0:T(8,128)(2,1)S(1)} %get-tuple-element.47), channel_id=1, source_target_pairs={{0,1},{1,0},{2,3},{3,2},{4,5},{5,4},{6,7},{7,6},{8,9},{9,8},{10,11... | collective-permute-start | bytes 516104 | tf_op jit(solution)/shard_map/ppermute | solution.py:237
  76.9 1.0 shard_map.58
  78.0 2.3 %collective-permute-start.16 = (bf16[8,12288]{1,0:T(8,128)(2,1)S(1)}, bf16[8,12288]{1,0:T(8,128)(2,1)S(1)}, u32[]{:S(2)}, u32[]{:S(2)}) collective-permute-start(bf16[8,12288]{1,0:T(8,128)(2,1)S(1)} %convert_element_type.35), channel_id=1, source_target_pairs={{0,256},{256,0},{1,257},{257,1},{2,258},{258,2},{3,259},{259,3},{4... | collective-permute-start | bytes 589832 | tf_op jit(solution)/shard_map/ppermute | solution.py:256
  81.3 4.0 %collective-permute-done.16 = bf16[8,12288]{1,0:T(8,128)(2,1)S(1)} collective-permute-done((bf16[8,12288]{1,0:T(8,128)(2,1)S(1)}, bf16[8,12288]{1,0:T(8,128)(2,1)S(1)}, u32[]{:S(2)}, u32[]{:S(2)}) %collective-permute-start.16) | collective-permute-done | bytes 196640 | tf_op jit(solution)/shard_map/ppermute | solution.py:256
  86.3 17.9 %all_to_all.20 = f16[16,16,128]{2,1,0:T(8,128)(2,1)S(1)} all-to-all(f16[16,16,128]{2,1,0:T(8,128)(2,1)S(1)} %broadcast_in_dim.8), channel_id=1, replica_groups=mesh['band'=2,'dx'=16,'dy'=16] {'dx'}, dimensions={0} | all-to-all | bytes 131072 | tf_op jit(solution)/shard_map/all_to_all | solution.py:251
  104.2 18.7 %all_to_all.21 = f16[16,16,128]{2,1,0:T(8,128)(2,1)S(1)} all-to-all(f16[16,16,128]{2,1,0:T(8,128)(2,1)S(1)} %broadcast_in_dim.9), channel_id=1, replica_groups=mesh['band'=2,'dx'=16,'dy'=16] {'dy'}, dimensions={0} | all-to-all | bytes 131072 | tf_op jit(solution)/shard_map/all_to_all | solution.py:251
  122.9 1.0 fusion
  124.0 2.2 %collective-permute-start.17 = (bf16[16,12288]{1,0:T(8,128)(2,1)S(1)}, bf16[16,12288]{1,0:T(8,128)(2,1)S(1)}, u32[]{:S(2)}, u32[]{:S(2)}) collective-permute-start(bf16[16,12288]{1,0:T(8,128)(2,1)S(1)} %pad_maximum_fusion), channel_id=1, source_target_pairs={{0,256},{256,0},{1,257},{257,1},{2,258},{258,2},{3,259},{259,3},{4... | collective-permute-start | bytes 1179656 | tf_op jit(solution)/shard_map/ppermute | solution.py:256
  126.2 9.9 %collective-permute-done.17 = bf16[16,12288]{1,0:T(8,128)(2,1)S(1)} collective-permute-done((bf16[16,12288]{1,0:T(8,128)(2,1)S(1)}, bf16[16,12288]{1,0:T(8,128)(2,1)S(1)}, u32[]{:S(2)}, u32[]{:S(2)}) %collective-permute-start.17) | collective-permute-done | bytes 393248 | tf_op jit(solution)/shard_map/ppermute | solution.py:256
  136.3 1.0 fusion.9
  137.4 14.2 %all_to_all.22 = f32[16,8,128]{2,1,0:T(8,128)S(1)} all-to-all(f32[16,8,128]{2,1,0:T(8,128)S(1)} %broadcast_in_dim.10), channel_id=1, replica_groups=mesh['band'=2,'dx'=16,'dy'=16] {'dx'}, dimensions={0} | all-to-all | bytes 131072 | tf_op jit(solution)/shard_map/all_to_all | solution.py:251
  152.3 5.9 %all-to-all-start.3 = ((f32[16,8,128]{2,1,0:T(8,128)}), f32[16,8,128]{2,1,0:T(8,128)S(1)}, u32[]{:S(2)}, u32[]{:S(2)}) async-start(f32[16,8,128]{2,1,0:T(8,128)} %broadcast_in_dim.11), calls=%async_computation.3 | async-start | bytes 131072 | tf_op jit(solution)/shard_map/all_to_all | solution.py:251
  159.0 6.6 %all-to-all-done.3 = f32[16,8,128]{2,1,0:T(8,128)S(1)} async-done(((f32[16,8,128]{2,1,0:T(8,128)}), f32[16,8,128]{2,1,0:T(8,128)S(1)}, u32[]{:S(2)}, u32[]{:S(2)}) %all-to-all-start.3) | async-done | bytes 65568 | tf_op jit(solution)/shard_map/all_to_all | solution.py:251
  (49 shorter events, 10.2 us)
Async XLA Ops:
  0.7 1.0 copy-start
  1.7 0.8 copy-start.1
  3.4 25.4 %collective-permute-start = (bf16[672,128]{1,0:T(8,128)(2,1)S(1)}, bf16[672,128]{1,0:T(8,128)(2,1)S(1)}, u32[]{:S(2)}, u32[]{:S(2)}) collective-permute-start(bf16[672,128]{1,0:T(8,128)(2,1)S(1)} %get-tuple-element.29), channel_id=1, source_target_pairs={{0,15},{1,2},{2,1},{3,4},{4,3},{5,6},{6,5},{7,8},{8,7},{9,10},{10,... | collective-permute-start | bytes 516104 | tf_op jit(solution)/shard_map/ppermute | solution.py:237
  9.5 19.4 %collective-permute-start.1 = (bf16[672,128]{1,0:T(8,128)(2,1)S(1)}, bf16[672,128]{1,0:T(8,128)(2,1)S(1)}, u32[]{:S(2)}, u32[]{:S(2)}) collective-permute-start(bf16[672,128]{1,0:T(8,128)(2,1)S(1)} %get-tuple-element.30), channel_id=1, source_target_pairs={{0,16},{16,0},{32,48},{48,32},{64,80},{80,64},{96,112},{112,96},{1... | collective-permute-start | bytes 516104 | tf_op jit(solution)/shard_map/ppermute | solution.py:237
  13.0 15.8 %collective-permute-start.2 = (bf16[672,128]{1,0:T(8,128)(2,1)S(1)}, bf16[672,128]{1,0:T(8,128)(2,1)S(1)}, u32[]{:S(2)}, u32[]{:S(2)}) collective-permute-start(bf16[672,128]{1,0:T(8,128)(2,1)S(1)} %get-tuple-element.31), channel_id=1, source_target_pairs={{0,240},{16,32},{32,16},{48,64},{64,48},{80,96},{96,80},{112,128},... | collective-permute-start | bytes 516104 | tf_op jit(solution)/shard_map/ppermute | solution.py:237
  23.2 5.8 %collective-permute-start.3 = (bf16[672,128]{1,0:T(8,128)(2,1)S(1)}, bf16[672,128]{1,0:T(8,128)(2,1)S(1)}, u32[]{:S(2)}, u32[]{:S(2)}) collective-permute-start(bf16[672,128]{1,0:T(8,128)(2,1)S(1)} %get-tuple-element.32), channel_id=1, source_target_pairs={{0,1},{1,0},{2,3},{3,2},{4,5},{5,4},{6,7},{7,6},{8,9},{9,8},{10,11... | collective-permute-start | bytes 516104 | tf_op jit(solution)/shard_map/ppermute | solution.py:237
  30.2 12.4 %collective-permute-start.4 = (bf16[672,128]{1,0:T(8,128)(2,1)S(1)}, bf16[672,128]{1,0:T(8,128)(2,1)S(1)}, u32[]{:S(2)}, u32[]{:S(2)}) collective-permute-start(bf16[672,128]{1,0:T(8,128)(2,1)S(1)} %get-tuple-element.34), channel_id=1, source_target_pairs={{0,15},{1,2},{2,1},{3,4},{4,3},{5,6},{6,5},{7,8},{8,7},{9,10},{10,... | collective-permute-start | bytes 516104 | tf_op jit(solution)/shard_map/ppermute | solution.py:237
  32.1 10.4 %collective-permute-start.5 = (bf16[672,128]{1,0:T(8,128)(2,1)S(1)}, bf16[672,128]{1,0:T(8,128)(2,1)S(1)}, u32[]{:S(2)}, u32[]{:S(2)}) collective-permute-start(bf16[672,128]{1,0:T(8,128)(2,1)S(1)} %get-tuple-element.35), channel_id=1, source_target_pairs={{0,16},{16,0},{32,48},{48,32},{64,80},{80,64},{96,112},{112,96},{1... | collective-permute-start | bytes 516104 | tf_op jit(solution)/shard_map/ppermute | solution.py:237
  34.0 8.5 %collective-permute-start.6 = (bf16[672,128]{1,0:T(8,128)(2,1)S(1)}, bf16[672,128]{1,0:T(8,128)(2,1)S(1)}, u32[]{:S(2)}, u32[]{:S(2)}) collective-permute-start(bf16[672,128]{1,0:T(8,128)(2,1)S(1)} %get-tuple-element.36), channel_id=1, source_target_pairs={{0,240},{16,32},{32,16},{48,64},{64,48},{80,96},{96,80},{112,128},... | collective-permute-start | bytes 516104 | tf_op jit(solution)/shard_map/ppermute | solution.py:237
  38.6 4.1 %collective-permute-start.7 = (bf16[672,128]{1,0:T(8,128)(2,1)S(1)}, bf16[672,128]{1,0:T(8,128)(2,1)S(1)}, u32[]{:S(2)}, u32[]{:S(2)}) collective-permute-start(bf16[672,128]{1,0:T(8,128)(2,1)S(1)} %get-tuple-element.37), channel_id=1, source_target_pairs={{0,1},{1,0},{2,3},{3,2},{4,5},{5,4},{6,7},{7,6},{8,9},{9,8},{10,11... | collective-permute-start | bytes 516104 | tf_op jit(solution)/shard_map/ppermute | solution.py:237
  43.8 36.5 %copy-start.2 = (bf16[128,12,8,128]{3,2,1,0:T(8,128)(2,1)S(1)}, bf16[128,12,8,128]{3,2,1,0:T(8,128)(2,1)}, u32[]{:S(2)}) copy-start(bf16[128,12,8,128]{3,2,1,0:T(8,128)(2,1)} %param.5) | copy-start | bytes 9437188
  43.8 18.1 %collective-permute-start.8 = (bf16[672,128]{1,0:T(8,128)(2,1)S(1)}, bf16[672,128]{1,0:T(8,128)(2,1)S(1)}, u32[]{:S(2)}, u32[]{:S(2)}) collective-permute-start(bf16[672,128]{1,0:T(8,128)(2,1)S(1)} %get-tuple-element.39), channel_id=1, source_target_pairs={{0,15},{1,2},{2,1},{3,4},{4,3},{5,6},{6,5},{7,8},{8,7},{9,10},{10,... | collective-permute-start | bytes 516104 | tf_op jit(solution)/shard_map/ppermute | solution.py:237
  50.5 11.5 %collective-permute-start.9 = (bf16[672,128]{1,0:T(8,128)(2,1)S(1)}, bf16[672,128]{1,0:T(8,128)(2,1)S(1)}, u32[]{:S(2)}, u32[]{:S(2)}) collective-permute-start(bf16[672,128]{1,0:T(8,128)(2,1)S(1)} %get-tuple-element.40), channel_id=1, source_target_pairs={{0,16},{16,0},{32,48},{48,32},{64,80},{80,64},{96,112},{112,96},{1... | collective-permute-start | bytes 516104 | tf_op jit(solution)/shard_map/ppermute | solution.py:237
  52.7 9.3 %collective-permute-start.10 = (bf16[672,128]{1,0:T(8,128)(2,1)S(1)}, bf16[672,128]{1,0:T(8,128)(2,1)S(1)}, u32[]{:S(2)}, u32[]{:S(2)}) collective-permute-start(bf16[672,128]{1,0:T(8,128)(2,1)S(1)} %get-tuple-element.41), channel_id=1, source_target_pairs={{0,240},{16,32},{32,16},{48,64},{64,48},{80,96},{96,80},{112,128},... | collective-permute-start | bytes 516104 | tf_op jit(solution)/shard_map/ppermute | solution.py:237
  56.0 6.1 %collective-permute-start.11 = (bf16[672,128]{1,0:T(8,128)(2,1)S(1)}, bf16[672,128]{1,0:T(8,128)(2,1)S(1)}, u32[]{:S(2)}, u32[]{:S(2)}) collective-permute-start(bf16[672,128]{1,0:T(8,128)(2,1)S(1)} %get-tuple-element.42), channel_id=1, source_target_pairs={{0,1},{1,0},{2,3},{3,2},{4,5},{5,4},{6,7},{7,6},{8,9},{9,8},{10,11... | collective-permute-start | bytes 516104 | tf_op jit(solution)/shard_map/ppermute | solution.py:237
  63.3 13.5 %collective-permute-start.12 = (bf16[672,128]{1,0:T(8,128)(2,1)S(1)}, bf16[672,128]{1,0:T(8,128)(2,1)S(1)}, u32[]{:S(2)}, u32[]{:S(2)}) collective-permute-start(bf16[672,128]{1,0:T(8,128)(2,1)S(1)} %get-tuple-element.44), channel_id=1, source_target_pairs={{0,15},{1,2},{2,1},{3,4},{4,3},{5,6},{6,5},{7,8},{8,7},{9,10},{10,... | collective-permute-start | bytes 516104 | tf_op jit(solution)/shard_map/ppermute | solution.py:237
  66.1 10.7 %collective-permute-start.13 = (bf16[672,128]{1,0:T(8,128)(2,1)S(1)}, bf16[672,128]{1,0:T(8,128)(2,1)S(1)}, u32[]{:S(2)}, u32[]{:S(2)}) collective-permute-start(bf16[672,128]{1,0:T(8,128)(2,1)S(1)} %get-tuple-element.45), channel_id=1, source_target_pairs={{0,16},{16,0},{32,48},{48,32},{64,80},{80,64},{96,112},{112,96},{1... | collective-permute-start | bytes 516104 | tf_op jit(solution)/shard_map/ppermute | solution.py:237
  68.0 8.8 %collective-permute-start.14 = (bf16[672,128]{1,0:T(8,128)(2,1)S(1)}, bf16[672,128]{1,0:T(8,128)(2,1)S(1)}, u32[]{:S(2)}, u32[]{:S(2)}) collective-permute-start(bf16[672,128]{1,0:T(8,128)(2,1)S(1)} %get-tuple-element.46), channel_id=1, source_target_pairs={{0,240},{16,32},{32,16},{48,64},{64,48},{80,96},{96,80},{112,128},... | collective-permute-start | bytes 516104 | tf_op jit(solution)/shard_map/ppermute | solution.py:237
  71.2 5.7 %collective-permute-start.15 = (bf16[672,128]{1,0:T(8,128)(2,1)S(1)}, bf16[672,128]{1,0:T(8,128)(2,1)S(1)}, u32[]{:S(2)}, u32[]{:S(2)}) collective-permute-start(bf16[672,128]{1,0:T(8,128)(2,1)S(1)} %get-tuple-element.47), channel_id=1, source_target_pairs={{0,1},{1,0},{2,3},{3,2},{4,5},{5,4},{6,7},{7,6},{8,9},{9,8},{10,11... | collective-permute-start | bytes 516104 | tf_op jit(solution)/shard_map/ppermute | solution.py:237
  78.0 7.3 %collective-permute-start.16 = (bf16[8,12288]{1,0:T(8,128)(2,1)S(1)}, bf16[8,12288]{1,0:T(8,128)(2,1)S(1)}, u32[]{:S(2)}, u32[]{:S(2)}) collective-permute-start(bf16[8,12288]{1,0:T(8,128)(2,1)S(1)} %convert_element_type.35), channel_id=1, source_target_pairs={{0,256},{256,0},{1,257},{257,1},{2,258},{258,2},{3,259},{259,3},{4... | collective-permute-start | bytes 589832 | tf_op jit(solution)/shard_map/ppermute | solution.py:256
  124.0 12.1 %collective-permute-start.17 = (bf16[16,12288]{1,0:T(8,128)(2,1)S(1)}, bf16[16,12288]{1,0:T(8,128)(2,1)S(1)}, u32[]{:S(2)}, u32[]{:S(2)}) collective-permute-start(bf16[16,12288]{1,0:T(8,128)(2,1)S(1)} %pad_maximum_fusion), channel_id=1, source_target_pairs={{0,256},{256,0},{1,257},{257,1},{2,258},{258,2},{3,259},{259,3},{4... | collective-permute-start | bytes 1179656 | tf_op jit(solution)/shard_map/ppermute | solution.py:256
  152.3 13.2 %all-to-all-start.3 = ((f32[16,8,128]{2,1,0:T(8,128)}), f32[16,8,128]{2,1,0:T(8,128)S(1)}, u32[]{:S(2)}, u32[]{:S(2)}) async-start(f32[16,8,128]{2,1,0:T(8,128)} %broadcast_in_dim.11), calls=%async_computation.3 | async-start | bytes 131072 | tf_op jit(solution)/shard_map/all_to_all | solution.py:251

commit v7 on v6

--- a/solution.py
+++ b/solution.py
@@ -72,8 +72,17 @@
                 halo[:, near] += read(WIDTH)
 
 
-def start_kernel(parity_ref, cells_ref, potential_ref, field_ref, kept_ref, band_ref, rest_ref, *messages):
-    size_x, size_y, own, depth = field_ref.shape
+def start_kernel(parity_ref, cells_ref, field_ref, *messages):
+    size_x, size_y, own = field_ref.shape[:3]
+    for x in range(size_x):
+        for y in range(size_y):
+            rows = pl.ds(x * size_y + y, own, stride=size_x * size_y)
+            field_ref[x, y] = cells_ref[rows, :]
+    pack_messages(parity_ref, field_ref, *messages)
+
+
+def fixed_kernel(potential_ref, kept_ref, band_ref, rest_ref):
+    depth = rest_ref.shape[0]
     kept_ref[...] = potential_ref[...]
     row = lax.broadcasted_iota(jnp.int32, (depth, depth), 0)
     away = jnp.abs(row - lax.broadcasted_iota(jnp.int32, (depth, depth), 1))
@@ -85,11 +94,6 @@
     band_ref[:depth, :] = high
     band_ref[depth:, :] = high
     rest_ref[...] = (matrix - high.astype(jnp.float32)).astype(jnp.bfloat16)
-    for x in range(size_x):
-        for y in range(size_y):
-            rows = pl.ds(x * size_y + y, own, stride=size_x * size_y)
-            field_ref[x, y] = cells_ref[rows, :]
-    pack_messages(parity_ref, field_ref, *messages)
 
 
 def inner_kernel(has_previous, field_ref, potential_ref, band_ref, rest_ref, *refs):
@@ -180,22 +184,34 @@
     return [pl.BlockSpec(memory_space=pltpu.VMEM)] * count
 
 
-def start(parity, orbital_block, potential):
+def start(parity, orbital_block):
     own, size_x, size_y, depth = orbital_block.shape
     field = jax.ShapeDtypeStruct((size_x, size_y, own, depth), jnp.float32)
     return pl.pallas_call(
         start_kernel,
+        out_shape=[field] + message_shapes(size_x, size_y, own, depth),
+        in_specs=[pl.BlockSpec(memory_space=pltpu.SMEM)] + in_vmem(1),
+        out_specs=in_vmem(5),
+        compiler_params=params(),
+    )(parity, orbital_block.reshape(own * size_x * size_y, depth))
+
+
+def fixed_arrays(potential):
+    depth = potential.shape[1]
+    return pl.pallas_call(
+        fixed_kernel,
         out_shape=[
-            field,
             jax.ShapeDtypeStruct(potential.shape, jnp.float32),
             jax.ShapeDtypeStruct((2 * depth, depth), jnp.bfloat16),
             jax.ShapeDtypeStruct((depth, depth), jnp.bfloat16),
-        ]
-        + message_shapes(size_x, size_y, own, depth),
-        in_specs=[pl.BlockSpec(memory_space=pltpu.SMEM)] + in_vmem(2),
-        out_specs=in_vmem(8),
+        ],
+        in_specs=in_vmem(1),
+        out_specs=in_vmem(3),
         compiler_params=params(),
-    )(parity, orbital_block.reshape(own * size_x * size_y, depth), potential)
+        cost_estimate=pl.CostEstimate(
+            flops=30 * depth * depth, bytes_accessed=16 * depth * depth, transcendentals=0
+        ),
+    )(potential)
 
 
 def filter_step(parity, field, fixed, messages, previous, last):
@@ -252,6 +268,14 @@
     return values
 
 
+def sum_at_once(values):
+    count = lax.axis_size("dx") * lax.axis_size("dy")
+    flat = values.reshape(1, 1, values.size)
+    sent = jnp.broadcast_to(flat, (count, 1, values.size))
+    got = lax.all_to_all(sent, ("dx", "dy"), 0, 0, tiled=True)
+    return jnp.sum(got, axis=0).reshape(values.shape)
+
+
 def other_band(values):
     return lax.ppermute(values, "band", [(0, 1), (1, 0)])
 
@@ -268,8 +292,8 @@
     flat_potential = potential.reshape(size_x * size_y, depth)
     parity = jnp.stack([lax.axis_index("dx") % 2, lax.axis_index("dy") % 2]).astype(jnp.int32)
 
-    field, *rest = start(parity, orbital_block, flat_potential)
-    fixed, messages = rest[:3], rest[3:]
+    field, *messages = start(parity, orbital_block)
+    fixed = fixed_arrays(flat_potential)
     previous = None
     for degree_step in range(DEGREE):
         last = degree_step == DEGREE - 1
@@ -296,10 +320,8 @@
     partial_gram = exact(projected, jnp.concatenate([projected, projected_other], axis=0))
     turned = jnp.roll(partial_gram, own_count, axis=1)
     partial_gram = jnp.where(lax.axis_index("band") == 0, partial_gram, turned)
-    lanes = 128
-    partial_gram = jnp.pad(partial_gram, ((0, 0), (0, lanes - 2 * own_count)))
     total_cells = cell_count * lax.axis_size("dx") * lax.axis_size("dy")
-    gram_matrix = sum_over_grid(partial_gram, jnp.float32)[:, : 2 * own_count] / total_cells
+    gram_matrix = sum_at_once(partial_gram) / total_cells
     return (projected.reshape(orbital_block.shape), gram_matrix)
 
 

time: 167 us -> 168 us (level)
  blocking collectives: 50.8 us -> 37.1 us
  waiting for transfers between devices: 21.1 us -> 33.9 us
    all_to_all x3 -> x2, blocking collectives: 50.8 us -> 37.1 us  [sum_over_grid(): lax.all_to_all(sent, axis, 0, 0).astype(jnp.float32)]
    all_to_all x1, waiting for transfers between devices: 6.57 us -> 19.6 us  [sum_at_once(): got = lax.all_to_all(sent, ('dx', 'dy'), 0, 0, tiled=True)]
    all_to_all x1, starting transfers between devices: 5.86 us -> 8.52 us  [sum_at_once(): got = lax.all_to_all(sent, ('dx', 'dy'), 0, 0, tiled=True)]
  transfers between devices with their start and end apart: 19 -> 19, of which waited for: 7 -> 6; matrix products, arithmetic and copies ran while one was open for 1% -> 1% of each run, Pallas kernels for 2% -> 2%
where the time goes in v7:
time: 168 us; the launch traced here: 167 us
  starting transfers between devices  77.9 us (46%)
  blocking collectives  37.1 us (22%)
  waiting for transfers between devices  33.9 us (20%)
  Pallas kernels  8.63 us (5%)
  local copies, waits for them, and re-layouts  4.27 us (3%)
  matrix products  3.8 us (2%)
    ppermute x16, starting transfers between devices, swapped(): lax.ppermute(values, axis, [(i, (i + step(i)) % count) for i in range(cou...  64.8 us
    all_to_all x2, blocking collectives, sum_over_grid(): lax.all_to_all(sent, axis, 0, 0).astype(jnp.float32)  37.1 us
    all_to_all x1, waiting for transfers between devices, sum_at_once(): got = lax.all_to_all(sent, ('dx', 'dy'), 0, 0, tiled=True)  19.6 us
    ppermute x2, waiting for transfers between devices, other_band(): return lax.ppermute(values, 'band', [(0, 1), (1, 0)])  13.4 us
    all_to_all x1, starting transfers between devices, sum_at_once(): got = lax.all_to_all(sent, ('dx', 'dy'), 0, 0, tiled=True)  8.52 us
    ppermute x2, starting transfers between devices, other_band(): return lax.ppermute(values, 'band', [(0, 1), (1, 0)])  4.54 us
    pallas_call x4, Pallas kernels, filter_step(): pl.pallas_call(functools.partial(outer_kernel, 1.0 if previous is None el...  4.41 us
  transfers between devices with their start and end apart: 19, of which 6 were waited for; matrix products, arithmetic and copies ran while one was open for 1% of the time, Pallas kernels for 2%

profile of v7, /device:TPU:1, one launch (start us, length us, event | category | flops | bytes accessed | tf_op | source)
XLA Modules:
  0.0 167.0 jit_solution(8323481736559373994)
XLA Ops:
  0.7 1.0 copy-done
  2.6 6.0 %collective-permute-start = (bf16[672,128]{1,0:T(8,128)(2,1)S(1)}, bf16[672,128]{1,0:T(8,128)(2,1)S(1)}, u32[]{:S(2)}, u32[]{:S(2)}) collective-permute-start(bf16[672,128]{1,0:T(8,128)(2,1)S(1)} %get-tuple-element.29), channel_id=1, source_target_pairs={{0,15},{1,2},{2,1},{3,4},{4,3},{5,6},{6,5},{7,8},{8,7},{9,10},{10,... | collective-permute-start | bytes 516104 | tf_op jit(solution)/shard_map/ppermute | solution.py:253
  8.6 3.5 %collective-permute-start.1 = (bf16[672,128]{1,0:T(8,128)(2,1)S(1)}, bf16[672,128]{1,0:T(8,128)(2,1)S(1)}, u32[]{:S(2)}, u32[]{:S(2)}) collective-permute-start(bf16[672,128]{1,0:T(8,128)(2,1)S(1)} %get-tuple-element.30), channel_id=1, source_target_pairs={{0,16},{16,0},{32,48},{48,32},{64,80},{80,64},{96,112},{112,96},{1... | collective-permute-start | bytes 516104 | tf_op jit(solution)/shard_map/ppermute | solution.py:253
  12.2 10.2 %collective-permute-start.2 = (bf16[672,128]{1,0:T(8,128)(2,1)S(1)}, bf16[672,128]{1,0:T(8,128)(2,1)S(1)}, u32[]{:S(2)}, u32[]{:S(2)}) collective-permute-start(bf16[672,128]{1,0:T(8,128)(2,1)S(1)} %get-tuple-element.31), channel_id=1, source_target_pairs={{0,240},{16,32},{32,16},{48,64},{64,48},{80,96},{96,80},{112,128},... | collective-permute-start | bytes 516104 | tf_op jit(solution)/shard_map/ppermute | solution.py:253
  22.4 4.8 %collective-permute-start.3 = (bf16[672,128]{1,0:T(8,128)(2,1)S(1)}, bf16[672,128]{1,0:T(8,128)(2,1)S(1)}, u32[]{:S(2)}, u32[]{:S(2)}) collective-permute-start(bf16[672,128]{1,0:T(8,128)(2,1)S(1)} %get-tuple-element.32), channel_id=1, source_target_pairs={{0,1},{1,0},{2,3},{3,2},{4,5},{5,4},{6,7},{7,6},{8,9},{9,8},{10,11... | collective-permute-start | bytes 516104 | tf_op jit(solution)/shard_map/ppermute | solution.py:253
  28.9 1.1 shard_map.53
  30.0 1.9 %collective-permute-start.4 = (bf16[672,128]{1,0:T(8,128)(2,1)S(1)}, bf16[672,128]{1,0:T(8,128)(2,1)S(1)}, u32[]{:S(2)}, u32[]{:S(2)}) collective-permute-start(bf16[672,128]{1,0:T(8,128)(2,1)S(1)} %get-tuple-element.34), channel_id=1, source_target_pairs={{0,15},{1,2},{2,1},{3,4},{4,3},{5,6},{6,5},{7,8},{8,7},{9,10},{10,... | collective-permute-start | bytes 516104 | tf_op jit(solution)/shard_map/ppermute | solution.py:253
  31.9 1.9 %collective-permute-start.5 = (bf16[672,128]{1,0:T(8,128)(2,1)S(1)}, bf16[672,128]{1,0:T(8,128)(2,1)S(1)}, u32[]{:S(2)}, u32[]{:S(2)}) collective-permute-start(bf16[672,128]{1,0:T(8,128)(2,1)S(1)} %get-tuple-element.35), channel_id=1, source_target_pairs={{0,16},{16,0},{32,48},{48,32},{64,80},{80,64},{96,112},{112,96},{1... | collective-permute-start | bytes 516104 | tf_op jit(solution)/shard_map/ppermute | solution.py:253
  33.9 3.9 %collective-permute-start.6 = (bf16[672,128]{1,0:T(8,128)(2,1)S(1)}, bf16[672,128]{1,0:T(8,128)(2,1)S(1)}, u32[]{:S(2)}, u32[]{:S(2)}) collective-permute-start(bf16[672,128]{1,0:T(8,128)(2,1)S(1)} %get-tuple-element.36), channel_id=1, source_target_pairs={{0,240},{16,32},{32,16},{48,64},{64,48},{80,96},{96,80},{112,128},... | collective-permute-start | bytes 516104 | tf_op jit(solution)/shard_map/ppermute | solution.py:253
  37.7 3.1 %collective-permute-start.7 = (bf16[672,128]{1,0:T(8,128)(2,1)S(1)}, bf16[672,128]{1,0:T(8,128)(2,1)S(1)}, u32[]{:S(2)}, u32[]{:S(2)}) collective-permute-start(bf16[672,128]{1,0:T(8,128)(2,1)S(1)} %get-tuple-element.37), channel_id=1, source_target_pairs={{0,1},{1,0},{2,3},{3,2},{4,5},{5,4},{6,7},{7,6},{8,9},{9,8},{10,11... | collective-permute-start | bytes 516104 | tf_op jit(solution)/shard_map/ppermute | solution.py:253
  42.2 1.1 shard_map.55
  43.4 6.3 %collective-permute-start.8 = (bf16[672,128]{1,0:T(8,128)(2,1)S(1)}, bf16[672,128]{1,0:T(8,128)(2,1)S(1)}, u32[]{:S(2)}, u32[]{:S(2)}) collective-permute-start(bf16[672,128]{1,0:T(8,128)(2,1)S(1)} %get-tuple-element.39), channel_id=1, source_target_pairs={{0,15},{1,2},{2,1},{3,4},{4,3},{5,6},{6,5},{7,8},{8,7},{9,10},{10,... | collective-permute-start | bytes 516104 | tf_op jit(solution)/shard_map/ppermute | solution.py:253
  49.7 2.2 %collective-permute-start.9 = (bf16[672,128]{1,0:T(8,128)(2,1)S(1)}, bf16[672,128]{1,0:T(8,128)(2,1)S(1)}, u32[]{:S(2)}, u32[]{:S(2)}) collective-permute-start(bf16[672,128]{1,0:T(8,128)(2,1)S(1)} %get-tuple-element.40), channel_id=1, source_target_pairs={{0,16},{16,0},{32,48},{48,32},{64,80},{80,64},{96,112},{112,96},{1... | collective-permute-start | bytes 516104 | tf_op jit(solution)/shard_map/ppermute | solution.py:253
  51.8 4.3 %collective-permute-start.10 = (bf16[672,128]{1,0:T(8,128)(2,1)S(1)}, bf16[672,128]{1,0:T(8,128)(2,1)S(1)}, u32[]{:S(2)}, u32[]{:S(2)}) collective-permute-start(bf16[672,128]{1,0:T(8,128)(2,1)S(1)} %get-tuple-element.41), channel_id=1, source_target_pairs={{0,240},{16,32},{32,16},{48,64},{64,48},{80,96},{96,80},{112,128},... | collective-permute-start | bytes 516104 | tf_op jit(solution)/shard_map/ppermute | solution.py:253
  56.2 4.1 %collective-permute-start.11 = (bf16[672,128]{1,0:T(8,128)(2,1)S(1)}, bf16[672,128]{1,0:T(8,128)(2,1)S(1)}, u32[]{:S(2)}, u32[]{:S(2)}) collective-permute-start(bf16[672,128]{1,0:T(8,128)(2,1)S(1)} %get-tuple-element.42), channel_id=1, source_target_pairs={{0,1},{1,0},{2,3},{3,2},{4,5},{5,4},{6,7},{7,6},{8,9},{9,8},{10,11... | collective-permute-start | bytes 516104 | tf_op jit(solution)/shard_map/ppermute | solution.py:253
  61.3 1.1 shard_map.57
  62.4 2.8 %collective-permute-start.12 = (bf16[672,128]{1,0:T(8,128)(2,1)S(1)}, bf16[672,128]{1,0:T(8,128)(2,1)S(1)}, u32[]{:S(2)}, u32[]{:S(2)}) collective-permute-start(bf16[672,128]{1,0:T(8,128)(2,1)S(1)} %get-tuple-element.44), channel_id=1, source_target_pairs={{0,15},{1,2},{2,1},{3,4},{4,3},{5,6},{6,5},{7,8},{8,7},{9,10},{10,... | collective-permute-start | bytes 516104 | tf_op jit(solution)/shard_map/ppermute | solution.py:253
  65.2 1.9 %collective-permute-start.13 = (bf16[672,128]{1,0:T(8,128)(2,1)S(1)}, bf16[672,128]{1,0:T(8,128)(2,1)S(1)}, u32[]{:S(2)}, u32[]{:S(2)}) collective-permute-start(bf16[672,128]{1,0:T(8,128)(2,1)S(1)} %get-tuple-element.45), channel_id=1, source_target_pairs={{0,16},{16,0},{32,48},{48,32},{64,80},{80,64},{96,112},{112,96},{1... | collective-permute-start | bytes 516104 | tf_op jit(solution)/shard_map/ppermute | solution.py:253
  67.2 4.6 %collective-permute-start.14 = (bf16[672,128]{1,0:T(8,128)(2,1)S(1)}, bf16[672,128]{1,0:T(8,128)(2,1)S(1)}, u32[]{:S(2)}, u32[]{:S(2)}) collective-permute-start(bf16[672,128]{1,0:T(8,128)(2,1)S(1)} %get-tuple-element.46), channel_id=1, source_target_pairs={{0,240},{16,32},{32,16},{48,64},{64,48},{80,96},{96,80},{112,128},... | collective-permute-start | bytes 516104 | tf_op jit(solution)/shard_map/ppermute | solution.py:253
  71.8 3.3 %collective-permute-start.15 = (bf16[672,128]{1,0:T(8,128)(2,1)S(1)}, bf16[672,128]{1,0:T(8,128)(2,1)S(1)}, u32[]{:S(2)}, u32[]{:S(2)}) collective-permute-start(bf16[672,128]{1,0:T(8,128)(2,1)S(1)} %get-tuple-element.47), channel_id=1, source_target_pairs={{0,1},{1,0},{2,3},{3,2},{4,5},{5,4},{6,7},{7,6},{8,9},{9,8},{10,11... | collective-permute-start | bytes 516104 | tf_op jit(solution)/shard_map/ppermute | solution.py:253
  76.1 1.0 shard_map.59
  77.1 2.3 %collective-permute-start.16 = (bf16[8,12288]{1,0:T(8,128)(2,1)S(1)}, bf16[8,12288]{1,0:T(8,128)(2,1)S(1)}, u32[]{:S(2)}, u32[]{:S(2)}) collective-permute-start(bf16[8,12288]{1,0:T(8,128)(2,1)S(1)} %convert_element_type.33), channel_id=1, source_target_pairs={{0,256},{256,0},{1,257},{257,1},{2,258},{258,2},{3,259},{259,3},{4... | collective-permute-start | bytes 589832 | tf_op jit(solution)/shard_map/ppermute | solution.py:280
  79.5 0.9 fusion.4
  80.4 3.5 %collective-permute-done.16 = bf16[8,12288]{1,0:T(8,128)(2,1)S(1)} collective-permute-done((bf16[8,12288]{1,0:T(8,128)(2,1)S(1)}, bf16[8,12288]{1,0:T(8,128)(2,1)S(1)}, u32[]{:S(2)}, u32[]{:S(2)}) %collective-permute-start.16) | collective-permute-done | bytes 196640 | tf_op jit(solution)/shard_map/ppermute | solution.py:280
  84.9 18.4 %all_to_all.15 = f16[16,16,128]{2,1,0:T(8,128)(2,1)S(1)} all-to-all(f16[16,16,128]{2,1,0:T(8,128)(2,1)S(1)} %broadcast_in_dim.8), channel_id=1, replica_groups=mesh['band'=2,'dx'=16,'dy'=16] {'dx'}, dimensions={0} | all-to-all | bytes 131072 | tf_op jit(solution)/shard_map/all_to_all | solution.py:267
  103.4 18.7 %all_to_all.16 = f16[16,16,128]{2,1,0:T(8,128)(2,1)S(1)} all-to-all(f16[16,16,128]{2,1,0:T(8,128)(2,1)S(1)} %broadcast_in_dim.9), channel_id=1, replica_groups=mesh['band'=2,'dx'=16,'dy'=16] {'dy'}, dimensions={0} | all-to-all | bytes 131072 | tf_op jit(solution)/shard_map/all_to_all | solution.py:267
  122.1 1.0 fusion
  123.1 2.2 %collective-permute-start.17 = (bf16[16,12288]{1,0:T(8,128)(2,1)S(1)}, bf16[16,12288]{1,0:T(8,128)(2,1)S(1)}, u32[]{:S(2)}, u32[]{:S(2)}) collective-permute-start(bf16[16,12288]{1,0:T(8,128)(2,1)S(1)} %pad_maximum_fusion), channel_id=1, source_target_pairs={{0,256},{256,0},{1,257},{257,1},{2,258},{258,2},{3,259},{259,3},{4... | collective-permute-start | bytes 1179656 | tf_op jit(solution)/shard_map/ppermute | solution.py:280
  125.4 9.9 %collective-permute-done.17 = bf16[16,12288]{1,0:T(8,128)(2,1)S(1)} collective-permute-done((bf16[16,12288]{1,0:T(8,128)(2,1)S(1)}, bf16[16,12288]{1,0:T(8,128)(2,1)S(1)}, u32[]{:S(2)}, u32[]{:S(2)}) %collective-permute-start.17) | collective-permute-done | bytes 393248 | tf_op jit(solution)/shard_map/ppermute | solution.py:280
  135.4 1.0 fusion.9
  137.4 8.5 %all-to-all-start.2 = ((f32[256,1,128]{2,1,0:T(1,128)}), f32[256,1,128]{2,1,0:T(1,128)S(1)}, u32[]{:S(2)}, u32[]{:S(2)}) async-start(f32[256,1,128]{2,1,0:T(1,128)} %broadcast_in_dim.22), calls=%async_computation.2 | async-start | bytes 262144 | tf_op jit(solution)/shard_map/all_to_all | solution.py:275
  146.7 19.6 %all-to-all-done.2 = f32[256,1,128]{2,1,0:T(1,128)S(1)} async-done(((f32[256,1,128]{2,1,0:T(1,128)}), f32[256,1,128]{2,1,0:T(1,128)S(1)}, u32[]{:S(2)}, u32[]{:S(2)}) %all-to-all-start.2) | async-done | bytes 131104 | tf_op jit(solution)/shard_map/all_to_all | solution.py:275
  (48 shorter events, 9.8 us)
Async XLA Ops:
  0.7 1.0 copy-start
  2.6 26.3 %collective-permute-start = (bf16[672,128]{1,0:T(8,128)(2,1)S(1)}, bf16[672,128]{1,0:T(8,128)(2,1)S(1)}, u32[]{:S(2)}, u32[]{:S(2)}) collective-permute-start(bf16[672,128]{1,0:T(8,128)(2,1)S(1)} %get-tuple-element.29), channel_id=1, source_target_pairs={{0,15},{1,2},{2,1},{3,4},{4,3},{5,6},{6,5},{7,8},{8,7},{9,10},{10,... | collective-permute-start | bytes 516104 | tf_op jit(solution)/shard_map/ppermute | solution.py:253
  8.6 20.2 %collective-permute-start.1 = (bf16[672,128]{1,0:T(8,128)(2,1)S(1)}, bf16[672,128]{1,0:T(8,128)(2,1)S(1)}, u32[]{:S(2)}, u32[]{:S(2)}) collective-permute-start(bf16[672,128]{1,0:T(8,128)(2,1)S(1)} %get-tuple-element.30), channel_id=1, source_target_pairs={{0,16},{16,0},{32,48},{48,32},{64,80},{80,64},{96,112},{112,96},{1... | collective-permute-start | bytes 516104 | tf_op jit(solution)/shard_map/ppermute | solution.py:253
  12.2 16.7 %collective-permute-start.2 = (bf16[672,128]{1,0:T(8,128)(2,1)S(1)}, bf16[672,128]{1,0:T(8,128)(2,1)S(1)}, u32[]{:S(2)}, u32[]{:S(2)}) collective-permute-start(bf16[672,128]{1,0:T(8,128)(2,1)S(1)} %get-tuple-element.31), channel_id=1, source_target_pairs={{0,240},{16,32},{32,16},{48,64},{64,48},{80,96},{96,80},{112,128},... | collective-permute-start | bytes 516104 | tf_op jit(solution)/shard_map/ppermute | solution.py:253
  22.4 6.5 %collective-permute-start.3 = (bf16[672,128]{1,0:T(8,128)(2,1)S(1)}, bf16[672,128]{1,0:T(8,128)(2,1)S(1)}, u32[]{:S(2)}, u32[]{:S(2)}) collective-permute-start(bf16[672,128]{1,0:T(8,128)(2,1)S(1)} %get-tuple-element.32), channel_id=1, source_target_pairs={{0,1},{1,0},{2,3},{3,2},{4,5},{5,4},{6,7},{7,6},{8,9},{9,8},{10,11... | collective-permute-start | bytes 516104 | tf_op jit(solution)/shard_map/ppermute | solution.py:253
  27.2 0.8 copy-start.1
  30.0 11.7 %collective-permute-start.4 = (bf16[672,128]{1,0:T(8,128)(2,1)S(1)}, bf16[672,128]{1,0:T(8,128)(2,1)S(1)}, u32[]{:S(2)}, u32[]{:S(2)}) collective-permute-start(bf16[672,128]{1,0:T(8,128)(2,1)S(1)} %get-tuple-element.34), channel_id=1, source_target_pairs={{0,15},{1,2},{2,1},{3,4},{4,3},{5,6},{6,5},{7,8},{8,7},{9,10},{10,... | collective-permute-start | bytes 516104 | tf_op jit(solution)/shard_map/ppermute | solution.py:253
  31.9 9.7 %collective-permute-start.5 = (bf16[672,128]{1,0:T(8,128)(2,1)S(1)}, bf16[672,128]{1,0:T(8,128)(2,1)S(1)}, u32[]{:S(2)}, u32[]{:S(2)}) collective-permute-start(bf16[672,128]{1,0:T(8,128)(2,1)S(1)} %get-tuple-element.35), channel_id=1, source_target_pairs={{0,16},{16,0},{32,48},{48,32},{64,80},{80,64},{96,112},{112,96},{1... | collective-permute-start | bytes 516104 | tf_op jit(solution)/shard_map/ppermute | solution.py:253
  33.9 8.3 %collective-permute-start.6 = (bf16[672,128]{1,0:T(8,128)(2,1)S(1)}, bf16[672,128]{1,0:T(8,128)(2,1)S(1)}, u32[]{:S(2)}, u32[]{:S(2)}) collective-permute-start(bf16[672,128]{1,0:T(8,128)(2,1)S(1)} %get-tuple-element.36), channel_id=1, source_target_pairs={{0,240},{16,32},{32,16},{48,64},{64,48},{80,96},{96,80},{112,128},... | collective-permute-start | bytes 516104 | tf_op jit(solution)/shard_map/ppermute | solution.py:253
  37.7 4.5 %collective-permute-start.7 = (bf16[672,128]{1,0:T(8,128)(2,1)S(1)}, bf16[672,128]{1,0:T(8,128)(2,1)S(1)}, u32[]{:S(2)}, u32[]{:S(2)}) collective-permute-start(bf16[672,128]{1,0:T(8,128)(2,1)S(1)} %get-tuple-element.37), channel_id=1, source_target_pairs={{0,1},{1,0},{2,3},{3,2},{4,5},{5,4},{6,7},{7,6},{8,9},{9,8},{10,11... | collective-permute-start | bytes 516104 | tf_op jit(solution)/shard_map/ppermute | solution.py:253
  43.4 36.1 %copy-start.2 = (bf16[128,12,8,128]{3,2,1,0:T(8,128)(2,1)S(1)}, bf16[128,12,8,128]{3,2,1,0:T(8,128)(2,1)}, u32[]{:S(2)}) copy-start(bf16[128,12,8,128]{3,2,1,0:T(8,128)(2,1)} %param.5) | copy-start | bytes 9437188
  43.4 17.8 %collective-permute-start.8 = (bf16[672,128]{1,0:T(8,128)(2,1)S(1)}, bf16[672,128]{1,0:T(8,128)(2,1)S(1)}, u32[]{:S(2)}, u32[]{:S(2)}) collective-permute-start(bf16[672,128]{1,0:T(8,128)(2,1)S(1)} %get-tuple-element.39), channel_id=1, source_target_pairs={{0,15},{1,2},{2,1},{3,4},{4,3},{5,6},{6,5},{7,8},{8,7},{9,10},{10,... | collective-permute-start | bytes 516104 | tf_op jit(solution)/shard_map/ppermute | solution.py:253
  49.7 11.5 %collective-permute-start.9 = (bf16[672,128]{1,0:T(8,128)(2,1)S(1)}, bf16[672,128]{1,0:T(8,128)(2,1)S(1)}, u32[]{:S(2)}, u32[]{:S(2)}) collective-permute-start(bf16[672,128]{1,0:T(8,128)(2,1)S(1)} %get-tuple-element.40), channel_id=1, source_target_pairs={{0,16},{16,0},{32,48},{48,32},{64,80},{80,64},{96,112},{112,96},{1... | collective-permute-start | bytes 516104 | tf_op jit(solution)/shard_map/ppermute | solution.py:253
  51.8 9.3 %collective-permute-start.10 = (bf16[672,128]{1,0:T(8,128)(2,1)S(1)}, bf16[672,128]{1,0:T(8,128)(2,1)S(1)}, u32[]{:S(2)}, u32[]{:S(2)}) collective-permute-start(bf16[672,128]{1,0:T(8,128)(2,1)S(1)} %get-tuple-element.41), channel_id=1, source_target_pairs={{0,240},{16,32},{32,16},{48,64},{64,48},{80,96},{96,80},{112,128},... | collective-permute-start | bytes 516104 | tf_op jit(solution)/shard_map/ppermute | solution.py:253
  56.2 5.1 %collective-permute-start.11 = (bf16[672,128]{1,0:T(8,128)(2,1)S(1)}, bf16[672,128]{1,0:T(8,128)(2,1)S(1)}, u32[]{:S(2)}, u32[]{:S(2)}) collective-permute-start(bf16[672,128]{1,0:T(8,128)(2,1)S(1)} %get-tuple-element.42), channel_id=1, source_target_pairs={{0,1},{1,0},{2,3},{3,2},{4,5},{5,4},{6,7},{7,6},{8,9},{9,8},{10,11... | collective-permute-start | bytes 516104 | tf_op jit(solution)/shard_map/ppermute | solution.py:253
  62.4 13.5 %collective-permute-start.12 = (bf16[672,128]{1,0:T(8,128)(2,1)S(1)}, bf16[672,128]{1,0:T(8,128)(2,1)S(1)}, u32[]{:S(2)}, u32[]{:S(2)}) collective-permute-start(bf16[672,128]{1,0:T(8,128)(2,1)S(1)} %get-tuple-element.44), channel_id=1, source_target_pairs={{0,15},{1,2},{2,1},{3,4},{4,3},{5,6},{6,5},{7,8},{8,7},{9,10},{10,... | collective-permute-start | bytes 516104 | tf_op jit(solution)/shard_map/ppermute | solution.py:253
  65.2 10.7 %collective-permute-start.13 = (bf16[672,128]{1,0:T(8,128)(2,1)S(1)}, bf16[672,128]{1,0:T(8,128)(2,1)S(1)}, u32[]{:S(2)}, u32[]{:S(2)}) collective-permute-start(bf16[672,128]{1,0:T(8,128)(2,1)S(1)} %get-tuple-element.45), channel_id=1, source_target_pairs={{0,16},{16,0},{32,48},{48,32},{64,80},{80,64},{96,112},{112,96},{1... | collective-permute-start | bytes 516104 | tf_op jit(solution)/shard_map/ppermute | solution.py:253
  67.2 8.8 %collective-permute-start.14 = (bf16[672,128]{1,0:T(8,128)(2,1)S(1)}, bf16[672,128]{1,0:T(8,128)(2,1)S(1)}, u32[]{:S(2)}, u32[]{:S(2)}) collective-permute-start(bf16[672,128]{1,0:T(8,128)(2,1)S(1)} %get-tuple-element.46), channel_id=1, source_target_pairs={{0,240},{16,32},{32,16},{48,64},{64,48},{80,96},{96,80},{112,128},... | collective-permute-start | bytes 516104 | tf_op jit(solution)/shard_map/ppermute | solution.py:253
  71.8 4.3 %collective-permute-start.15 = (bf16[672,128]{1,0:T(8,128)(2,1)S(1)}, bf16[672,128]{1,0:T(8,128)(2,1)S(1)}, u32[]{:S(2)}, u32[]{:S(2)}) collective-permute-start(bf16[672,128]{1,0:T(8,128)(2,1)S(1)} %get-tuple-element.47), channel_id=1, source_target_pairs={{0,1},{1,0},{2,3},{3,2},{4,5},{5,4},{6,7},{7,6},{8,9},{9,8},{10,11... | collective-permute-start | bytes 516104 | tf_op jit(solution)/shard_map/ppermute | solution.py:253
  77.1 6.8 %collective-permute-start.16 = (bf16[8,12288]{1,0:T(8,128)(2,1)S(1)}, bf16[8,12288]{1,0:T(8,128)(2,1)S(1)}, u32[]{:S(2)}, u32[]{:S(2)}) collective-permute-start(bf16[8,12288]{1,0:T(8,128)(2,1)S(1)} %convert_element_type.33), channel_id=1, source_target_pairs={{0,256},{256,0},{1,257},{257,1},{2,258},{258,2},{3,259},{259,3},{4... | collective-permute-start | bytes 589832 | tf_op jit(solution)/shard_map/ppermute | solution.py:280
  123.1 12.1 %collective-permute-start.17 = (bf16[16,12288]{1,0:T(8,128)(2,1)S(1)}, bf16[16,12288]{1,0:T(8,128)(2,1)S(1)}, u32[]{:S(2)}, u32[]{:S(2)}) collective-permute-start(bf16[16,12288]{1,0:T(8,128)(2,1)S(1)} %pad_maximum_fusion), channel_id=1, source_target_pairs={{0,256},{256,0},{1,257},{257,1},{2,258},{258,2},{3,259},{259,3},{4... | collective-permute-start | bytes 1179656 | tf_op jit(solution)/shard_map/ppermute | solution.py:280
  137.4 28.9 %all-to-all-start.2 = ((f32[256,1,128]{2,1,0:T(1,128)}), f32[256,1,128]{2,1,0:T(1,128)S(1)}, u32[]{:S(2)}, u32[]{:S(2)}) async-start(f32[256,1,128]{2,1,0:T(1,128)} %broadcast_in_dim.22), calls=%async_computation.2 | async-start | bytes 262144 | tf_op jit(solution)/shard_map/all_to_all | solution.py:275

commit v8 on v7

--- a/solution.py
+++ b/solution.py
@@ -44,8 +44,10 @@
             for at in range(WIDTH):
                 pack_layer(out_ref, at, layer(dim, tail * (size - WIDTH) + at))
             nearest = layer(dim, tail * (size - 1))
+            used = SENT * nearest.shape[0] * nearest.shape[1]
+            if used > out_ref.shape[0]:
+                continue
             pack_layer(out_ref, WIDTH, nearest - nearest.astype(jnp.bfloat16).astype(jnp.float32))
-            used = SENT * nearest.shape[0] * nearest.shape[1]
             if used < out_ref.shape[0]:
                 rows = out_ref.shape[0] - used
                 out_ref[used:, :] = jnp.zeros((rows, out_ref.shape[1]), jnp.bfloat16)
@@ -66,6 +68,8 @@
                     halo[place] = read(at)
                 else:
                     halo[:, place] = read(at)
+            if got.shape[0] < SENT * rows:
+                continue
             if dim == 0:
                 halo[near] += read(WIDTH)
             else:
@@ -172,8 +176,9 @@
 
 
 def message_shapes(size_x, size_y, own, depth):
-    rows = SENT * max(size_x, size_y) * own
-    return [jax.ShapeDtypeStruct((rows, depth), jnp.bfloat16)] * 4
+    short = max(WIDTH * size_x, SENT * size_y) * own
+    sizes = (SENT * size_x * own, short, short, WIDTH * size_x * own)
+    return [jax.ShapeDtypeStruct((rows, depth), jnp.bfloat16) for rows in sizes]
 
 
 def params():
@@ -268,14 +273,6 @@
     return values
 
 
-def sum_at_once(values):
-    count = lax.axis_size("dx") * lax.axis_size("dy")
-    flat = values.reshape(1, 1, values.size)
-    sent = jnp.broadcast_to(flat, (count, 1, values.size))
-    got = lax.all_to_all(sent, ("dx", "dy"), 0, 0, tiled=True)
-    return jnp.sum(got, axis=0).reshape(values.shape)
-
-
 def other_band(values):
     return lax.ppermute(values, "band", [(0, 1), (1, 0)])
 
@@ -312,16 +309,18 @@
     correlations = (sum_over_grid(local, jnp.float16) / SENT_SCALE).astype(jnp.bfloat16)
     correction = jnp.dot(correlations, own_resident, preferred_element_type=jnp.float32)
     mine, theirs = correction[:own_count], correction[own_count:]
-    sent = jnp.concatenate([theirs, mine], axis=0).astype(jnp.bfloat16)
-    got = other_band(sent).astype(jnp.float32)
-    projected = filtered - mine - got[:own_count]
-    projected_other = rounded_other.astype(jnp.float32) - theirs - got[own_count:]
+    got = other_band(theirs.astype(jnp.bfloat16)).astype(jnp.float32)
+    got_other = other_band(mine.astype(jnp.bfloat16)).astype(jnp.float32)
+    projected = filtered - mine - got
+    projected_other = rounded_other.astype(jnp.float32) - theirs - got_other
     exact = functools.partial(rows_dot, precision=lax.Precision.HIGHEST)
     partial_gram = exact(projected, jnp.concatenate([projected, projected_other], axis=0))
     turned = jnp.roll(partial_gram, own_count, axis=1)
     partial_gram = jnp.where(lax.axis_index("band") == 0, partial_gram, turned)
+    lanes = 128
+    partial_gram = jnp.pad(partial_gram, ((0, 0), (0, lanes - 2 * own_count)))
     total_cells = cell_count * lax.axis_size("dx") * lax.axis_size("dy")
-    gram_matrix = sum_at_once(partial_gram) / total_cells
+    gram_matrix = sum_over_grid(partial_gram, jnp.float32)[:, : 2 * own_count] / total_cells
     return (projected.reshape(orbital_block.shape), gram_matrix)
 
 

time: 168 us -> 163 us (0.970)
  waiting for transfers between devices: 33.9 us -> 17.5 us
  blocking collectives: 37.1 us -> 50.2 us
    all_to_all x2 -> x3, blocking collectives: 37.1 us -> 50.2 us  [sum_over_grid(): lax.all_to_all(sent, axis, 0, 0).astype(jnp.float32)]
    all_to_all x1, waiting for transfers between devices: 19.6 us -> 6.57 us  [sum_over_grid(): lax.all_to_all(sent, axis, 0, 0).astype(jnp.float32)]
    ppermute x2 -> x3, starting transfers between devices: 4.54 us -> 8.16 us  [other_band(): return lax.ppermute(values, 'band', [(0, 1), (1, 0)])]
    ppermute x2 -> x3, waiting for transfers between devices: 13.4 us -> 10.2 us  [other_band(): return lax.ppermute(values, 'band', [(0, 1), (1, 0)])]
    all_to_all x1, starting transfers between devices: 8.52 us -> 5.86 us  [sum_over_grid(): lax.all_to_all(sent, axis, 0, 0).astype(jnp.float32)]
    ppermute x16, starting transfers between devices: 64.8 us -> 63.1 us  [swapped(): lax.ppermute(values, axis, [(i, (i + step(i)) % count) for i in range(cou...]
  transfers between devices with their start and end apart: 19 -> 20, of which waited for: 6 -> 7; matrix products, arithmetic and copies ran while one was open for 1% -> 1% of each run, Pallas kernels for 2% -> 2%
where the time goes in v8:
time: 163 us
  starting transfers between devices  77.1 us (47%)
  blocking collectives  50.2 us (31%)
  waiting for transfers between devices  17.5 us (11%)
  Pallas kernels  8.57 us (5%)
  matrix products  3.8 us (2%)
  local copies, waits for them, and re-layouts  3.41 us (2%)
    ppermute x16, starting transfers between devices, swapped(): lax.ppermute(values, axis, [(i, (i + step(i)) % count) for i in range(cou...  63.1 us
    all_to_all x3, blocking collectives, sum_over_grid(): lax.all_to_all(sent, axis, 0, 0).astype(jnp.float32)  50.2 us
    ppermute x3, waiting for transfers between devices, other_band(): return lax.ppermute(values, 'band', [(0, 1), (1, 0)])  10.2 us
    ppermute x3, starting transfers between devices, other_band(): return lax.ppermute(values, 'band', [(0, 1), (1, 0)])  8.16 us
    all_to_all x1, waiting for transfers between devices, sum_over_grid(): lax.all_to_all(sent, axis, 0, 0).astype(jnp.float32)  6.57 us
    all_to_all x1, starting transfers between devices, sum_over_grid(): lax.all_to_all(sent, axis, 0, 0).astype(jnp.float32)  5.86 us
    pallas_call x4, Pallas kernels, filter_step(): pl.pallas_call(functools.partial(outer_kernel, 1.0 if previous is None el...  4.35 us
    pallas_call x4, Pallas kernels, filter_step(): pl.pallas_call(functools.partial(inner_kernel, previous is not None), out...  3.32 us
  transfers between devices with their start and end apart: 20, of which 7 were waited for; matrix products, arithmetic and copies ran while one was open for 1% of the time, Pallas kernels for 2%

profile of v8, /device:TPU:1, one launch (start us, length us, event | category | flops | bytes accessed | tf_op | source)
XLA Modules:
  0.0 162.6 jit_solution(12201198094093088311)
XLA Ops:
  0.7 1.0 copy-done
  2.6 6.0 %collective-permute-start = (bf16[672,128]{1,0:T(8,128)(2,1)S(1)}, bf16[672,128]{1,0:T(8,128)(2,1)S(1)}, u32[]{:S(2)}, u32[]{:S(2)}) collective-permute-start(bf16[672,128]{1,0:T(8,128)(2,1)S(1)} %get-tuple-element.29), channel_id=1, source_target_pairs={{0,15},{1,2},{2,1},{3,4},{4,3},{5,6},{6,5},{7,8},{8,7},{9,10},{10,... | collective-permute-start | bytes 516104 | tf_op jit(solution)/shard_map/ppermute | solution.py:258
  8.6 3.5 %collective-permute-start.1 = (bf16[576,128]{1,0:T(8,128)(2,1)S(1)}, bf16[576,128]{1,0:T(8,128)(2,1)S(1)}, u32[]{:S(2)}, u32[]{:S(2)}) collective-permute-start(bf16[576,128]{1,0:T(8,128)(2,1)S(1)} %get-tuple-element.30), channel_id=1, source_target_pairs={{0,16},{16,0},{32,48},{48,32},{64,80},{80,64},{96,112},{112,96},{1... | collective-permute-start | bytes 442376 | tf_op jit(solution)/shard_map/ppermute | solution.py:258
  12.2 10.2 %collective-permute-start.2 = (bf16[576,128]{1,0:T(8,128)(2,1)S(1)}, bf16[576,128]{1,0:T(8,128)(2,1)S(1)}, u32[]{:S(2)}, u32[]{:S(2)}) collective-permute-start(bf16[576,128]{1,0:T(8,128)(2,1)S(1)} %get-tuple-element.31), channel_id=1, source_target_pairs={{0,240},{16,32},{32,16},{48,64},{64,48},{80,96},{96,80},{112,128},... | collective-permute-start | bytes 442376 | tf_op jit(solution)/shard_map/ppermute | solution.py:258
  22.4 4.8 %collective-permute-start.3 = (bf16[576,128]{1,0:T(8,128)(2,1)S(1)}, bf16[576,128]{1,0:T(8,128)(2,1)S(1)}, u32[]{:S(2)}, u32[]{:S(2)}) collective-permute-start(bf16[576,128]{1,0:T(8,128)(2,1)S(1)} %get-tuple-element.32), channel_id=1, source_target_pairs={{0,1},{1,0},{2,3},{3,2},{4,5},{5,4},{6,7},{7,6},{8,9},{9,8},{10,11... | collective-permute-start | bytes 442376 | tf_op jit(solution)/shard_map/ppermute | solution.py:258
  28.9 1.1 shard_map.53
  30.0 1.9 %collective-permute-start.4 = (bf16[672,128]{1,0:T(8,128)(2,1)S(1)}, bf16[672,128]{1,0:T(8,128)(2,1)S(1)}, u32[]{:S(2)}, u32[]{:S(2)}) collective-permute-start(bf16[672,128]{1,0:T(8,128)(2,1)S(1)} %get-tuple-element.34), channel_id=1, source_target_pairs={{0,15},{1,2},{2,1},{3,4},{4,3},{5,6},{6,5},{7,8},{8,7},{9,10},{10,... | collective-permute-start | bytes 516104 | tf_op jit(solution)/shard_map/ppermute | solution.py:258
  31.9 1.9 %collective-permute-start.5 = (bf16[576,128]{1,0:T(8,128)(2,1)S(1)}, bf16[576,128]{1,0:T(8,128)(2,1)S(1)}, u32[]{:S(2)}, u32[]{:S(2)}) collective-permute-start(bf16[576,128]{1,0:T(8,128)(2,1)S(1)} %get-tuple-element.35), channel_id=1, source_target_pairs={{0,16},{16,0},{32,48},{48,32},{64,80},{80,64},{96,112},{112,96},{1... | collective-permute-start | bytes 442376 | tf_op jit(solution)/shard_map/ppermute | solution.py:258
  33.8 3.4 %collective-permute-start.6 = (bf16[576,128]{1,0:T(8,128)(2,1)S(1)}, bf16[576,128]{1,0:T(8,128)(2,1)S(1)}, u32[]{:S(2)}, u32[]{:S(2)}) collective-permute-start(bf16[576,128]{1,0:T(8,128)(2,1)S(1)} %get-tuple-element.36), channel_id=1, source_target_pairs={{0,240},{16,32},{32,16},{48,64},{64,48},{80,96},{96,80},{112,128},... | collective-permute-start | bytes 442376 | tf_op jit(solution)/shard_map/ppermute | solution.py:258
  37.2 3.2 %collective-permute-start.7 = (bf16[576,128]{1,0:T(8,128)(2,1)S(1)}, bf16[576,128]{1,0:T(8,128)(2,1)S(1)}, u32[]{:S(2)}, u32[]{:S(2)}) collective-permute-start(bf16[576,128]{1,0:T(8,128)(2,1)S(1)} %get-tuple-element.37), channel_id=1, source_target_pairs={{0,1},{1,0},{2,3},{3,2},{4,5},{5,4},{6,7},{7,6},{8,9},{9,8},{10,11... | collective-permute-start | bytes 442376 | tf_op jit(solution)/shard_map/ppermute | solution.py:258
  41.7 1.1 shard_map.55
  42.8 5.6 %collective-permute-start.8 = (bf16[672,128]{1,0:T(8,128)(2,1)S(1)}, bf16[672,128]{1,0:T(8,128)(2,1)S(1)}, u32[]{:S(2)}, u32[]{:S(2)}) collective-permute-start(bf16[672,128]{1,0:T(8,128)(2,1)S(1)} %get-tuple-element.39), channel_id=1, source_target_pairs={{0,15},{1,2},{2,1},{3,4},{4,3},{5,6},{6,5},{7,8},{8,7},{9,10},{10,... | collective-permute-start | bytes 516104 | tf_op jit(solution)/shard_map/ppermute | solution.py:258
  48.4 2.4 %collective-permute-start.9 = (bf16[576,128]{1,0:T(8,128)(2,1)S(1)}, bf16[576,128]{1,0:T(8,128)(2,1)S(1)}, u32[]{:S(2)}, u32[]{:S(2)}) collective-permute-start(bf16[576,128]{1,0:T(8,128)(2,1)S(1)} %get-tuple-element.40), channel_id=1, source_target_pairs={{0,16},{16,0},{32,48},{48,32},{64,80},{80,64},{96,112},{112,96},{1... | collective-permute-start | bytes 442376 | tf_op jit(solution)/shard_map/ppermute | solution.py:258
  50.8 4.2 %collective-permute-start.10 = (bf16[576,128]{1,0:T(8,128)(2,1)S(1)}, bf16[576,128]{1,0:T(8,128)(2,1)S(1)}, u32[]{:S(2)}, u32[]{:S(2)}) collective-permute-start(bf16[576,128]{1,0:T(8,128)(2,1)S(1)} %get-tuple-element.41), channel_id=1, source_target_pairs={{0,240},{16,32},{32,16},{48,64},{64,48},{80,96},{96,80},{112,128},... | collective-permute-start | bytes 442376 | tf_op jit(solution)/shard_map/ppermute | solution.py:258
  55.0 3.9 %collective-permute-start.11 = (bf16[576,128]{1,0:T(8,128)(2,1)S(1)}, bf16[576,128]{1,0:T(8,128)(2,1)S(1)}, u32[]{:S(2)}, u32[]{:S(2)}) collective-permute-start(bf16[576,128]{1,0:T(8,128)(2,1)S(1)} %get-tuple-element.42), channel_id=1, source_target_pairs={{0,1},{1,0},{2,3},{3,2},{4,5},{5,4},{6,7},{7,6},{8,9},{9,8},{10,11... | collective-permute-start | bytes 442376 | tf_op jit(solution)/shard_map/ppermute | solution.py:258
  59.9 1.1 shard_map.57
  61.0 2.3 %collective-permute-start.12 = (bf16[672,128]{1,0:T(8,128)(2,1)S(1)}, bf16[672,128]{1,0:T(8,128)(2,1)S(1)}, u32[]{:S(2)}, u32[]{:S(2)}) collective-permute-start(bf16[672,128]{1,0:T(8,128)(2,1)S(1)} %get-tuple-element.44), channel_id=1, source_target_pairs={{0,15},{1,2},{2,1},{3,4},{4,3},{5,6},{6,5},{7,8},{8,7},{9,10},{10,... | collective-permute-start | bytes 516104 | tf_op jit(solution)/shard_map/ppermute | solution.py:258
  63.4 1.9 %collective-permute-start.13 = (bf16[576,128]{1,0:T(8,128)(2,1)S(1)}, bf16[576,128]{1,0:T(8,128)(2,1)S(1)}, u32[]{:S(2)}, u32[]{:S(2)}) collective-permute-start(bf16[576,128]{1,0:T(8,128)(2,1)S(1)} %get-tuple-element.45), channel_id=1, source_target_pairs={{0,16},{16,0},{32,48},{48,32},{64,80},{80,64},{96,112},{112,96},{1... | collective-permute-start | bytes 442376 | tf_op jit(solution)/shard_map/ppermute | solution.py:258
  65.3 4.6 %collective-permute-start.14 = (bf16[576,128]{1,0:T(8,128)(2,1)S(1)}, bf16[576,128]{1,0:T(8,128)(2,1)S(1)}, u32[]{:S(2)}, u32[]{:S(2)}) collective-permute-start(bf16[576,128]{1,0:T(8,128)(2,1)S(1)} %get-tuple-element.46), channel_id=1, source_target_pairs={{0,240},{16,32},{32,16},{48,64},{64,48},{80,96},{96,80},{112,128},... | collective-permute-start | bytes 442376 | tf_op jit(solution)/shard_map/ppermute | solution.py:258
  69.9 3.3 %collective-permute-start.15 = (bf16[576,128]{1,0:T(8,128)(2,1)S(1)}, bf16[576,128]{1,0:T(8,128)(2,1)S(1)}, u32[]{:S(2)}, u32[]{:S(2)}) collective-permute-start(bf16[576,128]{1,0:T(8,128)(2,1)S(1)} %get-tuple-element.47), channel_id=1, source_target_pairs={{0,1},{1,0},{2,3},{3,2},{4,5},{5,4},{6,7},{7,6},{8,9},{9,8},{10,11... | collective-permute-start | bytes 442376 | tf_op jit(solution)/shard_map/ppermute | solution.py:258
  74.1 1.0 shard_map.59
  75.2 2.9 %collective-permute-start.16 = (bf16[8,12288]{1,0:T(8,128)(2,1)S(1)}, bf16[8,12288]{1,0:T(8,128)(2,1)S(1)}, u32[]{:S(2)}, u32[]{:S(2)}) collective-permute-start(bf16[8,12288]{1,0:T(8,128)(2,1)S(1)} %convert_element_type.43), channel_id=1, source_target_pairs={{0,256},{256,0},{1,257},{257,1},{2,258},{258,2},{3,259},{259,3},{4... | collective-permute-start | bytes 589832 | tf_op jit(solution)/shard_map/ppermute | solution.py:277
  79.0 3.4 %collective-permute-done.16 = bf16[8,12288]{1,0:T(8,128)(2,1)S(1)} collective-permute-done((bf16[8,12288]{1,0:T(8,128)(2,1)S(1)}, bf16[8,12288]{1,0:T(8,128)(2,1)S(1)}, u32[]{:S(2)}, u32[]{:S(2)}) %collective-permute-start.16) | collective-permute-done | bytes 196640 | tf_op jit(solution)/shard_map/ppermute | solution.py:277
  83.4 18.2 %all_to_all.20 = f16[16,16,128]{2,1,0:T(8,128)(2,1)S(1)} all-to-all(f16[16,16,128]{2,1,0:T(8,128)(2,1)S(1)} %broadcast_in_dim.8), channel_id=1, replica_groups=mesh['band'=2,'dx'=16,'dy'=16] {'dx'}, dimensions={0} | all-to-all | bytes 131072 | tf_op jit(solution)/shard_map/all_to_all | solution.py:272
  101.6 17.8 %all_to_all.21 = f16[16,16,128]{2,1,0:T(8,128)(2,1)S(1)} all-to-all(f16[16,16,128]{2,1,0:T(8,128)(2,1)S(1)} %broadcast_in_dim.9), channel_id=1, replica_groups=mesh['band'=2,'dx'=16,'dy'=16] {'dy'}, dimensions={0} | all-to-all | bytes 131072 | tf_op jit(solution)/shard_map/all_to_all | solution.py:272
  120.5 2.2 %collective-permute-start.18 = (bf16[8,12288]{1,0:T(8,128)(2,1)S(1)}, bf16[8,12288]{1,0:T(8,128)(2,1)S(1)}, u32[]{:S(2)}, u32[]{:S(2)}) collective-permute-start(bf16[8,12288]{1,0:T(8,128)(2,1)S(1)} %get-tuple-element.54), channel_id=1, source_target_pairs={{0,256},{256,0},{1,257},{257,1},{2,258},{258,2},{3,259},{259,3},{4... | collective-permute-start | bytes 589832 | tf_op jit(solution)/shard_map/ppermute | solution.py:277
  122.7 3.1 %collective-permute-start.17 = (bf16[8,12288]{1,0:T(8,128)(2,1)S(1)}, bf16[8,12288]{1,0:T(8,128)(2,1)S(1)}, u32[]{:S(2)}, u32[]{:S(2)}) collective-permute-start(bf16[8,12288]{1,0:T(8,128)(2,1)S(1)} %get-tuple-element.55), channel_id=1, source_target_pairs={{0,256},{256,0},{1,257},{257,1},{2,258},{258,2},{3,259},{259,3},{4... | collective-permute-start | bytes 589832 | tf_op jit(solution)/shard_map/ppermute | solution.py:277
  125.8 2.6 %collective-permute-done.18 = bf16[8,12288]{1,0:T(8,128)(2,1)S(1)} collective-permute-done((bf16[8,12288]{1,0:T(8,128)(2,1)S(1)}, bf16[8,12288]{1,0:T(8,128)(2,1)S(1)}, u32[]{:S(2)}, u32[]{:S(2)}) %collective-permute-start.18) | collective-permute-done | bytes 196640 | tf_op jit(solution)/shard_map/ppermute | solution.py:277
  128.4 4.2 %collective-permute-done.17 = bf16[8,12288]{1,0:T(8,128)(2,1)S(1)} collective-permute-done((bf16[8,12288]{1,0:T(8,128)(2,1)S(1)}, bf16[8,12288]{1,0:T(8,128)(2,1)S(1)}, u32[]{:S(2)}, u32[]{:S(2)}) %collective-permute-start.17) | collective-permute-done | bytes 196640 | tf_op jit(solution)/shard_map/ppermute | solution.py:277
  133.8 14.2 %all_to_all.22 = f32[16,8,128]{2,1,0:T(8,128)S(1)} all-to-all(f32[16,8,128]{2,1,0:T(8,128)S(1)} %broadcast_in_dim.10), channel_id=1, replica_groups=mesh['band'=2,'dx'=16,'dy'=16] {'dx'}, dimensions={0} | all-to-all | bytes 131072 | tf_op jit(solution)/shard_map/all_to_all | solution.py:272
  148.7 5.9 %all-to-all-start.3 = ((f32[16,8,128]{2,1,0:T(8,128)}), f32[16,8,128]{2,1,0:T(8,128)S(1)}, u32[]{:S(2)}, u32[]{:S(2)}) async-start(f32[16,8,128]{2,1,0:T(8,128)} %broadcast_in_dim.11), calls=%async_computation.3 | async-start | bytes 131072 | tf_op jit(solution)/shard_map/all_to_all | solution.py:272
  155.4 6.6 %all-to-all-done.3 = f32[16,8,128]{2,1,0:T(8,128)S(1)} async-done(((f32[16,8,128]{2,1,0:T(8,128)}), f32[16,8,128]{2,1,0:T(8,128)S(1)}, u32[]{:S(2)}, u32[]{:S(2)}) %all-to-all-start.3) | async-done | bytes 65568 | tf_op jit(solution)/shard_map/all_to_all | solution.py:272
  (50 shorter events, 12.1 us)
Async XLA Ops:
  0.7 1.0 copy-start
  2.6 26.3 %collective-permute-start = (bf16[672,128]{1,0:T(8,128)(2,1)S(1)}, bf16[672,128]{1,0:T(8,128)(2,1)S(1)}, u32[]{:S(2)}, u32[]{:S(2)}) collective-permute-start(bf16[672,128]{1,0:T(8,128)(2,1)S(1)} %get-tuple-element.29), channel_id=1, source_target_pairs={{0,15},{1,2},{2,1},{3,4},{4,3},{5,6},{6,5},{7,8},{8,7},{9,10},{10,... | collective-permute-start | bytes 516104 | tf_op jit(solution)/shard_map/ppermute | solution.py:258
  8.6 20.2 %collective-permute-start.1 = (bf16[576,128]{1,0:T(8,128)(2,1)S(1)}, bf16[576,128]{1,0:T(8,128)(2,1)S(1)}, u32[]{:S(2)}, u32[]{:S(2)}) collective-permute-start(bf16[576,128]{1,0:T(8,128)(2,1)S(1)} %get-tuple-element.30), channel_id=1, source_target_pairs={{0,16},{16,0},{32,48},{48,32},{64,80},{80,64},{96,112},{112,96},{1... | collective-permute-start | bytes 442376 | tf_op jit(solution)/shard_map/ppermute | solution.py:258
  12.2 16.7 %collective-permute-start.2 = (bf16[576,128]{1,0:T(8,128)(2,1)S(1)}, bf16[576,128]{1,0:T(8,128)(2,1)S(1)}, u32[]{:S(2)}, u32[]{:S(2)}) collective-permute-start(bf16[576,128]{1,0:T(8,128)(2,1)S(1)} %get-tuple-element.31), channel_id=1, source_target_pairs={{0,240},{16,32},{32,16},{48,64},{64,48},{80,96},{96,80},{112,128},... | collective-permute-start | bytes 442376 | tf_op jit(solution)/shard_map/ppermute | solution.py:258
  22.4 6.5 %collective-permute-start.3 = (bf16[576,128]{1,0:T(8,128)(2,1)S(1)}, bf16[576,128]{1,0:T(8,128)(2,1)S(1)}, u32[]{:S(2)}, u32[]{:S(2)}) collective-permute-start(bf16[576,128]{1,0:T(8,128)(2,1)S(1)} %get-tuple-element.32), channel_id=1, source_target_pairs={{0,1},{1,0},{2,3},{3,2},{4,5},{5,4},{6,7},{7,6},{8,9},{9,8},{10,11... | collective-permute-start | bytes 442376 | tf_op jit(solution)/shard_map/ppermute | solution.py:258
  27.2 0.8 copy-start.1
  30.0 11.7 %collective-permute-start.4 = (bf16[672,128]{1,0:T(8,128)(2,1)S(1)}, bf16[672,128]{1,0:T(8,128)(2,1)S(1)}, u32[]{:S(2)}, u32[]{:S(2)}) collective-permute-start(bf16[672,128]{1,0:T(8,128)(2,1)S(1)} %get-tuple-element.34), channel_id=1, source_target_pairs={{0,15},{1,2},{2,1},{3,4},{4,3},{5,6},{6,5},{7,8},{8,7},{9,10},{10,... | collective-permute-start | bytes 516104 | tf_op jit(solution)/shard_map/ppermute | solution.py:258
  31.9 9.3 %collective-permute-start.5 = (bf16[576,128]{1,0:T(8,128)(2,1)S(1)}, bf16[576,128]{1,0:T(8,128)(2,1)S(1)}, u32[]{:S(2)}, u32[]{:S(2)}) collective-permute-start(bf16[576,128]{1,0:T(8,128)(2,1)S(1)} %get-tuple-element.35), channel_id=1, source_target_pairs={{0,16},{16,0},{32,48},{48,32},{64,80},{80,64},{96,112},{112,96},{1... | collective-permute-start | bytes 442376 | tf_op jit(solution)/shard_map/ppermute | solution.py:258
  33.8 7.8 %collective-permute-start.6 = (bf16[576,128]{1,0:T(8,128)(2,1)S(1)}, bf16[576,128]{1,0:T(8,128)(2,1)S(1)}, u32[]{:S(2)}, u32[]{:S(2)}) collective-permute-start(bf16[576,128]{1,0:T(8,128)(2,1)S(1)} %get-tuple-element.36), channel_id=1, source_target_pairs={{0,240},{16,32},{32,16},{48,64},{64,48},{80,96},{96,80},{112,128},... | collective-permute-start | bytes 442376 | tf_op jit(solution)/shard_map/ppermute | solution.py:258
  37.2 4.5 %collective-permute-start.7 = (bf16[576,128]{1,0:T(8,128)(2,1)S(1)}, bf16[576,128]{1,0:T(8,128)(2,1)S(1)}, u32[]{:S(2)}, u32[]{:S(2)}) collective-permute-start(bf16[576,128]{1,0:T(8,128)(2,1)S(1)} %get-tuple-element.37), channel_id=1, source_target_pairs={{0,1},{1,0},{2,3},{3,2},{4,5},{5,4},{6,7},{7,6},{8,9},{9,8},{10,11... | collective-permute-start | bytes 442376 | tf_op jit(solution)/shard_map/ppermute | solution.py:258
  41.2 36.9 %copy-start.2 = (bf16[128,12,8,128]{3,2,1,0:T(8,128)(2,1)S(1)}, bf16[128,12,8,128]{3,2,1,0:T(8,128)(2,1)}, u32[]{:S(2)}) copy-start(bf16[128,12,8,128]{3,2,1,0:T(8,128)(2,1)} %param.5) | copy-start | bytes 9437188
  42.8 17.1 %collective-permute-start.8 = (bf16[672,128]{1,0:T(8,128)(2,1)S(1)}, bf16[672,128]{1,0:T(8,128)(2,1)S(1)}, u32[]{:S(2)}, u32[]{:S(2)}) collective-permute-start(bf16[672,128]{1,0:T(8,128)(2,1)S(1)} %get-tuple-element.39), channel_id=1, source_target_pairs={{0,15},{1,2},{2,1},{3,4},{4,3},{5,6},{6,5},{7,8},{8,7},{9,10},{10,... | collective-permute-start | bytes 516104 | tf_op jit(solution)/shard_map/ppermute | solution.py:258
  48.4 11.4 %collective-permute-start.9 = (bf16[576,128]{1,0:T(8,128)(2,1)S(1)}, bf16[576,128]{1,0:T(8,128)(2,1)S(1)}, u32[]{:S(2)}, u32[]{:S(2)}) collective-permute-start(bf16[576,128]{1,0:T(8,128)(2,1)S(1)} %get-tuple-element.40), channel_id=1, source_target_pairs={{0,16},{16,0},{32,48},{48,32},{64,80},{80,64},{96,112},{112,96},{1... | collective-permute-start | bytes 442376 | tf_op jit(solution)/shard_map/ppermute | solution.py:258
  50.8 9.0 %collective-permute-start.10 = (bf16[576,128]{1,0:T(8,128)(2,1)S(1)}, bf16[576,128]{1,0:T(8,128)(2,1)S(1)}, u32[]{:S(2)}, u32[]{:S(2)}) collective-permute-start(bf16[576,128]{1,0:T(8,128)(2,1)S(1)} %get-tuple-element.41), channel_id=1, source_target_pairs={{0,240},{16,32},{32,16},{48,64},{64,48},{80,96},{96,80},{112,128},... | collective-permute-start | bytes 442376 | tf_op jit(solution)/shard_map/ppermute | solution.py:258
  55.0 4.9 %collective-permute-start.11 = (bf16[576,128]{1,0:T(8,128)(2,1)S(1)}, bf16[576,128]{1,0:T(8,128)(2,1)S(1)}, u32[]{:S(2)}, u32[]{:S(2)}) collective-permute-start(bf16[576,128]{1,0:T(8,128)(2,1)S(1)} %get-tuple-element.42), channel_id=1, source_target_pairs={{0,1},{1,0},{2,3},{3,2},{4,5},{5,4},{6,7},{7,6},{8,9},{9,8},{10,11... | collective-permute-start | bytes 442376 | tf_op jit(solution)/shard_map/ppermute | solution.py:258
  61.0 13.1 %collective-permute-start.12 = (bf16[672,128]{1,0:T(8,128)(2,1)S(1)}, bf16[672,128]{1,0:T(8,128)(2,1)S(1)}, u32[]{:S(2)}, u32[]{:S(2)}) collective-permute-start(bf16[672,128]{1,0:T(8,128)(2,1)S(1)} %get-tuple-element.44), channel_id=1, source_target_pairs={{0,15},{1,2},{2,1},{3,4},{4,3},{5,6},{6,5},{7,8},{8,7},{9,10},{10,... | collective-permute-start | bytes 516104 | tf_op jit(solution)/shard_map/ppermute | solution.py:258
  63.4 10.7 %collective-permute-start.13 = (bf16[576,128]{1,0:T(8,128)(2,1)S(1)}, bf16[576,128]{1,0:T(8,128)(2,1)S(1)}, u32[]{:S(2)}, u32[]{:S(2)}) collective-permute-start(bf16[576,128]{1,0:T(8,128)(2,1)S(1)} %get-tuple-element.45), channel_id=1, source_target_pairs={{0,16},{16,0},{32,48},{48,32},{64,80},{80,64},{96,112},{112,96},{1... | collective-permute-start | bytes 442376 | tf_op jit(solution)/shard_map/ppermute | solution.py:258
  65.3 8.7 %collective-permute-start.14 = (bf16[576,128]{1,0:T(8,128)(2,1)S(1)}, bf16[576,128]{1,0:T(8,128)(2,1)S(1)}, u32[]{:S(2)}, u32[]{:S(2)}) collective-permute-start(bf16[576,128]{1,0:T(8,128)(2,1)S(1)} %get-tuple-element.46), channel_id=1, source_target_pairs={{0,240},{16,32},{32,16},{48,64},{64,48},{80,96},{96,80},{112,128},... | collective-permute-start | bytes 442376 | tf_op jit(solution)/shard_map/ppermute | solution.py:258
  69.9 4.3 %collective-permute-start.15 = (bf16[576,128]{1,0:T(8,128)(2,1)S(1)}, bf16[576,128]{1,0:T(8,128)(2,1)S(1)}, u32[]{:S(2)}, u32[]{:S(2)}) collective-permute-start(bf16[576,128]{1,0:T(8,128)(2,1)S(1)} %get-tuple-element.47), channel_id=1, source_target_pairs={{0,1},{1,0},{2,3},{3,2},{4,5},{5,4},{6,7},{7,6},{8,9},{9,8},{10,11... | collective-permute-start | bytes 442376 | tf_op jit(solution)/shard_map/ppermute | solution.py:258
  75.2 7.2 %collective-permute-start.16 = (bf16[8,12288]{1,0:T(8,128)(2,1)S(1)}, bf16[8,12288]{1,0:T(8,128)(2,1)S(1)}, u32[]{:S(2)}, u32[]{:S(2)}) collective-permute-start(bf16[8,12288]{1,0:T(8,128)(2,1)S(1)} %convert_element_type.43), channel_id=1, source_target_pairs={{0,256},{256,0},{1,257},{257,1},{2,258},{258,2},{3,259},{259,3},{4... | collective-permute-start | bytes 589832 | tf_op jit(solution)/shard_map/ppermute | solution.py:277
  120.5 7.9 %collective-permute-start.18 = (bf16[8,12288]{1,0:T(8,128)(2,1)S(1)}, bf16[8,12288]{1,0:T(8,128)(2,1)S(1)}, u32[]{:S(2)}, u32[]{:S(2)}) collective-permute-start(bf16[8,12288]{1,0:T(8,128)(2,1)S(1)} %get-tuple-element.54), channel_id=1, source_target_pairs={{0,256},{256,0},{1,257},{257,1},{2,258},{258,2},{3,259},{259,3},{4... | collective-permute-start | bytes 589832 | tf_op jit(solution)/shard_map/ppermute | solution.py:277
  122.7 9.9 %collective-permute-start.17 = (bf16[8,12288]{1,0:T(8,128)(2,1)S(1)}, bf16[8,12288]{1,0:T(8,128)(2,1)S(1)}, u32[]{:S(2)}, u32[]{:S(2)}) collective-permute-start(bf16[8,12288]{1,0:T(8,128)(2,1)S(1)} %get-tuple-element.55), channel_id=1, source_target_pairs={{0,256},{256,0},{1,257},{257,1},{2,258},{258,2},{3,259},{259,3},{4... | collective-permute-start | bytes 589832 | tf_op jit(solution)/shard_map/ppermute | solution.py:277
  148.7 13.2 %all-to-all-start.3 = ((f32[16,8,128]{2,1,0:T(8,128)}), f32[16,8,128]{2,1,0:T(8,128)S(1)}, u32[]{:S(2)}, u32[]{:S(2)}) async-start(f32[16,8,128]{2,1,0:T(8,128)} %broadcast_in_dim.11), calls=%async_computation.3 | async-start | bytes 131072 | tf_op jit(solution)/shard_map/all_to_all | solution.py:272

commit v9 on v8

--- a/solution.py
+++ b/solution.py
@@ -34,7 +34,7 @@
     )
 
 
-def pack_messages(parity_ref, field_ref, y_odd, x_even, x_odd, y_even):
+def pack_messages(parity_ref, field_ref, x_even, y_odd, x_odd, y_even):
     def layer(dim, at):
         return field_ref[at] if dim == 0 else field_ref[:, at]
 
@@ -53,7 +53,7 @@
                 out_ref[used:, :] = jnp.zeros((rows, out_ref.shape[1]), jnp.bfloat16)
 
 
-def unpack_messages(parity_ref, halo_x, halo_y, y_odd, x_even, x_odd, y_even):
+def unpack_messages(parity_ref, halo_x, halo_y, x_even, y_odd, x_odd, y_even):
     for dim, halo, even, odd in ((0, halo_x, x_even, x_odd), (1, halo_y, y_even, y_odd)):
         shape = halo.shape[1:] if dim == 0 else halo.shape[:1] + halo.shape[2:]
         rows = shape[0] * shape[1]
@@ -177,7 +177,8 @@
 
 def message_shapes(size_x, size_y, own, depth):
     short = max(WIDTH * size_x, SENT * size_y) * own
-    sizes = (SENT * size_x * own, short, short, WIDTH * size_x * own)
+    long = max(SENT * size_x, SENT * size_y) * own
+    sizes = (long, SENT * size_x * own, short, WIDTH * size_x * own)
     return [jax.ShapeDtypeStruct((rows, depth), jnp.bfloat16) for rows in sizes]
 
 
@@ -251,15 +252,15 @@
     )(parity, inner, *messages)
 
 
-def swap(y_odd, x_even, x_odd, y_even):
+def swap(x_even, y_odd, x_odd, y_even):
     def swapped(values, axis, first):
         count = lax.axis_size(axis)
         step = lambda i: 1 if (i - first) % 2 == 0 else -1
         return lax.ppermute(values, axis, [(i, (i + step(i)) % count) for i in range(count)])
 
     return (
+        swapped(x_even, "dx", 0),
         swapped(y_odd, "dy", 1),
-        swapped(x_even, "dx", 0),
         swapped(x_odd, "dx", 1),
         swapped(y_even, "dy", 0),
     )
@@ -313,7 +314,7 @@
     got_other = other_band(mine.astype(jnp.bfloat16)).astype(jnp.float32)
     projected = filtered - mine - got
     projected_other = rounded_other.astype(jnp.float32) - theirs - got_other
-    exact = functools.partial(rows_dot, precision=lax.Precision.HIGHEST)
+    exact = functools.partial(rows_dot, precision=lax.Precision.HIGH)
     partial_gram = exact(projected, jnp.concatenate([projected, projected_other], axis=0))
     turned = jnp.roll(partial_gram, own_count, axis=1)
     partial_gram = jnp.where(lax.axis_index("band") == 0, partial_gram, turned)

time: 163 us -> 164 us (level)
  no operation moved by 1% of the time
where the time goes in v9:
time: 164 us; the launch traced here: 163 us
  starting transfers between devices  77.9 us (48%)
  blocking collectives  50.2 us (31%)
  waiting for transfers between devices  17.7 us (11%)
  Pallas kernels  8.58 us (5%)
  local copies, waits for them, and re-layouts  3.41 us (2%)
  matrix products  3.39 us (2%)
    ppermute x16, starting transfers between devices, swapped(): lax.ppermute(values, axis, [(i, (i + step(i)) % count) for i in range(cou...  64.4 us
    all_to_all x3, blocking collectives, sum_over_grid(): lax.all_to_all(sent, axis, 0, 0).astype(jnp.float32)  50.2 us
    ppermute x3, waiting for transfers between devices, other_band(): return lax.ppermute(values, 'band', [(0, 1), (1, 0)])  10.7 us
    ppermute x3, starting transfers between devices, other_band(): return lax.ppermute(values, 'band', [(0, 1), (1, 0)])  7.6 us
    all_to_all x1, waiting for transfers between devices, sum_over_grid(): lax.all_to_all(sent, axis, 0, 0).astype(jnp.float32)  6.57 us
    all_to_all x1, starting transfers between devices, sum_over_grid(): lax.all_to_all(sent, axis, 0, 0).astype(jnp.float32)  5.96 us
    pallas_call x4, Pallas kernels, filter_step(): pl.pallas_call(functools.partial(outer_kernel, 1.0 if previous is None el...  4.36 us
    pallas_call x4, Pallas kernels, filter_step(): pl.pallas_call(functools.partial(inner_kernel, previous is not None), out...  3.32 us
  transfers between devices with their start and end apart: 20, of which 7 were waited for; matrix products, arithmetic and copies ran while one was open for 1% of the time, Pallas kernels for 2%

profile of v9, /device:TPU:1, one launch (start us, length us, event | category | flops | bytes accessed | tf_op | source)
XLA Modules:
  0.0 163.1 jit_solution(5665381602784992993)
XLA Ops:
  0.7 1.0 copy-done
  2.6 4.4 %collective-permute-start = (bf16[672,128]{1,0:T(8,128)(2,1)S(1)}, bf16[672,128]{1,0:T(8,128)(2,1)S(1)}, u32[]{:S(2)}, u32[]{:S(2)}) collective-permute-start(bf16[672,128]{1,0:T(8,128)(2,1)S(1)} %get-tuple-element.29), channel_id=1, source_target_pairs={{0,16},{16,0},{32,48},{48,32},{64,80},{80,64},{96,112},{112,96},{1... | collective-permute-start | bytes 516104 | tf_op jit(solution)/shard_map/ppermute | solution.py:259
  7.0 5.5 %collective-permute-start.1 = (bf16[672,128]{1,0:T(8,128)(2,1)S(1)}, bf16[672,128]{1,0:T(8,128)(2,1)S(1)}, u32[]{:S(2)}, u32[]{:S(2)}) collective-permute-start(bf16[672,128]{1,0:T(8,128)(2,1)S(1)} %get-tuple-element.30), channel_id=1, source_target_pairs={{0,15},{1,2},{2,1},{3,4},{4,3},{5,6},{6,5},{7,8},{8,7},{9,10},{10,... | collective-permute-start | bytes 516104 | tf_op jit(solution)/shard_map/ppermute | solution.py:259
  12.5 10.2 %collective-permute-start.2 = (bf16[576,128]{1,0:T(8,128)(2,1)S(1)}, bf16[576,128]{1,0:T(8,128)(2,1)S(1)}, u32[]{:S(2)}, u32[]{:S(2)}) collective-permute-start(bf16[576,128]{1,0:T(8,128)(2,1)S(1)} %get-tuple-element.31), channel_id=1, source_target_pairs={{0,240},{16,32},{32,16},{48,64},{64,48},{80,96},{96,80},{112,128},... | collective-permute-start | bytes 442376 | tf_op jit(solution)/shard_map/ppermute | solution.py:259
  22.7 4.2 %collective-permute-start.3 = (bf16[576,128]{1,0:T(8,128)(2,1)S(1)}, bf16[576,128]{1,0:T(8,128)(2,1)S(1)}, u32[]{:S(2)}, u32[]{:S(2)}) collective-permute-start(bf16[576,128]{1,0:T(8,128)(2,1)S(1)} %get-tuple-element.32), channel_id=1, source_target_pairs={{0,1},{1,0},{2,3},{3,2},{4,5},{5,4},{6,7},{7,6},{8,9},{9,8},{10,11... | collective-permute-start | bytes 442376 | tf_op jit(solution)/shard_map/ppermute | solution.py:259
  28.6 1.1 shard_map.53
  29.7 1.9 %collective-permute-start.4 = (bf16[672,128]{1,0:T(8,128)(2,1)S(1)}, bf16[672,128]{1,0:T(8,128)(2,1)S(1)}, u32[]{:S(2)}, u32[]{:S(2)}) collective-permute-start(bf16[672,128]{1,0:T(8,128)(2,1)S(1)} %get-tuple-element.34), channel_id=1, source_target_pairs={{0,16},{16,0},{32,48},{48,32},{64,80},{80,64},{96,112},{112,96},{1... | collective-permute-start | bytes 516104 | tf_op jit(solution)/shard_map/ppermute | solution.py:259
  31.6 1.9 %collective-permute-start.5 = (bf16[672,128]{1,0:T(8,128)(2,1)S(1)}, bf16[672,128]{1,0:T(8,128)(2,1)S(1)}, u32[]{:S(2)}, u32[]{:S(2)}) collective-permute-start(bf16[672,128]{1,0:T(8,128)(2,1)S(1)} %get-tuple-element.35), channel_id=1, source_target_pairs={{0,15},{1,2},{2,1},{3,4},{4,3},{5,6},{6,5},{7,8},{8,7},{9,10},{10,... | collective-permute-start | bytes 516104 | tf_op jit(solution)/shard_map/ppermute | solution.py:259
  33.6 3.4 %collective-permute-start.6 = (bf16[576,128]{1,0:T(8,128)(2,1)S(1)}, bf16[576,128]{1,0:T(8,128)(2,1)S(1)}, u32[]{:S(2)}, u32[]{:S(2)}) collective-permute-start(bf16[576,128]{1,0:T(8,128)(2,1)S(1)} %get-tuple-element.36), channel_id=1, source_target_pairs={{0,240},{16,32},{32,16},{48,64},{64,48},{80,96},{96,80},{112,128},... | collective-permute-start | bytes 442376 | tf_op jit(solution)/shard_map/ppermute | solution.py:259
  36.9 4.0 %collective-permute-start.7 = (bf16[576,128]{1,0:T(8,128)(2,1)S(1)}, bf16[576,128]{1,0:T(8,128)(2,1)S(1)}, u32[]{:S(2)}, u32[]{:S(2)}) collective-permute-start(bf16[576,128]{1,0:T(8,128)(2,1)S(1)} %get-tuple-element.37), channel_id=1, source_target_pairs={{0,1},{1,0},{2,3},{3,2},{4,5},{5,4},{6,7},{7,6},{8,9},{9,8},{10,11... | collective-permute-start | bytes 442376 | tf_op jit(solution)/shard_map/ppermute | solution.py:259
  42.0 1.1 shard_map.55
  43.1 2.2 %collective-permute-start.8 = (bf16[672,128]{1,0:T(8,128)(2,1)S(1)}, bf16[672,128]{1,0:T(8,128)(2,1)S(1)}, u32[]{:S(2)}, u32[]{:S(2)}) collective-permute-start(bf16[672,128]{1,0:T(8,128)(2,1)S(1)} %get-tuple-element.39), channel_id=1, source_target_pairs={{0,16},{16,0},{32,48},{48,32},{64,80},{80,64},{96,112},{112,96},{1... | collective-permute-start | bytes 516104 | tf_op jit(solution)/shard_map/ppermute | solution.py:259
  45.3 5.3 %collective-permute-start.9 = (bf16[672,128]{1,0:T(8,128)(2,1)S(1)}, bf16[672,128]{1,0:T(8,128)(2,1)S(1)}, u32[]{:S(2)}, u32[]{:S(2)}) collective-permute-start(bf16[672,128]{1,0:T(8,128)(2,1)S(1)} %get-tuple-element.40), channel_id=1, source_target_pairs={{0,15},{1,2},{2,1},{3,4},{4,3},{5,6},{6,5},{7,8},{8,7},{9,10},{10,... | collective-permute-start | bytes 516104 | tf_op jit(solution)/shard_map/ppermute | solution.py:259
  50.7 4.2 %collective-permute-start.10 = (bf16[576,128]{1,0:T(8,128)(2,1)S(1)}, bf16[576,128]{1,0:T(8,128)(2,1)S(1)}, u32[]{:S(2)}, u32[]{:S(2)}) collective-permute-start(bf16[576,128]{1,0:T(8,128)(2,1)S(1)} %get-tuple-element.41), channel_id=1, source_target_pairs={{0,240},{16,32},{32,16},{48,64},{64,48},{80,96},{96,80},{112,128},... | collective-permute-start | bytes 442376 | tf_op jit(solution)/shard_map/ppermute | solution.py:259
  54.9 4.3 %collective-permute-start.11 = (bf16[576,128]{1,0:T(8,128)(2,1)S(1)}, bf16[576,128]{1,0:T(8,128)(2,1)S(1)}, u32[]{:S(2)}, u32[]{:S(2)}) collective-permute-start(bf16[576,128]{1,0:T(8,128)(2,1)S(1)} %get-tuple-element.42), channel_id=1, source_target_pairs={{0,1},{1,0},{2,3},{3,2},{4,5},{5,4},{6,7},{7,6},{8,9},{9,8},{10,11... | collective-permute-start | bytes 442376 | tf_op jit(solution)/shard_map/ppermute | solution.py:259
  60.2 1.1 shard_map.57
  61.3 1.9 %collective-permute-start.12 = (bf16[672,128]{1,0:T(8,128)(2,1)S(1)}, bf16[672,128]{1,0:T(8,128)(2,1)S(1)}, u32[]{:S(2)}, u32[]{:S(2)}) collective-permute-start(bf16[672,128]{1,0:T(8,128)(2,1)S(1)} %get-tuple-element.44), channel_id=1, source_target_pairs={{0,16},{16,0},{32,48},{48,32},{64,80},{80,64},{96,112},{112,96},{1... | collective-permute-start | bytes 516104 | tf_op jit(solution)/shard_map/ppermute | solution.py:259
  63.2 2.5 %collective-permute-start.13 = (bf16[672,128]{1,0:T(8,128)(2,1)S(1)}, bf16[672,128]{1,0:T(8,128)(2,1)S(1)}, u32[]{:S(2)}, u32[]{:S(2)}) collective-permute-start(bf16[672,128]{1,0:T(8,128)(2,1)S(1)} %get-tuple-element.45), channel_id=1, source_target_pairs={{0,15},{1,2},{2,1},{3,4},{4,3},{5,6},{6,5},{7,8},{8,7},{9,10},{10,... | collective-permute-start | bytes 516104 | tf_op jit(solution)/shard_map/ppermute | solution.py:259
  65.7 4.4 %collective-permute-start.14 = (bf16[576,128]{1,0:T(8,128)(2,1)S(1)}, bf16[576,128]{1,0:T(8,128)(2,1)S(1)}, u32[]{:S(2)}, u32[]{:S(2)}) collective-permute-start(bf16[576,128]{1,0:T(8,128)(2,1)S(1)} %get-tuple-element.46), channel_id=1, source_target_pairs={{0,240},{16,32},{32,16},{48,64},{64,48},{80,96},{96,80},{112,128},... | collective-permute-start | bytes 442376 | tf_op jit(solution)/shard_map/ppermute | solution.py:259
  70.1 4.0 %collective-permute-start.15 = (bf16[576,128]{1,0:T(8,128)(2,1)S(1)}, bf16[576,128]{1,0:T(8,128)(2,1)S(1)}, u32[]{:S(2)}, u32[]{:S(2)}) collective-permute-start(bf16[576,128]{1,0:T(8,128)(2,1)S(1)} %get-tuple-element.47), channel_id=1, source_target_pairs={{0,1},{1,0},{2,3},{3,2},{4,5},{5,4},{6,7},{7,6},{8,9},{9,8},{10,11... | collective-permute-start | bytes 442376 | tf_op jit(solution)/shard_map/ppermute | solution.py:259
  75.1 1.0 shard_map.59
  76.2 2.3 %collective-permute-start.16 = (bf16[8,12288]{1,0:T(8,128)(2,1)S(1)}, bf16[8,12288]{1,0:T(8,128)(2,1)S(1)}, u32[]{:S(2)}, u32[]{:S(2)}) collective-permute-start(bf16[8,12288]{1,0:T(8,128)(2,1)S(1)} %convert_element_type.43), channel_id=1, source_target_pairs={{0,256},{256,0},{1,257},{257,1},{2,258},{258,2},{3,259},{259,3},{4... | collective-permute-start | bytes 589832 | tf_op jit(solution)/shard_map/ppermute | solution.py:278
  79.4 3.9 %collective-permute-done.16 = bf16[8,12288]{1,0:T(8,128)(2,1)S(1)} collective-permute-done((bf16[8,12288]{1,0:T(8,128)(2,1)S(1)}, bf16[8,12288]{1,0:T(8,128)(2,1)S(1)}, u32[]{:S(2)}, u32[]{:S(2)}) %collective-permute-start.16) | collective-permute-done | bytes 196640 | tf_op jit(solution)/shard_map/ppermute | solution.py:278
  84.3 17.4 %all_to_all.20 = f16[16,16,128]{2,1,0:T(8,128)(2,1)S(1)} all-to-all(f16[16,16,128]{2,1,0:T(8,128)(2,1)S(1)} %broadcast_in_dim.8), channel_id=1, replica_groups=mesh['band'=2,'dx'=16,'dy'=16] {'dx'}, dimensions={0} | all-to-all | bytes 131072 | tf_op jit(solution)/shard_map/all_to_all | solution.py:273
  101.7 18.6 %all_to_all.21 = f16[16,16,128]{2,1,0:T(8,128)(2,1)S(1)} all-to-all(f16[16,16,128]{2,1,0:T(8,128)(2,1)S(1)} %broadcast_in_dim.9), channel_id=1, replica_groups=mesh['band'=2,'dx'=16,'dy'=16] {'dy'}, dimensions={0} | all-to-all | bytes 131072 | tf_op jit(solution)/shard_map/all_to_all | solution.py:273
  121.3 2.2 %collective-permute-start.18 = (bf16[8,12288]{1,0:T(8,128)(2,1)S(1)}, bf16[8,12288]{1,0:T(8,128)(2,1)S(1)}, u32[]{:S(2)}, u32[]{:S(2)}) collective-permute-start(bf16[8,12288]{1,0:T(8,128)(2,1)S(1)} %get-tuple-element.54), channel_id=1, source_target_pairs={{0,256},{256,0},{1,257},{257,1},{2,258},{258,2},{3,259},{259,3},{4... | collective-permute-start | bytes 589832 | tf_op jit(solution)/shard_map/ppermute | solution.py:278
  123.5 3.1 %collective-permute-start.17 = (bf16[8,12288]{1,0:T(8,128)(2,1)S(1)}, bf16[8,12288]{1,0:T(8,128)(2,1)S(1)}, u32[]{:S(2)}, u32[]{:S(2)}) collective-permute-start(bf16[8,12288]{1,0:T(8,128)(2,1)S(1)} %get-tuple-element.55), channel_id=1, source_target_pairs={{0,256},{256,0},{1,257},{257,1},{2,258},{258,2},{3,259},{259,3},{4... | collective-permute-start | bytes 589832 | tf_op jit(solution)/shard_map/ppermute | solution.py:278
  126.6 2.6 %collective-permute-done.18 = bf16[8,12288]{1,0:T(8,128)(2,1)S(1)} collective-permute-done((bf16[8,12288]{1,0:T(8,128)(2,1)S(1)}, bf16[8,12288]{1,0:T(8,128)(2,1)S(1)}, u32[]{:S(2)}, u32[]{:S(2)}) %collective-permute-start.18) | collective-permute-done | bytes 196640 | tf_op jit(solution)/shard_map/ppermute | solution.py:278
  129.2 4.2 %collective-permute-done.17 = bf16[8,12288]{1,0:T(8,128)(2,1)S(1)} collective-permute-done((bf16[8,12288]{1,0:T(8,128)(2,1)S(1)}, bf16[8,12288]{1,0:T(8,128)(2,1)S(1)}, u32[]{:S(2)}, u32[]{:S(2)}) %collective-permute-start.17) | collective-permute-done | bytes 196640 | tf_op jit(solution)/shard_map/ppermute | solution.py:278
  134.3 14.2 %all_to_all.22 = f32[16,8,128]{2,1,0:T(8,128)S(1)} all-to-all(f32[16,8,128]{2,1,0:T(8,128)S(1)} %broadcast_in_dim.10), channel_id=1, replica_groups=mesh['band'=2,'dx'=16,'dy'=16] {'dx'}, dimensions={0} | all-to-all | bytes 131072 | tf_op jit(solution)/shard_map/all_to_all | solution.py:273
  149.1 6.0 %all-to-all-start.3 = ((f32[16,8,128]{2,1,0:T(8,128)}), f32[16,8,128]{2,1,0:T(8,128)S(1)}, u32[]{:S(2)}, u32[]{:S(2)}) async-start(f32[16,8,128]{2,1,0:T(8,128)} %broadcast_in_dim.11), calls=%async_computation.3 | async-start | bytes 131072 | tf_op jit(solution)/shard_map/all_to_all | solution.py:273
  155.9 6.6 %all-to-all-done.3 = f32[16,8,128]{2,1,0:T(8,128)S(1)} async-done(((f32[16,8,128]{2,1,0:T(8,128)}), f32[16,8,128]{2,1,0:T(8,128)S(1)}, u32[]{:S(2)}, u32[]{:S(2)}) %all-to-all-start.3) | async-done | bytes 65568 | tf_op jit(solution)/shard_map/all_to_all | solution.py:273
  (50 shorter events, 11.4 us)
Async XLA Ops:
  0.7 1.0 copy-start
  2.6 26.0 %collective-permute-start = (bf16[672,128]{1,0:T(8,128)(2,1)S(1)}, bf16[672,128]{1,0:T(8,128)(2,1)S(1)}, u32[]{:S(2)}, u32[]{:S(2)}) collective-permute-start(bf16[672,128]{1,0:T(8,128)(2,1)S(1)} %get-tuple-element.29), channel_id=1, source_target_pairs={{0,16},{16,0},{32,48},{48,32},{64,80},{80,64},{96,112},{112,96},{1... | collective-permute-start | bytes 516104 | tf_op jit(solution)/shard_map/ppermute | solution.py:259
  7.0 21.6 %collective-permute-start.1 = (bf16[672,128]{1,0:T(8,128)(2,1)S(1)}, bf16[672,128]{1,0:T(8,128)(2,1)S(1)}, u32[]{:S(2)}, u32[]{:S(2)}) collective-permute-start(bf16[672,128]{1,0:T(8,128)(2,1)S(1)} %get-tuple-element.30), channel_id=1, source_target_pairs={{0,15},{1,2},{2,1},{3,4},{4,3},{5,6},{6,5},{7,8},{8,7},{9,10},{10,... | collective-permute-start | bytes 516104 | tf_op jit(solution)/shard_map/ppermute | solution.py:259
  12.5 16.1 %collective-permute-start.2 = (bf16[576,128]{1,0:T(8,128)(2,1)S(1)}, bf16[576,128]{1,0:T(8,128)(2,1)S(1)}, u32[]{:S(2)}, u32[]{:S(2)}) collective-permute-start(bf16[576,128]{1,0:T(8,128)(2,1)S(1)} %get-tuple-element.31), channel_id=1, source_target_pairs={{0,240},{16,32},{32,16},{48,64},{64,48},{80,96},{96,80},{112,128},... | collective-permute-start | bytes 442376 | tf_op jit(solution)/shard_map/ppermute | solution.py:259
  22.7 5.9 %collective-permute-start.3 = (bf16[576,128]{1,0:T(8,128)(2,1)S(1)}, bf16[576,128]{1,0:T(8,128)(2,1)S(1)}, u32[]{:S(2)}, u32[]{:S(2)}) collective-permute-start(bf16[576,128]{1,0:T(8,128)(2,1)S(1)} %get-tuple-element.32), channel_id=1, source_target_pairs={{0,1},{1,0},{2,3},{3,2},{4,5},{5,4},{6,7},{7,6},{8,9},{9,8},{10,11... | collective-permute-start | bytes 442376 | tf_op jit(solution)/shard_map/ppermute | solution.py:259
  26.9 0.8 copy-start.1
  29.7 12.3 %collective-permute-start.4 = (bf16[672,128]{1,0:T(8,128)(2,1)S(1)}, bf16[672,128]{1,0:T(8,128)(2,1)S(1)}, u32[]{:S(2)}, u32[]{:S(2)}) collective-permute-start(bf16[672,128]{1,0:T(8,128)(2,1)S(1)} %get-tuple-element.34), channel_id=1, source_target_pairs={{0,16},{16,0},{32,48},{48,32},{64,80},{80,64},{96,112},{112,96},{1... | collective-permute-start | bytes 516104 | tf_op jit(solution)/shard_map/ppermute | solution.py:259
  31.6 10.3 %collective-permute-start.5 = (bf16[672,128]{1,0:T(8,128)(2,1)S(1)}, bf16[672,128]{1,0:T(8,128)(2,1)S(1)}, u32[]{:S(2)}, u32[]{:S(2)}) collective-permute-start(bf16[672,128]{1,0:T(8,128)(2,1)S(1)} %get-tuple-element.35), channel_id=1, source_target_pairs={{0,15},{1,2},{2,1},{3,4},{4,3},{5,6},{6,5},{7,8},{8,7},{9,10},{10,... | collective-permute-start | bytes 516104 | tf_op jit(solution)/shard_map/ppermute | solution.py:259
  33.6 8.3 %collective-permute-start.6 = (bf16[576,128]{1,0:T(8,128)(2,1)S(1)}, bf16[576,128]{1,0:T(8,128)(2,1)S(1)}, u32[]{:S(2)}, u32[]{:S(2)}) collective-permute-start(bf16[576,128]{1,0:T(8,128)(2,1)S(1)} %get-tuple-element.36), channel_id=1, source_target_pairs={{0,240},{16,32},{32,16},{48,64},{64,48},{80,96},{96,80},{112,128},... | collective-permute-start | bytes 442376 | tf_op jit(solution)/shard_map/ppermute | solution.py:259
  36.9 5.0 %collective-permute-start.7 = (bf16[576,128]{1,0:T(8,128)(2,1)S(1)}, bf16[576,128]{1,0:T(8,128)(2,1)S(1)}, u32[]{:S(2)}, u32[]{:S(2)}) collective-permute-start(bf16[576,128]{1,0:T(8,128)(2,1)S(1)} %get-tuple-element.37), channel_id=1, source_target_pairs={{0,1},{1,0},{2,3},{3,2},{4,5},{5,4},{6,7},{7,6},{8,9},{9,8},{10,11... | collective-permute-start | bytes 442376 | tf_op jit(solution)/shard_map/ppermute | solution.py:259
  41.8 36.7 %copy-start.2 = (bf16[128,12,8,128]{3,2,1,0:T(8,128)(2,1)S(1)}, bf16[128,12,8,128]{3,2,1,0:T(8,128)(2,1)}, u32[]{:S(2)}) copy-start(bf16[128,12,8,128]{3,2,1,0:T(8,128)(2,1)} %param.5) | copy-start | bytes 9437188
  43.1 17.1 %collective-permute-start.8 = (bf16[672,128]{1,0:T(8,128)(2,1)S(1)}, bf16[672,128]{1,0:T(8,128)(2,1)S(1)}, u32[]{:S(2)}, u32[]{:S(2)}) collective-permute-start(bf16[672,128]{1,0:T(8,128)(2,1)S(1)} %get-tuple-element.39), channel_id=1, source_target_pairs={{0,16},{16,0},{32,48},{48,32},{64,80},{80,64},{96,112},{112,96},{1... | collective-permute-start | bytes 516104 | tf_op jit(solution)/shard_map/ppermute | solution.py:259
  45.3 14.8 %collective-permute-start.9 = (bf16[672,128]{1,0:T(8,128)(2,1)S(1)}, bf16[672,128]{1,0:T(8,128)(2,1)S(1)}, u32[]{:S(2)}, u32[]{:S(2)}) collective-permute-start(bf16[672,128]{1,0:T(8,128)(2,1)S(1)} %get-tuple-element.40), channel_id=1, source_target_pairs={{0,15},{1,2},{2,1},{3,4},{4,3},{5,6},{6,5},{7,8},{8,7},{9,10},{10,... | collective-permute-start | bytes 516104 | tf_op jit(solution)/shard_map/ppermute | solution.py:259
  50.7 9.3 %collective-permute-start.10 = (bf16[576,128]{1,0:T(8,128)(2,1)S(1)}, bf16[576,128]{1,0:T(8,128)(2,1)S(1)}, u32[]{:S(2)}, u32[]{:S(2)}) collective-permute-start(bf16[576,128]{1,0:T(8,128)(2,1)S(1)} %get-tuple-element.41), channel_id=1, source_target_pairs={{0,240},{16,32},{32,16},{48,64},{64,48},{80,96},{96,80},{112,128},... | collective-permute-start | bytes 442376 | tf_op jit(solution)/shard_map/ppermute | solution.py:259
  54.9 5.2 %collective-permute-start.11 = (bf16[576,128]{1,0:T(8,128)(2,1)S(1)}, bf16[576,128]{1,0:T(8,128)(2,1)S(1)}, u32[]{:S(2)}, u32[]{:S(2)}) collective-permute-start(bf16[576,128]{1,0:T(8,128)(2,1)S(1)} %get-tuple-element.42), channel_id=1, source_target_pairs={{0,1},{1,0},{2,3},{3,2},{4,5},{5,4},{6,7},{7,6},{8,9},{9,8},{10,11... | collective-permute-start | bytes 442376 | tf_op jit(solution)/shard_map/ppermute | solution.py:259
  61.3 13.8 %collective-permute-start.12 = (bf16[672,128]{1,0:T(8,128)(2,1)S(1)}, bf16[672,128]{1,0:T(8,128)(2,1)S(1)}, u32[]{:S(2)}, u32[]{:S(2)}) collective-permute-start(bf16[672,128]{1,0:T(8,128)(2,1)S(1)} %get-tuple-element.44), channel_id=1, source_target_pairs={{0,16},{16,0},{32,48},{48,32},{64,80},{80,64},{96,112},{112,96},{1... | collective-permute-start | bytes 516104 | tf_op jit(solution)/shard_map/ppermute | solution.py:259
  63.2 11.9 %collective-permute-start.13 = (bf16[672,128]{1,0:T(8,128)(2,1)S(1)}, bf16[672,128]{1,0:T(8,128)(2,1)S(1)}, u32[]{:S(2)}, u32[]{:S(2)}) collective-permute-start(bf16[672,128]{1,0:T(8,128)(2,1)S(1)} %get-tuple-element.45), channel_id=1, source_target_pairs={{0,15},{1,2},{2,1},{3,4},{4,3},{5,6},{6,5},{7,8},{8,7},{9,10},{10,... | collective-permute-start | bytes 516104 | tf_op jit(solution)/shard_map/ppermute | solution.py:259
  65.7 9.2 %collective-permute-start.14 = (bf16[576,128]{1,0:T(8,128)(2,1)S(1)}, bf16[576,128]{1,0:T(8,128)(2,1)S(1)}, u32[]{:S(2)}, u32[]{:S(2)}) collective-permute-start(bf16[576,128]{1,0:T(8,128)(2,1)S(1)} %get-tuple-element.46), channel_id=1, source_target_pairs={{0,240},{16,32},{32,16},{48,64},{64,48},{80,96},{96,80},{112,128},... | collective-permute-start | bytes 442376 | tf_op jit(solution)/shard_map/ppermute | solution.py:259
  70.1 5.0 %collective-permute-start.15 = (bf16[576,128]{1,0:T(8,128)(2,1)S(1)}, bf16[576,128]{1,0:T(8,128)(2,1)S(1)}, u32[]{:S(2)}, u32[]{:S(2)}) collective-permute-start(bf16[576,128]{1,0:T(8,128)(2,1)S(1)} %get-tuple-element.47), channel_id=1, source_target_pairs={{0,1},{1,0},{2,3},{3,2},{4,5},{5,4},{6,7},{7,6},{8,9},{9,8},{10,11... | collective-permute-start | bytes 442376 | tf_op jit(solution)/shard_map/ppermute | solution.py:259
  76.2 7.1 %collective-permute-start.16 = (bf16[8,12288]{1,0:T(8,128)(2,1)S(1)}, bf16[8,12288]{1,0:T(8,128)(2,1)S(1)}, u32[]{:S(2)}, u32[]{:S(2)}) collective-permute-start(bf16[8,12288]{1,0:T(8,128)(2,1)S(1)} %convert_element_type.43), channel_id=1, source_target_pairs={{0,256},{256,0},{1,257},{257,1},{2,258},{258,2},{3,259},{259,3},{4... | collective-permute-start | bytes 589832 | tf_op jit(solution)/shard_map/ppermute | solution.py:278
  121.3 7.9 %collective-permute-start.18 = (bf16[8,12288]{1,0:T(8,128)(2,1)S(1)}, bf16[8,12288]{1,0:T(8,128)(2,1)S(1)}, u32[]{:S(2)}, u32[]{:S(2)}) collective-permute-start(bf16[8,12288]{1,0:T(8,128)(2,1)S(1)} %get-tuple-element.54), channel_id=1, source_target_pairs={{0,256},{256,0},{1,257},{257,1},{2,258},{258,2},{3,259},{259,3},{4... | collective-permute-start | bytes 589832 | tf_op jit(solution)/shard_map/ppermute | solution.py:278
  123.5 9.9 %collective-permute-start.17 = (bf16[8,12288]{1,0:T(8,128)(2,1)S(1)}, bf16[8,12288]{1,0:T(8,128)(2,1)S(1)}, u32[]{:S(2)}, u32[]{:S(2)}) collective-permute-start(bf16[8,12288]{1,0:T(8,128)(2,1)S(1)} %get-tuple-element.55), channel_id=1, source_target_pairs={{0,256},{256,0},{1,257},{257,1},{2,258},{258,2},{3,259},{259,3},{4... | collective-permute-start | bytes 589832 | tf_op jit(solution)/shard_map/ppermute | solution.py:278
  149.1 13.3 %all-to-all-start.3 = ((f32[16,8,128]{2,1,0:T(8,128)}), f32[16,8,128]{2,1,0:T(8,128)S(1)}, u32[]{:S(2)}, u32[]{:S(2)}) async-start(f32[16,8,128]{2,1,0:T(8,128)} %broadcast_in_dim.11), calls=%async_computation.3 | async-start | bytes 131072 | tf_op jit(solution)/shard_map/all_to_all | solution.py:273

commit v10 on v8

--- a/solution.py
+++ b/solution.py
@@ -53,27 +53,23 @@
                 out_ref[used:, :] = jnp.zeros((rows, out_ref.shape[1]), jnp.bfloat16)
 
 
-def unpack_messages(parity_ref, halo_x, halo_y, y_odd, x_even, x_odd, y_even):
-    for dim, halo, even, odd in ((0, halo_x, x_even, x_odd), (1, halo_y, y_even, y_odd)):
-        shape = halo.shape[1:] if dim == 0 else halo.shape[:1] + halo.shape[2:]
-        rows = shape[0] * shape[1]
-        parity = parity_ref[dim]
-        for got, after, near in ((even, 1 - parity, WIDTH - parity), (odd, parity, WIDTH - 1 + parity)):
-            def read(at):
-                return got[at * rows : (at + 1) * rows, :].astype(jnp.float32).reshape(shape)
-
-            for at in range(WIDTH):
-                place = after * WIDTH + at
-                if dim == 0:
-                    halo[place] = read(at)
-                else:
-                    halo[:, place] = read(at)
-            if got.shape[0] < SENT * rows:
-                continue
-            if dim == 0:
-                halo[near] += read(WIDTH)
-            else:
-                halo[:, near] += read(WIDTH)
+def unpack(got, halo, dim, base, near):
+    shape = halo.shape[1:] if dim == 0 else halo.shape[:1] + halo.shape[2:]
+    rows = shape[0] * shape[1]
+
+    def read(at):
+        return got[at * rows : (at + 1) * rows, :].astype(jnp.float32).reshape(shape)
+
+    for at in range(WIDTH):
+        if dim == 0:
+            halo[base + at] = read(at)
+        else:
+            halo[:, base + at] = read(at)
+    if got.shape[0] >= SENT * rows:
+        if dim == 0:
+            halo[near] += read(WIDTH)
+        else:
+            halo[:, near] += read(WIDTH)
 
 
 def start_kernel(parity_ref, cells_ref, field_ref, *messages):
@@ -140,36 +136,85 @@
             total_ref[x, y] = inside(total_ref[x, y], line, y)
 
 
-def outer_kernel(factor, last, parity_ref, inner_ref, *refs):
-    messages, outs, (halo_x, halo_y, total_ref) = refs[:4], refs[4:-3], refs[-3:]
-    size_x, size_y, own, depth = inner_ref.shape
-    unpack_messages(parity_ref, halo_x, halo_y, *messages)
-    weights = [-2.0 * factor / FILTER_HALF * w for w in STENCIL_WEIGHTS]
-
-    def outside(total, line, at, size):
-        for k in range(1, WIDTH + 1):
-            if at - k < 0:
-                total = total + weights[k] * line[WIDTH + at - k]
-            if at + k >= size:
-                total = total + weights[k] * line[WIDTH + at + k - size]
-        return total
+def add_side(right, halo, source, weights, store):
+    size_x, size_y = source.shape[:2]
 
     @pl.loop(0, size_y)
     def _(y):
-        line = [halo_x[k, y] for k in range(2 * WIDTH)]
-        for x in range(size_x):
-            total_ref[x, y] = outside(inner_ref[x, y], line, x, size_x)
+        line = [halo[k, y] for k in range(WIDTH)]
+        for i in range(WIDTH):
+            x = size_x - WIDTH + i if right else i
+            total = source[x, y]
+            for k in range(1, WIDTH + 1):
+                if right and x + k >= size_x:
+                    total = total + weights[k] * line[x + k - size_x]
+                if not right and x - k < 0:
+                    total = total + weights[k] * line[WIDTH + x - k]
+            store(x, y, total)
+
+
+def outer_first_kernel(factor, parity_ref, inner_ref, y_odd, x_even, y_even, total_ref, halo_x, halo_y):
+    size_x, size_y, own, depth = inner_ref.shape
+    weights = [-2.0 * factor / FILTER_HALF * w for w in STENCIL_WEIGHTS]
+    odd = parity_ref[1]
+    unpack(y_odd, halo_y, 1, odd * WIDTH, WIDTH - 1 + odd)
+    unpack(y_even, halo_y, 1, (1 - odd) * WIDTH, WIDTH - odd)
+    odd_x = parity_ref[0]
+    unpack(x_even, halo_x, 0, 0, odd_x * (WIDTH - 1))
 
     @pl.loop(0, size_x)
     def _(x):
         line = [halo_y[x, k] for k in range(2 * WIDTH)]
         for y in range(size_y):
-            total = outside(total_ref[x, y], line, y, size_y)
-            if last:
-                place = pl.multiple_of((x * size_y + y) * depth, depth)
-                outs[0][:, pl.ds(place, depth)] = total
-            else:
-                outs[0][x, y] = total
+            total = inner_ref[x, y]
+            for k in range(1, WIDTH + 1):
+                if y - k < 0:
+                    total = total + weights[k] * line[WIDTH + y - k]
+                if y + k >= size_y:
+                    total = total + weights[k] * line[WIDTH + y + k - size_y]
+            total_ref[x, y] = total
+
+    def store(x, y, total):
+        total_ref[x, y] = total
+
+    @pl.when(odd_x == 0)
+    def _():
+        add_side(True, halo_x, total_ref, weights, store)
+
+    @pl.when(odd_x == 1)
+    def _():
+        add_side(False, halo_x, total_ref, weights, store)
+
+
+def outer_last_kernel(factor, last, parity_ref, total_ref, x_odd, *refs):
+    outs, halo_x = refs[:-1], refs[-1]
+    size_x, size_y, own, depth = total_ref.shape
+    weights = [-2.0 * factor / FILTER_HALF * w for w in STENCIL_WEIGHTS]
+    odd_x = parity_ref[0]
+    unpack(x_odd, halo_x, 0, 0, (1 - odd_x) * (WIDTH - 1))
+
+    def store(x, y, total):
+        if last:
+            place = pl.multiple_of((x * size_y + y) * depth, depth)
+            outs[0][:, pl.ds(place, depth)] = total
+        else:
+            outs[0][x, y] = total
+
+    def keep(first):
+        @pl.loop(0, size_y)
+        def _(y):
+            for x in range(first, first + size_x - WIDTH):
+                store(x, y, total_ref[x, y])
+
+    @pl.when(odd_x == 1)
+    def _():
+        add_side(True, halo_x, total_ref, weights, store)
+        keep(0)
+
+    @pl.when(odd_x == 0)
+    def _():
+        add_side(False, halo_x, total_ref, weights, store)
+        keep(WIDTH)
 
     if not last:
         pack_messages(parity_ref, *outs)
@@ -177,7 +222,8 @@
 
 def message_shapes(size_x, size_y, own, depth):
     short = max(WIDTH * size_x, SENT * size_y) * own
-    sizes = (SENT * size_x * own, short, short, WIDTH * size_x * own)
+    long = SENT * size_x * own
+    sizes = (long, max(long, short), (long + short) // 2 // 16 * 16, WIDTH * size_x * own)
     return [jax.ShapeDtypeStruct((rows, depth), jnp.bfloat16) for rows in sizes]
 
 
@@ -233,22 +279,34 @@
             flops=6 * field.size * depth, bytes_accessed=12 * field.size, transcendentals=0
         ),
     )(field, *fixed, *before)
+    y_odd, x_even, x_odd, y_even = messages
+    factor = 1.0 if previous is None else 2.0
+    scratch_x = pltpu.VMEM((WIDTH, size_y, own, depth), jnp.float32)
+    scratch_y = pltpu.VMEM((size_x, 2 * WIDTH, own, depth), jnp.float32)
+    smem = pl.BlockSpec(memory_space=pltpu.SMEM)
+    total = pl.pallas_call(
+        functools.partial(outer_first_kernel, factor),
+        out_shape=field_shape,
+        in_specs=[smem] + in_vmem(4),
+        out_specs=in_vmem(1)[0],
+        scratch_shapes=[scratch_x, scratch_y],
+        compiler_params=params(),
+        cost_estimate=pl.CostEstimate(
+            flops=field.size, bytes_accessed=field.size, transcendentals=0
+        ),
+    )(parity, inner, y_odd, x_even, y_even)
     if last:
         out_shape = [jax.ShapeDtypeStruct((own, size_x * size_y * depth), jnp.float32)]
     else:
         out_shape = [field_shape] + message_shapes(size_x, size_y, own, depth)
     return pl.pallas_call(
-        functools.partial(outer_kernel, 1.0 if previous is None else 2.0, last),
+        functools.partial(outer_last_kernel, factor, last),
         out_shape=out_shape,
-        in_specs=[pl.BlockSpec(memory_space=pltpu.SMEM)] + in_vmem(5),
+        in_specs=[smem] + in_vmem(2),
         out_specs=in_vmem(len(out_shape)),
-        scratch_shapes=[
-            pltpu.VMEM((2 * WIDTH, size_y, own, depth), jnp.float32),
-            pltpu.VMEM((size_x, 2 * WIDTH, own, depth), jnp.float32),
-            pltpu.VMEM(field.shape, jnp.float32),
-        ],
-        compiler_params=params(),
-    )(parity, inner, *messages)
+        scratch_shapes=[scratch_x],
+        compiler_params=params(),
+    )(parity, total, x_odd)
 
 
 def swap(y_odd, x_even, x_odd, y_even):
@@ -313,7 +371,7 @@
     got_other = other_band(mine.astype(jnp.bfloat16)).astype(jnp.float32)
     projected = filtered - mine - got
     projected_other = rounded_other.astype(jnp.float32) - theirs - got_other
-    exact = functools.partial(rows_dot, precision=lax.Precision.HIGHEST)
+    exact = functools.partial(rows_dot, precision=lax.Precision.HIGH)
     partial_gram = exact(projected, jnp.concatenate([projected, projected_other], axis=0))
     turned = jnp.roll(partial_gram, own_count, axis=1)
     partial_gram = jnp.where(lax.axis_index("band") == 0, partial_gram, turned)

time: 163 us -> 163 us (level)
  Pallas kernels: 8.57 us -> 11.2 us
  blocking collectives: 50.2 us -> 48 us
    pallas_call x4 -> x8, Pallas kernels: 4.35 us -> 6.95 us  [the longest x4 3.81 us: filter_step(): pl.pallas_call(functools.partial(outer_first_kernel, factor), out_shape=f...]
    all_to_all x3, blocking collectives: 50.2 us -> 48 us  [sum_over_grid(): lax.all_to_all(sent, axis, 0, 0).astype(jnp.float32)]
  transfers between devices with their start and end apart: 20 -> 20, of which waited for: 7 -> 7; matrix products, arithmetic and copies ran while one was open for 1% -> 1% of each run, Pallas kernels for 2% -> 4%
where the time goes in v10:
time: 163 us; the launch traced here: 162 us
  starting transfers between devices  76 us (47%)
  blocking collectives  48 us (29%)
  waiting for transfers between devices  18 us (11%)
  Pallas kernels  11.2 us (7%)
  local copies, waits for them, and re-layouts  3.41 us (2%)
  matrix products  3.39 us (2%)
    ppermute x16, starting transfers between devices, swapped(): lax.ppermute(values, axis, [(i, (i + step(i)) % count) for i in range(cou...  62 us
    all_to_all x3, blocking collectives, sum_over_grid(): lax.all_to_all(sent, axis, 0, 0).astype(jnp.float32)  48 us
    ppermute x3, waiting for transfers between devices, other_band(): return lax.ppermute(values, 'band', [(0, 1), (1, 0)])  11 us
    ppermute x3, starting transfers between devices, other_band(): return lax.ppermute(values, 'band', [(0, 1), (1, 0)])  8.2 us
    all_to_all x1, waiting for transfers between devices, sum_over_grid(): lax.all_to_all(sent, axis, 0, 0).astype(jnp.float32)  6.57 us
    all_to_all x1, starting transfers between devices, sum_over_grid(): lax.all_to_all(sent, axis, 0, 0).astype(jnp.float32)  5.86 us
    pallas_call x4, Pallas kernels, filter_step(): pl.pallas_call(functools.partial(outer_first_kernel, factor), out_shape=f...  3.81 us
    pallas_call x4, Pallas kernels, filter_step(): pl.pallas_call(functools.partial(inner_kernel, previous is not None), out...  3.32 us
  transfers between devices with their start and end apart: 20, of which 7 were waited for; matrix products, arithmetic and copies ran while one was open for 1% of the time, Pallas kernels for 4%

profile of v10, /device:TPU:1, one launch (start us, length us, event | category | flops | bytes accessed | tf_op | source)
XLA Modules:
  0.0 162.0 jit_solution(17164373817428010599)
XLA Ops:
  0.7 1.0 copy-done
  2.6 6.0 %collective-permute-start = (bf16[672,128]{1,0:T(8,128)(2,1)S(1)}, bf16[672,128]{1,0:T(8,128)(2,1)S(1)}, u32[]{:S(2)}, u32[]{:S(2)}) collective-permute-start(bf16[672,128]{1,0:T(8,128)(2,1)S(1)} %get-tuple-element.29), channel_id=1, source_target_pairs={{0,15},{1,2},{2,1},{3,4},{4,3},{5,6},{6,5},{7,8},{8,7},{9,10},{10,... | collective-permute-start | bytes 516104 | tf_op jit(solution)/shard_map/ppermute | solution.py:316
  8.6 3.5 %collective-permute-start.1 = (bf16[672,128]{1,0:T(8,128)(2,1)S(1)}, bf16[672,128]{1,0:T(8,128)(2,1)S(1)}, u32[]{:S(2)}, u32[]{:S(2)}) collective-permute-start(bf16[672,128]{1,0:T(8,128)(2,1)S(1)} %get-tuple-element.30), channel_id=1, source_target_pairs={{0,16},{16,0},{32,48},{48,32},{64,80},{80,64},{96,112},{112,96},{1... | collective-permute-start | bytes 516104 | tf_op jit(solution)/shard_map/ppermute | solution.py:316
  12.2 10.2 %collective-permute-start.3 = (bf16[624,128]{1,0:T(8,128)(2,1)S(1)}, bf16[624,128]{1,0:T(8,128)(2,1)S(1)}, u32[]{:S(2)}, u32[]{:S(2)}) collective-permute-start(bf16[624,128]{1,0:T(8,128)(2,1)S(1)} %get-tuple-element.32), channel_id=1, source_target_pairs={{0,240},{16,32},{32,16},{48,64},{64,48},{80,96},{96,80},{112,128},... | collective-permute-start | bytes 479240 | tf_op jit(solution)/shard_map/ppermute | solution.py:316
  22.4 4.8 %collective-permute-start.2 = (bf16[576,128]{1,0:T(8,128)(2,1)S(1)}, bf16[576,128]{1,0:T(8,128)(2,1)S(1)}, u32[]{:S(2)}, u32[]{:S(2)}) collective-permute-start(bf16[576,128]{1,0:T(8,128)(2,1)S(1)} %get-tuple-element.31), channel_id=1, source_target_pairs={{0,1},{1,0},{2,3},{3,2},{4,5},{5,4},{6,7},{7,6},{8,9},{9,8},{10,11... | collective-permute-start | bytes 442376 | tf_op jit(solution)/shard_map/ppermute | solution.py:316
  28.9 1.0 shard_map.53.total_ref
  30.6 1.9 %collective-permute-start.4 = (bf16[672,128]{1,0:T(8,128)(2,1)S(1)}, bf16[672,128]{1,0:T(8,128)(2,1)S(1)}, u32[]{:S(2)}, u32[]{:S(2)}) collective-permute-start(bf16[672,128]{1,0:T(8,128)(2,1)S(1)} %get-tuple-element.34), channel_id=1, source_target_pairs={{0,15},{1,2},{2,1},{3,4},{4,3},{5,6},{6,5},{7,8},{8,7},{9,10},{10,... | collective-permute-start | bytes 516104 | tf_op jit(solution)/shard_map/ppermute | solution.py:316
  32.6 1.9 %collective-permute-start.5 = (bf16[672,128]{1,0:T(8,128)(2,1)S(1)}, bf16[672,128]{1,0:T(8,128)(2,1)S(1)}, u32[]{:S(2)}, u32[]{:S(2)}) collective-permute-start(bf16[672,128]{1,0:T(8,128)(2,1)S(1)} %get-tuple-element.35), channel_id=1, source_target_pairs={{0,16},{16,0},{32,48},{48,32},{64,80},{80,64},{96,112},{112,96},{1... | collective-permute-start | bytes 516104 | tf_op jit(solution)/shard_map/ppermute | solution.py:316
  34.5 3.4 %collective-permute-start.7 = (bf16[624,128]{1,0:T(8,128)(2,1)S(1)}, bf16[624,128]{1,0:T(8,128)(2,1)S(1)}, u32[]{:S(2)}, u32[]{:S(2)}) collective-permute-start(bf16[624,128]{1,0:T(8,128)(2,1)S(1)} %get-tuple-element.37), channel_id=1, source_target_pairs={{0,240},{16,32},{32,16},{48,64},{64,48},{80,96},{96,80},{112,128},... | collective-permute-start | bytes 479240 | tf_op jit(solution)/shard_map/ppermute | solution.py:316
  37.8 3.1 %collective-permute-start.6 = (bf16[576,128]{1,0:T(8,128)(2,1)S(1)}, bf16[576,128]{1,0:T(8,128)(2,1)S(1)}, u32[]{:S(2)}, u32[]{:S(2)}) collective-permute-start(bf16[576,128]{1,0:T(8,128)(2,1)S(1)} %get-tuple-element.36), channel_id=1, source_target_pairs={{0,1},{1,0},{2,3},{3,2},{4,5},{5,4},{6,7},{7,6},{8,9},{9,8},{10,11... | collective-permute-start | bytes 442376 | tf_op jit(solution)/shard_map/ppermute | solution.py:316
  42.0 1.0 shard_map.56.total_ref
  43.8 5.0 %collective-permute-start.8 = (bf16[672,128]{1,0:T(8,128)(2,1)S(1)}, bf16[672,128]{1,0:T(8,128)(2,1)S(1)}, u32[]{:S(2)}, u32[]{:S(2)}) collective-permute-start(bf16[672,128]{1,0:T(8,128)(2,1)S(1)} %get-tuple-element.39), channel_id=1, source_target_pairs={{0,15},{1,2},{2,1},{3,4},{4,3},{5,6},{6,5},{7,8},{8,7},{9,10},{10,... | collective-permute-start | bytes 516104 | tf_op jit(solution)/shard_map/ppermute | solution.py:316
  48.8 2.5 %collective-permute-start.9 = (bf16[672,128]{1,0:T(8,128)(2,1)S(1)}, bf16[672,128]{1,0:T(8,128)(2,1)S(1)}, u32[]{:S(2)}, u32[]{:S(2)}) collective-permute-start(bf16[672,128]{1,0:T(8,128)(2,1)S(1)} %get-tuple-element.40), channel_id=1, source_target_pairs={{0,16},{16,0},{32,48},{48,32},{64,80},{80,64},{96,112},{112,96},{1... | collective-permute-start | bytes 516104 | tf_op jit(solution)/shard_map/ppermute | solution.py:316
  51.3 3.8 %collective-permute-start.11 = (bf16[624,128]{1,0:T(8,128)(2,1)S(1)}, bf16[624,128]{1,0:T(8,128)(2,1)S(1)}, u32[]{:S(2)}, u32[]{:S(2)}) collective-permute-start(bf16[624,128]{1,0:T(8,128)(2,1)S(1)} %get-tuple-element.42), channel_id=1, source_target_pairs={{0,240},{16,32},{32,16},{48,64},{64,48},{80,96},{96,80},{112,128},... | collective-permute-start | bytes 479240 | tf_op jit(solution)/shard_map/ppermute | solution.py:316
  55.1 4.0 %collective-permute-start.10 = (bf16[576,128]{1,0:T(8,128)(2,1)S(1)}, bf16[576,128]{1,0:T(8,128)(2,1)S(1)}, u32[]{:S(2)}, u32[]{:S(2)}) collective-permute-start(bf16[576,128]{1,0:T(8,128)(2,1)S(1)} %get-tuple-element.41), channel_id=1, source_target_pairs={{0,1},{1,0},{2,3},{3,2},{4,5},{5,4},{6,7},{7,6},{8,9},{9,8},{10,11... | collective-permute-start | bytes 442376 | tf_op jit(solution)/shard_map/ppermute | solution.py:316
  61.9 2.0 %collective-permute-start.12 = (bf16[672,128]{1,0:T(8,128)(2,1)S(1)}, bf16[672,128]{1,0:T(8,128)(2,1)S(1)}, u32[]{:S(2)}, u32[]{:S(2)}) collective-permute-start(bf16[672,128]{1,0:T(8,128)(2,1)S(1)} %get-tuple-element.44), channel_id=1, source_target_pairs={{0,15},{1,2},{2,1},{3,4},{4,3},{5,6},{6,5},{7,8},{8,7},{9,10},{10,... | collective-permute-start | bytes 516104 | tf_op jit(solution)/shard_map/ppermute | solution.py:316
  63.9 1.9 %collective-permute-start.13 = (bf16[672,128]{1,0:T(8,128)(2,1)S(1)}, bf16[672,128]{1,0:T(8,128)(2,1)S(1)}, u32[]{:S(2)}, u32[]{:S(2)}) collective-permute-start(bf16[672,128]{1,0:T(8,128)(2,1)S(1)} %get-tuple-element.45), channel_id=1, source_target_pairs={{0,16},{16,0},{32,48},{48,32},{64,80},{80,64},{96,112},{112,96},{1... | collective-permute-start | bytes 516104 | tf_op jit(solution)/shard_map/ppermute | solution.py:316
  65.8 3.9 %collective-permute-start.15 = (bf16[624,128]{1,0:T(8,128)(2,1)S(1)}, bf16[624,128]{1,0:T(8,128)(2,1)S(1)}, u32[]{:S(2)}, u32[]{:S(2)}) collective-permute-start(bf16[624,128]{1,0:T(8,128)(2,1)S(1)} %get-tuple-element.47), channel_id=1, source_target_pairs={{0,240},{16,32},{32,16},{48,64},{64,48},{80,96},{96,80},{112,128},... | collective-permute-start | bytes 479240 | tf_op jit(solution)/shard_map/ppermute | solution.py:316
  69.7 4.0 %collective-permute-start.14 = (bf16[576,128]{1,0:T(8,128)(2,1)S(1)}, bf16[576,128]{1,0:T(8,128)(2,1)S(1)}, u32[]{:S(2)}, u32[]{:S(2)}) collective-permute-start(bf16[576,128]{1,0:T(8,128)(2,1)S(1)} %get-tuple-element.46), channel_id=1, source_target_pairs={{0,1},{1,0},{2,3},{3,2},{4,5},{5,4},{6,7},{7,6},{8,9},{9,8},{10,11... | collective-permute-start | bytes 442376 | tf_op jit(solution)/shard_map/ppermute | solution.py:316
  74.6 1.0 shard_map.62.total_ref
  76.4 2.9 %collective-permute-start.16 = (bf16[8,12288]{1,0:T(8,128)(2,1)S(1)}, bf16[8,12288]{1,0:T(8,128)(2,1)S(1)}, u32[]{:S(2)}, u32[]{:S(2)}) collective-permute-start(bf16[8,12288]{1,0:T(8,128)(2,1)S(1)} %convert_element_type.43), channel_id=1, source_target_pairs={{0,256},{256,0},{1,257},{257,1},{2,258},{258,2},{3,259},{259,3},{4... | collective-permute-start | bytes 589832 | tf_op jit(solution)/shard_map/ppermute | solution.py:335
  80.3 4.1 %collective-permute-done.16 = bf16[8,12288]{1,0:T(8,128)(2,1)S(1)} collective-permute-done((bf16[8,12288]{1,0:T(8,128)(2,1)S(1)}, bf16[8,12288]{1,0:T(8,128)(2,1)S(1)}, u32[]{:S(2)}, u32[]{:S(2)}) %collective-permute-start.16) | collective-permute-done | bytes 196640 | tf_op jit(solution)/shard_map/ppermute | solution.py:335
  85.4 18.2 %all_to_all.20 = f16[16,16,128]{2,1,0:T(8,128)(2,1)S(1)} all-to-all(f16[16,16,128]{2,1,0:T(8,128)(2,1)S(1)} %broadcast_in_dim.8), channel_id=1, replica_groups=mesh['band'=2,'dx'=16,'dy'=16] {'dx'}, dimensions={0} | all-to-all | bytes 131072 | tf_op jit(solution)/shard_map/all_to_all | solution.py:330
  103.6 15.7 %all_to_all.21 = f16[16,16,128]{2,1,0:T(8,128)(2,1)S(1)} all-to-all(f16[16,16,128]{2,1,0:T(8,128)(2,1)S(1)} %broadcast_in_dim.9), channel_id=1, replica_groups=mesh['band'=2,'dx'=16,'dy'=16] {'dy'}, dimensions={0} | all-to-all | bytes 131072 | tf_op jit(solution)/shard_map/all_to_all | solution.py:330
  119.3 1.0 fusion
  120.3 2.2 %collective-permute-start.18 = (bf16[8,12288]{1,0:T(8,128)(2,1)S(1)}, bf16[8,12288]{1,0:T(8,128)(2,1)S(1)}, u32[]{:S(2)}, u32[]{:S(2)}) collective-permute-start(bf16[8,12288]{1,0:T(8,128)(2,1)S(1)} %get-tuple-element.54), channel_id=1, source_target_pairs={{0,256},{256,0},{1,257},{257,1},{2,258},{258,2},{3,259},{259,3},{4... | collective-permute-start | bytes 589832 | tf_op jit(solution)/shard_map/ppermute | solution.py:335
  122.5 3.1 %collective-permute-start.17 = (bf16[8,12288]{1,0:T(8,128)(2,1)S(1)}, bf16[8,12288]{1,0:T(8,128)(2,1)S(1)}, u32[]{:S(2)}, u32[]{:S(2)}) collective-permute-start(bf16[8,12288]{1,0:T(8,128)(2,1)S(1)} %get-tuple-element.55), channel_id=1, source_target_pairs={{0,256},{256,0},{1,257},{257,1},{2,258},{258,2},{3,259},{259,3},{4... | collective-permute-start | bytes 589832 | tf_op jit(solution)/shard_map/ppermute | solution.py:335
  125.6 2.6 %collective-permute-done.18 = bf16[8,12288]{1,0:T(8,128)(2,1)S(1)} collective-permute-done((bf16[8,12288]{1,0:T(8,128)(2,1)S(1)}, bf16[8,12288]{1,0:T(8,128)(2,1)S(1)}, u32[]{:S(2)}, u32[]{:S(2)}) %collective-permute-start.18) | collective-permute-done | bytes 196640 | tf_op jit(solution)/shard_map/ppermute | solution.py:335
  128.3 4.2 %collective-permute-done.17 = bf16[8,12288]{1,0:T(8,128)(2,1)S(1)} collective-permute-done((bf16[8,12288]{1,0:T(8,128)(2,1)S(1)}, bf16[8,12288]{1,0:T(8,128)(2,1)S(1)}, u32[]{:S(2)}, u32[]{:S(2)}) %collective-permute-start.17) | collective-permute-done | bytes 196640 | tf_op jit(solution)/shard_map/ppermute | solution.py:335
  133.3 14.2 %all_to_all.22 = f32[16,8,128]{2,1,0:T(8,128)S(1)} all-to-all(f32[16,8,128]{2,1,0:T(8,128)S(1)} %broadcast_in_dim.10), channel_id=1, replica_groups=mesh['band'=2,'dx'=16,'dy'=16] {'dx'}, dimensions={0} | all-to-all | bytes 131072 | tf_op jit(solution)/shard_map/all_to_all | solution.py:330
  148.2 5.9 %all-to-all-start.3 = ((f32[16,8,128]{2,1,0:T(8,128)}), f32[16,8,128]{2,1,0:T(8,128)S(1)}, u32[]{:S(2)}, u32[]{:S(2)}) async-start(f32[16,8,128]{2,1,0:T(8,128)} %broadcast_in_dim.11), calls=%async_computation.3 | async-start | bytes 131072 | tf_op jit(solution)/shard_map/all_to_all | solution.py:330
  154.8 6.6 %all-to-all-done.3 = f32[16,8,128]{2,1,0:T(8,128)S(1)} async-done(((f32[16,8,128]{2,1,0:T(8,128)}), f32[16,8,128]{2,1,0:T(8,128)S(1)}, u32[]{:S(2)}, u32[]{:S(2)}) %all-to-all-start.3) | async-done | bytes 65568 | tf_op jit(solution)/shard_map/all_to_all | solution.py:330
  (54 shorter events, 14.6 us)
Async XLA Ops:
  0.7 1.0 copy-start
  2.6 26.3 %collective-permute-start = (bf16[672,128]{1,0:T(8,128)(2,1)S(1)}, bf16[672,128]{1,0:T(8,128)(2,1)S(1)}, u32[]{:S(2)}, u32[]{:S(2)}) collective-permute-start(bf16[672,128]{1,0:T(8,128)(2,1)S(1)} %get-tuple-element.29), channel_id=1, source_target_pairs={{0,15},{1,2},{2,1},{3,4},{4,3},{5,6},{6,5},{7,8},{8,7},{9,10},{10,... | collective-permute-start | bytes 516104 | tf_op jit(solution)/shard_map/ppermute | solution.py:316
  8.6 20.2 %collective-permute-start.1 = (bf16[672,128]{1,0:T(8,128)(2,1)S(1)}, bf16[672,128]{1,0:T(8,128)(2,1)S(1)}, u32[]{:S(2)}, u32[]{:S(2)}) collective-permute-start(bf16[672,128]{1,0:T(8,128)(2,1)S(1)} %get-tuple-element.30), channel_id=1, source_target_pairs={{0,16},{16,0},{32,48},{48,32},{64,80},{80,64},{96,112},{112,96},{1... | collective-permute-start | bytes 516104 | tf_op jit(solution)/shard_map/ppermute | solution.py:316
  12.2 17.7 %collective-permute-start.3 = (bf16[624,128]{1,0:T(8,128)(2,1)S(1)}, bf16[624,128]{1,0:T(8,128)(2,1)S(1)}, u32[]{:S(2)}, u32[]{:S(2)}) collective-permute-start(bf16[624,128]{1,0:T(8,128)(2,1)S(1)} %get-tuple-element.32), channel_id=1, source_target_pairs={{0,240},{16,32},{32,16},{48,64},{64,48},{80,96},{96,80},{112,128},... | collective-permute-start | bytes 479240 | tf_op jit(solution)/shard_map/ppermute | solution.py:316
  22.4 6.4 %collective-permute-start.2 = (bf16[576,128]{1,0:T(8,128)(2,1)S(1)}, bf16[576,128]{1,0:T(8,128)(2,1)S(1)}, u32[]{:S(2)}, u32[]{:S(2)}) collective-permute-start(bf16[576,128]{1,0:T(8,128)(2,1)S(1)} %get-tuple-element.31), channel_id=1, source_target_pairs={{0,1},{1,0},{2,3},{3,2},{4,5},{5,4},{6,7},{7,6},{8,9},{9,8},{10,11... | collective-permute-start | bytes 442376 | tf_op jit(solution)/shard_map/ppermute | solution.py:316
  27.2 0.8 copy-start.1
  30.6 11.4 %collective-permute-start.4 = (bf16[672,128]{1,0:T(8,128)(2,1)S(1)}, bf16[672,128]{1,0:T(8,128)(2,1)S(1)}, u32[]{:S(2)}, u32[]{:S(2)}) collective-permute-start(bf16[672,128]{1,0:T(8,128)(2,1)S(1)} %get-tuple-element.34), channel_id=1, source_target_pairs={{0,15},{1,2},{2,1},{3,4},{4,3},{5,6},{6,5},{7,8},{8,7},{9,10},{10,... | collective-permute-start | bytes 516104 | tf_op jit(solution)/shard_map/ppermute | solution.py:316
  32.6 9.4 %collective-permute-start.5 = (bf16[672,128]{1,0:T(8,128)(2,1)S(1)}, bf16[672,128]{1,0:T(8,128)(2,1)S(1)}, u32[]{:S(2)}, u32[]{:S(2)}) collective-permute-start(bf16[672,128]{1,0:T(8,128)(2,1)S(1)} %get-tuple-element.35), channel_id=1, source_target_pairs={{0,16},{16,0},{32,48},{48,32},{64,80},{80,64},{96,112},{112,96},{1... | collective-permute-start | bytes 516104 | tf_op jit(solution)/shard_map/ppermute | solution.py:316
  34.5 8.5 %collective-permute-start.7 = (bf16[624,128]{1,0:T(8,128)(2,1)S(1)}, bf16[624,128]{1,0:T(8,128)(2,1)S(1)}, u32[]{:S(2)}, u32[]{:S(2)}) collective-permute-start(bf16[624,128]{1,0:T(8,128)(2,1)S(1)} %get-tuple-element.37), channel_id=1, source_target_pairs={{0,240},{16,32},{32,16},{48,64},{64,48},{80,96},{96,80},{112,128},... | collective-permute-start | bytes 479240 | tf_op jit(solution)/shard_map/ppermute | solution.py:316
  37.8 4.1 %collective-permute-start.6 = (bf16[576,128]{1,0:T(8,128)(2,1)S(1)}, bf16[576,128]{1,0:T(8,128)(2,1)S(1)}, u32[]{:S(2)}, u32[]{:S(2)}) collective-permute-start(bf16[576,128]{1,0:T(8,128)(2,1)S(1)} %get-tuple-element.36), channel_id=1, source_target_pairs={{0,1},{1,0},{2,3},{3,2},{4,5},{5,4},{6,7},{7,6},{8,9},{9,8},{10,11... | collective-permute-start | bytes 442376 | tf_op jit(solution)/shard_map/ppermute | solution.py:316
  43.8 16.4 %collective-permute-start.8 = (bf16[672,128]{1,0:T(8,128)(2,1)S(1)}, bf16[672,128]{1,0:T(8,128)(2,1)S(1)}, u32[]{:S(2)}, u32[]{:S(2)}) collective-permute-start(bf16[672,128]{1,0:T(8,128)(2,1)S(1)} %get-tuple-element.39), channel_id=1, source_target_pairs={{0,15},{1,2},{2,1},{3,4},{4,3},{5,6},{6,5},{7,8},{8,7},{9,10},{10,... | collective-permute-start | bytes 516104 | tf_op jit(solution)/shard_map/ppermute | solution.py:316
  48.8 11.3 %collective-permute-start.9 = (bf16[672,128]{1,0:T(8,128)(2,1)S(1)}, bf16[672,128]{1,0:T(8,128)(2,1)S(1)}, u32[]{:S(2)}, u32[]{:S(2)}) collective-permute-start(bf16[672,128]{1,0:T(8,128)(2,1)S(1)} %get-tuple-element.40), channel_id=1, source_target_pairs={{0,16},{16,0},{32,48},{48,32},{64,80},{80,64},{96,112},{112,96},{1... | collective-permute-start | bytes 516104 | tf_op jit(solution)/shard_map/ppermute | solution.py:316
  51.3 9.8 %collective-permute-start.11 = (bf16[624,128]{1,0:T(8,128)(2,1)S(1)}, bf16[624,128]{1,0:T(8,128)(2,1)S(1)}, u32[]{:S(2)}, u32[]{:S(2)}) collective-permute-start(bf16[624,128]{1,0:T(8,128)(2,1)S(1)} %get-tuple-element.42), channel_id=1, source_target_pairs={{0,240},{16,32},{32,16},{48,64},{64,48},{80,96},{96,80},{112,128},... | collective-permute-start | bytes 479240 | tf_op jit(solution)/shard_map/ppermute | solution.py:316
  55.1 5.0 %collective-permute-start.10 = (bf16[576,128]{1,0:T(8,128)(2,1)S(1)}, bf16[576,128]{1,0:T(8,128)(2,1)S(1)}, u32[]{:S(2)}, u32[]{:S(2)}) collective-permute-start(bf16[576,128]{1,0:T(8,128)(2,1)S(1)} %get-tuple-element.41), channel_id=1, source_target_pairs={{0,1},{1,0},{2,3},{3,2},{4,5},{5,4},{6,7},{7,6},{8,9},{9,8},{10,11... | collective-permute-start | bytes 442376 | tf_op jit(solution)/shard_map/ppermute | solution.py:316
  60.0 19.4 %copy-start.2 = (bf16[128,12,8,128]{3,2,1,0:T(8,128)(2,1)S(1)}, bf16[128,12,8,128]{3,2,1,0:T(8,128)(2,1)}, u32[]{:S(2)}) copy-start(bf16[128,12,8,128]{3,2,1,0:T(8,128)(2,1)} %param.5) | copy-start | bytes 9437188
  61.9 12.8 %collective-permute-start.12 = (bf16[672,128]{1,0:T(8,128)(2,1)S(1)}, bf16[672,128]{1,0:T(8,128)(2,1)S(1)}, u32[]{:S(2)}, u32[]{:S(2)}) collective-permute-start(bf16[672,128]{1,0:T(8,128)(2,1)S(1)} %get-tuple-element.44), channel_id=1, source_target_pairs={{0,15},{1,2},{2,1},{3,4},{4,3},{5,6},{6,5},{7,8},{8,7},{9,10},{10,... | collective-permute-start | bytes 516104 | tf_op jit(solution)/shard_map/ppermute | solution.py:316
  63.9 10.8 %collective-permute-start.13 = (bf16[672,128]{1,0:T(8,128)(2,1)S(1)}, bf16[672,128]{1,0:T(8,128)(2,1)S(1)}, u32[]{:S(2)}, u32[]{:S(2)}) collective-permute-start(bf16[672,128]{1,0:T(8,128)(2,1)S(1)} %get-tuple-element.45), channel_id=1, source_target_pairs={{0,16},{16,0},{32,48},{48,32},{64,80},{80,64},{96,112},{112,96},{1... | collective-permute-start | bytes 516104 | tf_op jit(solution)/shard_map/ppermute | solution.py:316
  65.8 9.8 %collective-permute-start.15 = (bf16[624,128]{1,0:T(8,128)(2,1)S(1)}, bf16[624,128]{1,0:T(8,128)(2,1)S(1)}, u32[]{:S(2)}, u32[]{:S(2)}) collective-permute-start(bf16[624,128]{1,0:T(8,128)(2,1)S(1)} %get-tuple-element.47), channel_id=1, source_target_pairs={{0,240},{16,32},{32,16},{48,64},{64,48},{80,96},{96,80},{112,128},... | collective-permute-start | bytes 479240 | tf_op jit(solution)/shard_map/ppermute | solution.py:316
  69.7 5.0 %collective-permute-start.14 = (bf16[576,128]{1,0:T(8,128)(2,1)S(1)}, bf16[576,128]{1,0:T(8,128)(2,1)S(1)}, u32[]{:S(2)}, u32[]{:S(2)}) collective-permute-start(bf16[576,128]{1,0:T(8,128)(2,1)S(1)} %get-tuple-element.46), channel_id=1, source_target_pairs={{0,1},{1,0},{2,3},{3,2},{4,5},{5,4},{6,7},{7,6},{8,9},{9,8},{10,11... | collective-permute-start | bytes 442376 | tf_op jit(solution)/shard_map/ppermute | solution.py:316
  76.4 8.0 %collective-permute-start.16 = (bf16[8,12288]{1,0:T(8,128)(2,1)S(1)}, bf16[8,12288]{1,0:T(8,128)(2,1)S(1)}, u32[]{:S(2)}, u32[]{:S(2)}) collective-permute-start(bf16[8,12288]{1,0:T(8,128)(2,1)S(1)} %convert_element_type.43), channel_id=1, source_target_pairs={{0,256},{256,0},{1,257},{257,1},{2,258},{258,2},{3,259},{259,3},{4... | collective-permute-start | bytes 589832 | tf_op jit(solution)/shard_map/ppermute | solution.py:335
  120.3 7.9 %collective-permute-start.18 = (bf16[8,12288]{1,0:T(8,128)(2,1)S(1)}, bf16[8,12288]{1,0:T(8,128)(2,1)S(1)}, u32[]{:S(2)}, u32[]{:S(2)}) collective-permute-start(bf16[8,12288]{1,0:T(8,128)(2,1)S(1)} %get-tuple-element.54), channel_id=1, source_target_pairs={{0,256},{256,0},{1,257},{257,1},{2,258},{258,2},{3,259},{259,3},{4... | collective-permute-start | bytes 589832 | tf_op jit(solution)/shard_map/ppermute | solution.py:335
  122.5 9.9 %collective-permute-start.17 = (bf16[8,12288]{1,0:T(8,128)(2,1)S(1)}, bf16[8,12288]{1,0:T(8,128)(2,1)S(1)}, u32[]{:S(2)}, u32[]{:S(2)}) collective-permute-start(bf16[8,12288]{1,0:T(8,128)(2,1)S(1)} %get-tuple-element.55), channel_id=1, source_target_pairs={{0,256},{256,0},{1,257},{257,1},{2,258},{258,2},{3,259},{259,3},{4... | collective-permute-start | bytes 589832 | tf_op jit(solution)/shard_map/ppermute | solution.py:335
  148.2 13.2 %all-to-all-start.3 = ((f32[16,8,128]{2,1,0:T(8,128)}), f32[16,8,128]{2,1,0:T(8,128)S(1)}, u32[]{:S(2)}, u32[]{:S(2)}) async-start(f32[16,8,128]{2,1,0:T(8,128)} %broadcast_in_dim.11), calls=%async_computation.3 | async-start | bytes 131072 | tf_op jit(solution)/shard_map/all_to_all | solution.py:330

commit v11 on v10

--- a/solution.py
+++ b/solution.py
@@ -119,7 +119,7 @@
                 total = total + weights[k] * sum(near[1:], near[0])
         return total
 
-    @pl.loop(0, size_y)
+    @pl.loop(0, size_y, unroll=4)
     def _(y):
         line = [field_ref[x, y] for x in range(size_x)]
         for x in range(size_x):
@@ -129,7 +129,7 @@
                 total = total - previous_ref[x, y]
             total_ref[x, y] = inside(total, line, x)
 
-    @pl.loop(0, size_x)
+    @pl.loop(0, size_x, unroll=4)
     def _(x):
         line = [field_ref[x, y] for y in range(size_y)]
         for y in range(size_y):
@@ -139,7 +139,7 @@
 def add_side(right, halo, source, weights, store):
     size_x, size_y = source.shape[:2]
 
-    @pl.loop(0, size_y)
+    @pl.loop(0, size_y, unroll=4)
     def _(y):
         line = [halo[k, y] for k in range(WIDTH)]
         for i in range(WIDTH):
@@ -162,7 +162,7 @@
     odd_x = parity_ref[0]
     unpack(x_even, halo_x, 0, 0, odd_x * (WIDTH - 1))
 
-    @pl.loop(0, size_x)
+    @pl.loop(0, size_x, unroll=4)
     def _(x):
         line = [halo_y[x, k] for k in range(2 * WIDTH)]
         for y in range(size_y):
@@ -201,7 +201,7 @@
             outs[0][x, y] = total
 
     def keep(first):
-        @pl.loop(0, size_y)
+        @pl.loop(0, size_y, unroll=4)
         def _(y):
             for x in range(first, first + size_x - WIDTH):
                 store(x, y, total_ref[x, y])

time: 163 us -> 163 us (level)
  no operation moved by 1% of the time
where the time goes in v11:
time: 163 us; the launch traced here: 162 us
  starting transfers between devices  76.5 us (47%)
  blocking collectives  48.2 us (30%)
  waiting for transfers between devices  18.2 us (11%)
  Pallas kernels  10 us (6%)
  local copies, waits for them, and re-layouts  3.41 us (2%)
  matrix products  3.39 us (2%)
    ppermute x16, starting transfers between devices, swapped(): lax.ppermute(values, axis, [(i, (i + step(i)) % count) for i in range(cou...  62.4 us
    all_to_all x3, blocking collectives, sum_over_grid(): lax.all_to_all(sent, axis, 0, 0).astype(jnp.float32)  48.2 us
    ppermute x3, waiting for transfers between devices, other_band(): return lax.ppermute(values, 'band', [(0, 1), (1, 0)])  10.9 us
    ppermute x3, starting transfers between devices, other_band(): return lax.ppermute(values, 'band', [(0, 1), (1, 0)])  8.31 us
    all_to_all x1, waiting for transfers between devices, sum_over_grid(): lax.all_to_all(sent, axis, 0, 0).astype(jnp.float32)  6.57 us
    all_to_all x1, starting transfers between devices, sum_over_grid(): lax.all_to_all(sent, axis, 0, 0).astype(jnp.float32)  5.86 us
    pallas_call x4, Pallas kernels, filter_step(): pl.pallas_call(functools.partial(outer_first_kernel, factor), out_shape=f...  3.4 us
  transfers between devices with their start and end apart: 20, of which 7 were waited for; matrix products, arithmetic and copies ran while one was open for 1% of the time, Pallas kernels for 4%

profile of v11, /device:TPU:1, one launch (start us, length us, event | category | flops | bytes accessed | tf_op | source)
XLA Modules:
  0.0 161.8 jit_solution(3976202443104931862)
XLA Ops:
  0.7 1.0 copy-done
  2.6 6.0 %collective-permute-start = (bf16[672,128]{1,0:T(8,128)(2,1)S(1)}, bf16[672,128]{1,0:T(8,128)(2,1)S(1)}, u32[]{:S(2)}, u32[]{:S(2)}) collective-permute-start(bf16[672,128]{1,0:T(8,128)(2,1)S(1)} %get-tuple-element.29), channel_id=1, source_target_pairs={{0,15},{1,2},{2,1},{3,4},{4,3},{5,6},{6,5},{7,8},{8,7},{9,10},{10,... | collective-permute-start | bytes 516104 | tf_op jit(solution)/shard_map/ppermute | solution.py:316
  8.6 3.5 %collective-permute-start.1 = (bf16[672,128]{1,0:T(8,128)(2,1)S(1)}, bf16[672,128]{1,0:T(8,128)(2,1)S(1)}, u32[]{:S(2)}, u32[]{:S(2)}) collective-permute-start(bf16[672,128]{1,0:T(8,128)(2,1)S(1)} %get-tuple-element.30), channel_id=1, source_target_pairs={{0,16},{16,0},{32,48},{48,32},{64,80},{80,64},{96,112},{112,96},{1... | collective-permute-start | bytes 516104 | tf_op jit(solution)/shard_map/ppermute | solution.py:316
  12.2 10.2 %collective-permute-start.3 = (bf16[624,128]{1,0:T(8,128)(2,1)S(1)}, bf16[624,128]{1,0:T(8,128)(2,1)S(1)}, u32[]{:S(2)}, u32[]{:S(2)}) collective-permute-start(bf16[624,128]{1,0:T(8,128)(2,1)S(1)} %get-tuple-element.32), channel_id=1, source_target_pairs={{0,240},{16,32},{32,16},{48,64},{64,48},{80,96},{96,80},{112,128},... | collective-permute-start | bytes 479240 | tf_op jit(solution)/shard_map/ppermute | solution.py:316
  22.4 4.8 %collective-permute-start.2 = (bf16[576,128]{1,0:T(8,128)(2,1)S(1)}, bf16[576,128]{1,0:T(8,128)(2,1)S(1)}, u32[]{:S(2)}, u32[]{:S(2)}) collective-permute-start(bf16[576,128]{1,0:T(8,128)(2,1)S(1)} %get-tuple-element.31), channel_id=1, source_target_pairs={{0,1},{1,0},{2,3},{3,2},{4,5},{5,4},{6,7},{7,6},{8,9},{9,8},{10,11... | collective-permute-start | bytes 442376 | tf_op jit(solution)/shard_map/ppermute | solution.py:316
  28.8 0.9 shard_map.53.total_ref
  30.4 1.9 %collective-permute-start.4 = (bf16[672,128]{1,0:T(8,128)(2,1)S(1)}, bf16[672,128]{1,0:T(8,128)(2,1)S(1)}, u32[]{:S(2)}, u32[]{:S(2)}) collective-permute-start(bf16[672,128]{1,0:T(8,128)(2,1)S(1)} %get-tuple-element.34), channel_id=1, source_target_pairs={{0,15},{1,2},{2,1},{3,4},{4,3},{5,6},{6,5},{7,8},{8,7},{9,10},{10,... | collective-permute-start | bytes 516104 | tf_op jit(solution)/shard_map/ppermute | solution.py:316
  32.3 1.9 %collective-permute-start.5 = (bf16[672,128]{1,0:T(8,128)(2,1)S(1)}, bf16[672,128]{1,0:T(8,128)(2,1)S(1)}, u32[]{:S(2)}, u32[]{:S(2)}) collective-permute-start(bf16[672,128]{1,0:T(8,128)(2,1)S(1)} %get-tuple-element.35), channel_id=1, source_target_pairs={{0,16},{16,0},{32,48},{48,32},{64,80},{80,64},{96,112},{112,96},{1... | collective-permute-start | bytes 516104 | tf_op jit(solution)/shard_map/ppermute | solution.py:316
  34.2 3.4 %collective-permute-start.7 = (bf16[624,128]{1,0:T(8,128)(2,1)S(1)}, bf16[624,128]{1,0:T(8,128)(2,1)S(1)}, u32[]{:S(2)}, u32[]{:S(2)}) collective-permute-start(bf16[624,128]{1,0:T(8,128)(2,1)S(1)} %get-tuple-element.37), channel_id=1, source_target_pairs={{0,240},{16,32},{32,16},{48,64},{64,48},{80,96},{96,80},{112,128},... | collective-permute-start | bytes 479240 | tf_op jit(solution)/shard_map/ppermute | solution.py:316
  37.6 3.1 %collective-permute-start.6 = (bf16[576,128]{1,0:T(8,128)(2,1)S(1)}, bf16[576,128]{1,0:T(8,128)(2,1)S(1)}, u32[]{:S(2)}, u32[]{:S(2)}) collective-permute-start(bf16[576,128]{1,0:T(8,128)(2,1)S(1)} %get-tuple-element.36), channel_id=1, source_target_pairs={{0,1},{1,0},{2,3},{3,2},{4,5},{5,4},{6,7},{7,6},{8,9},{9,8},{10,11... | collective-permute-start | bytes 442376 | tf_op jit(solution)/shard_map/ppermute | solution.py:316
  43.3 5.2 %collective-permute-start.8 = (bf16[672,128]{1,0:T(8,128)(2,1)S(1)}, bf16[672,128]{1,0:T(8,128)(2,1)S(1)}, u32[]{:S(2)}, u32[]{:S(2)}) collective-permute-start(bf16[672,128]{1,0:T(8,128)(2,1)S(1)} %get-tuple-element.39), channel_id=1, source_target_pairs={{0,15},{1,2},{2,1},{3,4},{4,3},{5,6},{6,5},{7,8},{8,7},{9,10},{10,... | collective-permute-start | bytes 516104 | tf_op jit(solution)/shard_map/ppermute | solution.py:316
  48.5 2.4 %collective-permute-start.9 = (bf16[672,128]{1,0:T(8,128)(2,1)S(1)}, bf16[672,128]{1,0:T(8,128)(2,1)S(1)}, u32[]{:S(2)}, u32[]{:S(2)}) collective-permute-start(bf16[672,128]{1,0:T(8,128)(2,1)S(1)} %get-tuple-element.40), channel_id=1, source_target_pairs={{0,16},{16,0},{32,48},{48,32},{64,80},{80,64},{96,112},{112,96},{1... | collective-permute-start | bytes 516104 | tf_op jit(solution)/shard_map/ppermute | solution.py:316
  50.9 3.8 %collective-permute-start.11 = (bf16[624,128]{1,0:T(8,128)(2,1)S(1)}, bf16[624,128]{1,0:T(8,128)(2,1)S(1)}, u32[]{:S(2)}, u32[]{:S(2)}) collective-permute-start(bf16[624,128]{1,0:T(8,128)(2,1)S(1)} %get-tuple-element.42), channel_id=1, source_target_pairs={{0,240},{16,32},{32,16},{48,64},{64,48},{80,96},{96,80},{112,128},... | collective-permute-start | bytes 479240 | tf_op jit(solution)/shard_map/ppermute | solution.py:316
  54.8 3.9 %collective-permute-start.10 = (bf16[576,128]{1,0:T(8,128)(2,1)S(1)}, bf16[576,128]{1,0:T(8,128)(2,1)S(1)}, u32[]{:S(2)}, u32[]{:S(2)}) collective-permute-start(bf16[576,128]{1,0:T(8,128)(2,1)S(1)} %get-tuple-element.41), channel_id=1, source_target_pairs={{0,1},{1,0},{2,3},{3,2},{4,5},{5,4},{6,7},{7,6},{8,9},{9,8},{10,11... | collective-permute-start | bytes 442376 | tf_op jit(solution)/shard_map/ppermute | solution.py:316
  61.3 2.2 %collective-permute-start.12 = (bf16[672,128]{1,0:T(8,128)(2,1)S(1)}, bf16[672,128]{1,0:T(8,128)(2,1)S(1)}, u32[]{:S(2)}, u32[]{:S(2)}) collective-permute-start(bf16[672,128]{1,0:T(8,128)(2,1)S(1)} %get-tuple-element.44), channel_id=1, source_target_pairs={{0,15},{1,2},{2,1},{3,4},{4,3},{5,6},{6,5},{7,8},{8,7},{9,10},{10,... | collective-permute-start | bytes 516104 | tf_op jit(solution)/shard_map/ppermute | solution.py:316
  63.4 1.9 %collective-permute-start.13 = (bf16[672,128]{1,0:T(8,128)(2,1)S(1)}, bf16[672,128]{1,0:T(8,128)(2,1)S(1)}, u32[]{:S(2)}, u32[]{:S(2)}) collective-permute-start(bf16[672,128]{1,0:T(8,128)(2,1)S(1)} %get-tuple-element.45), channel_id=1, source_target_pairs={{0,16},{16,0},{32,48},{48,32},{64,80},{80,64},{96,112},{112,96},{1... | collective-permute-start | bytes 516104 | tf_op jit(solution)/shard_map/ppermute | solution.py:316
  65.4 4.1 %collective-permute-start.15 = (bf16[624,128]{1,0:T(8,128)(2,1)S(1)}, bf16[624,128]{1,0:T(8,128)(2,1)S(1)}, u32[]{:S(2)}, u32[]{:S(2)}) collective-permute-start(bf16[624,128]{1,0:T(8,128)(2,1)S(1)} %get-tuple-element.47), channel_id=1, source_target_pairs={{0,240},{16,32},{32,16},{48,64},{64,48},{80,96},{96,80},{112,128},... | collective-permute-start | bytes 479240 | tf_op jit(solution)/shard_map/ppermute | solution.py:316
  69.4 4.0 %collective-permute-start.14 = (bf16[576,128]{1,0:T(8,128)(2,1)S(1)}, bf16[576,128]{1,0:T(8,128)(2,1)S(1)}, u32[]{:S(2)}, u32[]{:S(2)}) collective-permute-start(bf16[576,128]{1,0:T(8,128)(2,1)S(1)} %get-tuple-element.46), channel_id=1, source_target_pairs={{0,1},{1,0},{2,3},{3,2},{4,5},{5,4},{6,7},{7,6},{8,9},{9,8},{10,11... | collective-permute-start | bytes 442376 | tf_op jit(solution)/shard_map/ppermute | solution.py:316
  76.0 3.0 %collective-permute-start.16 = (bf16[8,12288]{1,0:T(8,128)(2,1)S(1)}, bf16[8,12288]{1,0:T(8,128)(2,1)S(1)}, u32[]{:S(2)}, u32[]{:S(2)}) collective-permute-start(bf16[8,12288]{1,0:T(8,128)(2,1)S(1)} %convert_element_type.43), channel_id=1, source_target_pairs={{0,256},{256,0},{1,257},{257,1},{2,258},{258,2},{3,259},{259,3},{4... | collective-permute-start | bytes 589832 | tf_op jit(solution)/shard_map/ppermute | solution.py:335
  79.1 0.9 fusion.4
  80.0 4.0 %collective-permute-done.16 = bf16[8,12288]{1,0:T(8,128)(2,1)S(1)} collective-permute-done((bf16[8,12288]{1,0:T(8,128)(2,1)S(1)}, bf16[8,12288]{1,0:T(8,128)(2,1)S(1)}, u32[]{:S(2)}, u32[]{:S(2)}) %collective-permute-start.16) | collective-permute-done | bytes 196640 | tf_op jit(solution)/shard_map/ppermute | solution.py:335
  84.0 0.9 fusion.2
  85.0 17.6 %all_to_all.20 = f16[16,16,128]{2,1,0:T(8,128)(2,1)S(1)} all-to-all(f16[16,16,128]{2,1,0:T(8,128)(2,1)S(1)} %broadcast_in_dim.8), channel_id=1, replica_groups=mesh['band'=2,'dx'=16,'dy'=16] {'dx'}, dimensions={0} | all-to-all | bytes 131072 | tf_op jit(solution)/shard_map/all_to_all | solution.py:330
  102.6 16.5 %all_to_all.21 = f16[16,16,128]{2,1,0:T(8,128)(2,1)S(1)} all-to-all(f16[16,16,128]{2,1,0:T(8,128)(2,1)S(1)} %broadcast_in_dim.9), channel_id=1, replica_groups=mesh['band'=2,'dx'=16,'dy'=16] {'dy'}, dimensions={0} | all-to-all | bytes 131072 | tf_op jit(solution)/shard_map/all_to_all | solution.py:330
  119.1 1.0 fusion
  120.1 2.2 %collective-permute-start.18 = (bf16[8,12288]{1,0:T(8,128)(2,1)S(1)}, bf16[8,12288]{1,0:T(8,128)(2,1)S(1)}, u32[]{:S(2)}, u32[]{:S(2)}) collective-permute-start(bf16[8,12288]{1,0:T(8,128)(2,1)S(1)} %get-tuple-element.54), channel_id=1, source_target_pairs={{0,256},{256,0},{1,257},{257,1},{2,258},{258,2},{3,259},{259,3},{4... | collective-permute-start | bytes 589832 | tf_op jit(solution)/shard_map/ppermute | solution.py:335
  122.3 3.1 %collective-permute-start.17 = (bf16[8,12288]{1,0:T(8,128)(2,1)S(1)}, bf16[8,12288]{1,0:T(8,128)(2,1)S(1)}, u32[]{:S(2)}, u32[]{:S(2)}) collective-permute-start(bf16[8,12288]{1,0:T(8,128)(2,1)S(1)} %get-tuple-element.55), channel_id=1, source_target_pairs={{0,256},{256,0},{1,257},{257,1},{2,258},{258,2},{3,259},{259,3},{4... | collective-permute-start | bytes 589832 | tf_op jit(solution)/shard_map/ppermute | solution.py:335
  125.4 2.6 %collective-permute-done.18 = bf16[8,12288]{1,0:T(8,128)(2,1)S(1)} collective-permute-done((bf16[8,12288]{1,0:T(8,128)(2,1)S(1)}, bf16[8,12288]{1,0:T(8,128)(2,1)S(1)}, u32[]{:S(2)}, u32[]{:S(2)}) %collective-permute-start.18) | collective-permute-done | bytes 196640 | tf_op jit(solution)/shard_map/ppermute | solution.py:335
  128.0 4.2 %collective-permute-done.17 = bf16[8,12288]{1,0:T(8,128)(2,1)S(1)} collective-permute-done((bf16[8,12288]{1,0:T(8,128)(2,1)S(1)}, bf16[8,12288]{1,0:T(8,128)(2,1)S(1)}, u32[]{:S(2)}, u32[]{:S(2)}) %collective-permute-start.17) | collective-permute-done | bytes 196640 | tf_op jit(solution)/shard_map/ppermute | solution.py:335
  133.1 14.2 %all_to_all.22 = f32[16,8,128]{2,1,0:T(8,128)S(1)} all-to-all(f32[16,8,128]{2,1,0:T(8,128)S(1)} %broadcast_in_dim.10), channel_id=1, replica_groups=mesh['band'=2,'dx'=16,'dy'=16] {'dx'}, dimensions={0} | all-to-all | bytes 131072 | tf_op jit(solution)/shard_map/all_to_all | solution.py:330
  147.9 5.9 %all-to-all-start.3 = ((f32[16,8,128]{2,1,0:T(8,128)}), f32[16,8,128]{2,1,0:T(8,128)S(1)}, u32[]{:S(2)}, u32[]{:S(2)}) async-start(f32[16,8,128]{2,1,0:T(8,128)} %broadcast_in_dim.11), calls=%async_computation.3 | async-start | bytes 131072 | tf_op jit(solution)/shard_map/all_to_all | solution.py:330
  154.6 6.6 %all-to-all-done.3 = f32[16,8,128]{2,1,0:T(8,128)S(1)} async-done(((f32[16,8,128]{2,1,0:T(8,128)}), f32[16,8,128]{2,1,0:T(8,128)S(1)}, u32[]{:S(2)}, u32[]{:S(2)}) %all-to-all-start.3) | async-done | bytes 65568 | tf_op jit(solution)/shard_map/all_to_all | solution.py:330
  (54 shorter events, 13.9 us)
Async XLA Ops:
  0.7 1.0 copy-start
  2.6 26.2 %collective-permute-start = (bf16[672,128]{1,0:T(8,128)(2,1)S(1)}, bf16[672,128]{1,0:T(8,128)(2,1)S(1)}, u32[]{:S(2)}, u32[]{:S(2)}) collective-permute-start(bf16[672,128]{1,0:T(8,128)(2,1)S(1)} %get-tuple-element.29), channel_id=1, source_target_pairs={{0,15},{1,2},{2,1},{3,4},{4,3},{5,6},{6,5},{7,8},{8,7},{9,10},{10,... | collective-permute-start | bytes 516104 | tf_op jit(solution)/shard_map/ppermute | solution.py:316
  8.6 20.1 %collective-permute-start.1 = (bf16[672,128]{1,0:T(8,128)(2,1)S(1)}, bf16[672,128]{1,0:T(8,128)(2,1)S(1)}, u32[]{:S(2)}, u32[]{:S(2)}) collective-permute-start(bf16[672,128]{1,0:T(8,128)(2,1)S(1)} %get-tuple-element.30), channel_id=1, source_target_pairs={{0,16},{16,0},{32,48},{48,32},{64,80},{80,64},{96,112},{112,96},{1... | collective-permute-start | bytes 516104 | tf_op jit(solution)/shard_map/ppermute | solution.py:316
  12.2 17.5 %collective-permute-start.3 = (bf16[624,128]{1,0:T(8,128)(2,1)S(1)}, bf16[624,128]{1,0:T(8,128)(2,1)S(1)}, u32[]{:S(2)}, u32[]{:S(2)}) collective-permute-start(bf16[624,128]{1,0:T(8,128)(2,1)S(1)} %get-tuple-element.32), channel_id=1, source_target_pairs={{0,240},{16,32},{32,16},{48,64},{64,48},{80,96},{96,80},{112,128},... | collective-permute-start | bytes 479240 | tf_op jit(solution)/shard_map/ppermute | solution.py:316
  22.4 6.3 %collective-permute-start.2 = (bf16[576,128]{1,0:T(8,128)(2,1)S(1)}, bf16[576,128]{1,0:T(8,128)(2,1)S(1)}, u32[]{:S(2)}, u32[]{:S(2)}) collective-permute-start(bf16[576,128]{1,0:T(8,128)(2,1)S(1)} %get-tuple-element.31), channel_id=1, source_target_pairs={{0,1},{1,0},{2,3},{3,2},{4,5},{5,4},{6,7},{7,6},{8,9},{9,8},{10,11... | collective-permute-start | bytes 442376 | tf_op jit(solution)/shard_map/ppermute | solution.py:316
  27.2 0.8 copy-start.1
  30.4 11.4 %collective-permute-start.4 = (bf16[672,128]{1,0:T(8,128)(2,1)S(1)}, bf16[672,128]{1,0:T(8,128)(2,1)S(1)}, u32[]{:S(2)}, u32[]{:S(2)}) collective-permute-start(bf16[672,128]{1,0:T(8,128)(2,1)S(1)} %get-tuple-element.34), channel_id=1, source_target_pairs={{0,15},{1,2},{2,1},{3,4},{4,3},{5,6},{6,5},{7,8},{8,7},{9,10},{10,... | collective-permute-start | bytes 516104 | tf_op jit(solution)/shard_map/ppermute | solution.py:316
  32.3 9.4 %collective-permute-start.5 = (bf16[672,128]{1,0:T(8,128)(2,1)S(1)}, bf16[672,128]{1,0:T(8,128)(2,1)S(1)}, u32[]{:S(2)}, u32[]{:S(2)}) collective-permute-start(bf16[672,128]{1,0:T(8,128)(2,1)S(1)} %get-tuple-element.35), channel_id=1, source_target_pairs={{0,16},{16,0},{32,48},{48,32},{64,80},{80,64},{96,112},{112,96},{1... | collective-permute-start | bytes 516104 | tf_op jit(solution)/shard_map/ppermute | solution.py:316
  34.2 8.4 %collective-permute-start.7 = (bf16[624,128]{1,0:T(8,128)(2,1)S(1)}, bf16[624,128]{1,0:T(8,128)(2,1)S(1)}, u32[]{:S(2)}, u32[]{:S(2)}) collective-permute-start(bf16[624,128]{1,0:T(8,128)(2,1)S(1)} %get-tuple-element.37), channel_id=1, source_target_pairs={{0,240},{16,32},{32,16},{48,64},{64,48},{80,96},{96,80},{112,128},... | collective-permute-start | bytes 479240 | tf_op jit(solution)/shard_map/ppermute | solution.py:316
  37.6 4.1 %collective-permute-start.6 = (bf16[576,128]{1,0:T(8,128)(2,1)S(1)}, bf16[576,128]{1,0:T(8,128)(2,1)S(1)}, u32[]{:S(2)}, u32[]{:S(2)}) collective-permute-start(bf16[576,128]{1,0:T(8,128)(2,1)S(1)} %get-tuple-element.36), channel_id=1, source_target_pairs={{0,1},{1,0},{2,3},{3,2},{4,5},{5,4},{6,7},{7,6},{8,9},{9,8},{10,11... | collective-permute-start | bytes 442376 | tf_op jit(solution)/shard_map/ppermute | solution.py:316
  43.3 16.4 %collective-permute-start.8 = (bf16[672,128]{1,0:T(8,128)(2,1)S(1)}, bf16[672,128]{1,0:T(8,128)(2,1)S(1)}, u32[]{:S(2)}, u32[]{:S(2)}) collective-permute-start(bf16[672,128]{1,0:T(8,128)(2,1)S(1)} %get-tuple-element.39), channel_id=1, source_target_pairs={{0,15},{1,2},{2,1},{3,4},{4,3},{5,6},{6,5},{7,8},{8,7},{9,10},{10,... | collective-permute-start | bytes 516104 | tf_op jit(solution)/shard_map/ppermute | solution.py:316
  48.5 11.2 %collective-permute-start.9 = (bf16[672,128]{1,0:T(8,128)(2,1)S(1)}, bf16[672,128]{1,0:T(8,128)(2,1)S(1)}, u32[]{:S(2)}, u32[]{:S(2)}) collective-permute-start(bf16[672,128]{1,0:T(8,128)(2,1)S(1)} %get-tuple-element.40), channel_id=1, source_target_pairs={{0,16},{16,0},{32,48},{48,32},{64,80},{80,64},{96,112},{112,96},{1... | collective-permute-start | bytes 516104 | tf_op jit(solution)/shard_map/ppermute | solution.py:316
  50.9 9.6 %collective-permute-start.11 = (bf16[624,128]{1,0:T(8,128)(2,1)S(1)}, bf16[624,128]{1,0:T(8,128)(2,1)S(1)}, u32[]{:S(2)}, u32[]{:S(2)}) collective-permute-start(bf16[624,128]{1,0:T(8,128)(2,1)S(1)} %get-tuple-element.42), channel_id=1, source_target_pairs={{0,240},{16,32},{32,16},{48,64},{64,48},{80,96},{96,80},{112,128},... | collective-permute-start | bytes 479240 | tf_op jit(solution)/shard_map/ppermute | solution.py:316
  54.8 4.9 %collective-permute-start.10 = (bf16[576,128]{1,0:T(8,128)(2,1)S(1)}, bf16[576,128]{1,0:T(8,128)(2,1)S(1)}, u32[]{:S(2)}, u32[]{:S(2)}) collective-permute-start(bf16[576,128]{1,0:T(8,128)(2,1)S(1)} %get-tuple-element.41), channel_id=1, source_target_pairs={{0,1},{1,0},{2,3},{3,2},{4,5},{5,4},{6,7},{7,6},{8,9},{9,8},{10,11... | collective-permute-start | bytes 442376 | tf_op jit(solution)/shard_map/ppermute | solution.py:316
  59.4 19.6 %copy-start.2 = (bf16[128,12,8,128]{3,2,1,0:T(8,128)(2,1)S(1)}, bf16[128,12,8,128]{3,2,1,0:T(8,128)(2,1)}, u32[]{:S(2)}) copy-start(bf16[128,12,8,128]{3,2,1,0:T(8,128)(2,1)} %param.5) | copy-start | bytes 9437188
  61.3 13.1 %collective-permute-start.12 = (bf16[672,128]{1,0:T(8,128)(2,1)S(1)}, bf16[672,128]{1,0:T(8,128)(2,1)S(1)}, u32[]{:S(2)}, u32[]{:S(2)}) collective-permute-start(bf16[672,128]{1,0:T(8,128)(2,1)S(1)} %get-tuple-element.44), channel_id=1, source_target_pairs={{0,15},{1,2},{2,1},{3,4},{4,3},{5,6},{6,5},{7,8},{8,7},{9,10},{10,... | collective-permute-start | bytes 516104 | tf_op jit(solution)/shard_map/ppermute | solution.py:316
  63.4 11.0 %collective-permute-start.13 = (bf16[672,128]{1,0:T(8,128)(2,1)S(1)}, bf16[672,128]{1,0:T(8,128)(2,1)S(1)}, u32[]{:S(2)}, u32[]{:S(2)}) collective-permute-start(bf16[672,128]{1,0:T(8,128)(2,1)S(1)} %get-tuple-element.45), channel_id=1, source_target_pairs={{0,16},{16,0},{32,48},{48,32},{64,80},{80,64},{96,112},{112,96},{1... | collective-permute-start | bytes 516104 | tf_op jit(solution)/shard_map/ppermute | solution.py:316
  65.4 9.9 %collective-permute-start.15 = (bf16[624,128]{1,0:T(8,128)(2,1)S(1)}, bf16[624,128]{1,0:T(8,128)(2,1)S(1)}, u32[]{:S(2)}, u32[]{:S(2)}) collective-permute-start(bf16[624,128]{1,0:T(8,128)(2,1)S(1)} %get-tuple-element.47), channel_id=1, source_target_pairs={{0,240},{16,32},{32,16},{48,64},{64,48},{80,96},{96,80},{112,128},... | collective-permute-start | bytes 479240 | tf_op jit(solution)/shard_map/ppermute | solution.py:316
  69.4 5.0 %collective-permute-start.14 = (bf16[576,128]{1,0:T(8,128)(2,1)S(1)}, bf16[576,128]{1,0:T(8,128)(2,1)S(1)}, u32[]{:S(2)}, u32[]{:S(2)}) collective-permute-start(bf16[576,128]{1,0:T(8,128)(2,1)S(1)} %get-tuple-element.46), channel_id=1, source_target_pairs={{0,1},{1,0},{2,3},{3,2},{4,5},{5,4},{6,7},{7,6},{8,9},{9,8},{10,11... | collective-permute-start | bytes 442376 | tf_op jit(solution)/shard_map/ppermute | solution.py:316
  76.0 8.0 %collective-permute-start.16 = (bf16[8,12288]{1,0:T(8,128)(2,1)S(1)}, bf16[8,12288]{1,0:T(8,128)(2,1)S(1)}, u32[]{:S(2)}, u32[]{:S(2)}) collective-permute-start(bf16[8,12288]{1,0:T(8,128)(2,1)S(1)} %convert_element_type.43), channel_id=1, source_target_pairs={{0,256},{256,0},{1,257},{257,1},{2,258},{258,2},{3,259},{259,3},{4... | collective-permute-start | bytes 589832 | tf_op jit(solution)/shard_map/ppermute | solution.py:335
  120.1 7.9 %collective-permute-start.18 = (bf16[8,12288]{1,0:T(8,128)(2,1)S(1)}, bf16[8,12288]{1,0:T(8,128)(2,1)S(1)}, u32[]{:S(2)}, u32[]{:S(2)}) collective-permute-start(bf16[8,12288]{1,0:T(8,128)(2,1)S(1)} %get-tuple-element.54), channel_id=1, source_target_pairs={{0,256},{256,0},{1,257},{257,1},{2,258},{258,2},{3,259},{259,3},{4... | collective-permute-start | bytes 589832 | tf_op jit(solution)/shard_map/ppermute | solution.py:335
  122.3 9.9 %collective-permute-start.17 = (bf16[8,12288]{1,0:T(8,128)(2,1)S(1)}, bf16[8,12288]{1,0:T(8,128)(2,1)S(1)}, u32[]{:S(2)}, u32[]{:S(2)}) collective-permute-start(bf16[8,12288]{1,0:T(8,128)(2,1)S(1)} %get-tuple-element.55), channel_id=1, source_target_pairs={{0,256},{256,0},{1,257},{257,1},{2,258},{258,2},{3,259},{259,3},{4... | collective-permute-start | bytes 589832 | tf_op jit(solution)/shard_map/ppermute | solution.py:335
  147.9 13.2 %all-to-all-start.3 = ((f32[16,8,128]{2,1,0:T(8,128)}), f32[16,8,128]{2,1,0:T(8,128)S(1)}, u32[]{:S(2)}, u32[]{:S(2)}) async-start(f32[16,8,128]{2,1,0:T(8,128)} %broadcast_in_dim.11), calls=%async_computation.3 | async-start | bytes 131072 | tf_op jit(solution)/shard_map/all_to_all | solution.py:330

commit v12 on v8

--- a/solution.py
+++ b/solution.py
@@ -123,7 +123,7 @@
                 total = total + weights[k] * sum(near[1:], near[0])
         return total
 
-    @pl.loop(0, size_y)
+    @pl.loop(0, size_y, unroll=4)
     def _(y):
         line = [field_ref[x, y] for x in range(size_x)]
         for x in range(size_x):
@@ -133,7 +133,7 @@
                 total = total - previous_ref[x, y]
             total_ref[x, y] = inside(total, line, x)
 
-    @pl.loop(0, size_x)
+    @pl.loop(0, size_x, unroll=4)
     def _(x):
         line = [field_ref[x, y] for y in range(size_y)]
         for y in range(size_y):
@@ -154,13 +154,13 @@
                 total = total + weights[k] * line[WIDTH + at + k - size]
         return total
 
-    @pl.loop(0, size_y)
+    @pl.loop(0, size_y, unroll=4)
     def _(y):
         line = [halo_x[k, y] for k in range(2 * WIDTH)]
         for x in range(size_x):
             total_ref[x, y] = outside(inner_ref[x, y], line, x, size_x)
 
-    @pl.loop(0, size_x)
+    @pl.loop(0, size_x, unroll=4)
     def _(x):
         line = [halo_y[x, k] for k in range(2 * WIDTH)]
         for y in range(size_y):
@@ -313,7 +313,7 @@
     got_other = other_band(mine.astype(jnp.bfloat16)).astype(jnp.float32)
     projected = filtered - mine - got
     projected_other = rounded_other.astype(jnp.float32) - theirs - got_other
-    exact = functools.partial(rows_dot, precision=lax.Precision.HIGHEST)
+    exact = functools.partial(rows_dot, precision=lax.Precision.HIGH)
     partial_gram = exact(projected, jnp.concatenate([projected, projected_other], axis=0))
     turned = jnp.roll(partial_gram, own_count, axis=1)
     partial_gram = jnp.where(lax.axis_index("band") == 0, partial_gram, turned)

time: 163 us -> 163 us (level)
  no operation moved by 1% of the time
where the time goes in v12:
time: 163 us; the launch traced here: 162 us
  starting transfers between devices  77.3 us (47%)
  blocking collectives  50.2 us (31%)
  waiting for transfers between devices  17.7 us (11%)
  Pallas kernels  7.67 us (5%)
  local copies, waits for them, and re-layouts  3.41 us (2%)
  matrix products  3.39 us (2%)
    ppermute x16, starting transfers between devices, swapped(): lax.ppermute(values, axis, [(i, (i + step(i)) % count) for i in range(cou...  63.3 us
    all_to_all x3, blocking collectives, sum_over_grid(): lax.all_to_all(sent, axis, 0, 0).astype(jnp.float32)  50.2 us
    ppermute x3, waiting for transfers between devices, other_band(): return lax.ppermute(values, 'band', [(0, 1), (1, 0)])  10.2 us
    ppermute x3, starting transfers between devices, other_band(): return lax.ppermute(values, 'band', [(0, 1), (1, 0)])  8.16 us
    all_to_all x1, waiting for transfers between devices, sum_over_grid(): lax.all_to_all(sent, axis, 0, 0).astype(jnp.float32)  6.57 us
    all_to_all x1, starting transfers between devices, sum_over_grid(): lax.all_to_all(sent, axis, 0, 0).astype(jnp.float32)  5.86 us
    pallas_call x4, Pallas kernels, filter_step(): pl.pallas_call(functools.partial(outer_kernel, 1.0 if previous is None el...  3.85 us
  transfers between devices with their start and end apart: 20, of which 7 were waited for; matrix products, arithmetic and copies ran while one was open for 1% of the time, Pallas kernels for 2%

profile of v12, /device:TPU:1, one launch (start us, length us, event | category | flops | bytes accessed | tf_op | source)
XLA Modules:
  0.0 161.7 jit_solution(6874380189790388198)
XLA Ops:
  0.7 1.0 copy-done
  2.6 6.0 %collective-permute-start = (bf16[672,128]{1,0:T(8,128)(2,1)S(1)}, bf16[672,128]{1,0:T(8,128)(2,1)S(1)}, u32[]{:S(2)}, u32[]{:S(2)}) collective-permute-start(bf16[672,128]{1,0:T(8,128)(2,1)S(1)} %get-tuple-element.29), channel_id=1, source_target_pairs={{0,15},{1,2},{2,1},{3,4},{4,3},{5,6},{6,5},{7,8},{8,7},{9,10},{10,... | collective-permute-start | bytes 516104 | tf_op jit(solution)/shard_map/ppermute | solution.py:258
  8.6 3.5 %collective-permute-start.1 = (bf16[576,128]{1,0:T(8,128)(2,1)S(1)}, bf16[576,128]{1,0:T(8,128)(2,1)S(1)}, u32[]{:S(2)}, u32[]{:S(2)}) collective-permute-start(bf16[576,128]{1,0:T(8,128)(2,1)S(1)} %get-tuple-element.30), channel_id=1, source_target_pairs={{0,16},{16,0},{32,48},{48,32},{64,80},{80,64},{96,112},{112,96},{1... | collective-permute-start | bytes 442376 | tf_op jit(solution)/shard_map/ppermute | solution.py:258
  12.2 10.2 %collective-permute-start.2 = (bf16[576,128]{1,0:T(8,128)(2,1)S(1)}, bf16[576,128]{1,0:T(8,128)(2,1)S(1)}, u32[]{:S(2)}, u32[]{:S(2)}) collective-permute-start(bf16[576,128]{1,0:T(8,128)(2,1)S(1)} %get-tuple-element.31), channel_id=1, source_target_pairs={{0,240},{16,32},{32,16},{48,64},{64,48},{80,96},{96,80},{112,128},... | collective-permute-start | bytes 442376 | tf_op jit(solution)/shard_map/ppermute | solution.py:258
  22.4 4.8 %collective-permute-start.3 = (bf16[576,128]{1,0:T(8,128)(2,1)S(1)}, bf16[576,128]{1,0:T(8,128)(2,1)S(1)}, u32[]{:S(2)}, u32[]{:S(2)}) collective-permute-start(bf16[576,128]{1,0:T(8,128)(2,1)S(1)} %get-tuple-element.32), channel_id=1, source_target_pairs={{0,1},{1,0},{2,3},{3,2},{4,5},{5,4},{6,7},{7,6},{8,9},{9,8},{10,11... | collective-permute-start | bytes 442376 | tf_op jit(solution)/shard_map/ppermute | solution.py:258
  28.8 1.0 shard_map.53
  29.8 1.9 %collective-permute-start.4 = (bf16[672,128]{1,0:T(8,128)(2,1)S(1)}, bf16[672,128]{1,0:T(8,128)(2,1)S(1)}, u32[]{:S(2)}, u32[]{:S(2)}) collective-permute-start(bf16[672,128]{1,0:T(8,128)(2,1)S(1)} %get-tuple-element.34), channel_id=1, source_target_pairs={{0,15},{1,2},{2,1},{3,4},{4,3},{5,6},{6,5},{7,8},{8,7},{9,10},{10,... | collective-permute-start | bytes 516104 | tf_op jit(solution)/shard_map/ppermute | solution.py:258
  31.7 1.9 %collective-permute-start.5 = (bf16[576,128]{1,0:T(8,128)(2,1)S(1)}, bf16[576,128]{1,0:T(8,128)(2,1)S(1)}, u32[]{:S(2)}, u32[]{:S(2)}) collective-permute-start(bf16[576,128]{1,0:T(8,128)(2,1)S(1)} %get-tuple-element.35), channel_id=1, source_target_pairs={{0,16},{16,0},{32,48},{48,32},{64,80},{80,64},{96,112},{112,96},{1... | collective-permute-start | bytes 442376 | tf_op jit(solution)/shard_map/ppermute | solution.py:258
  33.6 3.4 %collective-permute-start.6 = (bf16[576,128]{1,0:T(8,128)(2,1)S(1)}, bf16[576,128]{1,0:T(8,128)(2,1)S(1)}, u32[]{:S(2)}, u32[]{:S(2)}) collective-permute-start(bf16[576,128]{1,0:T(8,128)(2,1)S(1)} %get-tuple-element.36), channel_id=1, source_target_pairs={{0,240},{16,32},{32,16},{48,64},{64,48},{80,96},{96,80},{112,128},... | collective-permute-start | bytes 442376 | tf_op jit(solution)/shard_map/ppermute | solution.py:258
  37.1 3.2 %collective-permute-start.7 = (bf16[576,128]{1,0:T(8,128)(2,1)S(1)}, bf16[576,128]{1,0:T(8,128)(2,1)S(1)}, u32[]{:S(2)}, u32[]{:S(2)}) collective-permute-start(bf16[576,128]{1,0:T(8,128)(2,1)S(1)} %get-tuple-element.37), channel_id=1, source_target_pairs={{0,1},{1,0},{2,3},{3,2},{4,5},{5,4},{6,7},{7,6},{8,9},{9,8},{10,11... | collective-permute-start | bytes 442376 | tf_op jit(solution)/shard_map/ppermute | solution.py:258
  41.4 1.0 shard_map.55
  42.4 5.6 %collective-permute-start.8 = (bf16[672,128]{1,0:T(8,128)(2,1)S(1)}, bf16[672,128]{1,0:T(8,128)(2,1)S(1)}, u32[]{:S(2)}, u32[]{:S(2)}) collective-permute-start(bf16[672,128]{1,0:T(8,128)(2,1)S(1)} %get-tuple-element.39), channel_id=1, source_target_pairs={{0,15},{1,2},{2,1},{3,4},{4,3},{5,6},{6,5},{7,8},{8,7},{9,10},{10,... | collective-permute-start | bytes 516104 | tf_op jit(solution)/shard_map/ppermute | solution.py:258
  48.1 2.4 %collective-permute-start.9 = (bf16[576,128]{1,0:T(8,128)(2,1)S(1)}, bf16[576,128]{1,0:T(8,128)(2,1)S(1)}, u32[]{:S(2)}, u32[]{:S(2)}) collective-permute-start(bf16[576,128]{1,0:T(8,128)(2,1)S(1)} %get-tuple-element.40), channel_id=1, source_target_pairs={{0,16},{16,0},{32,48},{48,32},{64,80},{80,64},{96,112},{112,96},{1... | collective-permute-start | bytes 442376 | tf_op jit(solution)/shard_map/ppermute | solution.py:258
  50.5 4.3 %collective-permute-start.10 = (bf16[576,128]{1,0:T(8,128)(2,1)S(1)}, bf16[576,128]{1,0:T(8,128)(2,1)S(1)}, u32[]{:S(2)}, u32[]{:S(2)}) collective-permute-start(bf16[576,128]{1,0:T(8,128)(2,1)S(1)} %get-tuple-element.41), channel_id=1, source_target_pairs={{0,240},{16,32},{32,16},{48,64},{64,48},{80,96},{96,80},{112,128},... | collective-permute-start | bytes 442376 | tf_op jit(solution)/shard_map/ppermute | solution.py:258
  54.8 3.9 %collective-permute-start.11 = (bf16[576,128]{1,0:T(8,128)(2,1)S(1)}, bf16[576,128]{1,0:T(8,128)(2,1)S(1)}, u32[]{:S(2)}, u32[]{:S(2)}) collective-permute-start(bf16[576,128]{1,0:T(8,128)(2,1)S(1)} %get-tuple-element.42), channel_id=1, source_target_pairs={{0,1},{1,0},{2,3},{3,2},{4,5},{5,4},{6,7},{7,6},{8,9},{9,8},{10,11... | collective-permute-start | bytes 442376 | tf_op jit(solution)/shard_map/ppermute | solution.py:258
  59.6 1.0 shard_map.57
  60.6 2.3 %collective-permute-start.12 = (bf16[672,128]{1,0:T(8,128)(2,1)S(1)}, bf16[672,128]{1,0:T(8,128)(2,1)S(1)}, u32[]{:S(2)}, u32[]{:S(2)}) collective-permute-start(bf16[672,128]{1,0:T(8,128)(2,1)S(1)} %get-tuple-element.44), channel_id=1, source_target_pairs={{0,15},{1,2},{2,1},{3,4},{4,3},{5,6},{6,5},{7,8},{8,7},{9,10},{10,... | collective-permute-start | bytes 516104 | tf_op jit(solution)/shard_map/ppermute | solution.py:258
  63.0 1.9 %collective-permute-start.13 = (bf16[576,128]{1,0:T(8,128)(2,1)S(1)}, bf16[576,128]{1,0:T(8,128)(2,1)S(1)}, u32[]{:S(2)}, u32[]{:S(2)}) collective-permute-start(bf16[576,128]{1,0:T(8,128)(2,1)S(1)} %get-tuple-element.45), channel_id=1, source_target_pairs={{0,16},{16,0},{32,48},{48,32},{64,80},{80,64},{96,112},{112,96},{1... | collective-permute-start | bytes 442376 | tf_op jit(solution)/shard_map/ppermute | solution.py:258
  64.9 4.6 %collective-permute-start.14 = (bf16[576,128]{1,0:T(8,128)(2,1)S(1)}, bf16[576,128]{1,0:T(8,128)(2,1)S(1)}, u32[]{:S(2)}, u32[]{:S(2)}) collective-permute-start(bf16[576,128]{1,0:T(8,128)(2,1)S(1)} %get-tuple-element.46), channel_id=1, source_target_pairs={{0,240},{16,32},{32,16},{48,64},{64,48},{80,96},{96,80},{112,128},... | collective-permute-start | bytes 442376 | tf_op jit(solution)/shard_map/ppermute | solution.py:258
  69.5 3.3 %collective-permute-start.15 = (bf16[576,128]{1,0:T(8,128)(2,1)S(1)}, bf16[576,128]{1,0:T(8,128)(2,1)S(1)}, u32[]{:S(2)}, u32[]{:S(2)}) collective-permute-start(bf16[576,128]{1,0:T(8,128)(2,1)S(1)} %get-tuple-element.47), channel_id=1, source_target_pairs={{0,1},{1,0},{2,3},{3,2},{4,5},{5,4},{6,7},{7,6},{8,9},{9,8},{10,11... | collective-permute-start | bytes 442376 | tf_op jit(solution)/shard_map/ppermute | solution.py:258
  74.7 2.9 %collective-permute-start.16 = (bf16[8,12288]{1,0:T(8,128)(2,1)S(1)}, bf16[8,12288]{1,0:T(8,128)(2,1)S(1)}, u32[]{:S(2)}, u32[]{:S(2)}) collective-permute-start(bf16[8,12288]{1,0:T(8,128)(2,1)S(1)} %convert_element_type.43), channel_id=1, source_target_pairs={{0,256},{256,0},{1,257},{257,1},{2,258},{258,2},{3,259},{259,3},{4... | collective-permute-start | bytes 589832 | tf_op jit(solution)/shard_map/ppermute | solution.py:277
  78.5 3.4 %collective-permute-done.16 = bf16[8,12288]{1,0:T(8,128)(2,1)S(1)} collective-permute-done((bf16[8,12288]{1,0:T(8,128)(2,1)S(1)}, bf16[8,12288]{1,0:T(8,128)(2,1)S(1)}, u32[]{:S(2)}, u32[]{:S(2)}) %collective-permute-start.16) | collective-permute-done | bytes 196640 | tf_op jit(solution)/shard_map/ppermute | solution.py:277
  82.9 18.2 %all_to_all.20 = f16[16,16,128]{2,1,0:T(8,128)(2,1)S(1)} all-to-all(f16[16,16,128]{2,1,0:T(8,128)(2,1)S(1)} %broadcast_in_dim.8), channel_id=1, replica_groups=mesh['band'=2,'dx'=16,'dy'=16] {'dx'}, dimensions={0} | all-to-all | bytes 131072 | tf_op jit(solution)/shard_map/all_to_all | solution.py:272
  101.2 17.8 %all_to_all.21 = f16[16,16,128]{2,1,0:T(8,128)(2,1)S(1)} all-to-all(f16[16,16,128]{2,1,0:T(8,128)(2,1)S(1)} %broadcast_in_dim.9), channel_id=1, replica_groups=mesh['band'=2,'dx'=16,'dy'=16] {'dy'}, dimensions={0} | all-to-all | bytes 131072 | tf_op jit(solution)/shard_map/all_to_all | solution.py:272
  119.0 1.0 fusion
  120.0 2.2 %collective-permute-start.18 = (bf16[8,12288]{1,0:T(8,128)(2,1)S(1)}, bf16[8,12288]{1,0:T(8,128)(2,1)S(1)}, u32[]{:S(2)}, u32[]{:S(2)}) collective-permute-start(bf16[8,12288]{1,0:T(8,128)(2,1)S(1)} %get-tuple-element.54), channel_id=1, source_target_pairs={{0,256},{256,0},{1,257},{257,1},{2,258},{258,2},{3,259},{259,3},{4... | collective-permute-start | bytes 589832 | tf_op jit(solution)/shard_map/ppermute | solution.py:277
  122.2 3.1 %collective-permute-start.17 = (bf16[8,12288]{1,0:T(8,128)(2,1)S(1)}, bf16[8,12288]{1,0:T(8,128)(2,1)S(1)}, u32[]{:S(2)}, u32[]{:S(2)}) collective-permute-start(bf16[8,12288]{1,0:T(8,128)(2,1)S(1)} %get-tuple-element.55), channel_id=1, source_target_pairs={{0,256},{256,0},{1,257},{257,1},{2,258},{258,2},{3,259},{259,3},{4... | collective-permute-start | bytes 589832 | tf_op jit(solution)/shard_map/ppermute | solution.py:277
  125.3 2.6 %collective-permute-done.18 = bf16[8,12288]{1,0:T(8,128)(2,1)S(1)} collective-permute-done((bf16[8,12288]{1,0:T(8,128)(2,1)S(1)}, bf16[8,12288]{1,0:T(8,128)(2,1)S(1)}, u32[]{:S(2)}, u32[]{:S(2)}) %collective-permute-start.18) | collective-permute-done | bytes 196640 | tf_op jit(solution)/shard_map/ppermute | solution.py:277
  127.9 4.2 %collective-permute-done.17 = bf16[8,12288]{1,0:T(8,128)(2,1)S(1)} collective-permute-done((bf16[8,12288]{1,0:T(8,128)(2,1)S(1)}, bf16[8,12288]{1,0:T(8,128)(2,1)S(1)}, u32[]{:S(2)}, u32[]{:S(2)}) %collective-permute-start.17) | collective-permute-done | bytes 196640 | tf_op jit(solution)/shard_map/ppermute | solution.py:277
  132.9 14.2 %all_to_all.22 = f32[16,8,128]{2,1,0:T(8,128)S(1)} all-to-all(f32[16,8,128]{2,1,0:T(8,128)S(1)} %broadcast_in_dim.10), channel_id=1, replica_groups=mesh['band'=2,'dx'=16,'dy'=16] {'dx'}, dimensions={0} | all-to-all | bytes 131072 | tf_op jit(solution)/shard_map/all_to_all | solution.py:272
  147.8 5.9 %all-to-all-start.3 = ((f32[16,8,128]{2,1,0:T(8,128)}), f32[16,8,128]{2,1,0:T(8,128)S(1)}, u32[]{:S(2)}, u32[]{:S(2)}) async-start(f32[16,8,128]{2,1,0:T(8,128)} %broadcast_in_dim.11), calls=%async_computation.3 | async-start | bytes 131072 | tf_op jit(solution)/shard_map/all_to_all | solution.py:272
  154.5 6.6 %all-to-all-done.3 = f32[16,8,128]{2,1,0:T(8,128)S(1)} async-done(((f32[16,8,128]{2,1,0:T(8,128)}), f32[16,8,128]{2,1,0:T(8,128)S(1)}, u32[]{:S(2)}, u32[]{:S(2)}) %all-to-all-start.3) | async-done | bytes 65568 | tf_op jit(solution)/shard_map/all_to_all | solution.py:272
  (50 shorter events, 11.4 us)
Async XLA Ops:
  0.7 1.0 copy-start
  2.6 26.2 %collective-permute-start = (bf16[672,128]{1,0:T(8,128)(2,1)S(1)}, bf16[672,128]{1,0:T(8,128)(2,1)S(1)}, u32[]{:S(2)}, u32[]{:S(2)}) collective-permute-start(bf16[672,128]{1,0:T(8,128)(2,1)S(1)} %get-tuple-element.29), channel_id=1, source_target_pairs={{0,15},{1,2},{2,1},{3,4},{4,3},{5,6},{6,5},{7,8},{8,7},{9,10},{10,... | collective-permute-start | bytes 516104 | tf_op jit(solution)/shard_map/ppermute | solution.py:258
  8.6 20.1 %collective-permute-start.1 = (bf16[576,128]{1,0:T(8,128)(2,1)S(1)}, bf16[576,128]{1,0:T(8,128)(2,1)S(1)}, u32[]{:S(2)}, u32[]{:S(2)}) collective-permute-start(bf16[576,128]{1,0:T(8,128)(2,1)S(1)} %get-tuple-element.30), channel_id=1, source_target_pairs={{0,16},{16,0},{32,48},{48,32},{64,80},{80,64},{96,112},{112,96},{1... | collective-permute-start | bytes 442376 | tf_op jit(solution)/shard_map/ppermute | solution.py:258
  12.2 16.6 %collective-permute-start.2 = (bf16[576,128]{1,0:T(8,128)(2,1)S(1)}, bf16[576,128]{1,0:T(8,128)(2,1)S(1)}, u32[]{:S(2)}, u32[]{:S(2)}) collective-permute-start(bf16[576,128]{1,0:T(8,128)(2,1)S(1)} %get-tuple-element.31), channel_id=1, source_target_pairs={{0,240},{16,32},{32,16},{48,64},{64,48},{80,96},{96,80},{112,128},... | collective-permute-start | bytes 442376 | tf_op jit(solution)/shard_map/ppermute | solution.py:258
  22.4 6.4 %collective-permute-start.3 = (bf16[576,128]{1,0:T(8,128)(2,1)S(1)}, bf16[576,128]{1,0:T(8,128)(2,1)S(1)}, u32[]{:S(2)}, u32[]{:S(2)}) collective-permute-start(bf16[576,128]{1,0:T(8,128)(2,1)S(1)} %get-tuple-element.32), channel_id=1, source_target_pairs={{0,1},{1,0},{2,3},{3,2},{4,5},{5,4},{6,7},{7,6},{8,9},{9,8},{10,11... | collective-permute-start | bytes 442376 | tf_op jit(solution)/shard_map/ppermute | solution.py:258
  27.2 0.8 copy-start.1
  29.8 11.7 %collective-permute-start.4 = (bf16[672,128]{1,0:T(8,128)(2,1)S(1)}, bf16[672,128]{1,0:T(8,128)(2,1)S(1)}, u32[]{:S(2)}, u32[]{:S(2)}) collective-permute-start(bf16[672,128]{1,0:T(8,128)(2,1)S(1)} %get-tuple-element.34), channel_id=1, source_target_pairs={{0,15},{1,2},{2,1},{3,4},{4,3},{5,6},{6,5},{7,8},{8,7},{9,10},{10,... | collective-permute-start | bytes 516104 | tf_op jit(solution)/shard_map/ppermute | solution.py:258
  31.7 9.3 %collective-permute-start.5 = (bf16[576,128]{1,0:T(8,128)(2,1)S(1)}, bf16[576,128]{1,0:T(8,128)(2,1)S(1)}, u32[]{:S(2)}, u32[]{:S(2)}) collective-permute-start(bf16[576,128]{1,0:T(8,128)(2,1)S(1)} %get-tuple-element.35), channel_id=1, source_target_pairs={{0,16},{16,0},{32,48},{48,32},{64,80},{80,64},{96,112},{112,96},{1... | collective-permute-start | bytes 442376 | tf_op jit(solution)/shard_map/ppermute | solution.py:258
  33.6 7.8 %collective-permute-start.6 = (bf16[576,128]{1,0:T(8,128)(2,1)S(1)}, bf16[576,128]{1,0:T(8,128)(2,1)S(1)}, u32[]{:S(2)}, u32[]{:S(2)}) collective-permute-start(bf16[576,128]{1,0:T(8,128)(2,1)S(1)} %get-tuple-element.36), channel_id=1, source_target_pairs={{0,240},{16,32},{32,16},{48,64},{64,48},{80,96},{96,80},{112,128},... | collective-permute-start | bytes 442376 | tf_op jit(solution)/shard_map/ppermute | solution.py:258
  37.1 4.4 %collective-permute-start.7 = (bf16[576,128]{1,0:T(8,128)(2,1)S(1)}, bf16[576,128]{1,0:T(8,128)(2,1)S(1)}, u32[]{:S(2)}, u32[]{:S(2)}) collective-permute-start(bf16[576,128]{1,0:T(8,128)(2,1)S(1)} %get-tuple-element.37), channel_id=1, source_target_pairs={{0,1},{1,0},{2,3},{3,2},{4,5},{5,4},{6,7},{7,6},{8,9},{9,8},{10,11... | collective-permute-start | bytes 442376 | tf_op jit(solution)/shard_map/ppermute | solution.py:258
  41.0 36.6 %copy-start.2 = (bf16[128,12,8,128]{3,2,1,0:T(8,128)(2,1)S(1)}, bf16[128,12,8,128]{3,2,1,0:T(8,128)(2,1)}, u32[]{:S(2)}) copy-start(bf16[128,12,8,128]{3,2,1,0:T(8,128)(2,1)} %param.5) | copy-start | bytes 9437188
  42.4 17.2 %collective-permute-start.8 = (bf16[672,128]{1,0:T(8,128)(2,1)S(1)}, bf16[672,128]{1,0:T(8,128)(2,1)S(1)}, u32[]{:S(2)}, u32[]{:S(2)}) collective-permute-start(bf16[672,128]{1,0:T(8,128)(2,1)S(1)} %get-tuple-element.39), channel_id=1, source_target_pairs={{0,15},{1,2},{2,1},{3,4},{4,3},{5,6},{6,5},{7,8},{8,7},{9,10},{10,... | collective-permute-start | bytes 516104 | tf_op jit(solution)/shard_map/ppermute | solution.py:258
  48.1 11.4 %collective-permute-start.9 = (bf16[576,128]{1,0:T(8,128)(2,1)S(1)}, bf16[576,128]{1,0:T(8,128)(2,1)S(1)}, u32[]{:S(2)}, u32[]{:S(2)}) collective-permute-start(bf16[576,128]{1,0:T(8,128)(2,1)S(1)} %get-tuple-element.40), channel_id=1, source_target_pairs={{0,16},{16,0},{32,48},{48,32},{64,80},{80,64},{96,112},{112,96},{1... | collective-permute-start | bytes 442376 | tf_op jit(solution)/shard_map/ppermute | solution.py:258
  50.5 9.0 %collective-permute-start.10 = (bf16[576,128]{1,0:T(8,128)(2,1)S(1)}, bf16[576,128]{1,0:T(8,128)(2,1)S(1)}, u32[]{:S(2)}, u32[]{:S(2)}) collective-permute-start(bf16[576,128]{1,0:T(8,128)(2,1)S(1)} %get-tuple-element.41), channel_id=1, source_target_pairs={{0,240},{16,32},{32,16},{48,64},{64,48},{80,96},{96,80},{112,128},... | collective-permute-start | bytes 442376 | tf_op jit(solution)/shard_map/ppermute | solution.py:258
  54.8 4.9 %collective-permute-start.11 = (bf16[576,128]{1,0:T(8,128)(2,1)S(1)}, bf16[576,128]{1,0:T(8,128)(2,1)S(1)}, u32[]{:S(2)}, u32[]{:S(2)}) collective-permute-start(bf16[576,128]{1,0:T(8,128)(2,1)S(1)} %get-tuple-element.42), channel_id=1, source_target_pairs={{0,1},{1,0},{2,3},{3,2},{4,5},{5,4},{6,7},{7,6},{8,9},{9,8},{10,11... | collective-permute-start | bytes 442376 | tf_op jit(solution)/shard_map/ppermute | solution.py:258
  60.6 13.1 %collective-permute-start.12 = (bf16[672,128]{1,0:T(8,128)(2,1)S(1)}, bf16[672,128]{1,0:T(8,128)(2,1)S(1)}, u32[]{:S(2)}, u32[]{:S(2)}) collective-permute-start(bf16[672,128]{1,0:T(8,128)(2,1)S(1)} %get-tuple-element.44), channel_id=1, source_target_pairs={{0,15},{1,2},{2,1},{3,4},{4,3},{5,6},{6,5},{7,8},{8,7},{9,10},{10,... | collective-permute-start | bytes 516104 | tf_op jit(solution)/shard_map/ppermute | solution.py:258
  63.0 10.6 %collective-permute-start.13 = (bf16[576,128]{1,0:T(8,128)(2,1)S(1)}, bf16[576,128]{1,0:T(8,128)(2,1)S(1)}, u32[]{:S(2)}, u32[]{:S(2)}) collective-permute-start(bf16[576,128]{1,0:T(8,128)(2,1)S(1)} %get-tuple-element.45), channel_id=1, source_target_pairs={{0,16},{16,0},{32,48},{48,32},{64,80},{80,64},{96,112},{112,96},{1... | collective-permute-start | bytes 442376 | tf_op jit(solution)/shard_map/ppermute | solution.py:258
  64.9 8.6 %collective-permute-start.14 = (bf16[576,128]{1,0:T(8,128)(2,1)S(1)}, bf16[576,128]{1,0:T(8,128)(2,1)S(1)}, u32[]{:S(2)}, u32[]{:S(2)}) collective-permute-start(bf16[576,128]{1,0:T(8,128)(2,1)S(1)} %get-tuple-element.46), channel_id=1, source_target_pairs={{0,240},{16,32},{32,16},{48,64},{64,48},{80,96},{96,80},{112,128},... | collective-permute-start | bytes 442376 | tf_op jit(solution)/shard_map/ppermute | solution.py:258
  69.5 4.3 %collective-permute-start.15 = (bf16[576,128]{1,0:T(8,128)(2,1)S(1)}, bf16[576,128]{1,0:T(8,128)(2,1)S(1)}, u32[]{:S(2)}, u32[]{:S(2)}) collective-permute-start(bf16[576,128]{1,0:T(8,128)(2,1)S(1)} %get-tuple-element.47), channel_id=1, source_target_pairs={{0,1},{1,0},{2,3},{3,2},{4,5},{5,4},{6,7},{7,6},{8,9},{9,8},{10,11... | collective-permute-start | bytes 442376 | tf_op jit(solution)/shard_map/ppermute | solution.py:258
  74.7 7.2 %collective-permute-start.16 = (bf16[8,12288]{1,0:T(8,128)(2,1)S(1)}, bf16[8,12288]{1,0:T(8,128)(2,1)S(1)}, u32[]{:S(2)}, u32[]{:S(2)}) collective-permute-start(bf16[8,12288]{1,0:T(8,128)(2,1)S(1)} %convert_element_type.43), channel_id=1, source_target_pairs={{0,256},{256,0},{1,257},{257,1},{2,258},{258,2},{3,259},{259,3},{4... | collective-permute-start | bytes 589832 | tf_op jit(solution)/shard_map/ppermute | solution.py:277
  120.0 7.9 %collective-permute-start.18 = (bf16[8,12288]{1,0:T(8,128)(2,1)S(1)}, bf16[8,12288]{1,0:T(8,128)(2,1)S(1)}, u32[]{:S(2)}, u32[]{:S(2)}) collective-permute-start(bf16[8,12288]{1,0:T(8,128)(2,1)S(1)} %get-tuple-element.54), channel_id=1, source_target_pairs={{0,256},{256,0},{1,257},{257,1},{2,258},{258,2},{3,259},{259,3},{4... | collective-permute-start | bytes 589832 | tf_op jit(solution)/shard_map/ppermute | solution.py:277
  122.2 9.9 %collective-permute-start.17 = (bf16[8,12288]{1,0:T(8,128)(2,1)S(1)}, bf16[8,12288]{1,0:T(8,128)(2,1)S(1)}, u32[]{:S(2)}, u32[]{:S(2)}) collective-permute-start(bf16[8,12288]{1,0:T(8,128)(2,1)S(1)} %get-tuple-element.55), channel_id=1, source_target_pairs={{0,256},{256,0},{1,257},{257,1},{2,258},{258,2},{3,259},{259,3},{4... | collective-permute-start | bytes 589832 | tf_op jit(solution)/shard_map/ppermute | solution.py:277
  147.8 13.2 %all-to-all-start.3 = ((f32[16,8,128]{2,1,0:T(8,128)}), f32[16,8,128]{2,1,0:T(8,128)S(1)}, u32[]{:S(2)}, u32[]{:S(2)}) async-start(f32[16,8,128]{2,1,0:T(8,128)} %broadcast_in_dim.11), calls=%async_computation.3 | async-start | bytes 131072 | tf_op jit(solution)/shard_map/all_to_all | solution.py:272
